TPU v7x, 32 devices: a whole 2x2x4 slice. The times are simulated.
32 devices in a mesh: groups: 2 (over x), seq: 8 (over z, y), exp: 2 (over core).
Axes of the slice: x: 2, y: 2, z: 4, core: 2. Of those that a mesh axis runs over, the one named last changes fastest.
Arguments:
- stream: bfloat16 [2048, 2048], P(('groups', 'seq', 'exp')), parts along dimension 0, may hold values from -5 to 5
- queries: bfloat16 [2048, 4096], P(('groups', 'seq'), 'exp'), parts along dimension 0, may hold values from -131 to 131
- key_rows: bfloat16 [2048, 512], P(('groups', 'seq'), 'exp'), parts along dimension 0, may hold values from -4 to 4
- value_rows: bfloat16 [2048, 512], P(('groups', 'seq'), 'exp'), parts along dimension 0, may hold values from -4 to 4
- out_weight: bfloat16 [2048, 4096], P('seq', 'exp'), may hold values from -0.375 to 0.375
- norm_gain: float32 [2048], replicated, may hold values from 0.1 to 1.9
- expert_ids: int32 [2048, 8], P(('groups', 'seq', 'exp')), parts along dimension 0, may hold values from 0 to 63, all different within a row; in each aligned block of 64 rows (0 to 63, 64 to 127, ...) at most 12 rows name the same one
- gate_weights: float32 [2048, 8], P(('groups', 'seq', 'exp')), parts along dimension 0, may hold values from 0.05 to 0.5
- expert_in: bfloat16 [64, 2048, 1536], P(('seq', 'exp')), may hold values from -0.125 to 0.125
- expert_out: bfloat16 [64, 768, 2048], P(('seq', 'exp')), may hold values from -0.21875 to 0.21875
Outputs:
- layer_out: bfloat16 [2048, 2048], P(('groups', 'seq', 'exp')), parts along dimension 0
There are 2 independent parts, one for each index of `groups`. A program takes and returns all parts, laid end to end along the dimension named above; an argument that names none is the same for every part. Nothing has to cross between parts.
Inputs may be any that keep to these rules, and one draw needn't show every extreme that they name: `expert_ids`: each row names 8 different experts. Among the 64 rows of one device (aligned blocks of rows), no expert is named more than 12 times, a bound that some block reaches.
All inputs are finite; a program needn't handle non-finite values.
Results may differ from a plain program's by a relative error of at most 0.0095.
Values may be sent and summed in bfloat16 or wider, within the bound.
No kernel may reach another device: no remote copies, remote signals or barrier semaphores. Data moves between devices by JAX's collectives and lax.ppermute only.
A program may use at most 128 MiB of HBM per device.

v0:
```python
import jax
import jax.numpy as jnp
from jax import lax
from jax.sharding import PartitionSpec as P

HD = 128
EXPERTS = 64
TOPK = 8
CAP = 12


neg_large = -1e30


def attend_piece(state, query_group, key_piece, value_piece, key_start, query_start):
    largest, total, summed = state
    length = key_piece.shape[0]
    groups = query_group.shape[1]
    head_size = query_group.shape[3]
    rows = query_group.shape[0]
    keyed = key_piece.reshape(length, groups, head_size)
    valued = value_piece.reshape(length, groups, head_size)
    scores = jnp.einsum(
        "tghd,sgd->gths", query_group, keyed, preferred_element_type=jnp.float32
    ) / jnp.sqrt(jnp.float32(head_size))
    query_pos = query_start + jnp.arange(rows, dtype=jnp.int32)
    key_pos = key_start + jnp.arange(length, dtype=jnp.int32)
    allowed = (key_pos[None, :] <= query_pos[:, None])[None, :, None, :]
    scores = jnp.where(allowed, scores, neg_large)
    new_largest = jnp.maximum(largest, jnp.max(scores, axis=-1))
    rescale = jnp.exp(largest - new_largest)
    exps = jnp.where(allowed, jnp.exp(scores - new_largest[..., None]), 0.0)
    total = total * rescale + jnp.sum(exps, axis=-1)
    summed = summed * rescale[..., None] + jnp.einsum(
        "gths,sgd->gthd", exps.astype(jnp.bfloat16), valued, preferred_element_type=jnp.float32
    )
    return (new_largest, total, summed)


def on_device(
    stream,
    queries,
    key_rows,
    value_rows,
    out_weight,
    norm_gain,
    expert_ids,
    gate_weights,
    expert_in,
    expert_out,
):
    rows = queries.shape[0]
    local_groups = key_rows.shape[1] // HD
    per_group = queries.shape[1] // (local_groups * HD)
    query_group = queries.reshape(rows, local_groups, per_group, HD)
    query_start = lax.axis_index("seq") * rows
    initial = (
        jnp.full((local_groups, rows, per_group), neg_large, jnp.float32),
        jnp.zeros((local_groups, rows, per_group), jnp.float32),
        jnp.zeros((local_groups, rows, per_group, HD), jnp.float32),
    )
    state = initial
    key_piece = lax.all_gather(key_rows, "seq", axis=0, tiled=True)
    value_piece = lax.all_gather(value_rows, "seq", axis=0, tiled=True)
    length = key_piece.shape[0]
    count = length // 512
    key_blocks = key_piece.reshape(count, 512, key_piece.shape[1])
    value_blocks = value_piece.reshape(count, 512, value_piece.shape[1])
    offsets = jnp.arange(count, dtype=jnp.int32) * 512

    def step(carry, block):
        return (attend_piece(carry, query_group, block[0], block[1], block[2], query_start), None)

    state, unused = lax.scan(step, state, (key_blocks, value_blocks, offsets))
    largest, total, summed = state
    context = (
        (summed / total[..., None]).transpose(1, 0, 2, 3).reshape(rows, -1).astype(jnp.bfloat16)
    )
    seq_count = lax.axis_size("seq")
    exp_count = lax.axis_size("exp")
    local_rows = stream.shape[0]
    partial_heads = lax.dot_general(
        context,
        lax.all_gather(out_weight, "seq", axis=0, tiled=True),
        (((1,), (1,)), ((), ())),
        preferred_element_type=jnp.float32,
    )
    attn_out = lax.psum_scatter(
        partial_heads.astype(jnp.bfloat16), "exp", scatter_dimension=0, tiled=True
    ).astype(jnp.float32)
    mixed = stream.astype(jnp.float32) + attn_out
    normed = (
        mixed * lax.rsqrt(jnp.mean(mixed * mixed, axis=-1, keepdims=True) + 1e-06) * norm_gain
    ).astype(jnp.bfloat16)
    width = normed.shape[1]
    flat_ids = expert_ids.reshape(-1)
    onehot = (flat_ids[:, None] == jnp.arange(EXPERTS, dtype=jnp.int32)[None, :]).astype(jnp.int32)
    earlier = jnp.cumsum(onehot, axis=0) - onehot
    slots = jnp.sum(earlier * onehot, axis=1)
    destination = flat_ids * CAP + slots
    chooser = (destination[None, :] == jnp.arange(EXPERTS * CAP, dtype=jnp.int32)[:, None]).astype(
        jnp.int32
    )
    chooser = jnp.sum(chooser.reshape(EXPERTS * CAP, local_rows, TOPK), axis=-1).astype(
        jnp.bfloat16
    )
    outgoing = (
        jnp.dot(chooser, normed, preferred_element_type=jnp.float32)
        .astype(jnp.bfloat16)
        .reshape(EXPERTS, CAP, width)
    )
    local_experts = expert_in.shape[0]
    hidden_units = expert_out.shape[1]
    sectioned = outgoing.reshape(seq_count, exp_count, local_experts, CAP, width)
    arrived = lax.all_to_all(
        lax.all_to_all(sectioned, "seq", split_axis=0, concat_axis=0, tiled=True),
        "exp",
        split_axis=1,
        concat_axis=1,
        tiled=True,
    )
    received = arrived.reshape(-1, CAP, width)
    senders = received.shape[0] // local_experts
    slots_here = received.shape[1]
    arranged = received.reshape(senders, local_experts, slots_here, width)
    gate_up = jnp.einsum("secd,edf->secf", arranged, expert_in, preferred_element_type=jnp.float32)
    act = (jax.nn.silu(gate_up[..., :hidden_units]) * gate_up[..., hidden_units:]).astype(
        jnp.bfloat16
    )
    result = jnp.einsum(
        "secf,efd->secd", act, expert_out, preferred_element_type=jnp.float32
    ).astype(jnp.bfloat16)
    finished = result.reshape(received.shape).reshape(sectioned.shape)
    back = lax.all_to_all(
        lax.all_to_all(finished, "seq", split_axis=0, concat_axis=0, tiled=True),
        "exp",
        split_axis=1,
        concat_axis=1,
        tiled=True,
    ).reshape(EXPERTS, CAP, width)
    picked = back.reshape(EXPERTS * CAP, width)[destination].reshape(local_rows, TOPK, width)
    combined = jnp.sum(gate_weights[..., None] * picked.astype(jnp.float32), axis=1)
    return (mixed + combined).astype(jnp.bfloat16)


def solution(mesh):
    in_specs = (
        P(("groups", "seq", "exp"), None),
        P(("groups", "seq"), "exp"),
        P(("groups", "seq"), "exp"),
        P(("groups", "seq"), "exp"),
        P("seq", "exp"),
        P(),
        P(("groups", "seq", "exp"), None),
        P(("groups", "seq", "exp"), None),
        P(("seq", "exp"), None, None),
        P(("seq", "exp"), None, None),
    )
    out_specs = P(("groups", "seq", "exp"), None)
    return jax.shard_map(
        on_device, mesh=mesh, in_specs=in_specs, out_specs=out_specs, check_vma=False
    )
```

profile of v0, /device:TPU:0, one launch (start us, length us, event | category | flops | bytes accessed | tf_op | source)
XLA Modules:
  0.0 391.7 jit_solution(11619472551129220449)
XLA Ops:
  9.0 35.0 %all_gather.9 = bf16[1024,256]{1,0:T(8,128)(2,1)S(1)} all-gather(bf16[128,256]{1,0:T(8,128)(2,1)} %param.14), channel_id=1, replica_groups=mesh['groups'=2,'seq'=8,'exp'=2] {'seq'}, dimensions={0}, use_global_device_ids=true | all-gather | bytes 589824 | tf_op jit(solution)/shard_map/all_gather | solution.py:63
  43.9 32.8 %all_gather.10 = bf16[1024,256]{1,0:T(8,128)(2,1)S(1)} all-gather(bf16[128,256]{1,0:T(8,128)(2,1)} %param.15), channel_id=1, replica_groups=mesh['groups'=2,'seq'=8,'exp'=2] {'seq'}, dimensions={0}, use_global_device_ids=true | all-gather | bytes 589824 | tf_op jit(solution)/shard_map/all_gather | solution.py:64
  76.7 23.1 %while.15 = (s32[]{:T(128)}, f32[2,128,8]{1,2,0:T(8,128)S(1)}, f32[2,128,8]{1,2,0:T(8,128)S(1)}, f32[2,128,8,128]{3,1,2,0:T(8,128)S(1)}, s32[2]{0:T(128)S(1)}, /...) while((s32[]{:T(128)}, f32[2,128,8]{1,2,0:T(8,128)S(1)}, ...), condition=%wide.region_3.4_spmd.clone, body=%wide.region_0.3_spmd.clone.sunk | while | flops 551365248 | bytes 18224280 | solution.py:74
  78.2 2.8 fusion.57
  81.0 3.2 fusion.58
  84.3 3.9 fusion.60
  89.7 2.8 fusion.57
  92.6 3.2 fusion.58
  95.9 3.9 %fusion.60 = f32[2,128,8,128]{3,1,2,0:T(8,128)S(1)} fusion(bf16[512,2,128,1]{0,2,3,1:T(8,128)(2,1)S(1)} %bitcast.103, f32[2,512,128,8]{2,1,3,0:T(8,128)} %get-tuple-element.210, f32[2,128,8]{1,2,0:T(8,128)S(1)} %select_maximum_fusion.2, pred[128,512]{0,1:T(8,128)(4,1)S(1)} %broadcast_compare_fusion.2, f32[2,128,8,128]{3,1,2,0:T(8,128)S(1)} %get-tuple-element.228, ...), kind=kOutput, calls=%fused_computation.8.clone.1 | convolution fusion | flops 274464768 | bytes 6635521 | tf_op jit(solution)/shard_map/while/body/eval_jaxpr/gths,sgd->gthd/dot_general | solution.py:34
  100.3 43.5 %all-gather.2.cloned.1.call-done = bf16[2048,2048]{1,0:T(8,128)(2,1)} async-done(((bf16[256,2048]{1,0:T(8,128)(2,1)}), bf16[2048,2048]{1,0:T(8,128)(2,1)}) %all-gather.2.cloned.1.call-update) | async-done | bytes 8388624 | tf_op jit(solution)/shard_map/all_gather | solution.py:84
  143.8 7.2 %convolution_convert_fusion.1 = bf16[128,2048]{1,0:T(8,128)(2,1)} fusion(bf16[128,2048]{0,1:T(8,128)(2,1)S(1)} %bitcast.106, bf16[2048,2048]{1,0:T(8,128)(2,1)} %all-gather.2.cloned.1.call-done), kind=kOutput, calls=%fused_computation.32 | convolution fusion | flops 1074003968 | bytes 9437184 | tf_op jit(solution)/shard_map/dot_general | solution.py:82
  154.3 3.7 reduce-scatter.2.cloned.1.call-done
  159.1 2.1 convolution_convert_fusion
  161.2 2.7 reshape_reshape.12
  163.9 4.9 %copy.76 = bf16[8,2,4,12,2048]{4,2,3,1,0:T(4,128)(2,1)S(1)} copy(bf16[8,2,4,12,2048]{4,3,2,1,0:T(8,128)(2,1)} %reshape_reshape.12) | data formatting | bytes 6291456 | tf_op jit(solution)/shard_map/reshape;reshape | solution.py:114
  168.8 76.7 %all_to_all.20 = bf16[8,2,4,12,2048]{4,2,3,1,0:T(4,128)(2,1)S(1)} all-to-all(bf16[8,2,4,12,2048]{4,2,3,1,0:T(4,128)(2,1)S(1)} %copy.76), channel_id=1, replica_groups=mesh['groups'=2,'seq'=8,'exp'=2] {'seq'}, dimensions={0} | all-to-all | bytes 6291456 | tf_op jit(solution)/shard_map/all_to_all | solution.py:116
  245.5 1.7 copy.77
  247.2 6.3 %all_to_all.21 = bf16[8,2,4,12,2048]{4,0,3,2,1:T(8,128)(2,1)S(1)} all-to-all(bf16[8,2,4,12,2048]{4,0,3,2,1:T(8,128)(2,1)S(1)} %copy.77), channel_id=1, replica_groups=mesh['groups'=2,'seq'=8,'exp'=2] {'exp'}, dimensions={1} | all-to-all | bytes 6291456 | tf_op jit(solution)/shard_map/all_to_all | solution.py:115
  253.5 4.9 %copy.78 = bf16[8,2,4,12,2048]{4,1,0,3,2:T(2,128)(2,1)} copy(bf16[8,2,4,12,2048]{4,0,3,2,1:T(8,128)(2,1)S(1)} %all_to_all.21) | data formatting | bytes 6291456 | tf_op jit(solution)/shard_map/all_to_all | solution.py:115
  258.4 4.0 %reshape_reshape.13 = bf16[16,4,12,2048]{3,0,2,1:T(8,128)(2,1)S(1)} reshape(bf16[8,2,4,12,2048]{4,1,0,3,2:T(2,128)(2,1)} %copy.78) | data formatting | bytes 6291456 | tf_op jit(solution)/shard_map/reshape;reshape | solution.py:125
  262.5 10.8 %fusion.18 = f32[16,4,12,1536]{3,0,2,1:T(8,128)S(1)} fusion(bf16[16,4,12,2048]{3,0,2,1:T(8,128)(2,1)S(1)} %reshape_reshape.13, bf16[4,2048,1536]{2,1,0:T(8,128)(2,1)} %param.20), kind=kOutput, calls=%fused_computation.28 | convolution fusion | flops 4831838208 | bytes 33030144 | tf_op jit(solution)/shard_map/secd,edf->secf/dot_general | solution.py:126
  273.3 7.5 %fusion.24 = bf16[16,4,12,2048]{3,0,2,1:T(8,128)(2,1)S(1)} fusion(bf16[4,768,2048]{2,1,0:T(8,128)(2,1)} %param.21, f32[16,4,12,1536]{3,0,2,1:T(8,128)S(1)} %fusion.18), kind=kOutput, calls=%fused_computation.31 | convolution fusion | flops 2421030912 | bytes 20447232 | tf_op jit(solution)/shard_map/secf,efd->secd/dot_general | solution.py:130
  280.8 4.1 %copy.87 = bf16[16,4,12,2048]{3,1,2,0:T(4,128)(2,1)} copy(bf16[16,4,12,2048]{3,0,2,1:T(8,128)(2,1)S(1)} %fusion.24) | data formatting | bytes 6291456 | tf_op jit(solution)/shard_map/reshape;reshape | solution.py:133
  284.9 4.0 %all-to-all-start.2 = ((bf16[8,2,4,12,2048]{4,2,3,1,0:T(4,128)(2,1)}), bf16[8,2,4,12,2048]{4,2,3,1,0:T(4,128)(2,1)S(1)}, u32[]{:S(2)}, u32[]{:S(2)}) async-start(bf16[8,2,4,12,2048]{4,2,3,1,0:T(4,128)(2,1)} %bitcast.102), calls=%async_computation.3 | async-start | bytes 6291456 | tf_op jit(solution)/shard_map/all_to_all | solution.py:135
  289.1 70.8 %all-to-all-done.2 = bf16[8,2,4,12,2048]{4,2,3,1,0:T(4,128)(2,1)S(1)} async-done(((bf16[8,2,4,12,2048]{4,2,3,1,0:T(4,128)(2,1)}), bf16[8,2,4,12,2048]{4,2,3,1,0:T(4,128)(2,1)S(1)}, u32[]{:S(2)}, u32[]{:S(2)}) %all-to-all-start.2) | async-done | bytes 3145760 | tf_op jit(solution)/shard_map/all_to_all | solution.py:135
  359.9 1.7 copy.80
  361.6 6.3 %all_to_all.22 = bf16[8,2,4,12,2048]{4,0,3,2,1:T(8,128)(2,1)S(1)} all-to-all(bf16[8,2,4,12,2048]{4,0,3,2,1:T(8,128)(2,1)S(1)} %copy.80), channel_id=1, replica_groups=mesh['groups'=2,'seq'=8,'exp'=2] {'exp'}, dimensions={1} | all-to-all | bytes 6291456 | tf_op jit(solution)/shard_map/all_to_all | solution.py:134
  367.9 3.7 copy.81
  371.5 4.7 %reshape_reshape.15 = bf16[768,2048]{1,0:T(8,128)(2,1)S(1)} reshape(bf16[8,2,4,12,2048]{4,3,2,1,0:T(8,128)(2,1)} %copy.81) | data formatting | bytes 6291456 | tf_op jit(solution)/shard_map/reshape;reshape | solution.py:141
  376.3 3.3 gather_fusion
  379.6 3.4 fusion.17
  383.1 1.8 add_convert_fusion
  (58 shorter events, 10.6 us)
Async XLA Ops:
  6.5 137.3 %all-gather.2.cloned.1.call-start = ((), (), s32[]{:S(2)}) async-start(), calls=%async_computation.5 | async-start | bytes 9437184 | tf_op jit(solution)/shard_map/all_gather | solution.py:84
  7.3 150.7 %reduce-scatter.2.cloned.1.call-start = ((), (), s32[]{:S(2)}) async-start(), calls=%async_computation.6 | async-start | bytes 786432 | tf_op jit(solution)/shard_map/reduce_scatter | solution.py:88
  143.8 7.2 %copy-start.2 = (s32[64,8]{0,1:T(8,128)S(1)}, s32[64,8]{0,1:T(8,128)}, u32[]{:S(2)}) copy-start(s32[64,8]{0,1:T(8,128)} %param.18) | copy-start | bytes 6148
  143.8 14.2 %copy-start = (bf16[64,2048]{1,0:T(8,128)(2,1)S(1)}, bf16[64,2048]{1,0:T(8,128)(2,1)}, u32[]{:S(2)}) copy-start(bf16[64,2048]{1,0:T(8,128)(2,1)} %param.12) | copy-start | bytes 786436
  143.8 15.3 %copy-start.1 = (f32[2048]{0:T(1024)S(1)}, f32[2048]{0:T(1024)}, u32[]{:S(2)}) copy-start(f32[2048]{0:T(1024)} %param.17) | copy-start | bytes 24580
  284.9 4.1 %copy-start.3 = (f32[64,8]{0,1:T(8,128)S(1)}, f32[64,8]{0,1:T(8,128)}, u32[]{:S(2)}) copy-start(f32[64,8]{0,1:T(8,128)} %param.19) | copy-start | bytes 6148
  284.9 75.0 %all-to-all-start.2 = ((bf16[8,2,4,12,2048]{4,2,3,1,0:T(4,128)(2,1)}), bf16[8,2,4,12,2048]{4,2,3,1,0:T(4,128)(2,1)S(1)}, u32[]{:S(2)}, u32[]{:S(2)}) async-start(bf16[8,2,4,12,2048]{4,2,3,1,0:T(4,128)(2,1)} %bitcast.102), calls=%async_computation.3 | async-start | bytes 6291456 | tf_op jit(solution)/shard_map/all_to_all | solution.py:135
Sparse Core Ops, SparseCore 0:
  9.5 134.2 all-gather.1
  151.1 6.7 reduce-scatter.1
where the time goes:
time: 393 us; the launch traced here: 392 us
  blocking collectives  157 us (40%)
  waiting for transfers between devices  119 us (30%)
  matrix products  41 us (10%)
  local copies, waits for them, and re-layouts  40.3 us (10%)
  other arithmetic  16.9 us (4%)
  between operations  13.6 us (3%)
  starting transfers between devices  4.04 us (1%)
    all_to_all x1, blocking collectives, on_device(): lax.all_to_all(sectioned, 'seq', split_axis=0, concat_axis=0, tiled=True)  76.7 us
    all_to_all x1, waiting for transfers between devices, on_device(): lax.all_to_all(finished, 'seq', split_axis=0, concat_axis=0, tiled=True)  70.8 us
    all_gather x1, waiting for transfers between devices, on_device(): lax.all_gather(out_weight, 'seq', axis=0, tiled=True)  43.5 us
    all_gather x1, blocking collectives, on_device(): key_piece = lax.all_gather(key_rows, 'seq', axis=0, tiled=True)  35 us
    all_gather x1, blocking collectives, on_device(): value_piece = lax.all_gather(value_rows, 'seq', axis=0, tiled=True)  32.8 us
    dot_general x1, matrix products, on_device(): jnp.einsum('secd,edf->secf', arranged, expert_in, preferred_element_type=...  10.8 us
  transfers between devices with their start and end apart: 3, of which 3 were waited for; matrix products, arithmetic and copies ran while one was open for 7% of the time, Pallas kernels for 0%

commit v1 on v0

--- a/solution.py
+++ b/solution.py
@@ -1,12 +1,170 @@
 import jax
 import jax.numpy as jnp
 from jax import lax
+from jax.experimental import pallas as pl
+from jax.experimental.pallas import tpu as pltpu
 from jax.sharding import PartitionSpec as P
 
 HD = 128
-EXPERTS = 64
-TOPK = 8
 CAP = 12
+FCHUNK = 256
+
+
+def ring(size, step):
+    return [(i, (i + 2 * step) % size) for i in range(size)]
+
+
+def swap(size):
+    return [(i, i ^ 1) for i in range(size)]
+
+
+def gather_meta(meta, size, depth):
+    along = jnp.stack([meta] + [lax.ppermute(meta, "seq", ring(size, d)) for d in range(1, depth)])
+    both = jnp.stack([along, lax.ppermute(along, "seq", swap(size))], axis=1)
+    return jnp.stack([both, lax.ppermute(both, "exp", swap(2))], axis=2)
+
+
+def routing(ids, gates, first, local_experts):
+    blocks, rows, _ = ids.shape
+    subs = blocks // 4
+    experts = first + jnp.arange(local_experts, dtype=jnp.int32)
+    match = ids[..., None] == experts
+    hit = jnp.any(match, axis=2)
+    weight = jnp.sum(jnp.where(match, gates[..., None], 0.0), axis=2)
+    count = hit.astype(jnp.int32)
+    place = jnp.where(hit, jnp.cumsum(count, axis=1) - count, -1)
+    place = place.reshape(subs, 4, rows, local_experts).transpose(3, 0, 1, 2)
+    weight = weight.reshape(subs, 4, rows, local_experts).transpose(3, 0, 1, 2)
+    chosen = place[:, :, :, None, :] == jnp.arange(CAP, dtype=jnp.int32)[:, None]
+    row_gate = jnp.sum(jnp.where(chosen, weight[:, :, :, None, :], 0.0), axis=-1)
+    row_gate = row_gate.reshape(local_experts, subs * 4 * CAP, 1)
+    diagonal = jnp.eye(4, dtype=bool)[:, None, :, None]
+    full = chosen[:, :, :, :, None, :] & diagonal
+    select = full.reshape(local_experts, subs, 4 * CAP, 4 * rows).astype(jnp.bfloat16)
+    spread = select.transpose(1, 3, 0, 2).reshape(subs, 4 * rows, local_experts * 4 * CAP)
+    return select, spread, row_gate
+
+
+def expert_kernel(x_ref, select_ref, spread_ref, gate_ref, wg_ref, wu_ref, wo_ref, out_ref, xg, acc, res):
+    expert, chunk = pl.program_id(0), pl.program_id(1)
+    last = pl.num_programs(1) - 1
+    subs, slots = select_ref.shape[1], select_ref.shape[2]
+    tokens = x_ref.shape[1]
+
+    @pl.when(chunk == 0)
+    def _():
+        for s in range(subs):
+            xg[s * slots : (s + 1) * slots, :] = jnp.dot(
+                select_ref[expert, s], x_ref[s], preferred_element_type=jnp.float32
+            ).astype(jnp.bfloat16)
+
+    rows = xg[...]
+    gate = jnp.dot(rows, wg_ref[0], preferred_element_type=jnp.float32)
+    up = jnp.dot(rows, wu_ref[0], preferred_element_type=jnp.float32)
+    act = (gate / (1.0 + jnp.exp(-gate)) * up).astype(jnp.bfloat16)
+    part = jnp.dot(act, wo_ref[0], preferred_element_type=jnp.float32)
+
+    @pl.when(chunk == 0)
+    def _():
+        acc[...] = part
+
+    @pl.when(chunk > 0)
+    def _():
+        acc[...] += part
+
+    @pl.when(chunk == last)
+    def _():
+        scaled = (acc[...] * gate_ref[expert]).astype(jnp.bfloat16)
+        for s in range(subs):
+            res[s, expert] = scaled[s * slots : (s + 1) * slots, :]
+
+    @pl.when((chunk == last) & (expert == pl.num_programs(0) - 1))
+    def _():
+        for s in range(subs):
+            out_ref[s * tokens : (s + 1) * tokens, :] = jnp.dot(
+                spread_ref[s], res[s].reshape(-1, res.shape[-1]), preferred_element_type=jnp.float32
+            ).astype(jnp.bfloat16)
+
+
+def run_experts(x, select, spread, row_gate, expert_in, expert_out):
+    subs, tokens, width = x.shape
+    local_experts, hidden, _ = expert_out.shape
+    slots = select.shape[2]
+    chunks = hidden // FCHUNK
+    flops = local_experts * subs * slots * width * hidden * 6
+    moved = (expert_in.size + expert_out.size + 2 * x.size) * 2
+    whole = lambda shape: pl.BlockSpec(shape, lambda e, f: (0,) * len(shape), pipeline_mode=pl.Buffered(1))
+    return pl.pallas_call(
+        expert_kernel,
+        grid=(local_experts, chunks),
+        out_shape=jax.ShapeDtypeStruct((subs * tokens, width), jnp.bfloat16),
+        in_specs=[
+            whole(x.shape),
+            whole(select.shape),
+            whole(spread.shape),
+            whole(row_gate.shape),
+            pl.BlockSpec((1, width, FCHUNK), lambda e, f: (e, 0, f)),
+            pl.BlockSpec((1, width, FCHUNK), lambda e, f: (e, 0, f + chunks)),
+            pl.BlockSpec((1, FCHUNK, width), lambda e, f: (e, f, 0)),
+        ],
+        out_specs=whole((subs * tokens, width)),
+        scratch_shapes=[
+            pltpu.VMEM((subs * slots, width), jnp.bfloat16),
+            pltpu.VMEM((subs * slots, width), jnp.float32),
+            pltpu.VMEM((subs, local_experts, slots, width), jnp.bfloat16),
+        ],
+        compiler_params=pltpu.CompilerParams(vmem_limit_bytes=48 * 1024 * 1024),
+        cost_estimate=pl.CostEstimate(flops=flops, bytes_accessed=moved, transcendentals=0),
+        name="experts",
+    )(x, select, spread, row_gate, expert_in, expert_in, expert_out)
+
+
+def wide(value):
+    return value.astype(jnp.float32)
+
+
+def expert_block(mixed, norm_gain, expert_ids, gate_weights, expert_in, expert_out):
+    size = lax.axis_size("seq")
+    depth = size // 2
+    rows, width = mixed.shape
+    local_experts = expert_in.shape[0]
+    first = (lax.axis_index("seq") * 2 + lax.axis_index("exp")) * local_experts
+    gate_high = gate_weights.astype(jnp.bfloat16)
+    gate_low = (gate_weights - wide(gate_high)).astype(jnp.bfloat16)
+    meta = jnp.concatenate([expert_ids.astype(jnp.bfloat16), gate_high, gate_low], axis=1)
+    meta = gather_meta(meta, size, depth)
+    top = expert_ids.shape[1]
+    passes = [list(range(depth // 2)), list(range(depth // 2, depth))]
+    routes = []
+    for group in passes:
+        own = meta[group[0] : group[-1] + 1].transpose(2, 0, 1, 3, 4).reshape(-1, rows, 3 * top)
+        ids = own[..., :top].astype(jnp.int32)
+        gates = wide(own[..., top : 2 * top]) + wide(own[..., 2 * top :])
+        routes.append(routing(ids, gates, first, local_experts))
+
+    normed = (
+        mixed * lax.rsqrt(jnp.mean(mixed * mixed, axis=-1, keepdims=True) + 1e-06) * norm_gain
+    ).astype(jnp.bfloat16)
+    along, across = [normed], []
+    for d in range(depth):
+        if d + 1 < depth:
+            along.append(lax.ppermute(along[d], "seq", ring(size, 1)))
+        across.append(lax.ppermute(along[d], "seq", swap(size)))
+    total = mixed
+    for group, route in zip(passes, routes):
+        mine = jnp.concatenate([part for d in group for part in (along[d], across[d])])
+        other = lax.ppermute(mine, "exp", swap(2))
+        x = jnp.concatenate([mine, other]).reshape(-1, 4 * rows, width)
+        out = run_experts(x, *route, expert_in, expert_out).reshape(2, len(group), 2, rows, width)
+        arrived = lax.ppermute(out[1], "exp", swap(2))
+        pair = wide(out[0]) + wide(arrived)
+        for place, d in enumerate(group):
+            there = lax.ppermute(pair[place, 1].astype(jnp.bfloat16), "seq", swap(size))
+            chip = pair[place, 0] + wide(there)
+            if d:
+                chip = wide(lax.ppermute(chip.astype(jnp.bfloat16), "seq", ring(size, -d)))
+            total = total + chip
+    return total.astype(jnp.bfloat16)
 
 
 neg_large = -1e30
@@ -89,58 +247,7 @@
         partial_heads.astype(jnp.bfloat16), "exp", scatter_dimension=0, tiled=True
     ).astype(jnp.float32)
     mixed = stream.astype(jnp.float32) + attn_out
-    normed = (
-        mixed * lax.rsqrt(jnp.mean(mixed * mixed, axis=-1, keepdims=True) + 1e-06) * norm_gain
-    ).astype(jnp.bfloat16)
-    width = normed.shape[1]
-    flat_ids = expert_ids.reshape(-1)
-    onehot = (flat_ids[:, None] == jnp.arange(EXPERTS, dtype=jnp.int32)[None, :]).astype(jnp.int32)
-    earlier = jnp.cumsum(onehot, axis=0) - onehot
-    slots = jnp.sum(earlier * onehot, axis=1)
-    destination = flat_ids * CAP + slots
-    chooser = (destination[None, :] == jnp.arange(EXPERTS * CAP, dtype=jnp.int32)[:, None]).astype(
-        jnp.int32
-    )
-    chooser = jnp.sum(chooser.reshape(EXPERTS * CAP, local_rows, TOPK), axis=-1).astype(
-        jnp.bfloat16
-    )
-    outgoing = (
-        jnp.dot(chooser, normed, preferred_element_type=jnp.float32)
-        .astype(jnp.bfloat16)
-        .reshape(EXPERTS, CAP, width)
-    )
-    local_experts = expert_in.shape[0]
-    hidden_units = expert_out.shape[1]
-    sectioned = outgoing.reshape(seq_count, exp_count, local_experts, CAP, width)
-    arrived = lax.all_to_all(
-        lax.all_to_all(sectioned, "seq", split_axis=0, concat_axis=0, tiled=True),
-        "exp",
-        split_axis=1,
-        concat_axis=1,
-        tiled=True,
-    )
-    received = arrived.reshape(-1, CAP, width)
-    senders = received.shape[0] // local_experts
-    slots_here = received.shape[1]
-    arranged = received.reshape(senders, local_experts, slots_here, width)
-    gate_up = jnp.einsum("secd,edf->secf", arranged, expert_in, preferred_element_type=jnp.float32)
-    act = (jax.nn.silu(gate_up[..., :hidden_units]) * gate_up[..., hidden_units:]).astype(
-        jnp.bfloat16
-    )
-    result = jnp.einsum(
-        "secf,efd->secd", act, expert_out, preferred_element_type=jnp.float32
-    ).astype(jnp.bfloat16)
-    finished = result.reshape(received.shape).reshape(sectioned.shape)
-    back = lax.all_to_all(
-        lax.all_to_all(finished, "seq", split_axis=0, concat_axis=0, tiled=True),
-        "exp",
-        split_axis=1,
-        concat_axis=1,
-        tiled=True,
-    ).reshape(EXPERTS, CAP, width)
-    picked = back.reshape(EXPERTS * CAP, width)[destination].reshape(local_rows, TOPK, width)
-    combined = jnp.sum(gate_weights[..., None] * picked.astype(jnp.float32), axis=1)
-    return (mixed + combined).astype(jnp.bfloat16)
+    return expert_block(mixed, norm_gain, expert_ids, gate_weights, expert_in, expert_out)
 
 
 def solution(mesh):

time: 393 us -> 298 us (0.76)
  blocking collectives: 157 us -> 66.2 us
  Pallas kernels: 0 us -> 40.6 us
  local copies, waits for them, and re-layouts: 40.3 us -> 9.91 us
  matrix products: 41 us -> 20.5 us
  starting transfers between devices: 4.04 us -> 21 us
  waiting for transfers between devices: 119 us -> 107 us
    all_to_all x3 -> x0, blocking collectives: 89.2 us -> none  [the longest x1 76.7 us: on_device(): lax.all_to_all(sectioned, 'seq', split_axis=0, concat_axis=0, tiled=True)]
    all_to_all x1 -> x0, waiting for transfers between devices: 70.8 us -> none  [on_device(): lax.all_to_all(finished, 'seq', split_axis=0, concat_axis=0, tiled=True)]
    ppermute x0 -> x23, waiting for transfers between devices: none -> 69.6 us  [the longest x4 20.1 us: expert_block(): there = lax.ppermute(pair[place, 1].astype(jnp.bfloat16), 'seq', swap(size))]
    pallas_call x0 -> x2, Pallas kernels: none -> 40.6 us  [run_experts(): pl.pallas_call(expert_kernel, grid=(local_experts, chunks), out_shape=jax...]
    ppermute x0 -> x23, starting transfers between devices: none -> 21 us  [the longest x3 6.11 us: gather_meta(): lax.ppermute(meta, 'seq', ring(size, d))]
    another operation x6 -> x0, local copies, waits for them, and re-layouts: 20.4 us -> none  [the longest x2 7.57 us: on_device(): outgoing.reshape(seq_count, exp_count, local_experts, CAP, width)]
    dot_general x3 -> x0, matrix products: 20.4 us -> none  [the longest x1 10.8 us: on_device(): jnp.einsum('secd,edf->secf', arranged, expert_in, preferred_element_type=...]
    all_to_all x4 -> x0, local copies, waits for them, and re-layouts: 12.1 us -> none  [the longest x1 4.95 us: on_device(): lax.all_to_all(lax.all_to_all(sectioned, 'seq', split_axis=0, concat_axis...]
  transfers between devices with their start and end apart: 3 -> 25, of which waited for: 3 -> 14; matrix products, arithmetic and copies ran while one was open for 7% -> 13% of each run, Pallas kernels for 0% -> 14%
where the time goes in v1:
time: 298 us; the launch traced here: 297 us
  waiting for transfers between devices  107 us (36%)
  blocking collectives  66.2 us (22%)
  Pallas kernels  40.6 us (14%)
  starting transfers between devices  21 us (7%)
  matrix products  20.5 us (7%)
  other arithmetic  18.1 us (6%)
  between operations  13.9 us (5%)
  local copies, waits for them, and re-layouts  9.91 us (3%)
    pallas_call x2, Pallas kernels, run_experts(): pl.pallas_call(expert_kernel, grid=(local_experts, chunks), out_shape=jax...  40.6 us
    all_gather x1, blocking collectives, on_device(): key_piece = lax.all_gather(key_rows, 'seq', axis=0, tiled=True)  33.5 us
    all_gather x1, blocking collectives, on_device(): value_piece = lax.all_gather(value_rows, 'seq', axis=0, tiled=True)  32.7 us
    all_gather x1, waiting for transfers between devices, on_device(): lax.all_gather(out_weight, 'seq', axis=0, tiled=True)  32.7 us
    ppermute x4, waiting for transfers between devices, expert_block(): there = lax.ppermute(pair[place, 1].astype(jnp.bfloat16), 'seq', swap(size))  20.1 us
    ppermute x3, waiting for transfers between devices, expert_block(): chip = wide(lax.ppermute(chip.astype(jnp.bfloat16), 'seq', ring(size, -d)))  18.9 us
    ppermute x3, waiting for transfers between devices, expert_block(): along.append(lax.ppermute(along[d], 'seq', ring(size, 1)))  15.9 us
    ppermute x4, waiting for transfers between devices, expert_block(): across.append(lax.ppermute(along[d], 'seq', swap(size)))  10.4 us
  transfers between devices with their start and end apart: 25, of which 14 were waited for; matrix products, arithmetic and copies ran while one was open for 13% of the time, Pallas kernels for 14%

profile of v1, /device:TPU:0, one launch (start us, length us, event | category | flops | bytes accessed | tf_op | source)
XLA Modules:
  0.0 297.3 jit_solution(15944923233123564081)
XLA Ops:
  8.8 5.1 %collective-permute-start.6 = (bf16[64,24]{0,1:T(8,128)(2,1)S(1)}, bf16[64,24]{0,1:T(8,128)(2,1)S(1)}, u32[]{:S(2)}, u32[]{:S(2)}) collective-permute-start(bf16[64,24]{0,1:T(8,128)(2,1)S(1)} %get-tuple-element.169), channel_id=1, source_target_pairs={{0,12},{2,14},{4,0},{6,2},{8,4},{10,6},{12,8},{14,10},{1,13},{3,15... | collective-permute-start | bytes 9224 | tf_op jit(solution)/shard_map/ppermute | solution.py:22
  16.5 33.5 %all_gather.9 = bf16[1024,256]{1,0:T(8,128)(2,1)S(1)} all-gather(bf16[128,256]{1,0:T(8,128)(2,1)S(1)} %copy-done.3), channel_id=1, replica_groups=mesh['groups'=2,'seq'=8,'exp'=2] {'seq'}, dimensions={0}, use_global_device_ids=true | all-gather | bytes 589824 | tf_op jit(solution)/shard_map/all_gather | solution.py:221
  50.0 32.7 %all_gather.10 = bf16[1024,256]{1,0:T(8,128)(2,1)S(1)} all-gather(bf16[128,256]{1,0:T(8,128)(2,1)S(1)} %copy-done.4), channel_id=1, replica_groups=mesh['groups'=2,'seq'=8,'exp'=2] {'seq'}, dimensions={0}, use_global_device_ids=true | all-gather | bytes 589824 | tf_op jit(solution)/shard_map/all_gather | solution.py:222
  82.7 23.5 %while.15 = (s32[]{:T(128)}, f32[2,128,8]{1,2,0:T(8,128)S(1)}, f32[2,128,8]{1,2,0:T(8,128)S(1)}, f32[2,128,8,128]{3,1,2,0:T(8,128)S(1)}, s32[2]{0:T(128)S(1)}, /...) while((s32[]{:T(128)}, f32[2,128,8]{1,2,0:T(8,128)S(1)}, ...), condition=%wide.region_3.4_spmd.clone, body=%wide.region_0.3_spmd.clone.sunk | while | flops 551365248 | bytes 18224280 | solution.py:232
  84.4 2.8 fusion.55
  87.2 3.2 %fusion.56 = f32[2,128,8]{1,2,0:T(8,128)S(1)} fusion(f32[2,512,128,8]{2,1,3,0:T(8,128)} %get-tuple-element.239, f32[2,128,8]{1,2,0:T(8,128)S(1)} %select_maximum_fusion.2, pred[128,512]{0,1:T(8,128)(4,1)S(1)} %broadcast_compare_fusion.2), kind=kLoop, calls=%fused_computation.4.clone.1 | loop fusion | flops 5240832 | bytes 4276224 | tf_op jit(solution)/shard_map/while/body/eval_jaxpr/reduce_sum | solution.py:191
  90.6 3.9 %fusion.58 = f32[2,128,8,128]{3,1,2,0:T(8,128)S(1)} fusion(bf16[512,2,128,1]{0,2,3,1:T(8,128)(2,1)S(1)} %bitcast.141, f32[2,512,128,8]{2,1,3,0:T(8,128)} %get-tuple-element.239, f32[2,128,8]{1,2,0:T(8,128)S(1)} %select_maximum_fusion.2, pred[128,512]{0,1:T(8,128)(4,1)S(1)} %broadcast_compare_fusion.2, f32[2,128,8,128]{3,1,2,0:T(8,128)S(1)} %get-tuple-element.257, ...), kind=kOutput, calls=%fused_computation.7.clone.1 | convolution fusion | flops 274464768 | bytes 6635521 | tf_op jit(solution)/shard_map/while/body/eval_jaxpr/gths,sgd->gthd/dot_general | solution.py:192
  96.2 2.8 fusion.55
  99.0 3.2 %fusion.56 = f32[2,128,8]{1,2,0:T(8,128)S(1)} fusion(f32[2,512,128,8]{2,1,3,0:T(8,128)} %get-tuple-element.239, f32[2,128,8]{1,2,0:T(8,128)S(1)} %select_maximum_fusion.2, pred[128,512]{0,1:T(8,128)(4,1)S(1)} %broadcast_compare_fusion.2), kind=kLoop, calls=%fused_computation.4.clone.1 | loop fusion | flops 5240832 | bytes 4276224 | tf_op jit(solution)/shard_map/while/body/eval_jaxpr/reduce_sum | solution.py:191
  102.3 3.9 %fusion.58 = f32[2,128,8,128]{3,1,2,0:T(8,128)S(1)} fusion(bf16[512,2,128,1]{0,2,3,1:T(8,128)(2,1)S(1)} %bitcast.141, f32[2,512,128,8]{2,1,3,0:T(8,128)} %get-tuple-element.239, f32[2,128,8]{1,2,0:T(8,128)S(1)} %select_maximum_fusion.2, pred[128,512]{0,1:T(8,128)(4,1)S(1)} %broadcast_compare_fusion.2, f32[2,128,8,128]{3,1,2,0:T(8,128)S(1)} %get-tuple-element.257, ...), kind=kOutput, calls=%fused_computation.7.clone.1 | convolution fusion | flops 274464768 | bytes 6635521 | tf_op jit(solution)/shard_map/while/body/eval_jaxpr/gths,sgd->gthd/dot_general | solution.py:192
  107.8 3.3 %collective-permute-done.7 = bf16[4,64,24]{1,2,0:T(8,128)(2,1)S(1)} collective-permute-done((bf16[4,64,24]{1,2,0:T(8,128)(2,1)S(1)}, bf16[4,64,24]{1,2,0:T(8,128)(2,1)S(1)}, u32[]{:S(2)}, u32[]{:S(2)}) %collective-permute-start.7) | collective-permute-done | bytes 12320 | tf_op jit(solution)/shard_map/ppermute | solution.py:23
  113.3 32.7 %all-gather.2.cloned.1.call-done = bf16[2048,2048]{1,0:T(8,128)(2,1)} async-done(((bf16[256,2048]{1,0:T(8,128)(2,1)}), bf16[2048,2048]{1,0:T(8,128)(2,1)}) %all-gather.2.cloned.1.call-update) | async-done | bytes 8388624 | tf_op jit(solution)/shard_map/all_gather | solution.py:242
  146.0 7.2 %convolution_convert_fusion = bf16[128,2048]{1,0:T(8,128)(2,1)} fusion(bf16[128,2048]{0,1:T(8,128)(2,1)S(1)} %bitcast.146, bf16[2048,2048]{1,0:T(8,128)(2,1)} %all-gather.2.cloned.1.call-done), kind=kOutput, calls=%fused_computation.21 | convolution fusion | flops 1074003968 | bytes 9437184 | tf_op jit(solution)/shard_map/dot_general | solution.py:240
  155.8 3.9 %reduce-scatter.2.cloned.1.call-done = bf16[64,2048]{1,0:T(8,128)(2,1)} async-done(((bf16[128,2048]{1,0:T(8,128)(2,1)}), bf16[64,2048]{1,0:T(8,128)(2,1)}) %reduce-scatter.2.cloned.1.call-update) | async-done | bytes 262160 | tf_op jit(solution)/shard_map/reduce_scatter | solution.py:246
  160.9 1.8 constant_dynamic-update-slice_fusion.4
  162.7 1.7 collective-permute-start
  164.4 1.5 collective-permute-start.1
  167.9 6.9 %collective-permute-done.1 = bf16[64,2048]{1,0:T(8,128)(2,1)} collective-permute-done((bf16[64,2048]{1,0:T(8,128)(2,1)}, bf16[64,2048]{1,0:T(8,128)(2,1)}, u32[]{:S(2)}, u32[]{:S(2)}) %collective-permute-start.1) | collective-permute-done | bytes 262176 | tf_op jit(solution)/shard_map/ppermute | solution.py:151
  177.1 5.3 %collective-permute-done.2 = bf16[64,2048]{1,0:T(8,128)(2,1)S(1)} collective-permute-done((bf16[64,2048]{1,0:T(8,128)(2,1)}, bf16[64,2048]{1,0:T(8,128)(2,1)S(1)}, u32[]{:S(2)}, u32[]{:S(2)}) %collective-permute-start.2) | collective-permute-done | bytes 262176 | tf_op jit(solution)/shard_map/ppermute | solution.py:152
  184.4 1.6 collective-permute-start.14
  186.0 8.3 %collective-permute-done.15 = bf16[64,2048]{1,0:T(8,128)(2,1)S(1)} collective-permute-done((bf16[64,2048]{1,0:T(8,128)(2,1)S(1)}, bf16[64,2048]{1,0:T(8,128)(2,1)S(1)}, u32[]{:S(2)}, u32[]{:S(2)}) %collective-permute-start.15) | collective-permute-done | bytes 262176 | tf_op jit(solution)/shard_map/ppermute | solution.py:151
  194.4 1.6 collective-permute-start.16
  196.0 5.1 %collective-permute-done.16 = bf16[64,2048]{1,0:T(8,128)(2,1)S(1)} collective-permute-done((bf16[64,2048]{1,0:T(8,128)(2,1)S(1)}, bf16[64,2048]{1,0:T(8,128)(2,1)S(1)}, u32[]{:S(2)}, u32[]{:S(2)}) %collective-permute-start.16) | collective-permute-done | bytes 262176 | tf_op jit(solution)/shard_map/ppermute | solution.py:152
  201.4 20.3 %experts.2 = bf16[512,2048]{1,0:T(8,128)(2,1)S(1)} custom-call(bf16[2,256,2048]{2,1,0:T(8,128)(2,1)S(1)} %bitcast.139, bf16[4,2,48,256]{3,2,1,0:T(8,128)(2,1)S(1)} %get-tuple-element.166.select_ref, bf16[2,256,192]{2,1,0:T(8,128)(2,1)S(1)} %copy.68.spread_ref, f32[4,96,1]{2,1,0:T(8,128)S(1)} %reshape.175.gate_ref, bf16[4,2048,1536]{2,1,0:T(8,128)(2,1)} %wu_ref.3, ...), custom_call_target="tpu_custom_call" | custom-call | flops 3623878656 | bytes 41943040 | tf_op jit(solution)/shard_map/experts/pallas_call | solution.py:97
  222.6 20.3 %experts.3 = bf16[512,2048]{1,0:T(8,128)(2,1)S(1)} custom-call(bf16[2,256,2048]{2,1,0:T(8,128)(2,1)S(1)} %bitcast.138, bf16[4,2,48,256]{3,2,1,0:T(8,128)(2,1)S(1)} %get-tuple-element.157.select_ref, bf16[2,256,192]{2,1,0:T(8,128)(2,1)S(1)} %copy.74.spread_ref, f32[4,96,1]{2,1,0:T(8,128)S(1)} %reshape.176.gate_ref, bf16[4,2048,1536]{2,1,0:T(8,128)(2,1)} %wu_ref.3, ...), custom_call_target="tpu_custom_call" | custom-call | flops 3623878656 | bytes 41943040 | tf_op jit(solution)/shard_map/experts/pallas_call | solution.py:97
  243.6 1.8 collective-permute-start.11
  246.2 1.8 collective-permute-start.19
  248.3 4.4 %collective-permute-done.11 = bf16[64,2048]{1,0:T(8,128)(2,1)S(1)} collective-permute-done((bf16[64,2048]{1,0:T(8,128)(2,1)S(1)}, bf16[64,2048]{1,0:T(8,128)(2,1)S(1)}, u32[]{:S(2)}, u32[]{:S(2)}) %collective-permute-start.11) | collective-permute-done | bytes 262176 | tf_op jit(solution)/shard_map/ppermute | solution.py:162
  253.5 10.5 %collective-permute-done.19 = bf16[64,2048]{1,0:T(8,128)(2,1)S(1)} collective-permute-done((bf16[64,2048]{1,0:T(8,128)(2,1)S(1)}, bf16[64,2048]{1,0:T(8,128)(2,1)S(1)}, u32[]{:S(2)}, u32[]{:S(2)}) %collective-permute-start.19) | collective-permute-done | bytes 262176 | tf_op jit(solution)/shard_map/ppermute | solution.py:162
  264.0 5.2 %collective-permute-done.21 = bf16[64,2048]{1,0:T(8,128)(2,1)S(1)} collective-permute-done((bf16[64,2048]{1,0:T(8,128)(2,1)S(1)}, bf16[64,2048]{1,0:T(8,128)(2,1)S(1)}, u32[]{:S(2)}, u32[]{:S(2)}) %collective-permute-start.21) | collective-permute-done | bytes 262176 | tf_op jit(solution)/shard_map/ppermute | solution.py:162
  270.6 9.8 %collective-permute-done.22 = bf16[64,2048]{1,0:T(8,128)(2,1)S(1)} collective-permute-done((bf16[64,2048]{1,0:T(8,128)(2,1)S(1)}, bf16[64,2048]{1,0:T(8,128)(2,1)S(1)}, u32[]{:S(2)}, u32[]{:S(2)}) %collective-permute-start.22) | collective-permute-done | bytes 262176 | tf_op jit(solution)/shard_map/ppermute | solution.py:165
  280.4 9.1 %collective-permute-done.20 = bf16[64,2048]{1,0:T(8,128)(2,1)S(1)} collective-permute-done((bf16[64,2048]{1,0:T(8,128)(2,1)S(1)}, bf16[64,2048]{1,0:T(8,128)(2,1)S(1)}, u32[]{:S(2)}, u32[]{:S(2)}) %collective-permute-start.20) | collective-permute-done | bytes 262176 | tf_op jit(solution)/shard_map/ppermute | solution.py:165
  (136 shorter events, 28.2 us)
Async XLA Ops:
  6.5 10.0 %copy-start.3 = (bf16[128,256]{1,0:T(8,128)(2,1)S(1)}, bf16[128,256]{1,0:T(8,128)(2,1)}, u32[]{:S(2)}) copy-start(bf16[128,256]{1,0:T(8,128)(2,1)} %param.14) | copy-start | bytes 196612
  6.5 43.4 %copy-start.4 = (bf16[128,256]{1,0:T(8,128)(2,1)S(1)}, bf16[128,256]{1,0:T(8,128)(2,1)}, u32[]{:S(2)}) copy-start(bf16[128,256]{1,0:T(8,128)(2,1)} %param.15) | copy-start | bytes 196612
  6.5 139.4 %all-gather.2.cloned.1.call-start = ((), (), s32[]{:S(2)}) async-start(), calls=%async_computation.1 | async-start | bytes 9437184 | tf_op jit(solution)/shard_map/all_gather | solution.py:242
  7.3 152.5 %reduce-scatter.2.cloned.1.call-start = ((), (), s32[]{:S(2)}) async-start(), calls=%async_computation.2 | async-start | bytes 786432 | tf_op jit(solution)/shard_map/reduce_scatter | solution.py:246
  8.8 97.9 %collective-permute-start.6 = (bf16[64,24]{0,1:T(8,128)(2,1)S(1)}, bf16[64,24]{0,1:T(8,128)(2,1)S(1)}, u32[]{:S(2)}, u32[]{:S(2)}) collective-permute-start(bf16[64,24]{0,1:T(8,128)(2,1)S(1)} %get-tuple-element.169), channel_id=1, source_target_pairs={{0,12},{2,14},{4,0},{6,2},{8,4},{10,6},{12,8},{14,10},{1,13},{3,15... | collective-permute-start | bytes 9224 | tf_op jit(solution)/shard_map/ppermute | solution.py:22
  13.9 92.8 %collective-permute-start.5 = (bf16[64,24]{0,1:T(8,128)(2,1)S(1)}, bf16[64,24]{0,1:T(8,128)(2,1)S(1)}, u32[]{:S(2)}, u32[]{:S(2)}) collective-permute-start(bf16[64,24]{0,1:T(8,128)(2,1)S(1)} %get-tuple-element.169), channel_id=1, source_target_pairs={{0,8},{2,10},{4,12},{6,14},{8,0},{10,2},{12,4},{14,6},{1,9},{3,11}... | collective-permute-start | bytes 9224 | tf_op jit(solution)/shard_map/ppermute | solution.py:22
  13.9 92.8 %collective-permute-start.4 = (bf16[64,24]{0,1:T(8,128)(2,1)S(1)}, bf16[64,24]{0,1:T(8,128)(2,1)S(1)}, u32[]{:S(2)}, u32[]{:S(2)}) collective-permute-start(bf16[64,24]{0,1:T(8,128)(2,1)S(1)} %get-tuple-element.169), channel_id=1, source_target_pairs={{0,4},{2,6},{4,8},{6,10},{8,12},{10,14},{12,0},{14,2},{1,5},{3,7},... | collective-permute-start | bytes 9224 | tf_op jit(solution)/shard_map/ppermute | solution.py:22
  106.7 4.4 %collective-permute-start.7 = (bf16[4,64,24]{1,2,0:T(8,128)(2,1)S(1)}, bf16[4,64,24]{1,2,0:T(8,128)(2,1)S(1)}, u32[]{:S(2)}, u32[]{:S(2)}) collective-permute-start(bf16[4,64,24]{1,2,0:T(8,128)(2,1)S(1)} %get-tuple-element.165), channel_id=1, source_target_pairs={{0,2},{2,0},{4,6},{6,4},{8,10},{10,8},{12,14},{14,12},{1,3},{3,1},... | collective-permute-start | bytes 36872 | tf_op jit(solution)/shard_map/ppermute | solution.py:23
  111.1 1.3 collective-permute-start.8
  153.2 6.6 %copy-start = (bf16[64,2048]{1,0:T(8,128)(2,1)S(1)}, bf16[64,2048]{1,0:T(8,128)(2,1)}, u32[]{:S(2)}) copy-start(bf16[64,2048]{1,0:T(8,128)(2,1)} %param.12) | copy-start | bytes 786436
  153.8 7.2 %copy-start.5 = (f32[2048]{0:T(1024)S(1)}, f32[2048]{0:T(1024)}, u32[]{:S(2)}) copy-start(f32[2048]{0:T(1024)} %param.17) | copy-start | bytes 24580
  162.7 12.5 %collective-permute-start = (bf16[64,2048]{1,0:T(8,128)(2,1)}, bf16[64,2048]{1,0:T(8,128)(2,1)}, u32[]{:S(2)}, u32[]{:S(2)}) collective-permute-start(bf16[64,2048]{1,0:T(8,128)(2,1)} %get-tuple-element.137), channel_id=1, source_target_pairs={{0,2},{2,0},{4,6},{6,4},{8,10},{10,8},{12,14},{14,12},{1,3},{3,1},... | collective-permute-start | bytes 786440 | tf_op jit(solution)/shard_map/ppermute | solution.py:152
  164.4 10.4 %collective-permute-start.1 = (bf16[64,2048]{1,0:T(8,128)(2,1)}, bf16[64,2048]{1,0:T(8,128)(2,1)}, u32[]{:S(2)}, u32[]{:S(2)}) collective-permute-start(bf16[64,2048]{1,0:T(8,128)(2,1)} %get-tuple-element.137), channel_id=1, source_target_pairs={{0,4},{2,6},{4,8},{6,10},{8,12},{10,14},{12,0},{14,2},{1,5},{3,7},... | collective-permute-start | bytes 786440 | tf_op jit(solution)/shard_map/ppermute | solution.py:151
  174.8 7.6 %collective-permute-start.2 = (bf16[64,2048]{1,0:T(8,128)(2,1)}, bf16[64,2048]{1,0:T(8,128)(2,1)S(1)}, u32[]{:S(2)}, u32[]{:S(2)}) collective-permute-start(bf16[64,2048]{1,0:T(8,128)(2,1)} %collective-permute-done.1), channel_id=1, source_target_pairs={{0,2},{2,0},{4,6},{6,4},{8,10},{10,8},{12,14},{14,12},{1,3},{3,1},... | collective-permute-start | bytes 786440 | tf_op jit(solution)/shard_map/ppermute | solution.py:152
  175.2 9.2 %collective-permute-start.13 = (bf16[64,2048]{1,0:T(8,128)(2,1)}, bf16[64,2048]{1,0:T(8,128)(2,1)S(1)}, u32[]{:S(2)}, u32[]{:S(2)}) collective-permute-start(bf16[64,2048]{1,0:T(8,128)(2,1)} %collective-permute-done.1), channel_id=1, source_target_pairs={{0,4},{2,6},{4,8},{6,10},{8,12},{10,14},{12,0},{14,2},{1,5},{3,7},... | collective-permute-start | bytes 786440 | tf_op jit(solution)/shard_map/ppermute | solution.py:151
  183.6 17.7 %collective-permute-start.3 = (bf16[256,2048]{1,0:T(8,128)(2,1)S(1)}, bf16[256,2048]{1,0:T(8,128)(2,1)S(1)}, u32[]{:S(2)}, u32[]{:S(2)}) collective-permute-start(bf16[256,2048]{1,0:T(8,128)(2,1)S(1)} %pad_maximum_fusion), channel_id=1, source_target_pairs={{0,1},{1,0},{2,3},{3,2},{4,5},{5,4},{6,7},{7,6},{8,9},{9,8},{10,11... | collective-permute-start | bytes 3145736 | tf_op jit(solution)/shard_map/ppermute | solution.py:156
  184.4 11.6 %collective-permute-start.14 = (bf16[64,2048]{1,0:T(8,128)(2,1)S(1)}, bf16[64,2048]{1,0:T(8,128)(2,1)S(1)}, u32[]{:S(2)}, u32[]{:S(2)}) collective-permute-start(bf16[64,2048]{1,0:T(8,128)(2,1)S(1)} %collective-permute-done.13), channel_id=1, source_target_pairs={{0,2},{2,0},{4,6},{6,4},{8,10},{10,8},{12,14},{14,12},{1,3},{3,1},... | collective-permute-start | bytes 786440 | tf_op jit(solution)/shard_map/ppermute | solution.py:152
  186.0 8.4 %collective-permute-start.15 = (bf16[64,2048]{1,0:T(8,128)(2,1)S(1)}, bf16[64,2048]{1,0:T(8,128)(2,1)S(1)}, u32[]{:S(2)}, u32[]{:S(2)}) collective-permute-start(bf16[64,2048]{1,0:T(8,128)(2,1)S(1)} %collective-permute-done.13), channel_id=1, source_target_pairs={{0,4},{2,6},{4,8},{6,10},{8,12},{10,14},{12,0},{14,2},{1,5},{3,7},... | collective-permute-start | bytes 786440 | tf_op jit(solution)/shard_map/ppermute | solution.py:151
  194.4 6.7 %collective-permute-start.16 = (bf16[64,2048]{1,0:T(8,128)(2,1)S(1)}, bf16[64,2048]{1,0:T(8,128)(2,1)S(1)}, u32[]{:S(2)}, u32[]{:S(2)}) collective-permute-start(bf16[64,2048]{1,0:T(8,128)(2,1)S(1)} %collective-permute-done.15), channel_id=1, source_target_pairs={{0,2},{2,0},{4,6},{6,4},{8,10},{10,8},{12,14},{14,12},{1,3},{3,1},... | collective-permute-start | bytes 786440 | tf_op jit(solution)/shard_map/ppermute | solution.py:152
  201.2 21.2 %collective-permute-start.17 = (bf16[256,2048]{1,0:T(8,128)(2,1)S(1)}, bf16[256,2048]{1,0:T(8,128)(2,1)S(1)}, u32[]{:S(2)}, u32[]{:S(2)}) collective-permute-start(bf16[256,2048]{1,0:T(8,128)(2,1)S(1)} %pad_maximum_fusion.1), channel_id=1, source_target_pairs={{0,1},{1,0},{2,3},{3,2},{4,5},{5,4},{6,7},{7,6},{8,9},{9,8},{10,11... | collective-permute-start | bytes 3145736 | tf_op jit(solution)/shard_map/ppermute | solution.py:156
  221.9 21.2 %collective-permute-start.9 = (bf16[2,2,64,2048]{3,2,1,0:T(8,128)(2,1)S(1)}, bf16[2,2,64,2048]{3,2,1,0:T(8,128)(2,1)S(1)}, u32[]{:S(2)}, u32[]{:S(2)}) collective-permute-start(bf16[2,2,64,2048]{3,2,1,0:T(8,128)(2,1)S(1)} %bitcast.149), channel_id=1, source_target_pairs={{0,1},{1,0},{2,3},{3,2},{4,5},{5,4},{6,7},{7,6},{8,9},{9,8},{10,11... | collective-permute-start | bytes 3145736 | tf_op jit(solution)/shard_map/ppermute | solution.py:159
  243.0 2.7 collective-permute-start.18
  243.6 9.2 %collective-permute-start.11 = (bf16[64,2048]{1,0:T(8,128)(2,1)S(1)}, bf16[64,2048]{1,0:T(8,128)(2,1)S(1)}, u32[]{:S(2)}, u32[]{:S(2)}) collective-permute-start(bf16[64,2048]{1,0:T(8,128)(2,1)S(1)} %get-tuple-element.153), channel_id=1, source_target_pairs={{0,2},{2,0},{4,6},{6,4},{8,10},{10,8},{12,14},{14,12},{1,3},{3,1},... | collective-permute-start | bytes 786440 | tf_op jit(solution)/shard_map/ppermute | solution.py:162
  245.4 25.2 %collective-permute-start.10 = (bf16[64,2048]{1,0:T(8,128)(2,1)S(1)}, bf16[64,2048]{1,0:T(8,128)(2,1)S(1)}, u32[]{:S(2)}, u32[]{:S(2)}) collective-permute-start(bf16[64,2048]{1,0:T(8,128)(2,1)S(1)} %get-tuple-element.152), channel_id=1, source_target_pairs={{0,2},{2,0},{4,6},{6,4},{8,10},{10,8},{12,14},{14,12},{1,3},{3,1},... | collective-permute-start | bytes 786440 | tf_op jit(solution)/shard_map/ppermute | solution.py:162
  246.2 43.3 %copy-start.1 = (bf16[64,2048]{1,0:T(8,128)(2,1)S(1)}, bf16[64,2048]{1,0:T(8,128)(2,1)}, u32[]{:S(2)}) copy-start(bf16[64,2048]{1,0:T(8,128)(2,1)} %param.12) | copy-start | bytes 786436
  246.2 43.3 %copy-start.2 = (bf16[64,2048]{1,0:T(8,128)(2,1)S(1)}, bf16[64,2048]{1,0:T(8,128)(2,1)}, u32[]{:S(2)}) copy-start(bf16[64,2048]{1,0:T(8,128)(2,1)} %reduce-scatter.2.cloned.1.call-done) | copy-start | bytes 786436
  246.2 17.8 %collective-permute-start.19 = (bf16[64,2048]{1,0:T(8,128)(2,1)S(1)}, bf16[64,2048]{1,0:T(8,128)(2,1)S(1)}, u32[]{:S(2)}, u32[]{:S(2)}) collective-permute-start(bf16[64,2048]{1,0:T(8,128)(2,1)S(1)} %get-tuple-element.154), channel_id=1, source_target_pairs={{0,2},{2,0},{4,6},{6,4},{8,10},{10,8},{12,14},{14,12},{1,3},{3,1},... | collective-permute-start | bytes 786440 | tf_op jit(solution)/shard_map/ppermute | solution.py:162
  248.0 21.2 %collective-permute-start.21 = (bf16[64,2048]{1,0:T(8,128)(2,1)S(1)}, bf16[64,2048]{1,0:T(8,128)(2,1)S(1)}, u32[]{:S(2)}, u32[]{:S(2)}) collective-permute-start(bf16[64,2048]{1,0:T(8,128)(2,1)S(1)} %get-tuple-element.155), channel_id=1, source_target_pairs={{0,2},{2,0},{4,6},{6,4},{8,10},{10,8},{12,14},{14,12},{1,3},{3,1},... | collective-permute-start | bytes 786440 | tf_op jit(solution)/shard_map/ppermute | solution.py:162
  252.8 17.8 %collective-permute-start.12 = (bf16[64,2048]{1,0:T(8,128)(2,1)S(1)}, bf16[64,2048]{1,0:T(8,128)(2,1)S(1)}, u32[]{:S(2)}, u32[]{:S(2)}) collective-permute-start(bf16[64,2048]{1,0:T(8,128)(2,1)S(1)} %fusion.18), channel_id=1, source_target_pairs={{0,12},{2,14},{4,0},{6,2},{8,4},{10,6},{12,8},{14,10},{1,13},{3,15... | collective-permute-start | bytes 786440 | tf_op jit(solution)/shard_map/ppermute | solution.py:165
  269.3 11.1 %collective-permute-start.22 = (bf16[64,2048]{1,0:T(8,128)(2,1)S(1)}, bf16[64,2048]{1,0:T(8,128)(2,1)S(1)}, u32[]{:S(2)}, u32[]{:S(2)}) collective-permute-start(bf16[64,2048]{1,0:T(8,128)(2,1)S(1)} %get-tuple-element.145), channel_id=1, source_target_pairs={{0,4},{2,6},{4,8},{6,10},{8,12},{10,14},{12,0},{14,2},{1,5},{3,7},... | collective-permute-start | bytes 786440 | tf_op jit(solution)/shard_map/ppermute | solution.py:165
  269.4 20.1 %collective-permute-start.20 = (bf16[64,2048]{1,0:T(8,128)(2,1)S(1)}, bf16[64,2048]{1,0:T(8,128)(2,1)S(1)}, u32[]{:S(2)}, u32[]{:S(2)}) collective-permute-start(bf16[64,2048]{1,0:T(8,128)(2,1)S(1)} %get-tuple-element.144), channel_id=1, source_target_pairs={{0,8},{2,10},{4,12},{6,14},{8,0},{10,2},{12,4},{14,6},{1,9},{3,11}... | collective-permute-start | bytes 786440 | tf_op jit(solution)/shard_map/ppermute | solution.py:165
Sparse Core Ops, SparseCore 0:
  9.5 136.4 all-gather.1
  153.3 6.4 reduce-scatter.1

commit v2 on v1

--- a/solution.py
+++ b/solution.py
@@ -7,7 +7,7 @@
 
 HD = 128
 CAP = 12
-FCHUNK = 256
+FCHUNK = 768
 
 
 def ring(size, step):
@@ -16,6 +16,146 @@
 
 def swap(size):
     return [(i, i ^ 1) for i in range(size)]
+
+
+neg_large = -1e30
+
+
+def wide(value):
+    return value.astype(jnp.float32)
+
+
+def attend_kernel(starts_ref, key_pos_ref, query_ref, keyed_ref, out_ref):
+    rows = query_ref.shape[1]
+    heads = query_ref.shape[2] // HD
+    stacked = jnp.concatenate([query_ref[0, :, h * HD : (h + 1) * HD] for h in range(heads)], axis=0)
+    scores = lax.dot_general(
+        stacked, keyed_ref[:, :HD], (((1,), (1,)), ((), ())), preferred_element_type=jnp.float32
+    )
+    offset = lax.broadcasted_iota(jnp.int32, (heads * rows, 1), 0) % rows
+    allowed = key_pos_ref[...] <= starts_ref[pl.program_id(0)] + offset
+    scores = jnp.where(allowed, scores, neg_large)
+    largest = jnp.max(scores, axis=-1, keepdims=True)
+    exps = jnp.exp((scores - largest) * (HD**-0.5))
+    total = jnp.sum(exps, axis=-1, keepdims=True)
+    summed = jnp.dot(exps.astype(jnp.bfloat16), keyed_ref[:, HD:], preferred_element_type=jnp.float32)
+    context = (summed / total).astype(jnp.bfloat16)
+    for h in range(heads):
+        out_ref[0, :, h * HD : (h + 1) * HD] = context[h * rows : (h + 1) * rows]
+
+
+def attend(starts, key_pos, query_blocks, keyed):
+    blocks, rows, columns = query_blocks.shape
+    length = keyed.shape[0]
+    work = blocks * rows * columns * length
+    return pl.pallas_call(
+        attend_kernel,
+        grid_spec=pltpu.PrefetchScalarGridSpec(
+            num_scalar_prefetch=1,
+            grid=(blocks,),
+            in_specs=[
+                pl.BlockSpec((1, length), lambda i, s: (0, 0)),
+                pl.BlockSpec((1, rows, columns), lambda i, s: (i, 0, 0)),
+                pl.BlockSpec((length, 2 * HD), lambda i, s: (0, 0)),
+            ],
+            out_specs=pl.BlockSpec((1, rows, columns), lambda i, s: (i, 0, 0)),
+        ),
+        out_shape=jax.ShapeDtypeStruct(query_blocks.shape, jnp.bfloat16),
+        compiler_params=pltpu.CompilerParams(vmem_limit_bytes=32 * 1024 * 1024),
+        cost_estimate=pl.CostEstimate(flops=4 * work, bytes_accessed=4 * query_blocks.size, transcendentals=work // HD),
+        name="attend",
+    )(starts, key_pos, query_blocks, keyed)
+
+
+def project_kernel(place_ref, own_ref, other_ref, own_weight_ref, other_weight_ref, out_ref):
+    dims = (((1,), (1,)), ((), ()))
+    out_ref[...] = (
+        lax.dot_general(own_ref[...], own_weight_ref[0], dims, preferred_element_type=jnp.float32)
+        + lax.dot_general(other_ref[...], other_weight_ref[0], dims, preferred_element_type=jnp.float32)
+    ).astype(jnp.bfloat16)
+
+
+def project(place, own, other, own_weight, other_weight):
+    blocks, features, columns = own_weight.shape
+    rows = own.shape[0]
+    if features % HD:
+        order = jnp.argsort(place)
+        weight = jnp.concatenate([own_weight, other_weight], axis=2)[order]
+        both = jnp.concatenate([own, other], axis=1)
+        result = jnp.einsum("rc,bfc->rbf", both, weight, preferred_element_type=jnp.float32)
+        return result.reshape(rows, -1).astype(jnp.bfloat16)
+    return pl.pallas_call(
+        project_kernel,
+        grid_spec=pltpu.PrefetchScalarGridSpec(
+            num_scalar_prefetch=1,
+            grid=(blocks,),
+            in_specs=[
+                pl.BlockSpec((rows, columns), lambda i, p: (0, 0)),
+                pl.BlockSpec((rows, columns), lambda i, p: (0, 0)),
+                pl.BlockSpec((1, features, columns), lambda i, p: (i, 0, 0)),
+                pl.BlockSpec((1, features, columns), lambda i, p: (i, 0, 0)),
+            ],
+            out_specs=pl.BlockSpec((rows, features), lambda i, p: (0, p[i])),
+        ),
+        out_shape=jax.ShapeDtypeStruct((rows, blocks * features), jnp.bfloat16),
+        compiler_params=pltpu.CompilerParams(vmem_limit_bytes=16 * 1024 * 1024),
+        cost_estimate=pl.CostEstimate(
+            flops=4 * rows * columns * blocks * features, bytes_accessed=4 * own_weight.size, transcendentals=0
+        ),
+        name="project",
+    )(place, own, other, own_weight, other_weight)
+
+
+def attention_block(queries, key_rows, value_rows, out_weight):
+    size = lax.axis_size("seq")
+    depth = size // 2
+    z, y = lax.axis_index("seq") // 2, lax.axis_index("seq") % 2
+    rows = queries.shape[0]
+    columns = queries.shape[1] // depth
+    per_group = queries.shape[1] // key_rows.shape[1] * HD
+
+    def heads_of(array, step):
+        return lax.dynamic_slice_in_dim(array, (z + step) % depth * columns, columns, axis=1)
+
+    def keyed_of(step):
+        start = (z + step) % depth * columns // per_group * HD
+        return [lax.dynamic_slice_in_dim(array, start, HD, axis=1) for array in (key_rows, value_rows)]
+
+    steps = sorted(range(1, depth), key=lambda d: -min(d, depth - d))
+    message = {0: jnp.concatenate([heads_of(queries, 0)] + keyed_of(0), axis=1)}
+    for d in steps:
+        sent = jnp.concatenate([heads_of(queries, d)] + keyed_of(d), axis=1)
+        message[d] = lax.ppermute(sent, "seq", ring(size, d))
+    keyed = {d: message[d][:, columns:] for d in message}
+    across = {d: lax.ppermute(keyed[d], "seq", swap(size)) for d in [0] + steps}
+    weight = {0: heads_of(out_weight, 0)}
+    for d in steps:
+        weight[d] = lax.ppermute(heads_of(out_weight, d), "seq", ring(size, d))
+    weight_across = {d: lax.ppermute(weight[d], "seq", swap(size)) for d in [0] + steps}
+
+    behind = (z - jnp.arange(depth, dtype=jnp.int32)) % depth
+    block = (behind[:, None] * 2 + jnp.stack([y, 1 - y])[None, :]).astype(jnp.int32)
+    key_pos = (block.reshape(-1, 1) * rows + jnp.arange(rows, dtype=jnp.int32)).reshape(1, -1)
+    context = attend(
+        block[:, 0] * rows,
+        key_pos,
+        jnp.stack([message[d][:, :columns] for d in range(depth)]),
+        jnp.concatenate([part for d in range(depth) for part in (keyed[d], across[d])]),
+    )
+    halves = context.reshape(depth, 2, rows // 2, columns)
+    core = lax.axis_index("exp")
+    own = lax.dynamic_index_in_dim(halves, core, 1, keepdims=False).reshape(-1, columns)
+    given = lax.dynamic_index_in_dim(halves, 1 - core, 1, keepdims=False).reshape(-1, columns)
+    other = lax.ppermute(given, "exp", swap(2))
+
+    own_weight = jnp.stack([part for d in range(depth) for part in (weight[d], weight_across[d])])
+    other_weight = lax.ppermute(own_weight, "exp", swap(2))
+    partial = project(block.reshape(-1), own, other, own_weight, other_weight)
+    partial = partial.reshape(depth, rows // 2, -1)
+    total = wide(partial[0])
+    for d in steps:
+        total = total + wide(lax.ppermute(partial[d], "seq", ring(size, -d)))
+    return total
 
 
 def gather_meta(meta, size, depth):
@@ -119,10 +259,6 @@
     )(x, select, spread, row_gate, expert_in, expert_in, expert_out)
 
 
-def wide(value):
-    return value.astype(jnp.float32)
-
-
 def expert_block(mixed, norm_gain, expert_ids, gate_weights, expert_in, expert_out):
     size = lax.axis_size("seq")
     depth = size // 2
@@ -167,34 +303,6 @@
     return total.astype(jnp.bfloat16)
 
 
-neg_large = -1e30
-
-
-def attend_piece(state, query_group, key_piece, value_piece, key_start, query_start):
-    largest, total, summed = state
-    length = key_piece.shape[0]
-    groups = query_group.shape[1]
-    head_size = query_group.shape[3]
-    rows = query_group.shape[0]
-    keyed = key_piece.reshape(length, groups, head_size)
-    valued = value_piece.reshape(length, groups, head_size)
-    scores = jnp.einsum(
-        "tghd,sgd->gths", query_group, keyed, preferred_element_type=jnp.float32
-    ) / jnp.sqrt(jnp.float32(head_size))
-    query_pos = query_start + jnp.arange(rows, dtype=jnp.int32)
-    key_pos = key_start + jnp.arange(length, dtype=jnp.int32)
-    allowed = (key_pos[None, :] <= query_pos[:, None])[None, :, None, :]
-    scores = jnp.where(allowed, scores, neg_large)
-    new_largest = jnp.maximum(largest, jnp.max(scores, axis=-1))
-    rescale = jnp.exp(largest - new_largest)
-    exps = jnp.where(allowed, jnp.exp(scores - new_largest[..., None]), 0.0)
-    total = total * rescale + jnp.sum(exps, axis=-1)
-    summed = summed * rescale[..., None] + jnp.einsum(
-        "gths,sgd->gthd", exps.astype(jnp.bfloat16), valued, preferred_element_type=jnp.float32
-    )
-    return (new_largest, total, summed)
-
-
 def on_device(
     stream,
     queries,
@@ -207,46 +315,8 @@
     expert_in,
     expert_out,
 ):
-    rows = queries.shape[0]
-    local_groups = key_rows.shape[1] // HD
-    per_group = queries.shape[1] // (local_groups * HD)
-    query_group = queries.reshape(rows, local_groups, per_group, HD)
-    query_start = lax.axis_index("seq") * rows
-    initial = (
-        jnp.full((local_groups, rows, per_group), neg_large, jnp.float32),
-        jnp.zeros((local_groups, rows, per_group), jnp.float32),
-        jnp.zeros((local_groups, rows, per_group, HD), jnp.float32),
-    )
-    state = initial
-    key_piece = lax.all_gather(key_rows, "seq", axis=0, tiled=True)
-    value_piece = lax.all_gather(value_rows, "seq", axis=0, tiled=True)
-    length = key_piece.shape[0]
-    count = length // 512
-    key_blocks = key_piece.reshape(count, 512, key_piece.shape[1])
-    value_blocks = value_piece.reshape(count, 512, value_piece.shape[1])
-    offsets = jnp.arange(count, dtype=jnp.int32) * 512
-
-    def step(carry, block):
-        return (attend_piece(carry, query_group, block[0], block[1], block[2], query_start), None)
-
-    state, unused = lax.scan(step, state, (key_blocks, value_blocks, offsets))
-    largest, total, summed = state
-    context = (
-        (summed / total[..., None]).transpose(1, 0, 2, 3).reshape(rows, -1).astype(jnp.bfloat16)
-    )
-    seq_count = lax.axis_size("seq")
-    exp_count = lax.axis_size("exp")
-    local_rows = stream.shape[0]
-    partial_heads = lax.dot_general(
-        context,
-        lax.all_gather(out_weight, "seq", axis=0, tiled=True),
-        (((1,), (1,)), ((), ())),
-        preferred_element_type=jnp.float32,
-    )
-    attn_out = lax.psum_scatter(
-        partial_heads.astype(jnp.bfloat16), "exp", scatter_dimension=0, tiled=True
-    ).astype(jnp.float32)
-    mixed = stream.astype(jnp.float32) + attn_out
+    attn_out = attention_block(queries, key_rows, value_rows, out_weight)
+    mixed = wide(stream) + attn_out
     return expert_block(mixed, norm_gain, expert_ids, gate_weights, expert_in, expert_out)
 
 

time: 298 us -> 245 us (0.82)
  blocking collectives: 66.2 us -> 0 us
  starting transfers between devices: 21 us -> 43.6 us
  matrix products: 20.5 us -> 0 us
  waiting for transfers between devices: 107 us -> 121 us
  between operations: 13.9 us -> 0.72 us
  local copies, waits for them, and re-layouts: 9.91 us -> 23 us
  other arithmetic: 18.1 us -> 12.4 us
  Pallas kernels: 40.6 us -> 43.8 us
    all_gather x2 -> x0, blocking collectives: 66.2 us -> none  [the longest x1 33.5 us: on_device(): key_piece = lax.all_gather(key_rows, 'seq', axis=0, tiled=True)]
    ppermute x0 -> x19, waiting for transfers between devices: none -> 49.3 us  [the longest x3 21.3 us: attention_block(): total = total + wide(lax.ppermute(partial[d], 'seq', ring(size, -d)))]
    all_gather x1 -> x0, waiting for transfers between devices: 32.7 us -> none  [on_device(): lax.all_gather(out_weight, 'seq', axis=0, tiled=True)]
    ppermute x0 -> x19, starting transfers between devices: none -> 27.7 us  [the longest x3 7.69 us: attention_block(): weight[d] = lax.ppermute(heads_of(out_weight, d), 'seq', ring(size, d))]
    dot_general x5 -> x0, matrix products: 20.5 us -> none  [the longest x2 7.76 us: attend_piece(): jnp.einsum('gths,sgd->gthd', exps.astype(jnp.bfloat16), valued, preferred...]
    pallas_call x0 -> x2, Pallas kernels: none -> 13.3 us  [the longest x1 7.05 us: attend(): pl.pallas_call(attend_kernel, grid_spec=pltpu.PrefetchScalarGridSpec(num_...]
    pallas_call x2, Pallas kernels: 40.6 us -> 30.6 us  [run_experts(): pl.pallas_call(expert_kernel, grid=(local_experts, chunks), out_shape=jax...]
    reduce_sum x2 -> x0, other arithmetic: 6.37 us -> none  [attend_piece(): total = total * rescale + jnp.sum(exps, axis=-1)]
  transfers between devices with their start and end apart: 25 -> 42, of which waited for: 14 -> 22; matrix products, arithmetic and copies ran while one was open for 13% -> 12% of each run, Pallas kernels for 14% -> 15%
where the time goes in v2:
time: 245 us; the launch traced here: 244 us
  waiting for transfers between devices  121 us (49%)
  Pallas kernels  43.8 us (18%)
  starting transfers between devices  43.6 us (18%)
  local copies, waits for them, and re-layouts  23 us (9%)
  other arithmetic  12.4 us (5%)
    pallas_call x2, Pallas kernels, run_experts(): pl.pallas_call(expert_kernel, grid=(local_experts, chunks), out_shape=jax...  30.6 us
    ppermute x3, waiting for transfers between devices, attention_block(): total = total + wide(lax.ppermute(partial[d], 'seq', ring(size, -d)))  21.3 us
    ppermute x4, waiting for transfers between devices, expert_block(): there = lax.ppermute(pair[place, 1].astype(jnp.bfloat16), 'seq', swap(size))  20.8 us
    ppermute x3, waiting for transfers between devices, expert_block(): chip = wide(lax.ppermute(chip.astype(jnp.bfloat16), 'seq', ring(size, -d)))  20 us
    ppermute x3, waiting for transfers between devices, expert_block(): along.append(lax.ppermute(along[d], 'seq', ring(size, 1)))  17 us
    ppermute x4, waiting for transfers between devices, attention_block(): lax.ppermute(weight[d], 'seq', swap(size))  12.1 us
    ppermute x3, waiting for transfers between devices, attention_block(): weight[d] = lax.ppermute(heads_of(out_weight, d), 'seq', ring(size, d))  10 us
    ppermute x4, waiting for transfers between devices, expert_block(): across.append(lax.ppermute(along[d], 'seq', swap(size)))  9.66 us
  transfers between devices with their start and end apart: 42, of which 22 were waited for; matrix products, arithmetic and copies ran while one was open for 12% of the time, Pallas kernels for 15%

profile of v2, /device:TPU:0, one launch (start us, length us, event | category | flops | bytes accessed | tf_op | source)
XLA Modules:
  0.0 244.1 jit_solution(9289491882936052818)
XLA Ops:
  1.5 5.1 %collective-permute-start.25 = (bf16[64,24]{0,1:T(8,128)(2,1)S(1)}, bf16[64,24]{0,1:T(8,128)(2,1)S(1)}, u32[]{:S(2)}, u32[]{:S(2)}) collective-permute-start(bf16[64,24]{0,1:T(8,128)(2,1)S(1)} %get-tuple-element.70), channel_id=1, source_target_pairs={{0,12},{2,14},{4,0},{6,2},{8,4},{10,6},{12,8},{14,10},{1,13},{3,15... | collective-permute-start | bytes 9224 | tf_op jit(solution)/shard_map/ppermute | solution.py:162
  7.6 1.8 dynamic-slice_bitcast_fusion
  11.0 2.8 %collective-permute-start.2 = (bf16[128,768]{1,0:T(8,128)(2,1)}, bf16[128,768]{1,0:T(8,128)(2,1)}, u32[]{:S(2)}, u32[]{:S(2)}) collective-permute-start(bf16[128,768]{1,0:T(8,128)(2,1)} %pad_maximum_fusion.5), channel_id=1, source_target_pairs={{0,12},{2,14},{4,0},{6,2},{8,4},{10,6},{12,8},{14,10},{1,13},{3,15... | collective-permute-start | bytes 589832 | tf_op jit(solution)/shard_map/ppermute | solution.py:128
  19.1 1.6 collective-permute-start.3
  21.2 3.3 %collective-permute-done.26 = bf16[4,64,24]{1,2,0:T(8,128)(2,1)S(1)} collective-permute-done((bf16[4,64,24]{1,2,0:T(8,128)(2,1)S(1)}, bf16[4,64,24]{1,2,0:T(8,128)(2,1)S(1)}, u32[]{:S(2)}, u32[]{:S(2)}) %collective-permute-start.26) | collective-permute-done | bytes 12320 | tf_op jit(solution)/shard_map/ppermute | solution.py:163
  28.9 2.3 collective-permute-start.9
  32.1 2.0 collective-permute-start.11
  35.0 3.4 %collective-permute-start.13 = (bf16[256,512]{1,0:T(8,128)(2,1)}, bf16[256,512]{1,0:T(8,128)(2,1)S(1)}, u32[]{:S(2)}, u32[]{:S(2)}) collective-permute-start(bf16[256,512]{1,0:T(8,128)(2,1)} %get-tuple-element.32), channel_id=1, source_target_pairs={{0,12},{2,14},{4,0},{6,2},{8,4},{10,6},{12,8},{14,10},{1,13},{3,15... | collective-permute-start | bytes 786440 | tf_op jit(solution)/shard_map/ppermute | solution.py:133
  38.3 1.9 collective-permute-done.9
  42.4 8.2 %collective-permute-done.11 = bf16[256,512]{1,0:T(8,128)(2,1)S(1)} collective-permute-done((bf16[256,512]{1,0:T(8,128)(2,1)}, bf16[256,512]{1,0:T(8,128)(2,1)S(1)}, u32[]{:S(2)}, u32[]{:S(2)}) %collective-permute-start.11) | collective-permute-done | bytes 262176 | tf_op jit(solution)/shard_map/ppermute | solution.py:133
  53.8 7.3 %collective-permute-done.12 = bf16[256,512]{1,0:T(8,128)(2,1)S(1)} collective-permute-done((bf16[256,512]{1,0:T(8,128)(2,1)S(1)}, bf16[256,512]{1,0:T(8,128)(2,1)S(1)}, u32[]{:S(2)}, u32[]{:S(2)}) %collective-permute-start.12) | collective-permute-done | bytes 262176 | tf_op jit(solution)/shard_map/ppermute | solution.py:134
  61.2 4.7 %collective-permute-done.14 = bf16[256,512]{1,0:T(8,128)(2,1)S(1)} collective-permute-done((bf16[256,512]{1,0:T(8,128)(2,1)S(1)}, bf16[256,512]{1,0:T(8,128)(2,1)S(1)}, u32[]{:S(2)}, u32[]{:S(2)}) %collective-permute-start.14) | collective-permute-done | bytes 262176 | tf_op jit(solution)/shard_map/ppermute | solution.py:134
  70.7 2.6 %collective-permute-done.5 = bf16[128,256]{1,0:T(8,128)(2,1)S(1)} collective-permute-done((bf16[128,256]{1,0:T(8,128)(2,1)S(1)}, bf16[128,256]{1,0:T(8,128)(2,1)S(1)}, u32[]{:S(2)}, u32[]{:S(2)}) %collective-permute-start.5) | collective-permute-done | bytes 65568 | tf_op jit(solution)/shard_map/ppermute | solution.py:130
  75.3 3.2 %collective-permute-done.6 = bf16[128,256]{1,0:T(8,128)(2,1)S(1)} collective-permute-done((bf16[128,256]{1,0:T(8,128)(2,1)S(1)}, bf16[128,256]{1,0:T(8,128)(2,1)S(1)}, u32[]{:S(2)}, u32[]{:S(2)}) %collective-permute-start.6) | collective-permute-done | bytes 65568 | tf_op jit(solution)/shard_map/ppermute | solution.py:130
  78.5 7.1 %attend.1 = bf16[4,128,512]{2,1,0:T(8,128)(2,1)S(1)} custom-call(s32[4]{0:T(128)S(1)} %multiply_bitcast_fusion.starts_ref, s32[1,1024]{1,0:T(1,128)S(1)} %bitcast.125, bf16[4,128,512]{2,1,0:T(8,128)(2,1)S(1)} %pad_maximum_fusion.2.query_ref, bf16[1024,256]{1,0:T(8,128)(2,1)S(1)} %constant_dynamic-update-slice_fusion.keyed_ref), custom_call_target="tpu_custom_call" | custom-call | flops 1073741824 | bytes 1048576 | tf_op jit(solution)/shard_map/attend/pallas_call | solution.py:51
  88.9 6.2 %project.1 = bf16[256,2048]{1,0:T(8,128)(2,1)S(1)} custom-call(s32[8]{0:T(128)S(1)} %add.218.place_ref, bf16[256,512]{1,0:T(8,128)(2,1)S(1)} %bitcast.123, bf16[256,512]{1,0:T(8,128)(2,1)S(1)} %copy-done.1, bf16[8,256,512]{2,1,0:T(8,128)(2,1)S(1)} %bitcast_dynamic-update-slice_fusion.own_weight_ref, bf16[8,256,512]{2,1,0:T(8,128)(2,1)} %collective-permute-done.15.other_weight_ref), custom_call_target="tpu_custom_call" | custom-call | flops 1073741824 | bytes 4194304 | tf_op jit(solution)/shard_map/project/pallas_call | solution.py:87
  95.9 4.6 %collective-permute-start.18 = (bf16[64,2048]{1,0:T(8,128)(2,1)}, bf16[64,2048]{1,0:T(8,128)(2,1)S(1)}, u32[]{:S(2)}, u32[]{:S(2)}) collective-permute-start(bf16[64,2048]{1,0:T(8,128)(2,1)} %get-tuple-element.30), channel_id=1, source_target_pairs={{0,4},{2,6},{4,8},{6,10},{8,12},{10,14},{12,0},{14,2},{1,5},{3,7},... | collective-permute-start | bytes 786440 | tf_op jit(solution)/shard_map/ppermute | solution.py:157
  100.5 1.9 collective-permute-start.17
  104.9 4.8 %collective-permute-done.18 = bf16[64,2048]{1,0:T(8,128)(2,1)S(1)} collective-permute-done((bf16[64,2048]{1,0:T(8,128)(2,1)}, bf16[64,2048]{1,0:T(8,128)(2,1)S(1)}, u32[]{:S(2)}, u32[]{:S(2)}) %collective-permute-start.18) | collective-permute-done | bytes 262176 | tf_op jit(solution)/shard_map/ppermute | solution.py:157
  109.8 4.6 %collective-permute-done.17 = bf16[64,2048]{1,0:T(8,128)(2,1)S(1)} collective-permute-done((bf16[64,2048]{1,0:T(8,128)(2,1)S(1)}, bf16[64,2048]{1,0:T(8,128)(2,1)S(1)}, u32[]{:S(2)}, u32[]{:S(2)}) %collective-permute-start.17) | collective-permute-done | bytes 262176 | tf_op jit(solution)/shard_map/ppermute | solution.py:157
  114.4 11.8 %collective-permute-done.16 = bf16[64,2048]{1,0:T(8,128)(2,1)S(1)} collective-permute-done((bf16[64,2048]{1,0:T(8,128)(2,1)S(1)}, bf16[64,2048]{1,0:T(8,128)(2,1)S(1)}, u32[]{:S(2)}, u32[]{:S(2)}) %collective-permute-start.16) | collective-permute-done | bytes 262176 | tf_op jit(solution)/shard_map/ppermute | solution.py:157
  131.8 6.8 %collective-permute-done.20 = bf16[64,2048]{1,0:T(8,128)(2,1)} collective-permute-done((bf16[64,2048]{1,0:T(8,128)(2,1)}, bf16[64,2048]{1,0:T(8,128)(2,1)}, u32[]{:S(2)}, u32[]{:S(2)}) %collective-permute-start.20) | collective-permute-done | bytes 262176 | tf_op jit(solution)/shard_map/ppermute | solution.py:287
  141.5 4.3 %collective-permute-done.21 = bf16[64,2048]{1,0:T(8,128)(2,1)S(1)} collective-permute-done((bf16[64,2048]{1,0:T(8,128)(2,1)}, bf16[64,2048]{1,0:T(8,128)(2,1)S(1)}, u32[]{:S(2)}, u32[]{:S(2)}) %collective-permute-start.21) | collective-permute-done | bytes 262176 | tf_op jit(solution)/shard_map/ppermute | solution.py:288
  149.4 9.0 %collective-permute-done.34 = bf16[64,2048]{1,0:T(8,128)(2,1)S(1)} collective-permute-done((bf16[64,2048]{1,0:T(8,128)(2,1)S(1)}, bf16[64,2048]{1,0:T(8,128)(2,1)S(1)}, u32[]{:S(2)}, u32[]{:S(2)}) %collective-permute-start.34) | collective-permute-done | bytes 262176 | tf_op jit(solution)/shard_map/ppermute | solution.py:287
  159.4 5.3 %collective-permute-done.35 = bf16[64,2048]{1,0:T(8,128)(2,1)S(1)} collective-permute-done((bf16[64,2048]{1,0:T(8,128)(2,1)S(1)}, bf16[64,2048]{1,0:T(8,128)(2,1)S(1)}, u32[]{:S(2)}, u32[]{:S(2)}) %collective-permute-start.35) | collective-permute-done | bytes 262176 | tf_op jit(solution)/shard_map/ppermute | solution.py:288
  165.1 15.3 %experts.2 = bf16[512,2048]{1,0:T(8,128)(2,1)S(1)} custom-call(bf16[2,256,2048]{2,1,0:T(8,128)(2,1)S(1)} %bitcast.122, bf16[4,2,48,256]{3,2,1,0:T(8,128)(2,1)S(1)} %get-tuple-element.67.select_ref, bf16[2,256,192]{2,1,0:T(8,128)(2,1)S(1)} %copy.41.spread_ref, f32[4,96,1]{2,1,0:T(8,128)S(1)} %reshape.197.gate_ref, bf16[4,2048,1536]{2,1,0:T(8,128)(2,1)} %wu_ref.3, ...), custom_call_target="tpu_custom_call" | custom-call | flops 3623878656 | bytes 41943040 | tf_op jit(solution)/shard_map/experts/pallas_call | solution.py:237
  181.2 15.3 %experts.3 = bf16[512,2048]{1,0:T(8,128)(2,1)S(1)} custom-call(bf16[2,256,2048]{2,1,0:T(8,128)(2,1)S(1)} %bitcast.121, bf16[4,2,48,256]{3,2,1,0:T(8,128)(2,1)S(1)} %get-tuple-element.48.select_ref, bf16[2,256,192]{2,1,0:T(8,128)(2,1)S(1)} %copy.47.spread_ref, f32[4,96,1]{2,1,0:T(8,128)S(1)} %reshape.198.gate_ref, bf16[4,2048,1536]{2,1,0:T(8,128)(2,1)} %wu_ref.3, ...), custom_call_target="tpu_custom_call" | custom-call | flops 3623878656 | bytes 41943040 | tf_op jit(solution)/shard_map/experts/pallas_call | solution.py:237
  202.0 4.4 %collective-permute-done.30 = bf16[64,2048]{1,0:T(8,128)(2,1)S(1)} collective-permute-done((bf16[64,2048]{1,0:T(8,128)(2,1)S(1)}, bf16[64,2048]{1,0:T(8,128)(2,1)S(1)}, u32[]{:S(2)}, u32[]{:S(2)}) %collective-permute-start.30) | collective-permute-done | bytes 262176 | tf_op jit(solution)/shard_map/ppermute | solution.py:298
  206.5 11.1 %collective-permute-done.38 = bf16[64,2048]{1,0:T(8,128)(2,1)S(1)} collective-permute-done((bf16[64,2048]{1,0:T(8,128)(2,1)S(1)}, bf16[64,2048]{1,0:T(8,128)(2,1)S(1)}, u32[]{:S(2)}, u32[]{:S(2)}) %collective-permute-start.38) | collective-permute-done | bytes 262176 | tf_op jit(solution)/shard_map/ppermute | solution.py:298
  217.6 5.2 %collective-permute-done.40 = bf16[64,2048]{1,0:T(8,128)(2,1)S(1)} collective-permute-done((bf16[64,2048]{1,0:T(8,128)(2,1)S(1)}, bf16[64,2048]{1,0:T(8,128)(2,1)S(1)}, u32[]{:S(2)}, u32[]{:S(2)}) %collective-permute-start.40) | collective-permute-done | bytes 262176 | tf_op jit(solution)/shard_map/ppermute | solution.py:298
  223.2 11.0 %collective-permute-done.41 = bf16[64,2048]{1,0:T(8,128)(2,1)S(1)} collective-permute-done((bf16[64,2048]{1,0:T(8,128)(2,1)S(1)}, bf16[64,2048]{1,0:T(8,128)(2,1)S(1)}, u32[]{:S(2)}, u32[]{:S(2)}) %collective-permute-start.41) | collective-permute-done | bytes 262176 | tf_op jit(solution)/shard_map/ppermute | solution.py:301
  234.1 9.1 %collective-permute-done.39 = bf16[64,2048]{1,0:T(8,128)(2,1)S(1)} collective-permute-done((bf16[64,2048]{1,0:T(8,128)(2,1)S(1)}, bf16[64,2048]{1,0:T(8,128)(2,1)S(1)}, u32[]{:S(2)}, u32[]{:S(2)}) %collective-permute-start.39) | collective-permute-done | bytes 262176 | tf_op jit(solution)/shard_map/ppermute | solution.py:301
  (198 shorter events, 55.5 us)
Async XLA Ops:
  1.5 17.6 %collective-permute-start.25 = (bf16[64,24]{0,1:T(8,128)(2,1)S(1)}, bf16[64,24]{0,1:T(8,128)(2,1)S(1)}, u32[]{:S(2)}, u32[]{:S(2)}) collective-permute-start(bf16[64,24]{0,1:T(8,128)(2,1)S(1)} %get-tuple-element.70), channel_id=1, source_target_pairs={{0,12},{2,14},{4,0},{6,2},{8,4},{10,6},{12,8},{14,10},{1,13},{3,15... | collective-permute-start | bytes 9224 | tf_op jit(solution)/shard_map/ppermute | solution.py:162
  6.6 12.5 %collective-permute-start.24 = (bf16[64,24]{0,1:T(8,128)(2,1)S(1)}, bf16[64,24]{0,1:T(8,128)(2,1)S(1)}, u32[]{:S(2)}, u32[]{:S(2)}) collective-permute-start(bf16[64,24]{0,1:T(8,128)(2,1)S(1)} %get-tuple-element.70), channel_id=1, source_target_pairs={{0,8},{2,10},{4,12},{6,14},{8,0},{10,2},{12,4},{14,6},{1,9},{3,11}... | collective-permute-start | bytes 9224 | tf_op jit(solution)/shard_map/ppermute | solution.py:162
  6.6 14.1 %collective-permute-start.23 = (bf16[64,24]{0,1:T(8,128)(2,1)S(1)}, bf16[64,24]{0,1:T(8,128)(2,1)S(1)}, u32[]{:S(2)}, u32[]{:S(2)}) collective-permute-start(bf16[64,24]{0,1:T(8,128)(2,1)S(1)} %get-tuple-element.70), channel_id=1, source_target_pairs={{0,4},{2,6},{4,8},{6,10},{8,12},{10,14},{12,0},{14,2},{1,5},{3,7},... | collective-permute-start | bytes 9224 | tf_op jit(solution)/shard_map/ppermute | solution.py:162
  11.0 58.8 %collective-permute-start.2 = (bf16[128,768]{1,0:T(8,128)(2,1)}, bf16[128,768]{1,0:T(8,128)(2,1)}, u32[]{:S(2)}, u32[]{:S(2)}) collective-permute-start(bf16[128,768]{1,0:T(8,128)(2,1)} %pad_maximum_fusion.5), channel_id=1, source_target_pairs={{0,12},{2,14},{4,0},{6,2},{8,4},{10,6},{12,8},{14,10},{1,13},{3,15... | collective-permute-start | bytes 589832 | tf_op jit(solution)/shard_map/ppermute | solution.py:128
  14.5 52.5 %collective-permute-start.1 = (bf16[128,768]{1,0:T(8,128)(2,1)}, bf16[128,768]{1,0:T(8,128)(2,1)}, u32[]{:S(2)}, u32[]{:S(2)}) collective-permute-start(bf16[128,768]{1,0:T(8,128)(2,1)} %pad_maximum_fusion.4), channel_id=1, source_target_pairs={{0,8},{2,10},{4,12},{6,14},{8,0},{10,2},{12,4},{14,6},{1,9},{3,11}... | collective-permute-start | bytes 589832 | tf_op jit(solution)/shard_map/ppermute | solution.py:128
  19.1 13.0 %collective-permute-start = (bf16[128,768]{1,0:T(8,128)(2,1)}, bf16[128,768]{1,0:T(8,128)(2,1)}, u32[]{:S(2)}, u32[]{:S(2)}) collective-permute-start(bf16[128,768]{1,0:T(8,128)(2,1)} %pad_maximum_fusion.3), channel_id=1, source_target_pairs={{0,4},{2,6},{4,8},{6,10},{8,12},{10,14},{12,0},{14,2},{1,5},{3,7},... | collective-permute-start | bytes 589832 | tf_op jit(solution)/shard_map/ppermute | solution.py:128
  19.1 9.9 %collective-permute-start.3 = (bf16[128,256]{1,0:T(8,128)(2,1)}, bf16[128,256]{1,0:T(8,128)(2,1)}, u32[]{:S(2)}, u32[]{:S(2)}) collective-permute-start(bf16[128,256]{1,0:T(8,128)(2,1)} %get-tuple-element.53), channel_id=1, source_target_pairs={{0,2},{2,0},{4,6},{6,4},{8,10},{10,8},{12,14},{14,12},{1,3},{3,1},... | collective-permute-start | bytes 196616 | tf_op jit(solution)/shard_map/ppermute | solution.py:130
  25.9 9.1 %collective-permute-start.8 = (bf16[256,512]{1,0:T(8,128)(2,1)}, bf16[256,512]{1,0:T(8,128)(2,1)}, u32[]{:S(2)}, u32[]{:S(2)}) collective-permute-start(bf16[256,512]{1,0:T(8,128)(2,1)} %get-tuple-element.14), channel_id=1, source_target_pairs={{0,2},{2,0},{4,6},{6,4},{8,10},{10,8},{12,14},{14,12},{1,3},{3,1},... | collective-permute-start | bytes 786440 | tf_op jit(solution)/shard_map/ppermute | solution.py:134
  28.9 11.3 %collective-permute-start.9 = (bf16[256,512]{1,0:T(8,128)(2,1)}, bf16[256,512]{1,0:T(8,128)(2,1)S(1)}, u32[]{:S(2)}, u32[]{:S(2)}) collective-permute-start(bf16[256,512]{1,0:T(8,128)(2,1)} %get-tuple-element.33), channel_id=1, source_target_pairs={{0,4},{2,6},{4,8},{6,10},{8,12},{10,14},{12,0},{14,2},{1,5},{3,7},... | collective-permute-start | bytes 786440 | tf_op jit(solution)/shard_map/ppermute | solution.py:133
  32.1 18.5 %collective-permute-start.11 = (bf16[256,512]{1,0:T(8,128)(2,1)}, bf16[256,512]{1,0:T(8,128)(2,1)S(1)}, u32[]{:S(2)}, u32[]{:S(2)}) collective-permute-start(bf16[256,512]{1,0:T(8,128)(2,1)} %get-tuple-element.34), channel_id=1, source_target_pairs={{0,8},{2,10},{4,12},{6,14},{8,0},{10,2},{12,4},{14,6},{1,9},{3,11}... | collective-permute-start | bytes 786440 | tf_op jit(solution)/shard_map/ppermute | solution.py:133
  35.0 16.8 %collective-permute-start.13 = (bf16[256,512]{1,0:T(8,128)(2,1)}, bf16[256,512]{1,0:T(8,128)(2,1)S(1)}, u32[]{:S(2)}, u32[]{:S(2)}) collective-permute-start(bf16[256,512]{1,0:T(8,128)(2,1)} %get-tuple-element.32), channel_id=1, source_target_pairs={{0,12},{2,14},{4,0},{6,2},{8,4},{10,6},{12,8},{14,10},{1,13},{3,15... | collective-permute-start | bytes 786440 | tf_op jit(solution)/shard_map/ppermute | solution.py:133
  40.2 12.4 %collective-permute-start.10 = (bf16[256,512]{1,0:T(8,128)(2,1)S(1)}, bf16[256,512]{1,0:T(8,128)(2,1)S(1)}, u32[]{:S(2)}, u32[]{:S(2)}) collective-permute-start(bf16[256,512]{1,0:T(8,128)(2,1)S(1)} %collective-permute-done.9), channel_id=1, source_target_pairs={{0,2},{2,0},{4,6},{6,4},{8,10},{10,8},{12,14},{14,12},{1,3},{3,1},... | collective-permute-start | bytes 786440 | tf_op jit(solution)/shard_map/ppermute | solution.py:134
  50.6 17.3 %collective-permute-start.4 = (bf16[128,256]{1,0:T(8,128)(2,1)S(1)}, bf16[128,256]{1,0:T(8,128)(2,1)S(1)}, u32[]{:S(2)}, u32[]{:S(2)}) collective-permute-start(bf16[128,256]{1,0:T(8,128)(2,1)S(1)} %get-tuple-element.45), channel_id=1, source_target_pairs={{0,2},{2,0},{4,6},{6,4},{8,10},{10,8},{12,14},{14,12},{1,3},{3,1},... | collective-permute-start | bytes 196616 | tf_op jit(solution)/shard_map/ppermute | solution.py:130
  51.8 9.4 %collective-permute-start.12 = (bf16[256,512]{1,0:T(8,128)(2,1)S(1)}, bf16[256,512]{1,0:T(8,128)(2,1)S(1)}, u32[]{:S(2)}, u32[]{:S(2)}) collective-permute-start(bf16[256,512]{1,0:T(8,128)(2,1)S(1)} %collective-permute-done.11), channel_id=1, source_target_pairs={{0,2},{2,0},{4,6},{6,4},{8,10},{10,8},{12,14},{14,12},{1,3},{3,1},... | collective-permute-start | bytes 786440 | tf_op jit(solution)/shard_map/ppermute | solution.py:134
  52.6 13.3 %collective-permute-start.14 = (bf16[256,512]{1,0:T(8,128)(2,1)S(1)}, bf16[256,512]{1,0:T(8,128)(2,1)S(1)}, u32[]{:S(2)}, u32[]{:S(2)}) collective-permute-start(bf16[256,512]{1,0:T(8,128)(2,1)S(1)} %collective-permute-done.13), channel_id=1, source_target_pairs={{0,2},{2,0},{4,6},{6,4},{8,10},{10,8},{12,14},{14,12},{1,3},{3,1},... | collective-permute-start | bytes 786440 | tf_op jit(solution)/shard_map/ppermute | solution.py:134
  66.0 22.0 %collective-permute-start.15 = (bf16[8,256,512]{2,1,0:T(8,128)(2,1)S(1)}, bf16[8,256,512]{2,1,0:T(8,128)(2,1)}, u32[]{:S(2)}, u32[]{:S(2)}) collective-permute-start(bf16[8,256,512]{2,1,0:T(8,128)(2,1)S(1)} %bitcast_dynamic-update-slice_fusion.own_weight_ref), channel_id=1, source_target_pairs={{0,1},{1,0},{2,3},{3,2},{4,5},{5,4},{6,7},{7,6},{8,9},{9,8},{10,11... | collective-permute-start | bytes 6291464 | tf_op jit(solution)/shard_map/ppermute | solution.py:152
  95.9 13.8 %collective-permute-start.18 = (bf16[64,2048]{1,0:T(8,128)(2,1)}, bf16[64,2048]{1,0:T(8,128)(2,1)S(1)}, u32[]{:S(2)}, u32[]{:S(2)}) collective-permute-start(bf16[64,2048]{1,0:T(8,128)(2,1)} %get-tuple-element.30), channel_id=1, source_target_pairs={{0,4},{2,6},{4,8},{6,10},{8,12},{10,14},{12,0},{14,2},{1,5},{3,7},... | collective-permute-start | bytes 786440 | tf_op jit(solution)/shard_map/ppermute | solution.py:157
  100.5 13.9 %collective-permute-start.17 = (bf16[64,2048]{1,0:T(8,128)(2,1)S(1)}, bf16[64,2048]{1,0:T(8,128)(2,1)S(1)}, u32[]{:S(2)}, u32[]{:S(2)}) collective-permute-start(bf16[64,2048]{1,0:T(8,128)(2,1)S(1)} %get-tuple-element.31), channel_id=1, source_target_pairs={{0,12},{2,14},{4,0},{6,2},{8,4},{10,6},{12,8},{14,10},{1,13},{3,15... | collective-permute-start | bytes 786440 | tf_op jit(solution)/shard_map/ppermute | solution.py:157
  102.4 23.9 %collective-permute-start.16 = (bf16[64,2048]{1,0:T(8,128)(2,1)S(1)}, bf16[64,2048]{1,0:T(8,128)(2,1)S(1)}, u32[]{:S(2)}, u32[]{:S(2)}) collective-permute-start(bf16[64,2048]{1,0:T(8,128)(2,1)S(1)} %get-tuple-element.29), channel_id=1, source_target_pairs={{0,8},{2,10},{4,12},{6,14},{8,0},{10,2},{12,4},{14,6},{1,9},{3,11}... | collective-permute-start | bytes 786440 | tf_op jit(solution)/shard_map/ppermute | solution.py:157
  127.4 12.1 %collective-permute-start.19 = (bf16[64,2048]{1,0:T(8,128)(2,1)}, bf16[64,2048]{1,0:T(8,128)(2,1)}, u32[]{:S(2)}, u32[]{:S(2)}) collective-permute-start(bf16[64,2048]{1,0:T(8,128)(2,1)} %get-tuple-element.10), channel_id=1, source_target_pairs={{0,2},{2,0},{4,6},{6,4},{8,10},{10,8},{12,14},{14,12},{1,3},{3,1},... | collective-permute-start | bytes 786440 | tf_op jit(solution)/shard_map/ppermute | solution.py:288
  128.4 10.1 %collective-permute-start.20 = (bf16[64,2048]{1,0:T(8,128)(2,1)}, bf16[64,2048]{1,0:T(8,128)(2,1)}, u32[]{:S(2)}, u32[]{:S(2)}) collective-permute-start(bf16[64,2048]{1,0:T(8,128)(2,1)} %get-tuple-element.10), channel_id=1, source_target_pairs={{0,4},{2,6},{4,8},{6,10},{8,12},{10,14},{12,0},{14,2},{1,5},{3,7},... | collective-permute-start | bytes 786440 | tf_op jit(solution)/shard_map/ppermute | solution.py:287
  147.0 17.9 %collective-permute-start.22 = (bf16[256,2048]{1,0:T(8,128)(2,1)S(1)}, bf16[256,2048]{1,0:T(8,128)(2,1)S(1)}, u32[]{:S(2)}, u32[]{:S(2)}) collective-permute-start(bf16[256,2048]{1,0:T(8,128)(2,1)S(1)} %pad_maximum_fusion), channel_id=1, source_target_pairs={{0,1},{1,0},{2,3},{3,2},{4,5},{5,4},{6,7},{7,6},{8,9},{9,8},{10,11... | collective-permute-start | bytes 3145736 | tf_op jit(solution)/shard_map/ppermute | solution.py:292
  148.4 11.0 %collective-permute-start.33 = (bf16[64,2048]{1,0:T(8,128)(2,1)S(1)}, bf16[64,2048]{1,0:T(8,128)(2,1)S(1)}, u32[]{:S(2)}, u32[]{:S(2)}) collective-permute-start(bf16[64,2048]{1,0:T(8,128)(2,1)S(1)} %collective-permute-done.32), channel_id=1, source_target_pairs={{0,2},{2,0},{4,6},{6,4},{8,10},{10,8},{12,14},{14,12},{1,3},{3,1},... | collective-permute-start | bytes 786440 | tf_op jit(solution)/shard_map/ppermute | solution.py:288
  164.9 16.2 %collective-permute-start.36 = (bf16[256,2048]{1,0:T(8,128)(2,1)S(1)}, bf16[256,2048]{1,0:T(8,128)(2,1)S(1)}, u32[]{:S(2)}, u32[]{:S(2)}) collective-permute-start(bf16[256,2048]{1,0:T(8,128)(2,1)S(1)} %pad_maximum_fusion.1), channel_id=1, source_target_pairs={{0,1},{1,0},{2,3},{3,2},{4,5},{5,4},{6,7},{7,6},{8,9},{9,8},{10,11... | collective-permute-start | bytes 3145736 | tf_op jit(solution)/shard_map/ppermute | solution.py:292
  180.6 16.2 %collective-permute-start.28 = (bf16[2,2,64,2048]{3,2,1,0:T(8,128)(2,1)S(1)}, bf16[2,2,64,2048]{3,2,1,0:T(8,128)(2,1)S(1)}, u32[]{:S(2)}, u32[]{:S(2)}) collective-permute-start(bf16[2,2,64,2048]{3,2,1,0:T(8,128)(2,1)S(1)} %bitcast.129), channel_id=1, source_target_pairs={{0,1},{1,0},{2,3},{3,2},{4,5},{5,4},{6,7},{7,6},{8,9},{9,8},{10,11... | collective-permute-start | bytes 3145736 | tf_op jit(solution)/shard_map/ppermute | solution.py:295
  197.2 9.2 %collective-permute-start.30 = (bf16[64,2048]{1,0:T(8,128)(2,1)S(1)}, bf16[64,2048]{1,0:T(8,128)(2,1)S(1)}, u32[]{:S(2)}, u32[]{:S(2)}) collective-permute-start(bf16[64,2048]{1,0:T(8,128)(2,1)S(1)} %get-tuple-element.26), channel_id=1, source_target_pairs={{0,2},{2,0},{4,6},{6,4},{8,10},{10,8},{12,14},{14,12},{1,3},{3,1},... | collective-permute-start | bytes 786440 | tf_op jit(solution)/shard_map/ppermute | solution.py:298
  198.3 24.9 %collective-permute-start.29 = (bf16[64,2048]{1,0:T(8,128)(2,1)S(1)}, bf16[64,2048]{1,0:T(8,128)(2,1)S(1)}, u32[]{:S(2)}, u32[]{:S(2)}) collective-permute-start(bf16[64,2048]{1,0:T(8,128)(2,1)S(1)} %get-tuple-element.25), channel_id=1, source_target_pairs={{0,2},{2,0},{4,6},{6,4},{8,10},{10,8},{12,14},{14,12},{1,3},{3,1},... | collective-permute-start | bytes 786440 | tf_op jit(solution)/shard_map/ppermute | solution.py:298
  199.9 17.8 %collective-permute-start.38 = (bf16[64,2048]{1,0:T(8,128)(2,1)S(1)}, bf16[64,2048]{1,0:T(8,128)(2,1)S(1)}, u32[]{:S(2)}, u32[]{:S(2)}) collective-permute-start(bf16[64,2048]{1,0:T(8,128)(2,1)S(1)} %get-tuple-element.27), channel_id=1, source_target_pairs={{0,2},{2,0},{4,6},{6,4},{8,10},{10,8},{12,14},{14,12},{1,3},{3,1},... | collective-permute-start | bytes 786440 | tf_op jit(solution)/shard_map/ppermute | solution.py:298
  200.9 21.9 %collective-permute-start.40 = (bf16[64,2048]{1,0:T(8,128)(2,1)S(1)}, bf16[64,2048]{1,0:T(8,128)(2,1)S(1)}, u32[]{:S(2)}, u32[]{:S(2)}) collective-permute-start(bf16[64,2048]{1,0:T(8,128)(2,1)S(1)} %get-tuple-element.28), channel_id=1, source_target_pairs={{0,2},{2,0},{4,6},{6,4},{8,10},{10,8},{12,14},{14,12},{1,3},{3,1},... | collective-permute-start | bytes 786440 | tf_op jit(solution)/shard_map/ppermute | solution.py:298
  206.5 16.7 %collective-permute-start.31 = (bf16[64,2048]{1,0:T(8,128)(2,1)S(1)}, bf16[64,2048]{1,0:T(8,128)(2,1)S(1)}, u32[]{:S(2)}, u32[]{:S(2)}) collective-permute-start(bf16[64,2048]{1,0:T(8,128)(2,1)S(1)} %fusion.5), channel_id=1, source_target_pairs={{0,12},{2,14},{4,0},{6,2},{8,4},{10,6},{12,8},{14,10},{1,13},{3,15... | collective-permute-start | bytes 786440 | tf_op jit(solution)/shard_map/ppermute | solution.py:301
  223.0 11.1 %collective-permute-start.41 = (bf16[64,2048]{1,0:T(8,128)(2,1)S(1)}, bf16[64,2048]{1,0:T(8,128)(2,1)S(1)}, u32[]{:S(2)}, u32[]{:S(2)}) collective-permute-start(bf16[64,2048]{1,0:T(8,128)(2,1)S(1)} %get-tuple-element.18), channel_id=1, source_target_pairs={{0,4},{2,6},{4,8},{6,10},{8,12},{10,14},{12,0},{14,2},{1,5},{3,7},... | collective-permute-start | bytes 786440 | tf_op jit(solution)/shard_map/ppermute | solution.py:301
  223.1 20.1 %collective-permute-start.39 = (bf16[64,2048]{1,0:T(8,128)(2,1)S(1)}, bf16[64,2048]{1,0:T(8,128)(2,1)S(1)}, u32[]{:S(2)}, u32[]{:S(2)}) collective-permute-start(bf16[64,2048]{1,0:T(8,128)(2,1)S(1)} %get-tuple-element.17), channel_id=1, source_target_pairs={{0,8},{2,10},{4,12},{6,14},{8,0},{10,2},{12,4},{14,6},{1,9},{3,11}... | collective-permute-start | bytes 786440 | tf_op jit(solution)/shard_map/ppermute | solution.py:301
  (31 other events, 361.0 us)

commit v3 on v0

v3 whole, which is shorter than its diff:
```python
import jax
import jax.numpy as jnp
from jax import lax
from jax.experimental import pallas as pl
from jax.experimental.pallas import tpu as pltpu
from jax.sharding import PartitionSpec as P

HD = 128
CAP = 12

neg_large = -1e30
smem = pl.BlockSpec(memory_space=pltpu.SMEM)
vmem = pl.BlockSpec(memory_space=pltpu.VMEM)


def limit(mebibytes):
    return pltpu.CompilerParams(vmem_limit_bytes=mebibytes * 1024 * 1024)


def ring(size, step):
    return [(i, (i + 2 * step) % size) for i in range(size)]


def swap(size):
    return [(i, i ^ 1) for i in range(size)]


def far_first(depth):
    return sorted(range(1, depth), key=lambda d: -min(d, depth - d))


def wide(value):
    return value.astype(jnp.float32)


def narrow(value):
    return value.astype(jnp.bfloat16)


def after(value, *others):
    return lax.optimization_barrier((value,) + others)[0]


def pack_heads(z, queries, key_rows, value_rows, depth):
    rows = queries.shape[0]
    columns = queries.shape[1] // depth
    per_group = queries.shape[1] // key_rows.shape[1] * HD

    def kernel(z_ref, query_ref, key_ref, value_ref, *out_refs):
        for d, out_ref in enumerate(out_refs):
            start = (z_ref[0] + d) % depth * columns
            group = pl.ds(pl.multiple_of(start // per_group * HD, HD), HD)
            out_ref[:, :columns] = query_ref[:, pl.ds(pl.multiple_of(start, HD), columns)]
            out_ref[:, columns : columns + HD] = key_ref[:, group]
            out_ref[:, columns + HD :] = value_ref[:, group]

    return pl.pallas_call(
        kernel,
        out_shape=[jax.ShapeDtypeStruct((rows, columns + 2 * HD), queries.dtype)] * depth,
        in_specs=[smem, vmem, vmem, vmem],
        out_specs=[vmem] * depth,
        compiler_params=limit(16),
        name="pack_heads",
    )(z, queries, key_rows, value_rows)


def pack_weight(z, out_weight, depth):
    rows = out_weight.shape[0]
    columns = out_weight.shape[1] // depth

    def kernel(z_ref, weight_ref, *out_refs):
        for d, out_ref in enumerate(out_refs):
            start = pl.multiple_of((z_ref[0] + d) % depth * columns, HD)
            out_ref[...] = weight_ref[:, pl.ds(start, columns)]

    return pl.pallas_call(
        kernel,
        out_shape=[jax.ShapeDtypeStruct((rows, columns), out_weight.dtype)] * depth,
        in_specs=[smem, vmem],
        out_specs=[vmem] * depth,
        compiler_params=limit(16),
        name="pack_weight",
    )(z, out_weight)


def attend(core, starts, key_pos, messages, across, columns):
    depth = len(messages)
    rows = messages[0].shape[0]
    heads = columns // HD
    length = 2 * depth * rows
    half = rows // 2

    def kernel(core_ref, starts_ref, key_pos_ref, *refs):
        message_refs, across_refs = refs[:depth], refs[depth : 2 * depth]
        out_ref, query, keyed = refs[2 * depth :]
        for d in range(depth):
            for h in range(heads):
                query[d, h * rows : (h + 1) * rows, :] = message_refs[d][:, h * HD : (h + 1) * HD]
            keyed[2 * d * rows : (2 * d + 1) * rows, :] = message_refs[d][:, columns:]
            keyed[(2 * d + 1) * rows : (2 * d + 2) * rows, :] = across_refs[d][...]
        mine = core_ref[0] == 0

        def block(d, carry):
            scores = lax.dot_general(
                query[d], keyed[:, :HD], (((1,), (1,)), ((), ())), preferred_element_type=jnp.float32
            )
            offset = lax.broadcasted_iota(jnp.int32, (heads * rows, 1), 0) % rows
            allowed = key_pos_ref[...] <= starts_ref[d] + offset
            scores = jnp.where(allowed, scores, neg_large)
            largest = jnp.max(scores, axis=-1, keepdims=True)
            exps = jnp.exp((scores - largest) * (HD**-0.5))
            total = jnp.sum(exps, axis=-1, keepdims=True)
            summed = jnp.dot(narrow(exps), keyed[:, HD:], preferred_element_type=jnp.float32)
            context = narrow(summed / total)
            place = pl.ds(pl.multiple_of(d * half, half), half)
            for h in range(heads):
                low, high = context[h * rows : h * rows + half], context[h * rows + half : (h + 1) * rows]
                out_ref[0, place, h * HD : (h + 1) * HD] = jnp.where(mine, low, high)
                out_ref[1, place, h * HD : (h + 1) * HD] = jnp.where(mine, high, low)
            return carry

        lax.fori_loop(0, depth, block, 0)

    work = depth * rows * columns * length
    return pl.pallas_call(
        kernel,
        out_shape=jax.ShapeDtypeStruct((2, depth * half, columns), jnp.bfloat16),
        in_specs=[smem, smem, vmem] + [vmem] * (2 * depth),
        out_specs=vmem,
        scratch_shapes=[
            pltpu.VMEM((depth, heads * rows, HD), jnp.bfloat16),
            pltpu.VMEM((length, 2 * HD), jnp.bfloat16),
        ],
        compiler_params=limit(32),
        cost_estimate=pl.CostEstimate(flops=4 * work, bytes_accessed=depth * rows * columns * 8, transcendentals=work // HD),
        name="attend",
    )(core, starts, key_pos, *messages, *across)


def project(place, context, weights):
    rows, columns = context.shape[1:]
    blocks, features = len(weights), weights[0].shape[0]
    if features % HD:
        weight = jnp.stack(weights)[jnp.argsort(place)]
        result = jnp.einsum("erc,bfc->erbf", context, weight, preferred_element_type=jnp.float32)
        result = narrow(result.reshape(2, rows, -1))
        return result[0], result[1]

    def kernel(place_ref, context_ref, *refs):
        weight_refs, kept_ref, given_ref = refs[:blocks], refs[blocks], refs[blocks + 1]
        left = context_ref[...].reshape(2 * rows, columns)
        for i in range(blocks):
            part = narrow(
                lax.dot_general(
                    left, weight_refs[i][...], (((1,), (1,)), ((), ())), preferred_element_type=jnp.float32
                )
            )
            there = pl.ds(pl.multiple_of(place_ref[i] * features, HD), features)
            kept_ref[:, there] = part[:rows]
            given_ref[:, there] = part[rows:]

    return pl.pallas_call(
        kernel,
        out_shape=[jax.ShapeDtypeStruct((rows, blocks * features), jnp.bfloat16)] * 2,
        in_specs=[smem, vmem] + [vmem] * blocks,
        out_specs=[vmem, vmem],
        compiler_params=limit(24),
        cost_estimate=pl.CostEstimate(
            flops=4 * rows * columns * blocks * features,
            bytes_accessed=2 * blocks * features * (columns + 2 * rows),
            transcendentals=0,
        ),
        name="project",
    )(place, context, *weights)


def attention_block(queries, key_rows, value_rows, out_weight):
    size = lax.axis_size("seq")
    depth = size // 2
    z, y = lax.axis_index("seq") // 2, lax.axis_index("seq") % 2
    core = lax.axis_index("exp").astype(jnp.int32).reshape(1)
    rows = queries.shape[0]
    columns = queries.shape[1] // depth
    steps = far_first(depth)
    here = z.astype(jnp.int32).reshape(1)

    message = list(pack_heads(here, queries, key_rows, value_rows, depth))
    for d in steps:
        message[d] = lax.ppermute(message[d], "seq", ring(size, d))
    across = {}
    for d in [0] + steps:
        across[d] = lax.ppermute(message[d][:, columns:], "seq", swap(size))
    weight = list(pack_weight(here, out_weight, depth))
    weight_across = {0: lax.ppermute(weight[0], "seq", swap(size))}
    for d in steps[::-1]:
        weight[d] = lax.ppermute(after(weight[d], *message), "seq", ring(size, d))

    behind = (z - jnp.arange(depth, dtype=jnp.int32)) % depth
    block = (behind[:, None] * 2 + jnp.stack([y, 1 - y])[None, :]).astype(jnp.int32)
    key_pos = (block.reshape(-1, 1) * rows + jnp.arange(rows, dtype=jnp.int32)).reshape(1, -1)
    context = attend(core, block[:, 0] * rows, key_pos, message, [across[d] for d in range(depth)], columns)
    for d in steps[::-1]:
        weight_across[d] = lax.ppermute(weight[d], "seq", swap(size))
    kept, given = project(
        block.reshape(-1), context, [part for d in range(depth) for part in (weight[d], weight_across[d])]
    )
    arrived = lax.ppermute(given, "exp", swap(2))
    chip = (wide(kept) + wide(arrived)).reshape(depth, rows // 2, -1)
    total = chip[0]
    for d in steps:
        total = total + wide(lax.ppermute(narrow(chip[d]), "seq", ring(size, -d)))
    return total, message[steps[-1]]


def gather_meta(meta, size, depth):
    along = jnp.stack([meta] + [lax.ppermute(meta, "seq", ring(size, d)) for d in range(1, depth)])
    both = jnp.stack([along, lax.ppermute(along, "seq", swap(size))], axis=1)
    return jnp.stack([both, lax.ppermute(both, "exp", swap(2))], axis=1)


def routing(ids, gates, first, local_experts):
    subs, blocks, rows, _ = ids.shape
    experts = first + jnp.arange(local_experts, dtype=jnp.int32)
    match = ids[..., None] == experts
    hit = jnp.any(match, axis=3)
    weight = jnp.sum(jnp.where(match, gates[..., None], 0.0), axis=3)
    count = hit.astype(jnp.int32)
    place = jnp.where(hit, jnp.cumsum(count, axis=2) - count, -1)
    place = place.transpose(3, 0, 1, 2)
    weight = weight.transpose(3, 0, 1, 2)
    chosen = place[:, :, :, None, :] == jnp.arange(CAP, dtype=jnp.int32)[:, None]
    row_gate = jnp.sum(jnp.where(chosen, weight[:, :, :, None, :], 0.0), axis=-1)
    row_gate = row_gate.reshape(local_experts, subs * blocks * CAP, 1)
    diagonal = jnp.eye(blocks, dtype=bool)[:, None, :, None]
    full = chosen[:, :, :, :, None, :] & diagonal
    select = full.reshape(local_experts, subs, blocks * CAP, blocks * rows).astype(jnp.bfloat16)
    spread = select.transpose(1, 3, 0, 2).reshape(subs, blocks * rows, local_experts * blocks * CAP)
    return select, spread, row_gate


def run_experts(mine, other, select, spread, row_gate, expert_in, expert_out):
    subs = len(mine)
    tokens, width = mine[0].shape
    local_experts, hidden, _ = expert_out.shape
    slots = select.shape[2]

    def kernel(select_ref, spread_ref, gate_ref, wg_ref, wu_ref, wo_ref, *refs):
        mine_refs, other_refs = refs[:subs], refs[subs : 2 * subs]
        kept_refs, given_refs = refs[2 * subs : 3 * subs], refs[3 * subs : 4 * subs]
        xg, res = refs[4 * subs :]
        expert = pl.program_id(0)
        for s in range(subs):
            xg[s * slots : (s + 1) * slots, :] = narrow(
                jnp.dot(select_ref[expert, s, :, :tokens], mine_refs[s][...], preferred_element_type=jnp.float32)
                + jnp.dot(select_ref[expert, s, :, tokens:], other_refs[s][...], preferred_element_type=jnp.float32)
            )
        rows = xg[...]
        gate = jnp.dot(rows, wg_ref[0], preferred_element_type=jnp.float32)
        up = jnp.dot(rows, wu_ref[0], preferred_element_type=jnp.float32)
        act = narrow(gate / (1.0 + jnp.exp(-gate)) * up)
        part = jnp.dot(act, wo_ref[0], preferred_element_type=jnp.float32)
        scaled = narrow(part * gate_ref[expert])
        for s in range(subs):
            res[s, expert] = scaled[s * slots : (s + 1) * slots, :]

        @pl.when(expert == pl.num_programs(0) - 1)
        def _():
            for s in range(subs):
                both = narrow(
                    jnp.dot(spread_ref[s], res[s].reshape(-1, width), preferred_element_type=jnp.float32)
                )
                kept_refs[s][...] = both[:tokens]
                given_refs[s][...] = both[tokens:]

    flops = local_experts * subs * slots * width * hidden * 6
    moved = (expert_in.size + expert_out.size + 8 * subs * tokens * width) * 2

    def whole(shape):
        return pl.BlockSpec(shape, lambda e: (0,) * len(shape), pipeline_mode=pl.Buffered(1))

    piece = whole((tokens, width))
    outs = pl.pallas_call(
        kernel,
        grid=(local_experts,),
        out_shape=[jax.ShapeDtypeStruct((tokens, width), jnp.bfloat16)] * (2 * subs),
        in_specs=[
            whole(select.shape),
            whole(spread.shape),
            whole(row_gate.shape),
            pl.BlockSpec((1, width, hidden), lambda e: (e, 0, 0)),
            pl.BlockSpec((1, width, hidden), lambda e: (e, 0, 1)),
            pl.BlockSpec((1, hidden, width), lambda e: (e, 0, 0)),
        ]
        + [piece] * (2 * subs),
        out_specs=[piece] * (2 * subs),
        scratch_shapes=[
            pltpu.VMEM((subs * slots, width), jnp.bfloat16),
            pltpu.VMEM((subs, local_experts, slots, width), jnp.bfloat16),
        ],
        compiler_params=limit(56),
        cost_estimate=pl.CostEstimate(flops=flops, bytes_accessed=moved, transcendentals=0),
        name="experts",
    )(select, spread, row_gate, expert_in, expert_in, expert_out, *mine, *other)
    return outs[:subs], outs[subs:]


def expert_block(mixed, early, norm_gain, expert_ids, gate_weights, expert_in, expert_out):
    size = lax.axis_size("seq")
    depth = size // 2
    rows, width = mixed.shape
    local_experts = expert_in.shape[0]
    top = expert_ids.shape[1]
    first = (lax.axis_index("seq") * 2 + lax.axis_index("exp")) * local_experts
    gate_high = narrow(gate_weights)
    gate_low = narrow(gate_weights - wide(gate_high))
    meta = jnp.concatenate([narrow(expert_ids), gate_high, gate_low], axis=1)
    meta = gather_meta(after(meta, early), size, depth).reshape(depth, 4, rows, 3 * top)
    ids = meta[..., :top].astype(jnp.int32)
    gates = wide(meta[..., top : 2 * top]) + wide(meta[..., 2 * top :])
    route = routing(ids, gates, first, local_experts)

    normed = narrow(mixed * lax.rsqrt(jnp.mean(mixed * mixed, axis=-1, keepdims=True) + 1e-06) * norm_gain)
    along, mine, other = [normed], [], []
    for d in range(depth):
        if d + 1 < depth:
            along.append(lax.ppermute(along[d], "seq", ring(size, 1)))
        mine.append(jnp.concatenate([along[d], lax.ppermute(along[d], "seq", swap(size))]))
        other.append(lax.ppermute(mine[d], "exp", swap(2)))
    kept, given = run_experts(mine, other, *route, expert_in, expert_out)

    total = mixed
    for d in far_first(depth) + [0]:
        pair = wide(kept[d]) + wide(lax.ppermute(given[d], "exp", swap(2)))
        there = lax.ppermute(narrow(pair[rows:]), "seq", swap(size))
        chip = pair[:rows] + wide(there)
        if d:
            chip = wide(lax.ppermute(narrow(chip), "seq", ring(size, -d)))
        total = total + chip
    return narrow(total)


def on_device(
    stream,
    queries,
    key_rows,
    value_rows,
    out_weight,
    norm_gain,
    expert_ids,
    gate_weights,
    expert_in,
    expert_out,
):
    attn_out, early = attention_block(queries, key_rows, value_rows, out_weight)
    mixed = wide(stream) + attn_out
    return expert_block(mixed, early, norm_gain, expert_ids, gate_weights, expert_in, expert_out)


def solution(mesh):
    in_specs = (
        P(("groups", "seq", "exp"), None),
        P(("groups", "seq"), "exp"),
        P(("groups", "seq"), "exp"),
        P(("groups", "seq"), "exp"),
        P("seq", "exp"),
        P(),
        P(("groups", "seq", "exp"), None),
        P(("groups", "seq", "exp"), None),
        P(("seq", "exp"), None, None),
        P(("seq", "exp"), None, None),
    )
    out_specs = P(("groups", "seq", "exp"), None)
    return jax.shard_map(
        on_device, mesh=mesh, in_specs=in_specs, out_specs=out_specs, check_vma=False
    )
```

time: 393 us -> 208 us (0.53)
  blocking collectives: 157 us -> 0 us
  starting transfers between devices: 4.04 us -> 52.3 us
  matrix products: 41 us -> 0 us
  Pallas kernels: 0 us -> 30.5 us
  local copies, waits for them, and re-layouts: 40.3 us -> 13.4 us
  waiting for transfers between devices: 119 us -> 104 us
  between operations: 13.6 us -> 0.59 us
  other arithmetic: 16.9 us -> 6.61 us
    ppermute x0 -> x45, waiting for transfers between devices: none -> 104 us  [the longest x4 19.1 us: expert_block(): there = lax.ppermute(narrow(pair[rows:]), 'seq', swap(size))]
    all_to_all x3 -> x0, blocking collectives: 89.2 us -> none  [the longest x1 76.7 us: on_device(): lax.all_to_all(sectioned, 'seq', split_axis=0, concat_axis=0, tiled=True)]
    all_to_all x1 -> x0, waiting for transfers between devices: 70.8 us -> none  [on_device(): lax.all_to_all(finished, 'seq', split_axis=0, concat_axis=0, tiled=True)]
    all_gather x2 -> x0, blocking collectives: 67.7 us -> none  [the longest x1 35 us: on_device(): key_piece = lax.all_gather(key_rows, 'seq', axis=0, tiled=True)]
    ppermute x0 -> x45, starting transfers between devices: none -> 52.3 us  [the longest x3 14 us: expert_block(): along.append(lax.ppermute(along[d], 'seq', ring(size, 1)))]
    all_gather x1 -> x0, waiting for transfers between devices: 43.5 us -> none  [on_device(): lax.all_gather(out_weight, 'seq', axis=0, tiled=True)]
    dot_general x8 -> x0, matrix products: 41 us -> none  [the longest x1 10.8 us: on_device(): jnp.einsum('secd,edf->secf', arranged, expert_in, preferred_element_type=...]
    pallas_call x0 -> x5, Pallas kernels: none -> 30.5 us  [the longest x1 21.4 us: run_experts(): pl.pallas_call(kernel, grid=(local_experts,), out_shape=[jax.ShapeDtypeSt...]
  transfers between devices with their start and end apart: 3 -> 45, of which waited for: 3 -> 22; matrix products, arithmetic and copies ran while one was open for 7% -> 4% of each run, Pallas kernels for 0% -> 3%
where the time goes in v3:
time: 208 us
  waiting for transfers between devices  104 us (50%)
  starting transfers between devices  52.3 us (25%)
  Pallas kernels  30.5 us (15%)
  local copies, waits for them, and re-layouts  13.4 us (6%)
  other arithmetic  6.61 us (3%)
    pallas_call x1, Pallas kernels, run_experts(): pl.pallas_call(kernel, grid=(local_experts,), out_shape=[jax.ShapeDtypeSt...  21.4 us
    ppermute x4, waiting for transfers between devices, expert_block(): there = lax.ppermute(narrow(pair[rows:]), 'seq', swap(size))  19.1 us
    ppermute x3, waiting for transfers between devices, attention_block(): total = total + wide(lax.ppermute(narrow(chip[d]), 'seq', ring(size, -d)))  16.9 us
    ppermute x3, waiting for transfers between devices, expert_block(): along.append(lax.ppermute(along[d], 'seq', ring(size, 1)))  16.8 us
    ppermute x3, waiting for transfers between devices, attention_block(): weight[d] = lax.ppermute(after(weight[d], *message), 'seq', ring(size, d))  15.7 us
    ppermute x3, starting transfers between devices, expert_block(): along.append(lax.ppermute(along[d], 'seq', ring(size, 1)))  14 us
    unnamed x43, local copies, waits for them, and re-layouts  9.05 us
    ppermute x3, waiting for transfers between devices, attention_block(): message[d] = lax.ppermute(message[d], 'seq', ring(size, d))  8.81 us
  transfers between devices with their start and end apart: 45, of which 22 were waited for; matrix products, arithmetic and copies ran while one was open for 4% of the time, Pallas kernels for 3%

profile of v3, /device:TPU:0, one launch (start us, length us, event | category | flops | bytes accessed | tf_op | source)
XLA Modules:
  0.0 207.7 jit_solution(9254586625942529112)
XLA Ops:
  2.8 3.0 %collective-permute-start.3 = (bf16[128,256]{1,0:T(8,128)(2,1)S(1)}, bf16[128,256]{1,0:T(8,128)(2,1)S(1)}, u32[]{:S(2)}, u32[]{:S(2)}) collective-permute-start(bf16[128,256]{1,0:T(8,128)(2,1)S(1)} %slice.72), channel_id=1, source_target_pairs={{0,2},{2,0},{4,6},{6,4},{8,10},{10,8},{12,14},{14,12},{1,3},{3,1},... | collective-permute-start | bytes 196616 | tf_op jit(solution)/shard_map/ppermute | solution.py:192
  7.4 2.6 %collective-permute-start.1 = (bf16[128,768]{1,0:T(8,128)(2,1)S(1)}, bf16[128,768]{1,0:T(8,128)(2,1)S(1)}, u32[]{:S(2)}, u32[]{:S(2)}) collective-permute-start(bf16[128,768]{1,0:T(8,128)(2,1)S(1)} %get-tuple-element.29), channel_id=1, source_target_pairs={{0,8},{2,10},{4,12},{6,14},{8,0},{10,2},{12,4},{14,6},{1,9},{3,11}... | collective-permute-start | bytes 589832 | tf_op jit(solution)/shard_map/ppermute | solution.py:189
  13.8 1.8 collective-permute-done.refs_1_
  15.6 7.0 %collective-permute-done.1.refs_2_ = bf16[128,768]{1,0:T(8,128)(2,1)S(1)} collective-permute-done((bf16[128,768]{1,0:T(8,128)(2,1)S(1)}, bf16[128,768]{1,0:T(8,128)(2,1)S(1)}, u32[]{:S(2)}, u32[]{:S(2)}) %collective-permute-start.1) | collective-permute-done | bytes 196640 | tf_op jit(solution)/shard_map/ppermute | solution.py:189
  22.6 5.8 %collective-permute-start.12 = (bf16[256,512]{1,0:T(8,128)(2,1)S(1)}, bf16[256,512]{1,0:T(8,128)(2,1)S(1)}, u32[]{:S(2)}, u32[]{:S(2)}) collective-permute-start(bf16[256,512]{1,0:T(8,128)(2,1)S(1)} %get-tuple-element.37), channel_id=1, source_target_pairs={{0,12},{2,14},{4,0},{6,2},{8,4},{10,6},{12,8},{14,10},{1,13},{3,15... | collective-permute-start | bytes 786440 | tf_op jit(solution)/shard_map/ppermute | solution.py:196
  29.5 1.6 collective-permute-start.5
  31.2 2.1 %collective-permute-done.4.refs_5_ = bf16[128,256]{1,0:T(8,128)(2,1)S(1)} collective-permute-done((bf16[128,256]{1,0:T(8,128)(2,1)S(1)}, bf16[128,256]{1,0:T(8,128)(2,1)S(1)}, u32[]{:S(2)}, u32[]{:S(2)}) %collective-permute-start.4) | collective-permute-done | bytes 65568 | tf_op jit(solution)/shard_map/ppermute | solution.py:192
  34.1 1.8 collective-permute-start.6
  36.1 15.7 %collective-permute-done.10.refs_4_ = bf16[256,512]{1,0:T(8,128)(2,1)S(1)} collective-permute-done((bf16[256,512]{1,0:T(8,128)(2,1)S(1)}, bf16[256,512]{1,0:T(8,128)(2,1)S(1)}, u32[]{:S(2)}, u32[]{:S(2)}) %collective-permute-start.10) | collective-permute-done | bytes 262176 | tf_op jit(solution)/shard_map/ppermute | solution.py:196
  53.9 7.1 %attend.1.context_ref = bf16[2,256,512]{2,1,0:T(8,128)(2,1)S(1)} custom-call(s32[1]{0:T(128)} %bitcast.2.core_ref, s32[4]{0:T(128)S(1)} %multiply_bitcast_fusion.starts_ref, s32[1,1024]{1,0:T(1,128)S(1)} %bitcast.28, bf16[128,768]{1,0:T(8,128)(2,1)S(1)} %get-tuple-element.27.refs_0_, bf16[128,768]{1,0:T(8,128)(2,1)S(1)} %collective-permute-done.refs_1_, ...), custom_call_target="tpu_custom_call" | custom-call | flops 1073741824 | bytes 2097152 | tf_op jit(solution)/shard_map/attend/pallas_call | solution.py:125
  62.4 2.4 %collective-permute-done.9.refs_3_ = bf16[256,512]{1,0:T(8,128)(2,1)S(1)} collective-permute-done((bf16[256,512]{1,0:T(8,128)(2,1)S(1)}, bf16[256,512]{1,0:T(8,128)(2,1)S(1)}, u32[]{:S(2)}, u32[]{:S(2)}) %collective-permute-start.9) | collective-permute-done | bytes 262176 | tf_op jit(solution)/shard_map/ppermute | solution.py:203
  68.4 1.9 project.1
  70.5 1.9 collective-permute-start.18
  72.5 1.6 collective-permute-done.20
  77.1 3.3 %collective-permute-done.21 = bf16[4,64,24]{1,2,0:T(8,128)(2,1)S(1)} collective-permute-done((bf16[4,64,24]{1,2,0:T(8,128)(2,1)S(1)}, bf16[4,64,24]{1,2,0:T(8,128)(2,1)S(1)}, u32[]{:S(2)}, u32[]{:S(2)}) %collective-permute-start.21) | collective-permute-done | bytes 12320 | tf_op jit(solution)/shard_map/ppermute | solution.py:217
  83.0 1.9 collective-permute-start.17
  84.9 1.9 collective-permute-start.16
  87.0 16.0 %collective-permute-done.15 = bf16[64,2048]{1,0:T(8,128)(2,1)S(1)} collective-permute-done((bf16[64,2048]{1,0:T(8,128)(2,1)S(1)}, bf16[64,2048]{1,0:T(8,128)(2,1)S(1)}, u32[]{:S(2)}, u32[]{:S(2)}) %collective-permute-start.15) | collective-permute-done | bytes 262176 | tf_op jit(solution)/shard_map/ppermute | solution.py:211
  104.3 10.9 %collective-permute-start.24 = (bf16[64,2048]{1,0:T(8,128)(2,1)S(1)}, bf16[64,2048]{1,0:T(8,128)(2,1)S(1)}, u32[]{:S(2)}, u32[]{:S(2)}) collective-permute-start(bf16[64,2048]{1,0:T(8,128)(2,1)S(1)} %multiply_convert_fusion), channel_id=1, source_target_pairs={{0,4},{2,6},{4,8},{6,10},{8,12},{10,14},{12,0},{14,2},{1,5},{3,7},... | collective-permute-start | bytes 786440 | tf_op jit(solution)/shard_map/ppermute | solution.py:326
  117.2 3.7 %collective-permute-done.24 = bf16[64,2048]{1,0:T(8,128)(2,1)S(1)} collective-permute-done((bf16[64,2048]{1,0:T(8,128)(2,1)S(1)}, bf16[64,2048]{1,0:T(8,128)(2,1)S(1)}, u32[]{:S(2)}, u32[]{:S(2)}) %collective-permute-start.24) | collective-permute-done | bytes 262176 | tf_op jit(solution)/shard_map/ppermute | solution.py:326
  120.9 2.5 %collective-permute-start.26 = (bf16[64,2048]{1,0:T(8,128)(2,1)S(1)}, bf16[64,2048]{1,0:T(8,128)(2,1)S(1)}, u32[]{:S(2)}, u32[]{:S(2)}) collective-permute-start(bf16[64,2048]{1,0:T(8,128)(2,1)S(1)} %collective-permute-done.24), channel_id=1, source_target_pairs={{0,4},{2,6},{4,8},{6,10},{8,12},{10,14},{12,0},{14,2},{1,5},{3,7},... | collective-permute-start | bytes 786440 | tf_op jit(solution)/shard_map/ppermute | solution.py:326
  124.1 6.1 %collective-permute-done.26 = bf16[64,2048]{1,0:T(8,128)(2,1)S(1)} collective-permute-done((bf16[64,2048]{1,0:T(8,128)(2,1)S(1)}, bf16[64,2048]{1,0:T(8,128)(2,1)S(1)}, u32[]{:S(2)}, u32[]{:S(2)}) %collective-permute-start.26) | collective-permute-done | bytes 262176 | tf_op jit(solution)/shard_map/ppermute | solution.py:326
  131.5 7.0 %collective-permute-done.28 = bf16[64,2048]{1,0:T(8,128)(2,1)S(1)} collective-permute-done((bf16[64,2048]{1,0:T(8,128)(2,1)S(1)}, bf16[64,2048]{1,0:T(8,128)(2,1)S(1)}, u32[]{:S(2)}, u32[]{:S(2)}) %collective-permute-start.28) | collective-permute-done | bytes 262176 | tf_op jit(solution)/shard_map/ppermute | solution.py:326
  139.1 5.7 %collective-permute-done.29 = bf16[64,2048]{1,0:T(8,128)(2,1)S(1)} collective-permute-done((bf16[64,2048]{1,0:T(8,128)(2,1)S(1)}, bf16[64,2048]{1,0:T(8,128)(2,1)S(1)}, u32[]{:S(2)}, u32[]{:S(2)}) %collective-permute-start.29) | collective-permute-done | bytes 262176 | tf_op jit(solution)/shard_map/ppermute | solution.py:327
  149.1 21.4 %experts.1 = (bf16[128,2048]{1,0:T(8,128)(2,1)}, bf16[128,2048]{1,0:T(8,128)(2,1)}, bf16[128,2048]{1,0:T(8,128)(2,1)}, bf16[128,2048]{1,0:T(8,128)(2,1)}, bf16[1...) custom-call(bf16[4,4,48,256]{3,2,1,0:T(8,128)(2,1)} %get-tuple-element.5, ...), custom_call_target="tpu_custom_call" | custom-call | flops 7247757312 | bytes 54525952 | tf_op jit(solution)/shard_map/experts/pallas_call | solution.py:282
  174.7 1.6 collective-permute-start.38
  177.2 1.6 collective-permute-start.44
  178.8 4.3 %collective-permute-done.35 = bf16[64,2048]{1,0:T(8,128)(2,1)S(1)} collective-permute-done((bf16[64,2048]{1,0:T(8,128)(2,1)S(1)}, bf16[64,2048]{1,0:T(8,128)(2,1)S(1)}, u32[]{:S(2)}, u32[]{:S(2)}) %collective-permute-start.35) | collective-permute-done | bytes 262176 | tf_op jit(solution)/shard_map/ppermute | solution.py:334
  183.3 5.5 %collective-permute-done.38 = bf16[64,2048]{1,0:T(8,128)(2,1)S(1)} collective-permute-done((bf16[64,2048]{1,0:T(8,128)(2,1)S(1)}, bf16[64,2048]{1,0:T(8,128)(2,1)S(1)}, u32[]{:S(2)}, u32[]{:S(2)}) %collective-permute-start.38) | collective-permute-done | bytes 262176 | tf_op jit(solution)/shard_map/ppermute | solution.py:334
  190.0 4.3 %collective-permute-done.41 = bf16[64,2048]{1,0:T(8,128)(2,1)S(1)} collective-permute-done((bf16[64,2048]{1,0:T(8,128)(2,1)S(1)}, bf16[64,2048]{1,0:T(8,128)(2,1)S(1)}, u32[]{:S(2)}, u32[]{:S(2)}) %collective-permute-start.41) | collective-permute-done | bytes 262176 | tf_op jit(solution)/shard_map/ppermute | solution.py:334
  194.5 4.9 %collective-permute-done.44 = bf16[64,2048]{1,0:T(8,128)(2,1)S(1)} collective-permute-done((bf16[64,2048]{1,0:T(8,128)(2,1)S(1)}, bf16[64,2048]{1,0:T(8,128)(2,1)S(1)}, u32[]{:S(2)}, u32[]{:S(2)}) %collective-permute-start.44) | collective-permute-done | bytes 262176 | tf_op jit(solution)/shard_map/ppermute | solution.py:334
  199.5 7.3 %collective-permute-done.39 = bf16[64,2048]{1,0:T(8,128)(2,1)S(1)} collective-permute-done((bf16[64,2048]{1,0:T(8,128)(2,1)S(1)}, bf16[64,2048]{1,0:T(8,128)(2,1)S(1)}, u32[]{:S(2)}, u32[]{:S(2)}) %collective-permute-start.39) | collective-permute-done | bytes 262176 | tf_op jit(solution)/shard_map/ppermute | solution.py:337
  (169 shorter events, 40.9 us)
Async XLA Ops:
  2.8 26.7 %collective-permute-start.3 = (bf16[128,256]{1,0:T(8,128)(2,1)S(1)}, bf16[128,256]{1,0:T(8,128)(2,1)S(1)}, u32[]{:S(2)}, u32[]{:S(2)}) collective-permute-start(bf16[128,256]{1,0:T(8,128)(2,1)S(1)} %slice.72), channel_id=1, source_target_pairs={{0,2},{2,0},{4,6},{6,4},{8,10},{10,8},{12,14},{14,12},{1,3},{3,1},... | collective-permute-start | bytes 196616 | tf_op jit(solution)/shard_map/ppermute | solution.py:192
  5.9 9.7 %collective-permute-start = (bf16[128,768]{1,0:T(8,128)(2,1)S(1)}, bf16[128,768]{1,0:T(8,128)(2,1)S(1)}, u32[]{:S(2)}, u32[]{:S(2)}) collective-permute-start(bf16[128,768]{1,0:T(8,128)(2,1)S(1)} %get-tuple-element.28), channel_id=1, source_target_pairs={{0,4},{2,6},{4,8},{6,10},{8,12},{10,14},{12,0},{14,2},{1,5},{3,7},... | collective-permute-start | bytes 589832 | tf_op jit(solution)/shard_map/ppermute | solution.py:189
  7.4 15.2 %collective-permute-start.1 = (bf16[128,768]{1,0:T(8,128)(2,1)S(1)}, bf16[128,768]{1,0:T(8,128)(2,1)S(1)}, u32[]{:S(2)}, u32[]{:S(2)}) collective-permute-start(bf16[128,768]{1,0:T(8,128)(2,1)S(1)} %get-tuple-element.29), channel_id=1, source_target_pairs={{0,8},{2,10},{4,12},{6,14},{8,0},{10,2},{12,4},{14,6},{1,9},{3,11}... | collective-permute-start | bytes 589832 | tf_op jit(solution)/shard_map/ppermute | solution.py:189
  10.0 12.6 %collective-permute-start.2 = (bf16[128,768]{1,0:T(8,128)(2,1)S(1)}, bf16[128,768]{1,0:T(8,128)(2,1)S(1)}, u32[]{:S(2)}, u32[]{:S(2)}) collective-permute-start(bf16[128,768]{1,0:T(8,128)(2,1)S(1)} %get-tuple-element.30), channel_id=1, source_target_pairs={{0,12},{2,14},{4,0},{6,2},{8,4},{10,6},{12,8},{14,10},{1,13},{3,15... | collective-permute-start | bytes 589832 | tf_op jit(solution)/shard_map/ppermute | solution.py:189
  22.6 13.3 %collective-permute-start.12 = (bf16[256,512]{1,0:T(8,128)(2,1)S(1)}, bf16[256,512]{1,0:T(8,128)(2,1)S(1)}, u32[]{:S(2)}, u32[]{:S(2)}) collective-permute-start(bf16[256,512]{1,0:T(8,128)(2,1)S(1)} %get-tuple-element.37), channel_id=1, source_target_pairs={{0,12},{2,14},{4,0},{6,2},{8,4},{10,6},{12,8},{14,10},{1,13},{3,15... | collective-permute-start | bytes 786440 | tf_op jit(solution)/shard_map/ppermute | solution.py:196
  28.4 23.4 %collective-permute-start.10 = (bf16[256,512]{1,0:T(8,128)(2,1)S(1)}, bf16[256,512]{1,0:T(8,128)(2,1)S(1)}, u32[]{:S(2)}, u32[]{:S(2)}) collective-permute-start(bf16[256,512]{1,0:T(8,128)(2,1)S(1)} %get-tuple-element.35), channel_id=1, source_target_pairs={{0,8},{2,10},{4,12},{6,14},{8,0},{10,2},{12,4},{14,6},{1,9},{3,11}... | collective-permute-start | bytes 786440 | tf_op jit(solution)/shard_map/ppermute | solution.py:196
  28.8 23.6 %collective-permute-start.8 = (bf16[256,512]{1,0:T(8,128)(2,1)S(1)}, bf16[256,512]{1,0:T(8,128)(2,1)S(1)}, u32[]{:S(2)}, u32[]{:S(2)}) collective-permute-start(bf16[256,512]{1,0:T(8,128)(2,1)S(1)} %get-tuple-element.33), channel_id=1, source_target_pairs={{0,4},{2,6},{4,8},{6,10},{8,12},{10,14},{12,0},{14,2},{1,5},{3,7},... | collective-permute-start | bytes 786440 | tf_op jit(solution)/shard_map/ppermute | solution.py:196
  33.3 27.7 %collective-permute-start.7 = (bf16[256,512]{1,0:T(8,128)(2,1)S(1)}, bf16[256,512]{1,0:T(8,128)(2,1)S(1)}, u32[]{:S(2)}, u32[]{:S(2)}) collective-permute-start(bf16[256,512]{1,0:T(8,128)(2,1)S(1)} %get-tuple-element.31.refs_0_), channel_id=1, source_target_pairs={{0,2},{2,0},{4,6},{6,4},{8,10},{10,8},{12,14},{14,12},{1,3},{3,1},... | collective-permute-start | bytes 786440 | tf_op jit(solution)/shard_map/ppermute | solution.py:194
  34.1 19.7 %collective-permute-start.6 = (bf16[128,256]{1,0:T(8,128)(2,1)S(1)}, bf16[128,256]{1,0:T(8,128)(2,1)S(1)}, u32[]{:S(2)}, u32[]{:S(2)}) collective-permute-start(bf16[128,256]{1,0:T(8,128)(2,1)S(1)} %slice.93), channel_id=1, source_target_pairs={{0,2},{2,0},{4,6},{6,4},{8,10},{10,8},{12,14},{14,12},{1,3},{3,1},... | collective-permute-start | bytes 196616 | tf_op jit(solution)/shard_map/ppermute | solution.py:192
  36.0 25.0 %collective-permute-start.13 = (bf16[256,512]{1,0:T(8,128)(2,1)S(1)}, bf16[256,512]{1,0:T(8,128)(2,1)S(1)}, u32[]{:S(2)}, u32[]{:S(2)}) collective-permute-start(bf16[256,512]{1,0:T(8,128)(2,1)S(1)} %collective-permute-done.12.refs_6_), channel_id=1, source_target_pairs={{0,2},{2,0},{4,6},{6,4},{8,10},{10,8},{12,14},{14,12},{1,3},{3,1},... | collective-permute-start | bytes 786440 | tf_op jit(solution)/shard_map/ppermute | solution.py:203
  51.8 9.9 %collective-permute-start.11 = (bf16[256,512]{1,0:T(8,128)(2,1)S(1)}, bf16[256,512]{1,0:T(8,128)(2,1)S(1)}, u32[]{:S(2)}, u32[]{:S(2)}) collective-permute-start(bf16[256,512]{1,0:T(8,128)(2,1)S(1)} %collective-permute-done.10.refs_4_), channel_id=1, source_target_pairs={{0,2},{2,0},{4,6},{6,4},{8,10},{10,8},{12,14},{14,12},{1,3},{3,1},... | collective-permute-start | bytes 786440 | tf_op jit(solution)/shard_map/ppermute | solution.py:203
  52.3 12.5 %collective-permute-start.9 = (bf16[256,512]{1,0:T(8,128)(2,1)S(1)}, bf16[256,512]{1,0:T(8,128)(2,1)S(1)}, u32[]{:S(2)}, u32[]{:S(2)}) collective-permute-start(bf16[256,512]{1,0:T(8,128)(2,1)S(1)} %collective-permute-done.8.refs_2_), channel_id=1, source_target_pairs={{0,2},{2,0},{4,6},{6,4},{8,10},{10,8},{12,14},{14,12},{1,3},{3,1},... | collective-permute-start | bytes 786440 | tf_op jit(solution)/shard_map/ppermute | solution.py:203
  70.3 11.5 %collective-permute-start.14 = (bf16[256,2048]{1,0:T(8,128)(2,1)S(1)}, bf16[256,2048]{1,0:T(8,128)(2,1)S(1)}, u32[]{:S(2)}, u32[]{:S(2)}) collective-permute-start(bf16[256,2048]{1,0:T(8,128)(2,1)S(1)} %get-tuple-element.39), channel_id=1, source_target_pairs={{0,1},{1,0},{2,3},{3,2},{4,5},{5,4},{6,7},{7,6},{8,9},{9,8},{10,11... | collective-permute-start | bytes 3145736 | tf_op jit(solution)/shard_map/ppermute | solution.py:207
  82.3 20.6 %collective-permute-start.15 = (bf16[64,2048]{1,0:T(8,128)(2,1)S(1)}, bf16[64,2048]{1,0:T(8,128)(2,1)S(1)}, u32[]{:S(2)}, u32[]{:S(2)}) collective-permute-start(bf16[64,2048]{1,0:T(8,128)(2,1)S(1)} %get-tuple-element.55), channel_id=1, source_target_pairs={{0,8},{2,10},{4,12},{6,14},{8,0},{10,2},{12,4},{14,6},{1,9},{3,11}... | collective-permute-start | bytes 786440 | tf_op jit(solution)/shard_map/ppermute | solution.py:211
  83.0 20.0 %collective-permute-start.17 = (bf16[64,2048]{1,0:T(8,128)(2,1)S(1)}, bf16[64,2048]{1,0:T(8,128)(2,1)S(1)}, u32[]{:S(2)}, u32[]{:S(2)}) collective-permute-start(bf16[64,2048]{1,0:T(8,128)(2,1)S(1)} %get-tuple-element.56), channel_id=1, source_target_pairs={{0,4},{2,6},{4,8},{6,10},{8,12},{10,14},{12,0},{14,2},{1,5},{3,7},... | collective-permute-start | bytes 786440 | tf_op jit(solution)/shard_map/ppermute | solution.py:211
  84.9 18.9 %collective-permute-start.16 = (bf16[64,2048]{1,0:T(8,128)(2,1)S(1)}, bf16[64,2048]{1,0:T(8,128)(2,1)S(1)}, u32[]{:S(2)}, u32[]{:S(2)}) collective-permute-start(bf16[64,2048]{1,0:T(8,128)(2,1)S(1)} %get-tuple-element.57), channel_id=1, source_target_pairs={{0,12},{2,14},{4,0},{6,2},{8,4},{10,6},{12,8},{14,10},{1,13},{3,15... | collective-permute-start | bytes 786440 | tf_op jit(solution)/shard_map/ppermute | solution.py:211
  104.3 16.6 %collective-permute-start.24 = (bf16[64,2048]{1,0:T(8,128)(2,1)S(1)}, bf16[64,2048]{1,0:T(8,128)(2,1)S(1)}, u32[]{:S(2)}, u32[]{:S(2)}) collective-permute-start(bf16[64,2048]{1,0:T(8,128)(2,1)S(1)} %multiply_convert_fusion), channel_id=1, source_target_pairs={{0,4},{2,6},{4,8},{6,10},{8,12},{10,14},{12,0},{14,2},{1,5},{3,7},... | collective-permute-start | bytes 786440 | tf_op jit(solution)/shard_map/ppermute | solution.py:326
  115.2 8.8 %collective-permute-start.23 = (bf16[64,2048]{1,0:T(8,128)(2,1)S(1)}, bf16[64,2048]{1,0:T(8,128)(2,1)S(1)}, u32[]{:S(2)}, u32[]{:S(2)}) collective-permute-start(bf16[64,2048]{1,0:T(8,128)(2,1)S(1)} %multiply_convert_fusion), channel_id=1, source_target_pairs={{0,2},{2,0},{4,6},{6,4},{8,10},{10,8},{12,14},{14,12},{1,3},{3,1},... | collective-permute-start | bytes 786440 | tf_op jit(solution)/shard_map/ppermute | solution.py:327
  120.9 9.2 %collective-permute-start.26 = (bf16[64,2048]{1,0:T(8,128)(2,1)S(1)}, bf16[64,2048]{1,0:T(8,128)(2,1)S(1)}, u32[]{:S(2)}, u32[]{:S(2)}) collective-permute-start(bf16[64,2048]{1,0:T(8,128)(2,1)S(1)} %collective-permute-done.24), channel_id=1, source_target_pairs={{0,4},{2,6},{4,8},{6,10},{8,12},{10,14},{12,0},{14,2},{1,5},{3,7},... | collective-permute-start | bytes 786440 | tf_op jit(solution)/shard_map/ppermute | solution.py:326
  123.4 7.9 %collective-permute-start.25 = (bf16[64,2048]{1,0:T(8,128)(2,1)S(1)}, bf16[64,2048]{1,0:T(8,128)(2,1)S(1)}, u32[]{:S(2)}, u32[]{:S(2)}) collective-permute-start(bf16[64,2048]{1,0:T(8,128)(2,1)S(1)} %collective-permute-done.24), channel_id=1, source_target_pairs={{0,2},{2,0},{4,6},{6,4},{8,10},{10,8},{12,14},{14,12},{1,3},{3,1},... | collective-permute-start | bytes 786440 | tf_op jit(solution)/shard_map/ppermute | solution.py:327
  124.0 25.1 %collective-permute-start.30 = (bf16[128,2048]{1,0:T(8,128)(2,1)S(1)}, bf16[128,2048]{1,0:T(8,128)(2,1)}, u32[]{:S(2)}, u32[]{:S(2)}) collective-permute-start(bf16[128,2048]{1,0:T(8,128)(2,1)S(1)} %pad_maximum_fusion.refs_0_), channel_id=1, source_target_pairs={{0,1},{1,0},{2,3},{3,2},{4,5},{5,4},{6,7},{7,6},{8,9},{9,8},{10,11... | collective-permute-start | bytes 1572872 | tf_op jit(solution)/shard_map/ppermute | solution.py:328
  130.1 8.3 %collective-permute-start.28 = (bf16[64,2048]{1,0:T(8,128)(2,1)S(1)}, bf16[64,2048]{1,0:T(8,128)(2,1)S(1)}, u32[]{:S(2)}, u32[]{:S(2)}) collective-permute-start(bf16[64,2048]{1,0:T(8,128)(2,1)S(1)} %collective-permute-done.26), channel_id=1, source_target_pairs={{0,4},{2,6},{4,8},{6,10},{8,12},{10,14},{12,0},{14,2},{1,5},{3,7},... | collective-permute-start | bytes 786440 | tf_op jit(solution)/shard_map/ppermute | solution.py:326
  130.8 8.1 %collective-permute-start.27 = (bf16[64,2048]{1,0:T(8,128)(2,1)S(1)}, bf16[64,2048]{1,0:T(8,128)(2,1)S(1)}, u32[]{:S(2)}, u32[]{:S(2)}) collective-permute-start(bf16[64,2048]{1,0:T(8,128)(2,1)S(1)} %collective-permute-done.26), channel_id=1, source_target_pairs={{0,2},{2,0},{4,6},{6,4},{8,10},{10,8},{12,14},{14,12},{1,3},{3,1},... | collective-permute-start | bytes 786440 | tf_op jit(solution)/shard_map/ppermute | solution.py:327
  131.4 17.7 %collective-permute-start.31 = (bf16[128,2048]{1,0:T(8,128)(2,1)S(1)}, bf16[128,2048]{1,0:T(8,128)(2,1)}, u32[]{:S(2)}, u32[]{:S(2)}) collective-permute-start(bf16[128,2048]{1,0:T(8,128)(2,1)S(1)} %constant_dynamic-update-slice_fusion.refs_1_), channel_id=1, source_target_pairs={{0,1},{1,0},{2,3},{3,2},{4,5},{5,4},{6,7},{7,6},{8,9},{9,8},{10,11... | collective-permute-start | bytes 1572872 | tf_op jit(solution)/shard_map/ppermute | solution.py:328
  139.0 10.1 %collective-permute-start.32 = (bf16[128,2048]{1,0:T(8,128)(2,1)S(1)}, bf16[128,2048]{1,0:T(8,128)(2,1)}, u32[]{:S(2)}, u32[]{:S(2)}) collective-permute-start(bf16[128,2048]{1,0:T(8,128)(2,1)S(1)} %constant_dynamic-update-slice_fusion.2.refs_2_), channel_id=1, source_target_pairs={{0,1},{1,0},{2,3},{3,2},{4,5},{5,4},{6,7},{7,6},{8,9},{9,8},{10,11... | collective-permute-start | bytes 1572872 | tf_op jit(solution)/shard_map/ppermute | solution.py:328
  174.0 9.2 %collective-permute-start.35 = (bf16[64,2048]{1,0:T(8,128)(2,1)S(1)}, bf16[64,2048]{1,0:T(8,128)(2,1)S(1)}, u32[]{:S(2)}, u32[]{:S(2)}) collective-permute-start(bf16[64,2048]{1,0:T(8,128)(2,1)S(1)} %slice.138), channel_id=1, source_target_pairs={{0,2},{2,0},{4,6},{6,4},{8,10},{10,8},{12,14},{14,12},{1,3},{3,1},... | collective-permute-start | bytes 786440 | tf_op jit(solution)/shard_map/ppermute | solution.py:334
  174.7 14.1 %collective-permute-start.38 = (bf16[64,2048]{1,0:T(8,128)(2,1)S(1)}, bf16[64,2048]{1,0:T(8,128)(2,1)S(1)}, u32[]{:S(2)}, u32[]{:S(2)}) collective-permute-start(bf16[64,2048]{1,0:T(8,128)(2,1)S(1)} %slice.137), channel_id=1, source_target_pairs={{0,2},{2,0},{4,6},{6,4},{8,10},{10,8},{12,14},{14,12},{1,3},{3,1},... | collective-permute-start | bytes 786440 | tf_op jit(solution)/shard_map/ppermute | solution.py:334
  176.5 17.9 %collective-permute-start.41 = (bf16[64,2048]{1,0:T(8,128)(2,1)S(1)}, bf16[64,2048]{1,0:T(8,128)(2,1)S(1)}, u32[]{:S(2)}, u32[]{:S(2)}) collective-permute-start(bf16[64,2048]{1,0:T(8,128)(2,1)S(1)} %slice.136), channel_id=1, source_target_pairs={{0,2},{2,0},{4,6},{6,4},{8,10},{10,8},{12,14},{14,12},{1,3},{3,1},... | collective-permute-start | bytes 786440 | tf_op jit(solution)/shard_map/ppermute | solution.py:334
  177.2 22.2 %collective-permute-start.44 = (bf16[64,2048]{1,0:T(8,128)(2,1)S(1)}, bf16[64,2048]{1,0:T(8,128)(2,1)S(1)}, u32[]{:S(2)}, u32[]{:S(2)}) collective-permute-start(bf16[64,2048]{1,0:T(8,128)(2,1)S(1)} %slice.135), channel_id=1, source_target_pairs={{0,2},{2,0},{4,6},{6,4},{8,10},{10,8},{12,14},{14,12},{1,3},{3,1},... | collective-permute-start | bytes 786440 | tf_op jit(solution)/shard_map/ppermute | solution.py:334
  183.2 16.2 %collective-permute-start.36 = (bf16[64,2048]{1,0:T(8,128)(2,1)S(1)}, bf16[64,2048]{1,0:T(8,128)(2,1)S(1)}, u32[]{:S(2)}, u32[]{:S(2)}) collective-permute-start(bf16[64,2048]{1,0:T(8,128)(2,1)S(1)} %fusion.4), channel_id=1, source_target_pairs={{0,8},{2,10},{4,12},{6,14},{8,0},{10,2},{12,4},{14,6},{1,9},{3,11}... | collective-permute-start | bytes 786440 | tf_op jit(solution)/shard_map/ppermute | solution.py:337
  188.8 17.9 %collective-permute-start.39 = (bf16[64,2048]{1,0:T(8,128)(2,1)S(1)}, bf16[64,2048]{1,0:T(8,128)(2,1)S(1)}, u32[]{:S(2)}, u32[]{:S(2)}) collective-permute-start(bf16[64,2048]{1,0:T(8,128)(2,1)S(1)} %fusion.3), channel_id=1, source_target_pairs={{0,12},{2,14},{4,0},{6,2},{8,4},{10,6},{12,8},{14,10},{1,13},{3,15... | collective-permute-start | bytes 786440 | tf_op jit(solution)/shard_map/ppermute | solution.py:337
  194.4 12.3 %collective-permute-start.42 = (bf16[64,2048]{1,0:T(8,128)(2,1)S(1)}, bf16[64,2048]{1,0:T(8,128)(2,1)S(1)}, u32[]{:S(2)}, u32[]{:S(2)}) collective-permute-start(bf16[64,2048]{1,0:T(8,128)(2,1)S(1)} %fusion.2), channel_id=1, source_target_pairs={{0,4},{2,6},{4,8},{6,10},{8,12},{10,14},{12,0},{14,2},{1,5},{3,7},... | collective-permute-start | bytes 786440 | tf_op jit(solution)/shard_map/ppermute | solution.py:337
  (33 other events, 223.2 us)

commit v4 on v3

v4 whole, which is shorter than its diff:
```python
import jax
import jax.numpy as jnp
from jax import lax
from jax.experimental import pallas as pl
from jax.experimental.pallas import tpu as pltpu
from jax.sharding import PartitionSpec as P

HD = 128
CAP = 12

neg_large = -1e30
smem = pl.BlockSpec(memory_space=pltpu.SMEM)
vmem = pl.BlockSpec(memory_space=pltpu.VMEM)
unread = pl.BlockSpec(memory_space=pl.ANY)


def limit(mebibytes):
    return pltpu.CompilerParams(vmem_limit_bytes=mebibytes * 1024 * 1024)


def ring(size, step):
    return [(i, (i + 2 * step) % size) for i in range(size)]


def swap(size):
    return [(i, i ^ 1) for i in range(size)]


def far_first(depth):
    return sorted(range(1, depth), key=lambda d: -min(d, depth - d))


def wide(value):
    return value.astype(jnp.float32)


def narrow(value):
    return value.astype(jnp.bfloat16)


def pack_heads(z, queries, key_rows, value_rows, out_weight, expert_ids, gate_weights, depth):
    rows = queries.shape[0]
    columns = queries.shape[1] // depth
    per_group = queries.shape[1] // key_rows.shape[1] * HD
    tokens, top = expert_ids.shape
    lines = tokens // 4

    def kernel(z_ref, query_ref, key_ref, value_ref, weight_ref, id_ref, gate_ref, *out_refs):
        gates = gate_ref[...]
        high = wide(narrow(gates))
        blank = jnp.zeros((tokens, HD // 2 - 3 * top), jnp.float32)
        meta = jnp.concatenate([wide(id_ref[...]), high, gates - high, blank], axis=1)
        meta = jnp.concatenate([meta[g * lines : (g + 1) * lines] for g in range(4)], axis=1)
        for d, out_ref in enumerate(out_refs[:depth]):
            start = (z_ref[0] + d) % depth * columns
            group = pl.ds(pl.multiple_of(start // per_group * HD, HD), HD)
            out_ref[:rows, :columns] = query_ref[:, pl.ds(pl.multiple_of(start, HD), columns)]
            out_ref[:rows, columns : columns + HD] = key_ref[:, group]
            out_ref[:rows, columns + HD :] = value_ref[:, group]
            out_ref[rows:, :columns] = jnp.zeros((lines, columns), jnp.bfloat16)
            out_ref[rows:, columns:] = narrow(meta)
        out_refs[depth][...] = weight_ref[:, pl.ds(pl.multiple_of(z_ref[0] * columns, HD), columns)]

    return pl.pallas_call(
        kernel,
        out_shape=[jax.ShapeDtypeStruct((rows + lines, columns + 2 * HD), queries.dtype)] * depth
        + [jax.ShapeDtypeStruct((out_weight.shape[0], columns), out_weight.dtype)],
        in_specs=[smem] + [vmem] * 6,
        out_specs=[vmem] * (depth + 1),
        compiler_params=limit(16),
        name="pack_heads",
    )(z, queries, key_rows, value_rows, out_weight, expert_ids, gate_weights)


def pack_weight(z, out_weight, depth, before):
    rows = out_weight.shape[0]
    columns = out_weight.shape[1] // depth

    def kernel(z_ref, weight_ref, *refs):
        for d, out_ref in enumerate(refs[len(before) :]):
            start = pl.multiple_of((z_ref[0] + d + 1) % depth * columns, HD)
            out_ref[...] = weight_ref[:, pl.ds(start, columns)]

    return pl.pallas_call(
        kernel,
        out_shape=[jax.ShapeDtypeStruct((rows, columns), out_weight.dtype)] * (depth - 1),
        in_specs=[smem, vmem] + [unread] * len(before),
        out_specs=[vmem] * (depth - 1),
        compiler_params=limit(16),
        name="pack_weight",
    )(z, out_weight, *before)


def collect_meta(near, across, rows):
    lines = across[0].shape[0] - rows
    parts = [part for pair in zip(near, across) for part in pair]

    def kernel(*refs):
        for i, ref in enumerate(refs[:-1]):
            refs[-1][i * lines : (i + 1) * lines, :] = ref[rows:, -2 * HD :]

    return pl.pallas_call(
        kernel,
        out_shape=jax.ShapeDtypeStruct((len(parts) * lines, 2 * HD), jnp.bfloat16),
        in_specs=[vmem] * len(parts),
        out_specs=vmem,
        compiler_params=limit(16),
        name="collect_meta",
    )(*parts)


def attend(core, starts, key_pos, messages, across, rows, columns):
    depth = len(messages)
    heads = columns // HD
    length = 2 * depth * rows
    half = rows // 2

    def kernel(core_ref, starts_ref, key_pos_ref, *refs):
        message_refs, across_refs = refs[:depth], refs[depth : 2 * depth]
        out_refs, (query, keyed) = refs[-2 - depth : -2], refs[-2:]
        for d in range(depth):
            for h in range(heads):
                query[d, h * rows : (h + 1) * rows, :] = message_refs[d][:rows, h * HD : (h + 1) * HD]
            keyed[2 * d * rows : (2 * d + 1) * rows, :] = message_refs[d][:rows, columns:]
            keyed[(2 * d + 1) * rows : (2 * d + 2) * rows, :] = across_refs[d][:rows, :]
        mine = core_ref[0] == 0

        for d in range(depth):
            scores = lax.dot_general(
                query[d], keyed[:, :HD], (((1,), (1,)), ((), ())), preferred_element_type=jnp.float32
            )
            offset = lax.broadcasted_iota(jnp.int32, (heads * rows, 1), 0) % rows
            allowed = key_pos_ref[...] <= starts_ref[d] + offset
            scores = jnp.where(allowed, scores, neg_large)
            largest = jnp.max(scores, axis=-1, keepdims=True)
            exps = jnp.exp((scores - largest) * (HD**-0.5))
            total = jnp.sum(exps, axis=-1, keepdims=True)
            summed = jnp.dot(narrow(exps), keyed[:, HD:], preferred_element_type=jnp.float32)
            context = narrow(summed / total)
            for h in range(heads):
                low, high = context[h * rows : h * rows + half], context[h * rows + half : (h + 1) * rows]
                out_refs[d][:half, h * HD : (h + 1) * HD] = jnp.where(mine, low, high)
                out_refs[d][half:, h * HD : (h + 1) * HD] = jnp.where(mine, high, low)

    work = depth * rows * columns * length
    return pl.pallas_call(
        kernel,
        out_shape=[jax.ShapeDtypeStruct((rows, columns), jnp.bfloat16)] * depth,
        in_specs=[smem, smem, vmem] + [vmem] * (2 * depth),
        out_specs=[vmem] * depth,
        scratch_shapes=[
            pltpu.VMEM((depth, heads * rows, HD), jnp.bfloat16),
            pltpu.VMEM((length, 2 * HD), jnp.bfloat16),
        ],
        compiler_params=limit(24),
        cost_estimate=pl.CostEstimate(flops=160 * work, bytes_accessed=depth * rows * columns * 8, transcendentals=work // HD),
        name="attend",
    )(core, starts, key_pos, *messages, *across)


def project(place, context, weights, before):
    depth, blocks = len(context), len(weights)
    rows, columns = context[0].shape[0] // 2, context[0].shape[1]
    features = weights[0].shape[0]
    shape = (depth, rows, blocks * features)
    if features % HD:
        weight = jnp.stack(weights)[jnp.argsort(place)]
        left = jnp.stack(context).reshape(depth, 2, rows, columns)
        result = jnp.einsum("dcrk,bfk->cdrbf", left, weight, preferred_element_type=jnp.float32)
        result = narrow(result.reshape((2,) + shape))
        return result[0], result[1]

    def kernel(place_ref, *refs):
        context_refs, weight_refs, out_refs = refs[:depth], refs[depth : depth + blocks], refs[-3:-1]
        left_ref = refs[-1]
        for d in range(depth):
            left_ref[2 * d * rows : 2 * (d + 1) * rows, :] = context_refs[d][...]
        left = left_ref[...]
        for i in range(blocks):
            part = narrow(
                lax.dot_general(
                    left, weight_refs[i][...], (((1,), (1,)), ((), ())), preferred_element_type=jnp.float32
                )
            ).reshape(depth, 2, rows, features)
            there = pl.ds(pl.multiple_of(place_ref[i] * features, HD), features)
            for core in range(2):
                out_refs[core][:, :, there] = part[:, core]

    return pl.pallas_call(
        kernel,
        out_shape=[jax.ShapeDtypeStruct(shape, jnp.bfloat16)] * 2,
        in_specs=[smem] + [vmem] * (depth + blocks) + [unread] * len(before),
        out_specs=[vmem, vmem],
        scratch_shapes=[pltpu.VMEM((2 * depth * rows, columns), jnp.bfloat16)],
        compiler_params=limit(20),
        cost_estimate=pl.CostEstimate(
            flops=4 * depth * rows * columns * blocks * features,
            bytes_accessed=2 * blocks * features * columns + 4 * depth * rows * (columns + 2 * blocks * features),
            transcendentals=0,
        ),
        name="project",
    )(place, *context, *weights, *before)


def add_up(parts):
    def kernel(*refs):
        total = wide(refs[0][...])
        for ref in refs[1 : len(parts)]:
            total = total + wide(ref[...])
        refs[-2][...] = total
        refs[-1][...] = narrow(total)

    return pl.pallas_call(
        kernel,
        out_shape=[
            jax.ShapeDtypeStruct(parts[0].shape, jnp.float32),
            jax.ShapeDtypeStruct(parts[0].shape, jnp.bfloat16),
        ],
        in_specs=[vmem] * len(parts),
        out_specs=[vmem, vmem],
        compiler_params=limit(32),
        name="add_up",
    )(*parts)


def attention_block(stream, queries, key_rows, value_rows, out_weight, expert_ids, gate_weights, local_experts):
    size = lax.axis_size("seq")
    depth = size // 2
    z, y = lax.axis_index("seq") // 2, lax.axis_index("seq") % 2
    core = lax.axis_index("exp").astype(jnp.int32).reshape(1)
    rows = queries.shape[0]
    columns = queries.shape[1] // depth
    steps = far_first(depth)
    here = z.astype(jnp.int32).reshape(1)

    *message, own_weight = pack_heads(
        here, queries, key_rows, value_rows, out_weight, expert_ids, gate_weights, depth
    )
    for d in steps:
        message[d] = lax.ppermute(message[d], "seq", ring(size, d))
    across = {}
    for d in [0] + steps:
        across[d] = lax.ppermute(message[d][:, columns:], "seq", swap(size))
    across = [across[d] for d in range(depth)]
    weight = [own_weight] + list(pack_weight(here, out_weight, depth, [message[d] for d in steps]))
    weight_across = {0: lax.ppermute(own_weight, "seq", swap(size))}
    for d in steps[::-1]:
        weight[d] = lax.ppermute(weight[d], "seq", ring(size, d))
        weight_across[d] = lax.ppermute(weight[d], "seq", swap(size))
    first = (lax.axis_index("seq") * 2 + lax.axis_index("exp")) * local_experts
    meta = collect_meta(message, across, rows)
    meta = [meta, lax.ppermute(meta, "exp", swap(2))]
    route = routing(first, meta, depth, *expert_ids.shape, local_experts, [weight_across[0]])

    behind = (z - jnp.arange(depth, dtype=jnp.int32)) % depth
    block = (behind[:, None] * 2 + jnp.stack([y, 1 - y])[None, :]).astype(jnp.int32)
    key_pos = (block.reshape(-1, 1) * rows + jnp.arange(rows, dtype=jnp.int32)).reshape(1, -1)
    context = attend(core, block[:, 0] * rows, key_pos, message, across, rows, columns)
    kept, given = project(
        block.reshape(-1), context, [part for d in range(depth) for part in (weight[d], weight_across[d])], route[1:]
    )
    chip = wide(kept) + wide(lax.ppermute(given, "exp", swap(2)))
    parts = [stream, chip[0]]
    for d in steps:
        parts.append(lax.ppermute(narrow(chip[d]), "seq", ring(size, -d)))
    return *add_up(parts), route


def routing(first, meta, subs, rows, top, local_experts, before):
    lines = rows // 4
    tokens = 4 * rows
    slots = 4 * CAP
    lanes = 128
    contract = lambda a, b, i, j: lax.dot_general(a, b, (((i,), (j,)), ((), ())), preferred_element_type=jnp.float32)
    iota = lambda shape, axis: lax.broadcasted_iota(jnp.int32, shape, axis)

    def kernel(first_ref, mine_ref, other_ref, *refs):
        select_ref, spread_ref, gate_ref = refs[len(before) :]
        token, other = iota((tokens, tokens), 0), iota((tokens, tokens), 1)
        earlier = narrow(wide((other < token) & (other // rows == token // rows)))
        same = narrow(wide(token == other))
        lane = iota((tokens, lanes), 1)
        owner = narrow(wide(iota((lanes, local_experts * slots), 1) // slots == iota((lanes, local_experts * slots), 0)))
        slot = iota((local_experts * slots, tokens), 0)
        fits = slot % slots // CAP == iota((local_experts * slots, tokens), 1) // rows
        for s in range(subs):
            packed = []
            for ref in (mine_ref, other_ref):
                for y in range(2):
                    block = wide(ref[(2 * s + y) * lines : (2 * s + y + 1) * lines, :])
                    packed += [block[:, g * HD // 2 : g * HD // 2 + 3 * top] for g in range(4)]
            packed = jnp.concatenate(packed, axis=0)
            hit = jnp.zeros((tokens, lanes), jnp.float32)
            high, low = hit, hit
            for j in range(local_experts):
                match = packed[:, :top] == wide(first_ref[0] + j)
                column = lambda kind: jnp.sum(jnp.where(match, kind, 0.0), axis=1, keepdims=True)
                here = lane == j
                hit = jnp.where(here, column(1.0), hit)
                high = jnp.where(here, column(packed[:, top : 2 * top]), high)
                low = jnp.where(here, column(packed[:, 2 * top :]), low)
            place = contract(earlier, narrow(hit), 1, 0)
            by_slot = lambda value: contract(owner, narrow(value), 0, 1)
            chosen = (by_slot(hit) > 0.5) & (jnp.abs(by_slot(place) - wide(slot % CAP)) < 0.5) & fits
            gates = jnp.sum(jnp.where(chosen, by_slot(high) + by_slot(low), 0.0), axis=1, keepdims=True)
            chosen = narrow(wide(chosen))
            spread_ref[s] = narrow(contract(same, chosen, 1, 1))
            for j in range(local_experts):
                select_ref[j, s] = chosen[j * slots : (j + 1) * slots]
                gate_ref[j, s * slots : (s + 1) * slots, :] = gates[j * slots : (j + 1) * slots]

    return pl.pallas_call(
        kernel,
        out_shape=[
            jax.ShapeDtypeStruct((local_experts, subs, slots, tokens), jnp.bfloat16),
            jax.ShapeDtypeStruct((subs, tokens, local_experts * slots), jnp.bfloat16),
            jax.ShapeDtypeStruct((local_experts, subs * slots, 1), jnp.float32),
        ],
        in_specs=[smem, vmem, vmem] + [unread] * len(before),
        out_specs=[vmem] * 3,
        compiler_params=limit(32),
        name="routing",
    )(first.astype(jnp.int32).reshape(1), *meta, *before)


def run_experts(mine, other, select, spread, row_gate, norm_gain, expert_in, expert_out):
    subs = len(mine)
    tokens, width = mine[0].shape
    local_experts, hidden, _ = expert_out.shape
    slots = select.shape[2]

    def kernel(select_ref, spread_ref, gate_ref, gain_ref, wg_ref, wu_ref, wo_ref, *refs):
        mine_refs, other_refs = refs[:subs], refs[subs : 2 * subs]
        kept_refs, given_refs = refs[2 * subs : 3 * subs], refs[3 * subs : 4 * subs]
        xg, res = refs[4 * subs :]
        expert = pl.program_id(0)

        @pl.when(expert == 0)
        def _():
            for s in range(subs):
                choose = select_ref[:, s].reshape(local_experts * slots, 2 * tokens)
                picked = jnp.dot(
                    choose[:, :tokens], mine_refs[s][...], preferred_element_type=jnp.float32
                ) + jnp.dot(choose[:, tokens:], other_refs[s][...], preferred_element_type=jnp.float32)
                scale = lax.rsqrt(jnp.sum(picked * picked, axis=1, keepdims=True) * (1.0 / width) + 1e-06)
                rows = narrow(picked * scale * gain_ref[...])
                for e in range(local_experts):
                    xg[e, s * slots : (s + 1) * slots, :] = rows[e * slots : (e + 1) * slots]

        rows = xg[expert]
        gate = jnp.dot(rows, wg_ref[0], preferred_element_type=jnp.float32)
        up = jnp.dot(rows, wu_ref[0], preferred_element_type=jnp.float32)
        act = narrow(gate / (1.0 + jnp.exp(-gate)) * up)
        part_out = jnp.dot(act, wo_ref[0], preferred_element_type=jnp.float32)
        scaled = narrow(part_out * gate_ref[expert])
        for s in range(subs):
            res[s, expert] = scaled[s * slots : (s + 1) * slots, :]

        @pl.when(expert == pl.num_programs(0) - 1)
        def _():
            for s in range(subs):
                both = narrow(
                    jnp.dot(spread_ref[s], res[s].reshape(-1, width), preferred_element_type=jnp.float32)
                )
                kept_refs[s][...] = both[:tokens]
                given_refs[s][...] = both[tokens:]

    flops = local_experts * subs * slots * width * hidden * 6
    moved = (expert_in.size + expert_out.size + 8 * subs * tokens * width) * 2

    def whole(shape):
        return pl.BlockSpec(shape, lambda e: (0,) * len(shape), pipeline_mode=pl.Buffered(1))

    outs = pl.pallas_call(
        kernel,
        grid=(local_experts,),
        out_shape=[jax.ShapeDtypeStruct((tokens, width), jnp.bfloat16)] * (2 * subs),
        in_specs=[
            whole(select.shape),
            whole(spread.shape),
            whole(row_gate.shape),
            whole((1, width)),
            pl.BlockSpec((1, width, hidden), lambda e: (e, 0, 0)),
            pl.BlockSpec((1, width, hidden), lambda e: (e, 0, 1)),
            pl.BlockSpec((1, hidden, width), lambda e: (e, 0, 0)),
        ]
        + [whole((tokens, width))] * (2 * subs),
        out_specs=[whole((tokens, width))] * (2 * subs),
        scratch_shapes=[
            pltpu.VMEM((local_experts, subs * slots, width), jnp.bfloat16),
            pltpu.VMEM((subs, local_experts, slots, width), jnp.bfloat16),
        ],
        compiler_params=limit(34),
        cost_estimate=pl.CostEstimate(flops=flops, bytes_accessed=moved, transcendentals=0),
        name="experts",
    )(
        select,
        spread,
        row_gate,
        norm_gain.reshape(1, -1),
        expert_in,
        expert_in,
        expert_out,
        *mine,
        *other,
    )
    return outs[:subs], outs[subs:]


def expert_block(mixed, rounded, route, norm_gain, expert_in, expert_out):
    size = lax.axis_size("seq")
    depth = size // 2
    rows = mixed.shape[0]

    along, mine, other = [rounded], [], []
    for d in range(depth):
        if d + 1 < depth:
            along.append(lax.ppermute(along[d], "seq", ring(size, 1)))
        mine.append(jnp.concatenate([along[d], lax.ppermute(along[d], "seq", swap(size))]))
        other.append(lax.ppermute(mine[d], "exp", swap(2)))
    kept, given = run_experts(mine, other, *route, norm_gain, expert_in, expert_out)

    total = mixed
    for d in far_first(depth) + [0]:
        pair = wide(kept[d]) + wide(lax.ppermute(given[d], "exp", swap(2)))
        there = lax.ppermute(narrow(pair[rows:]), "seq", swap(size))
        chip = pair[:rows] + wide(there)
        if d:
            chip = wide(lax.ppermute(narrow(chip), "seq", ring(size, -d)))
        total = total + chip
    return narrow(total)


def on_device(
    stream,
    queries,
    key_rows,
    value_rows,
    out_weight,
    norm_gain,
    expert_ids,
    gate_weights,
    expert_in,
    expert_out,
):
    mixed, rounded, route = attention_block(
        stream, queries, key_rows, value_rows, out_weight, expert_ids, gate_weights, expert_in.shape[0]
    )
    return expert_block(mixed, rounded, route, norm_gain, expert_in, expert_out)


def solution(mesh):
    in_specs = (
        P(("groups", "seq", "exp"), None),
        P(("groups", "seq"), "exp"),
        P(("groups", "seq"), "exp"),
        P(("groups", "seq"), "exp"),
        P("seq", "exp"),
        P(),
        P(("groups", "seq", "exp"), None),
        P(("groups", "seq", "exp"), None),
        P(("seq", "exp"), None, None),
        P(("seq", "exp"), None, None),
    )
    out_specs = P(("groups", "seq", "exp"), None)
    return jax.shard_map(
        on_device, mesh=mesh, in_specs=in_specs, out_specs=out_specs, check_vma=False
    )
```

time: 208 us -> 190 us (0.913)
  starting transfers between devices: 52.3 us -> 40.4 us
  waiting for transfers between devices: 104 us -> 112 us
  local copies, waits for them, and re-layouts: 13.4 us -> 6.06 us
  other arithmetic: 6.61 us -> 2.19 us
    ppermute x3, starting transfers between devices: 14 us -> 0.06 us  [expert_block(): along.append(lax.ppermute(along[d], 'seq', ring(size, 1)))]
    ppermute x3, waiting for transfers between devices: 16.8 us -> 25.6 us  [expert_block(): along.append(lax.ppermute(along[d], 'seq', ring(size, 1)))]
    ppermute x13 -> x9, waiting for transfers between devices: 40.9 us -> 33.9 us  [the longest x3 22.9 us: attention_block(): parts.append(lax.ppermute(narrow(chip[d]), 'seq', ring(size, -d)))]
    unnamed x43 -> x20, local copies, waits for them, and re-layouts: 9.05 us -> 5.57 us
    ppermute x3, waiting for transfers between devices: 8.81 us -> 12.2 us  [attention_block(): message[d] = lax.ppermute(message[d], 'seq', ring(size, d))]
    pallas_call x1, Pallas kernels: 21.4 us -> 18.1 us  [run_experts(): pl.pallas_call(kernel, grid=(local_experts,), out_shape=[jax.ShapeDtypeSt...]
    ppermute x13 -> x9, starting transfers between devices: 14.4 us -> 17.2 us  [the longest x3 8.36 us: attention_block(): parts.append(lax.ppermute(narrow(chip[d]), 'seq', ring(size, -d)))]
    pallas_call x3 -> x6, Pallas kernels: 9.11 us -> 10.6 us  [the longest x1 4.44 us: attend(): pl.pallas_call(kernel, out_shape=[jax.ShapeDtypeStruct((rows, columns), j...]
  transfers between devices with their start and end apart: 45 -> 41, of which waited for: 22 -> 21; matrix products, arithmetic and copies ran while one was open for 4% -> 1% of each run, Pallas kernels for 3% -> 4%
where the time goes in v4:
time: 190 us
  waiting for transfers between devices  112 us (59%)
  starting transfers between devices  40.4 us (21%)
  Pallas kernels  28.8 us (15%)
  local copies, waits for them, and re-layouts  6.06 us (3%)
  other arithmetic  2.19 us (1%)
    ppermute x3, waiting for transfers between devices, expert_block(): along.append(lax.ppermute(along[d], 'seq', ring(size, 1)))  25.6 us
    ppermute x3, waiting for transfers between devices, attention_block(): parts.append(lax.ppermute(narrow(chip[d]), 'seq', ring(size, -d)))  22.9 us
    ppermute x4, waiting for transfers between devices, expert_block(): there = lax.ppermute(narrow(pair[rows:]), 'seq', swap(size))  18.9 us
    pallas_call x1, Pallas kernels, run_experts(): pl.pallas_call(kernel, grid=(local_experts,), out_shape=[jax.ShapeDtypeSt...  18.1 us
    ppermute x3, waiting for transfers between devices, attention_block(): message[d] = lax.ppermute(message[d], 'seq', ring(size, d))  12.2 us
    ppermute x3, waiting for transfers between devices, attention_block(): weight[d] = lax.ppermute(weight[d], 'seq', ring(size, d))  8.41 us
    ppermute x3, starting transfers between devices, attention_block(): parts.append(lax.ppermute(narrow(chip[d]), 'seq', ring(size, -d)))  8.36 us
    ppermute x3, starting transfers between devices, attention_block(): weight[d] = lax.ppermute(weight[d], 'seq', ring(size, d))  7.7 us
  transfers between devices with their start and end apart: 41, of which 21 were waited for; matrix products, arithmetic and copies ran while one was open for 1% of the time, Pallas kernels for 4%

profile of v4, /device:TPU:0, one launch (start us, length us, event | category | flops | bytes accessed | tf_op | source)
XLA Modules:
  0.0 189.7 jit_solution(9460715986581616018)
XLA Ops:
  5.7 3.0 %collective-permute-start.3 = (bf16[144,256]{1,0:T(8,128)(2,1)S(1)}, bf16[144,256]{1,0:T(8,128)(2,1)S(1)}, u32[]{:S(2)}, u32[]{:S(2)}) collective-permute-start(bf16[144,256]{1,0:T(8,128)(2,1)S(1)} %slice.59), channel_id=1, source_target_pairs={{0,2},{2,0},{4,6},{6,4},{8,10},{10,8},{12,14},{14,12},{1,3},{3,1},... | collective-permute-start | bytes 221192 | tf_op jit(solution)/shard_map/ppermute | solution.py:243
  8.7 1.6 collective-permute-start
  10.3 2.6 %collective-permute-start.1 = (bf16[144,768]{1,0:T(8,128)(2,1)S(1)}, bf16[144,768]{1,0:T(8,128)(2,1)S(1)}, u32[]{:S(2)}, u32[]{:S(2)}) collective-permute-start(bf16[144,768]{1,0:T(8,128)(2,1)S(1)} %get-tuple-element.34), channel_id=1, source_target_pairs={{0,8},{2,10},{4,12},{6,14},{8,0},{10,2},{12,4},{14,6},{1,9},{3,11}... | collective-permute-start | bytes 663560 | tf_op jit(solution)/shard_map/ppermute | solution.py:240
  14.6 4.4 %collective-permute-done.refs_1_.refs_2_ = bf16[144,768]{1,0:T(8,128)(2,1)S(1)} collective-permute-done((bf16[144,768]{1,0:T(8,128)(2,1)S(1)}, bf16[144,768]{1,0:T(8,128)(2,1)S(1)}, u32[]{:S(2)}, u32[]{:S(2)}) %collective-permute-start) | collective-permute-done | bytes 221216 | tf_op jit(solution)/shard_map/ppermute | solution.py:240
  19.3 7.8 %collective-permute-done.1.refs_2_.refs_0_.refs_4_ = bf16[144,768]{1,0:T(8,128)(2,1)S(1)} collective-permute-done((bf16[144,768]{1,0:T(8,128)(2,1)S(1)}, bf16[144,768]{1,0:T(8,128)(2,1)S(1)}, u32[]{:S(2)}, u32[]{:S(2)}) %collective-permute-start.1) | collective-permute-done | bytes 221216 | tf_op jit(solution)/shard_map/ppermute | solution.py:240
  27.1 5.3 %collective-permute-start.8 = (bf16[256,512]{1,0:T(8,128)(2,1)S(1)}, bf16[256,512]{1,0:T(8,128)(2,1)S(1)}, u32[]{:S(2)}, u32[]{:S(2)}) collective-permute-start(bf16[256,512]{1,0:T(8,128)(2,1)S(1)} %get-tuple-element.41), channel_id=1, source_target_pairs={{0,4},{2,6},{4,8},{6,10},{8,12},{10,14},{12,0},{14,2},{1,5},{3,7},... | collective-permute-start | bytes 786440 | tf_op jit(solution)/shard_map/ppermute | solution.py:248
  32.4 1.6 collective-permute-start.10
  37.0 2.4 %collective-permute-done.5.refs_6_.refs_5_ = bf16[144,256]{1,0:T(8,128)(2,1)S(1)} collective-permute-done((bf16[144,256]{1,0:T(8,128)(2,1)S(1)}, bf16[144,256]{1,0:T(8,128)(2,1)S(1)}, u32[]{:S(2)}, u32[]{:S(2)}) %collective-permute-start.5) | collective-permute-done | bytes 73760 | tf_op jit(solution)/shard_map/ppermute | solution.py:243
  41.8 8.1 %collective-permute-done.10.refs_8_ = bf16[256,512]{1,0:T(8,128)(2,1)S(1)} collective-permute-done((bf16[256,512]{1,0:T(8,128)(2,1)S(1)}, bf16[256,512]{1,0:T(8,128)(2,1)S(1)}, u32[]{:S(2)}, u32[]{:S(2)}) %collective-permute-start.10) | collective-permute-done | bytes 262176 | tf_op jit(solution)/shard_map/ppermute | solution.py:248
  51.9 4.4 %attend.1 = (bf16[128,512]{1,0:T(8,128)(2,1)S(1)}, bf16[128,512]{1,0:T(8,128)(2,1)S(1)}, bf16[128,512]{1,0:T(8,128)(2,1)S(1)}, bf16[128,512]{1,0:T(8,128)(2,1)S(1)}) custom-call(s32[1]{0:T(128)} %bitcast.2.core_ref, s32[4]{0:T(128)S(1)} %multiply_bitcast_fusion.starts_ref, s32[1,1024]{1,0:T(1,128)S(1)} %bitcast.18, ...), custom_call_target="tpu_custom_call" | custom-call | flops 42949672960 | bytes 2097152 | tf_op jit(solution)/shard_map/attend/pallas_call | solution.py:146
  56.4 3.9 %routing.1 = (bf16[4,4,48,256]{3,2,1,0:T(8,128)(2,1)S(1)}, bf16[4,256,192]{2,1,0:T(8,128)(2,1)S(1)}, f32[4,192,1]{2,1,0:T(8,128)S(1)}) custom-call(s32[1]{0:T(128)} %bitcast.6.first_ref, bf16[128,256]{1,0:T(8,128)(2,1)S(1)} %collect_meta.1.mine_ref, bf16[128,256]{1,0:T(8,128)(2,1)S(1)} %collective-permute-done.14.other_ref, ...), custom_call_target="tpu_custom_call" | custom-call | tf_op jit(solution)/shard_map/routing/pallas_call | solution.py:312
  60.3 3.4 %collective-permute-done.13.refs_11_ = bf16[256,512]{1,0:T(8,128)(2,1)S(1)} collective-permute-done((bf16[256,512]{1,0:T(8,128)(2,1)S(1)}, bf16[256,512]{1,0:T(8,128)(2,1)S(1)}, u32[]{:S(2)}, u32[]{:S(2)}) %collective-permute-start.13) | collective-permute-done | bytes 262176 | tf_op jit(solution)/shard_map/ppermute | solution.py:249
  63.7 1.9 %project.1 = (bf16[4,64,2048]{2,1,0:T(8,128)(2,1)S(1)}, bf16[4,64,2048]{2,1,0:T(8,128)(2,1)S(1)}) custom-call(s32[8]{0:T(128)S(1)} %add.107.place_ref, bf16[128,512]{1,0:T(8,128)(2,1)S(1)} %get-tuple-element.36.refs_0_, bf16[128,512]{1,0:T(8,128)(2,1)S(1)} %get-tuple-element.37.refs_1_, bf16[128,512]{1,0:T(8,128)(2,1)S(1)} %get-tuple-element.38.refs_2_, ...), custom_call_target="tpu_custom_call" | custom-call | flops 1073741824 | bytes 6815744 | tf_op jit(solution)/shard_map/project/pallas_call | solution.py:189
  65.6 2.6 %collective-permute-done.15 = bf16[4,64,2048]{2,1,0:T(8,128)(2,1)S(1)} collective-permute-done((bf16[4,64,2048]{2,1,0:T(8,128)(2,1)S(1)}, bf16[4,64,2048]{2,1,0:T(8,128)(2,1)S(1)}, u32[]{:S(2)}, u32[]{:S(2)}) %collective-permute-start.15) | collective-permute-done | bytes 1048608 | tf_op jit(solution)/shard_map/ppermute | solution.py:262
  68.8 5.0 %collective-permute-start.18 = (bf16[64,2048]{1,0:T(8,128)(2,1)S(1)}, bf16[64,2048]{1,0:T(8,128)(2,1)S(1)}, u32[]{:S(2)}, u32[]{:S(2)}) collective-permute-start(bf16[64,2048]{1,0:T(8,128)(2,1)S(1)} %get-tuple-element.61), channel_id=1, source_target_pairs={{0,4},{2,6},{4,8},{6,10},{8,12},{10,14},{12,0},{14,2},{1,5},{3,7},... | collective-permute-start | bytes 786440 | tf_op jit(solution)/shard_map/ppermute | solution.py:265
  73.8 2.9 %collective-permute-start.17 = (bf16[64,2048]{1,0:T(8,128)(2,1)S(1)}, bf16[64,2048]{1,0:T(8,128)(2,1)S(1)}, u32[]{:S(2)}, u32[]{:S(2)}) collective-permute-start(bf16[64,2048]{1,0:T(8,128)(2,1)S(1)} %get-tuple-element.62), channel_id=1, source_target_pairs={{0,12},{2,14},{4,0},{6,2},{8,4},{10,6},{12,8},{14,10},{1,13},{3,15... | collective-permute-start | bytes 786440 | tf_op jit(solution)/shard_map/ppermute | solution.py:265
  77.2 6.5 %collective-permute-done.18.refs_4_ = bf16[64,2048]{1,0:T(8,128)(2,1)S(1)} collective-permute-done((bf16[64,2048]{1,0:T(8,128)(2,1)S(1)}, bf16[64,2048]{1,0:T(8,128)(2,1)S(1)}, u32[]{:S(2)}, u32[]{:S(2)}) %collective-permute-start.18) | collective-permute-done | bytes 262176 | tf_op jit(solution)/shard_map/ppermute | solution.py:265
  83.7 3.7 %collective-permute-done.17.refs_3_ = bf16[64,2048]{1,0:T(8,128)(2,1)S(1)} collective-permute-done((bf16[64,2048]{1,0:T(8,128)(2,1)S(1)}, bf16[64,2048]{1,0:T(8,128)(2,1)S(1)}, u32[]{:S(2)}, u32[]{:S(2)}) %collective-permute-start.17) | collective-permute-done | bytes 262176 | tf_op jit(solution)/shard_map/ppermute | solution.py:265
  87.5 12.6 %collective-permute-done.16.refs_2_ = bf16[64,2048]{1,0:T(8,128)(2,1)S(1)} collective-permute-done((bf16[64,2048]{1,0:T(8,128)(2,1)S(1)}, bf16[64,2048]{1,0:T(8,128)(2,1)S(1)}, u32[]{:S(2)}, u32[]{:S(2)}) %collective-permute-start.16) | collective-permute-done | bytes 262176 | tf_op jit(solution)/shard_map/ppermute | solution.py:265
  100.9 9.4 %collective-permute-done.20 = bf16[64,2048]{1,0:T(8,128)(2,1)S(1)} collective-permute-done((bf16[64,2048]{1,0:T(8,128)(2,1)S(1)}, bf16[64,2048]{1,0:T(8,128)(2,1)S(1)}, u32[]{:S(2)}, u32[]{:S(2)}) %collective-permute-start.20) | collective-permute-done | bytes 262176 | tf_op jit(solution)/shard_map/ppermute | solution.py:418
  111.0 8.5 %collective-permute-done.22 = bf16[64,2048]{1,0:T(8,128)(2,1)S(1)} collective-permute-done((bf16[64,2048]{1,0:T(8,128)(2,1)S(1)}, bf16[64,2048]{1,0:T(8,128)(2,1)S(1)}, u32[]{:S(2)}, u32[]{:S(2)}) %collective-permute-start.22) | collective-permute-done | bytes 262176 | tf_op jit(solution)/shard_map/ppermute | solution.py:418
  120.2 7.6 %collective-permute-done.24 = bf16[64,2048]{1,0:T(8,128)(2,1)S(1)} collective-permute-done((bf16[64,2048]{1,0:T(8,128)(2,1)S(1)}, bf16[64,2048]{1,0:T(8,128)(2,1)S(1)}, u32[]{:S(2)}, u32[]{:S(2)}) %collective-permute-start.24) | collective-permute-done | bytes 262176 | tf_op jit(solution)/shard_map/ppermute | solution.py:418
  128.5 5.7 %collective-permute-done.25 = bf16[64,2048]{1,0:T(8,128)(2,1)S(1)} collective-permute-done((bf16[64,2048]{1,0:T(8,128)(2,1)S(1)}, bf16[64,2048]{1,0:T(8,128)(2,1)S(1)}, u32[]{:S(2)}, u32[]{:S(2)}) %collective-permute-start.25) | collective-permute-done | bytes 262176 | tf_op jit(solution)/shard_map/ppermute | solution.py:419
  134.3 1.9 collective-permute-done.29.refs_7_
  136.2 18.1 %experts.1 = (bf16[128,2048]{1,0:T(8,128)(2,1)S(1)}, bf16[128,2048]{1,0:T(8,128)(2,1)S(1)}, bf16[128,2048]{1,0:T(8,128)(2,1)S(1)}, bf16[128,2048]{1,0:T(8,128)(2...) custom-call(bf16[4,4,48,256]{3,2,1,0:T(8,128)(2,1)S(1)} %get-tuple-e, ...), custom_call_target="tpu_custom_call" | custom-call | flops 7247757312 | bytes 54525952 | tf_op jit(solution)/shard_map/experts/pallas_call | solution.py:374
  157.2 1.6 collective-permute-start.34
  159.7 1.6 collective-permute-start.40
  161.3 4.4 %collective-permute-done.31 = bf16[64,2048]{1,0:T(8,128)(2,1)S(1)} collective-permute-done((bf16[64,2048]{1,0:T(8,128)(2,1)S(1)}, bf16[64,2048]{1,0:T(8,128)(2,1)S(1)}, u32[]{:S(2)}, u32[]{:S(2)}) %collective-permute-start.31) | collective-permute-done | bytes 262176 | tf_op jit(solution)/shard_map/ppermute | solution.py:426
  165.8 5.5 %collective-permute-done.34 = bf16[64,2048]{1,0:T(8,128)(2,1)S(1)} collective-permute-done((bf16[64,2048]{1,0:T(8,128)(2,1)S(1)}, bf16[64,2048]{1,0:T(8,128)(2,1)S(1)}, u32[]{:S(2)}, u32[]{:S(2)}) %collective-permute-start.34) | collective-permute-done | bytes 262176 | tf_op jit(solution)/shard_map/ppermute | solution.py:426
  172.6 4.3 %collective-permute-done.37 = bf16[64,2048]{1,0:T(8,128)(2,1)S(1)} collective-permute-done((bf16[64,2048]{1,0:T(8,128)(2,1)S(1)}, bf16[64,2048]{1,0:T(8,128)(2,1)S(1)}, u32[]{:S(2)}, u32[]{:S(2)}) %collective-permute-start.37) | collective-permute-done | bytes 262176 | tf_op jit(solution)/shard_map/ppermute | solution.py:426
  177.0 4.7 %collective-permute-done.40 = bf16[64,2048]{1,0:T(8,128)(2,1)S(1)} collective-permute-done((bf16[64,2048]{1,0:T(8,128)(2,1)S(1)}, bf16[64,2048]{1,0:T(8,128)(2,1)S(1)}, u32[]{:S(2)}, u32[]{:S(2)}) %collective-permute-start.40) | collective-permute-done | bytes 262176 | tf_op jit(solution)/shard_map/ppermute | solution.py:426
  181.7 7.1 %collective-permute-done.35 = bf16[64,2048]{1,0:T(8,128)(2,1)S(1)} collective-permute-done((bf16[64,2048]{1,0:T(8,128)(2,1)S(1)}, bf16[64,2048]{1,0:T(8,128)(2,1)S(1)}, u32[]{:S(2)}, u32[]{:S(2)}) %collective-permute-start.35) | collective-permute-done | bytes 262176 | tf_op jit(solution)/shard_map/ppermute | solution.py:429
  (109 shorter events, 25.3 us)
Async XLA Ops:
  5.7 29.2 %collective-permute-start.3 = (bf16[144,256]{1,0:T(8,128)(2,1)S(1)}, bf16[144,256]{1,0:T(8,128)(2,1)S(1)}, u32[]{:S(2)}, u32[]{:S(2)}) collective-permute-start(bf16[144,256]{1,0:T(8,128)(2,1)S(1)} %slice.59), channel_id=1, source_target_pairs={{0,2},{2,0},{4,6},{6,4},{8,10},{10,8},{12,14},{14,12},{1,3},{3,1},... | collective-permute-start | bytes 221192 | tf_op jit(solution)/shard_map/ppermute | solution.py:243
  8.7 10.3 %collective-permute-start = (bf16[144,768]{1,0:T(8,128)(2,1)S(1)}, bf16[144,768]{1,0:T(8,128)(2,1)S(1)}, u32[]{:S(2)}, u32[]{:S(2)}) collective-permute-start(bf16[144,768]{1,0:T(8,128)(2,1)S(1)} %get-tuple-element.33), channel_id=1, source_target_pairs={{0,4},{2,6},{4,8},{6,10},{8,12},{10,14},{12,0},{14,2},{1,5},{3,7},... | collective-permute-start | bytes 663560 | tf_op jit(solution)/shard_map/ppermute | solution.py:240
  10.3 16.8 %collective-permute-start.1 = (bf16[144,768]{1,0:T(8,128)(2,1)S(1)}, bf16[144,768]{1,0:T(8,128)(2,1)S(1)}, u32[]{:S(2)}, u32[]{:S(2)}) collective-permute-start(bf16[144,768]{1,0:T(8,128)(2,1)S(1)} %get-tuple-element.34), channel_id=1, source_target_pairs={{0,8},{2,10},{4,12},{6,14},{8,0},{10,2},{12,4},{14,6},{1,9},{3,11}... | collective-permute-start | bytes 663560 | tf_op jit(solution)/shard_map/ppermute | solution.py:240
  12.9 14.2 %collective-permute-start.2 = (bf16[144,768]{1,0:T(8,128)(2,1)S(1)}, bf16[144,768]{1,0:T(8,128)(2,1)S(1)}, u32[]{:S(2)}, u32[]{:S(2)}) collective-permute-start(bf16[144,768]{1,0:T(8,128)(2,1)S(1)} %get-tuple-element.35), channel_id=1, source_target_pairs={{0,12},{2,14},{4,0},{6,2},{8,4},{10,6},{12,8},{14,10},{1,13},{3,15... | collective-permute-start | bytes 663560 | tf_op jit(solution)/shard_map/ppermute | solution.py:240
  19.0 16.5 %collective-permute-start.4 = (bf16[144,256]{1,0:T(8,128)(2,1)S(1)}, bf16[144,256]{1,0:T(8,128)(2,1)S(1)}, u32[]{:S(2)}, u32[]{:S(2)}) collective-permute-start(bf16[144,256]{1,0:T(8,128)(2,1)S(1)} %slice.75), channel_id=1, source_target_pairs={{0,2},{2,0},{4,6},{6,4},{8,10},{10,8},{12,14},{14,12},{1,3},{3,1},... | collective-permute-start | bytes 221192 | tf_op jit(solution)/shard_map/ppermute | solution.py:243
  27.1 13.7 %collective-permute-start.8 = (bf16[256,512]{1,0:T(8,128)(2,1)S(1)}, bf16[256,512]{1,0:T(8,128)(2,1)S(1)}, u32[]{:S(2)}, u32[]{:S(2)}) collective-permute-start(bf16[256,512]{1,0:T(8,128)(2,1)S(1)} %get-tuple-element.41), channel_id=1, source_target_pairs={{0,4},{2,6},{4,8},{6,10},{8,12},{10,14},{12,0},{14,2},{1,5},{3,7},... | collective-permute-start | bytes 786440 | tf_op jit(solution)/shard_map/ppermute | solution.py:248
  32.4 17.5 %collective-permute-start.10 = (bf16[256,512]{1,0:T(8,128)(2,1)S(1)}, bf16[256,512]{1,0:T(8,128)(2,1)S(1)}, u32[]{:S(2)}, u32[]{:S(2)}) collective-permute-start(bf16[256,512]{1,0:T(8,128)(2,1)S(1)} %get-tuple-element.42), channel_id=1, source_target_pairs={{0,8},{2,10},{4,12},{6,14},{8,0},{10,2},{12,4},{14,6},{1,9},{3,11}... | collective-permute-start | bytes 786440 | tf_op jit(solution)/shard_map/ppermute | solution.py:248
  34.0 16.4 %collective-permute-start.12 = (bf16[256,512]{1,0:T(8,128)(2,1)S(1)}, bf16[256,512]{1,0:T(8,128)(2,1)S(1)}, u32[]{:S(2)}, u32[]{:S(2)}) collective-permute-start(bf16[256,512]{1,0:T(8,128)(2,1)S(1)} %get-tuple-element.43), channel_id=1, source_target_pairs={{0,12},{2,14},{4,0},{6,2},{8,4},{10,6},{12,8},{14,10},{1,13},{3,15... | collective-permute-start | bytes 786440 | tf_op jit(solution)/shard_map/ppermute | solution.py:248
  39.4 17.0 %collective-permute-start.7 = (bf16[256,512]{1,0:T(8,128)(2,1)S(1)}, bf16[256,512]{1,0:T(8,128)(2,1)S(1)}, u32[]{:S(2)}, u32[]{:S(2)}) collective-permute-start(bf16[256,512]{1,0:T(8,128)(2,1)S(1)} %get-tuple-element.40.refs_4_), channel_id=1, source_target_pairs={{0,2},{2,0},{4,6},{6,4},{8,10},{10,8},{12,14},{14,12},{1,3},{3,1},... | collective-permute-start | bytes 786440 | tf_op jit(solution)/shard_map/ppermute | solution.py:246
  40.4 16.0 %collective-permute-start.14 = (bf16[128,256]{1,0:T(8,128)(2,1)S(1)}, bf16[128,256]{1,0:T(8,128)(2,1)S(1)}, u32[]{:S(2)}, u32[]{:S(2)}) collective-permute-start(bf16[128,256]{1,0:T(8,128)(2,1)S(1)} %collect_meta.1.mine_ref), channel_id=1, source_target_pairs={{0,1},{1,0},{2,3},{3,2},{4,5},{5,4},{6,7},{7,6},{8,9},{9,8},{10,11... | collective-permute-start | bytes 196616 | tf_op jit(solution)/shard_map/ppermute | solution.py:252
  40.8 19.5 %collective-permute-start.9 = (bf16[256,512]{1,0:T(8,128)(2,1)S(1)}, bf16[256,512]{1,0:T(8,128)(2,1)S(1)}, u32[]{:S(2)}, u32[]{:S(2)}) collective-permute-start(bf16[256,512]{1,0:T(8,128)(2,1)S(1)} %collective-permute-done.8.refs_6_), channel_id=1, source_target_pairs={{0,2},{2,0},{4,6},{6,4},{8,10},{10,8},{12,14},{14,12},{1,3},{3,1},... | collective-permute-start | bytes 786440 | tf_op jit(solution)/shard_map/ppermute | solution.py:249
  49.9 10.4 %collective-permute-start.11 = (bf16[256,512]{1,0:T(8,128)(2,1)S(1)}, bf16[256,512]{1,0:T(8,128)(2,1)S(1)}, u32[]{:S(2)}, u32[]{:S(2)}) collective-permute-start(bf16[256,512]{1,0:T(8,128)(2,1)S(1)} %collective-permute-done.10.refs_8_), channel_id=1, source_target_pairs={{0,2},{2,0},{4,6},{6,4},{8,10},{10,8},{12,14},{14,12},{1,3},{3,1},... | collective-permute-start | bytes 786440 | tf_op jit(solution)/shard_map/ppermute | solution.py:249
  50.4 13.2 %collective-permute-start.13 = (bf16[256,512]{1,0:T(8,128)(2,1)S(1)}, bf16[256,512]{1,0:T(8,128)(2,1)S(1)}, u32[]{:S(2)}, u32[]{:S(2)}) collective-permute-start(bf16[256,512]{1,0:T(8,128)(2,1)S(1)} %collective-permute-done.12.refs_10_), channel_id=1, source_target_pairs={{0,2},{2,0},{4,6},{6,4},{8,10},{10,8},{12,14},{14,12},{1,3},{3,1},... | collective-permute-start | bytes 786440 | tf_op jit(solution)/shard_map/ppermute | solution.py:249
  68.8 14.9 %collective-permute-start.18 = (bf16[64,2048]{1,0:T(8,128)(2,1)S(1)}, bf16[64,2048]{1,0:T(8,128)(2,1)S(1)}, u32[]{:S(2)}, u32[]{:S(2)}) collective-permute-start(bf16[64,2048]{1,0:T(8,128)(2,1)S(1)} %get-tuple-element.61), channel_id=1, source_target_pairs={{0,4},{2,6},{4,8},{6,10},{8,12},{10,14},{12,0},{14,2},{1,5},{3,7},... | collective-permute-start | bytes 786440 | tf_op jit(solution)/shard_map/ppermute | solution.py:265
  73.8 13.7 %collective-permute-start.17 = (bf16[64,2048]{1,0:T(8,128)(2,1)S(1)}, bf16[64,2048]{1,0:T(8,128)(2,1)S(1)}, u32[]{:S(2)}, u32[]{:S(2)}) collective-permute-start(bf16[64,2048]{1,0:T(8,128)(2,1)S(1)} %get-tuple-element.62), channel_id=1, source_target_pairs={{0,12},{2,14},{4,0},{6,2},{8,4},{10,6},{12,8},{14,10},{1,13},{3,15... | collective-permute-start | bytes 786440 | tf_op jit(solution)/shard_map/ppermute | solution.py:265
  76.7 23.4 %collective-permute-start.16 = (bf16[64,2048]{1,0:T(8,128)(2,1)S(1)}, bf16[64,2048]{1,0:T(8,128)(2,1)S(1)}, u32[]{:S(2)}, u32[]{:S(2)}) collective-permute-start(bf16[64,2048]{1,0:T(8,128)(2,1)S(1)} %get-tuple-element.63), channel_id=1, source_target_pairs={{0,8},{2,10},{4,12},{6,14},{8,0},{10,2},{12,4},{14,6},{1,9},{3,11}... | collective-permute-start | bytes 786440 | tf_op jit(solution)/shard_map/ppermute | solution.py:265
  100.2 10.1 %collective-permute-start.20 = (bf16[64,2048]{1,0:T(8,128)(2,1)S(1)}, bf16[64,2048]{1,0:T(8,128)(2,1)S(1)}, u32[]{:S(2)}, u32[]{:S(2)}) collective-permute-start(bf16[64,2048]{1,0:T(8,128)(2,1)S(1)} %get-tuple-element.50), channel_id=1, source_target_pairs={{0,4},{2,6},{4,8},{6,10},{8,12},{10,14},{12,0},{14,2},{1,5},{3,7},... | collective-permute-start | bytes 786440 | tf_op jit(solution)/shard_map/ppermute | solution.py:418
  100.3 10.6 %collective-permute-start.19 = (bf16[64,2048]{1,0:T(8,128)(2,1)S(1)}, bf16[64,2048]{1,0:T(8,128)(2,1)S(1)}, u32[]{:S(2)}, u32[]{:S(2)}) collective-permute-start(bf16[64,2048]{1,0:T(8,128)(2,1)S(1)} %get-tuple-element.50), channel_id=1, source_target_pairs={{0,2},{2,0},{4,6},{6,4},{8,10},{10,8},{12,14},{14,12},{1,3},{3,1},... | collective-permute-start | bytes 786440 | tf_op jit(solution)/shard_map/ppermute | solution.py:419
  110.3 9.2 %collective-permute-start.22 = (bf16[64,2048]{1,0:T(8,128)(2,1)S(1)}, bf16[64,2048]{1,0:T(8,128)(2,1)S(1)}, u32[]{:S(2)}, u32[]{:S(2)}) collective-permute-start(bf16[64,2048]{1,0:T(8,128)(2,1)S(1)} %collective-permute-done.20), channel_id=1, source_target_pairs={{0,4},{2,6},{4,8},{6,10},{8,12},{10,14},{12,0},{14,2},{1,5},{3,7},... | collective-permute-start | bytes 786440 | tf_op jit(solution)/shard_map/ppermute | solution.py:418
  110.3 9.7 %collective-permute-start.21 = (bf16[64,2048]{1,0:T(8,128)(2,1)S(1)}, bf16[64,2048]{1,0:T(8,128)(2,1)S(1)}, u32[]{:S(2)}, u32[]{:S(2)}) collective-permute-start(bf16[64,2048]{1,0:T(8,128)(2,1)S(1)} %collective-permute-done.20), channel_id=1, source_target_pairs={{0,2},{2,0},{4,6},{6,4},{8,10},{10,8},{12,14},{14,12},{1,3},{3,1},... | collective-permute-start | bytes 786440 | tf_op jit(solution)/shard_map/ppermute | solution.py:419
  110.9 23.4 %collective-permute-start.26 = (bf16[128,2048]{1,0:T(8,128)(2,1)S(1)}, bf16[128,2048]{1,0:T(8,128)(2,1)S(1)}, u32[]{:S(2)}, u32[]{:S(2)}) collective-permute-start(bf16[128,2048]{1,0:T(8,128)(2,1)S(1)} %constant_dynamic-update-slice_fusion.refs_0_), channel_id=1, source_target_pairs={{0,1},{1,0},{2,3},{3,2},{4,5},{5,4},{6,7},{7,6},{8,9},{9,8},{10,11... | collective-permute-start | bytes 1572872 | tf_op jit(solution)/shard_map/ppermute | solution.py:420
  119.5 8.3 %collective-permute-start.24 = (bf16[64,2048]{1,0:T(8,128)(2,1)S(1)}, bf16[64,2048]{1,0:T(8,128)(2,1)S(1)}, u32[]{:S(2)}, u32[]{:S(2)}) collective-permute-start(bf16[64,2048]{1,0:T(8,128)(2,1)S(1)} %collective-permute-done.22), channel_id=1, source_target_pairs={{0,4},{2,6},{4,8},{6,10},{8,12},{10,14},{12,0},{14,2},{1,5},{3,7},... | collective-permute-start | bytes 786440 | tf_op jit(solution)/shard_map/ppermute | solution.py:418
  119.5 8.8 %collective-permute-start.23 = (bf16[64,2048]{1,0:T(8,128)(2,1)S(1)}, bf16[64,2048]{1,0:T(8,128)(2,1)S(1)}, u32[]{:S(2)}, u32[]{:S(2)}) collective-permute-start(bf16[64,2048]{1,0:T(8,128)(2,1)S(1)} %collective-permute-done.22), channel_id=1, source_target_pairs={{0,2},{2,0},{4,6},{6,4},{8,10},{10,8},{12,14},{14,12},{1,3},{3,1},... | collective-permute-start | bytes 786440 | tf_op jit(solution)/shard_map/ppermute | solution.py:419
  120.1 14.2 %collective-permute-start.27 = (bf16[128,2048]{1,0:T(8,128)(2,1)S(1)}, bf16[128,2048]{1,0:T(8,128)(2,1)S(1)}, u32[]{:S(2)}, u32[]{:S(2)}) collective-permute-start(bf16[128,2048]{1,0:T(8,128)(2,1)S(1)} %constant_dynamic-update-slice_fusion.2.refs_1_), channel_id=1, source_target_pairs={{0,1},{1,0},{2,3},{3,2},{4,5},{5,4},{6,7},{7,6},{8,9},{9,8},{10,11... | collective-permute-start | bytes 1572872 | tf_op jit(solution)/shard_map/ppermute | solution.py:420
  127.8 6.4 %collective-permute-start.25 = (bf16[64,2048]{1,0:T(8,128)(2,1)S(1)}, bf16[64,2048]{1,0:T(8,128)(2,1)S(1)}, u32[]{:S(2)}, u32[]{:S(2)}) collective-permute-start(bf16[64,2048]{1,0:T(8,128)(2,1)S(1)} %collective-permute-done.24), channel_id=1, source_target_pairs={{0,2},{2,0},{4,6},{6,4},{8,10},{10,8},{12,14},{14,12},{1,3},{3,1},... | collective-permute-start | bytes 786440 | tf_op jit(solution)/shard_map/ppermute | solution.py:419
  156.5 9.2 %collective-permute-start.31 = (bf16[64,2048]{1,0:T(8,128)(2,1)S(1)}, bf16[64,2048]{1,0:T(8,128)(2,1)S(1)}, u32[]{:S(2)}, u32[]{:S(2)}) collective-permute-start(bf16[64,2048]{1,0:T(8,128)(2,1)S(1)} %slice.116), channel_id=1, source_target_pairs={{0,2},{2,0},{4,6},{6,4},{8,10},{10,8},{12,14},{14,12},{1,3},{3,1},... | collective-permute-start | bytes 786440 | tf_op jit(solution)/shard_map/ppermute | solution.py:426
  157.2 14.1 %collective-permute-start.34 = (bf16[64,2048]{1,0:T(8,128)(2,1)S(1)}, bf16[64,2048]{1,0:T(8,128)(2,1)S(1)}, u32[]{:S(2)}, u32[]{:S(2)}) collective-permute-start(bf16[64,2048]{1,0:T(8,128)(2,1)S(1)} %slice.115), channel_id=1, source_target_pairs={{0,2},{2,0},{4,6},{6,4},{8,10},{10,8},{12,14},{14,12},{1,3},{3,1},... | collective-permute-start | bytes 786440 | tf_op jit(solution)/shard_map/ppermute | solution.py:426
  159.0 18.0 %collective-permute-start.37 = (bf16[64,2048]{1,0:T(8,128)(2,1)S(1)}, bf16[64,2048]{1,0:T(8,128)(2,1)S(1)}, u32[]{:S(2)}, u32[]{:S(2)}) collective-permute-start(bf16[64,2048]{1,0:T(8,128)(2,1)S(1)} %slice.114), channel_id=1, source_target_pairs={{0,2},{2,0},{4,6},{6,4},{8,10},{10,8},{12,14},{14,12},{1,3},{3,1},... | collective-permute-start | bytes 786440 | tf_op jit(solution)/shard_map/ppermute | solution.py:426
  159.7 22.0 %collective-permute-start.40 = (bf16[64,2048]{1,0:T(8,128)(2,1)S(1)}, bf16[64,2048]{1,0:T(8,128)(2,1)S(1)}, u32[]{:S(2)}, u32[]{:S(2)}) collective-permute-start(bf16[64,2048]{1,0:T(8,128)(2,1)S(1)} %slice.113), channel_id=1, source_target_pairs={{0,2},{2,0},{4,6},{6,4},{8,10},{10,8},{12,14},{14,12},{1,3},{3,1},... | collective-permute-start | bytes 786440 | tf_op jit(solution)/shard_map/ppermute | solution.py:426
  165.7 16.0 %collective-permute-start.32 = (bf16[64,2048]{1,0:T(8,128)(2,1)S(1)}, bf16[64,2048]{1,0:T(8,128)(2,1)S(1)}, u32[]{:S(2)}, u32[]{:S(2)}) collective-permute-start(bf16[64,2048]{1,0:T(8,128)(2,1)S(1)} %fusion.4), channel_id=1, source_target_pairs={{0,8},{2,10},{4,12},{6,14},{8,0},{10,2},{12,4},{14,6},{1,9},{3,11}... | collective-permute-start | bytes 786440 | tf_op jit(solution)/shard_map/ppermute | solution.py:429
  171.4 17.4 %collective-permute-start.35 = (bf16[64,2048]{1,0:T(8,128)(2,1)S(1)}, bf16[64,2048]{1,0:T(8,128)(2,1)S(1)}, u32[]{:S(2)}, u32[]{:S(2)}) collective-permute-start(bf16[64,2048]{1,0:T(8,128)(2,1)S(1)} %fusion.3), channel_id=1, source_target_pairs={{0,12},{2,14},{4,0},{6,2},{8,4},{10,6},{12,8},{14,10},{1,13},{3,15... | collective-permute-start | bytes 786440 | tf_op jit(solution)/shard_map/ppermute | solution.py:429
  177.0 11.8 %collective-permute-start.38 = (bf16[64,2048]{1,0:T(8,128)(2,1)S(1)}, bf16[64,2048]{1,0:T(8,128)(2,1)S(1)}, u32[]{:S(2)}, u32[]{:S(2)}) collective-permute-start(bf16[64,2048]{1,0:T(8,128)(2,1)S(1)} %fusion.2), channel_id=1, source_target_pairs={{0,4},{2,6},{4,8},{6,10},{8,12},{10,14},{12,0},{14,2},{1,5},{3,7},... | collective-permute-start | bytes 786440 | tf_op jit(solution)/shard_map/ppermute | solution.py:429
  (16 other events, 125.7 us)

commit v5 on v4

--- a/solution.py
+++ b/solution.py
@@ -38,18 +38,18 @@
     return value.astype(jnp.bfloat16)
 
 
-def pack_heads(z, queries, key_rows, value_rows, out_weight, expert_ids, gate_weights, depth):
+def pack_heads(z, queries, key_rows, value_rows, expert_ids, gate_weights, depth):
     rows = queries.shape[0]
     columns = queries.shape[1] // depth
     per_group = queries.shape[1] // key_rows.shape[1] * HD
-    tokens, top = expert_ids.shape
+    top, tokens = expert_ids.shape
     lines = tokens // 4
 
-    def kernel(z_ref, query_ref, key_ref, value_ref, weight_ref, id_ref, gate_ref, *out_refs):
+    def kernel(z_ref, query_ref, key_ref, value_ref, id_ref, gate_ref, *out_refs):
         gates = gate_ref[...]
         high = wide(narrow(gates))
-        blank = jnp.zeros((tokens, HD // 2 - 3 * top), jnp.float32)
-        meta = jnp.concatenate([wide(id_ref[...]), high, gates - high, blank], axis=1)
+        blank = jnp.zeros((HD // 2 - 3 * top, tokens), jnp.float32)
+        meta = jnp.concatenate([wide(id_ref[...]), high, gates - high, blank], axis=0).T
         meta = jnp.concatenate([meta[g * lines : (g + 1) * lines] for g in range(4)], axis=1)
         for d, out_ref in enumerate(out_refs[:depth]):
             start = (z_ref[0] + d) % depth * columns
@@ -59,17 +59,17 @@
             out_ref[:rows, columns + HD :] = value_ref[:, group]
             out_ref[rows:, :columns] = jnp.zeros((lines, columns), jnp.bfloat16)
             out_ref[rows:, columns:] = narrow(meta)
-        out_refs[depth][...] = weight_ref[:, pl.ds(pl.multiple_of(z_ref[0] * columns, HD), columns)]
+        out_refs[depth][...] = out_refs[0][:, columns:]
 
     return pl.pallas_call(
         kernel,
         out_shape=[jax.ShapeDtypeStruct((rows + lines, columns + 2 * HD), queries.dtype)] * depth
-        + [jax.ShapeDtypeStruct((out_weight.shape[0], columns), out_weight.dtype)],
-        in_specs=[smem] + [vmem] * 6,
+        + [jax.ShapeDtypeStruct((rows + lines, 2 * HD), queries.dtype)],
+        in_specs=[smem] + [vmem] * 5,
         out_specs=[vmem] * (depth + 1),
-        compiler_params=limit(16),
+        compiler_params=limit(56),
         name="pack_heads",
-    )(z, queries, key_rows, value_rows, out_weight, expert_ids, gate_weights)
+    )(z, queries, key_rows, value_rows, expert_ids, gate_weights)
 
 
 def pack_weight(z, out_weight, depth, before):
@@ -78,14 +78,14 @@
 
     def kernel(z_ref, weight_ref, *refs):
         for d, out_ref in enumerate(refs[len(before) :]):
-            start = pl.multiple_of((z_ref[0] + d + 1) % depth * columns, HD)
+            start = pl.multiple_of((z_ref[0] + d) % depth * columns, HD)
             out_ref[...] = weight_ref[:, pl.ds(start, columns)]
 
     return pl.pallas_call(
         kernel,
-        out_shape=[jax.ShapeDtypeStruct((rows, columns), out_weight.dtype)] * (depth - 1),
+        out_shape=[jax.ShapeDtypeStruct((rows, columns), out_weight.dtype)] * depth,
         in_specs=[smem, vmem] + [unread] * len(before),
-        out_specs=[vmem] * (depth - 1),
+        out_specs=[vmem] * depth,
         compiler_params=limit(16),
         name="pack_weight",
     )(z, out_weight, *before)
@@ -233,17 +233,15 @@
     steps = far_first(depth)
     here = z.astype(jnp.int32).reshape(1)
 
-    *message, own_weight = pack_heads(
-        here, queries, key_rows, value_rows, out_weight, expert_ids, gate_weights, depth
-    )
+    *message, keyed = pack_heads(here, queries, key_rows, value_rows, expert_ids.T, gate_weights.T, depth)
     for d in steps:
         message[d] = lax.ppermute(message[d], "seq", ring(size, d))
     across = {}
     for d in [0] + steps:
-        across[d] = lax.ppermute(message[d][:, columns:], "seq", swap(size))
+        across[d] = lax.ppermute(message[d][:, columns:] if d else keyed, "seq", swap(size))
     across = [across[d] for d in range(depth)]
-    weight = [own_weight] + list(pack_weight(here, out_weight, depth, [message[d] for d in steps]))
-    weight_across = {0: lax.ppermute(own_weight, "seq", swap(size))}
+    weight = list(pack_weight(here, out_weight, depth, [message[steps[0]]]))
+    weight_across = {0: lax.ppermute(weight[0], "seq", swap(size))}
     for d in steps[::-1]:
         weight[d] = lax.ppermute(weight[d], "seq", ring(size, d))
         weight_across[d] = lax.ppermute(weight[d], "seq", swap(size))
@@ -328,82 +326,78 @@
     tokens, width = mine[0].shape
     local_experts, hidden, _ = expert_out.shape
     slots = select.shape[2]
-
-    def kernel(select_ref, spread_ref, gate_ref, gain_ref, wg_ref, wu_ref, wo_ref, *refs):
+    held = min(local_experts, 2)
+    batch = min(subs, 4)
+    room = 8 * subs * tokens * width + 6 * held * hidden * width + 4 * local_experts * subs * slots * width
+
+    def kernel(select_ref, spread_ref, gate_ref, gain_ref, wi_ref, wo_ref, *refs):
         mine_refs, other_refs = refs[:subs], refs[subs : 2 * subs]
         kept_refs, given_refs = refs[2 * subs : 3 * subs], refs[3 * subs : 4 * subs]
-        xg, res = refs[4 * subs :]
-        expert = pl.program_id(0)
-
-        @pl.when(expert == 0)
-        def _():
-            for s in range(subs):
-                choose = select_ref[:, s].reshape(local_experts * slots, 2 * tokens)
-                picked = jnp.dot(
-                    choose[:, :tokens], mine_refs[s][...], preferred_element_type=jnp.float32
-                ) + jnp.dot(choose[:, tokens:], other_refs[s][...], preferred_element_type=jnp.float32)
-                scale = lax.rsqrt(jnp.sum(picked * picked, axis=1, keepdims=True) * (1.0 / width) + 1e-06)
-                rows = narrow(picked * scale * gain_ref[...])
-                for e in range(local_experts):
-                    xg[e, s * slots : (s + 1) * slots, :] = rows[e * slots : (e + 1) * slots]
-
-        rows = xg[expert]
-        gate = jnp.dot(rows, wg_ref[0], preferred_element_type=jnp.float32)
-        up = jnp.dot(rows, wu_ref[0], preferred_element_type=jnp.float32)
-        act = narrow(gate / (1.0 + jnp.exp(-gate)) * up)
-        part_out = jnp.dot(act, wo_ref[0], preferred_element_type=jnp.float32)
-        scaled = narrow(part_out * gate_ref[expert])
+        first, second, xg, res, sem = refs[4 * subs :]
+
+        def copy(e, part):
+            if part < 2:
+                source, target = wi_ref.at[e, :, part * hidden : (part + 1) * hidden], first.at[e % held, part]
+            else:
+                source, target = wo_ref.at[e], second.at[e % held]
+            return pltpu.make_async_copy(source, target, sem.at[e % held, part])
+
+        def arrive(e, part):
+            copy(e, part).wait()
+            if e + 1 < local_experts:
+                copy(e + 1, part).start()
+
+        for part in range(3):
+            copy(0, part).start()
         for s in range(subs):
-            res[s, expert] = scaled[s * slots : (s + 1) * slots, :]
-
-        @pl.when(expert == pl.num_programs(0) - 1)
-        def _():
-            for s in range(subs):
-                both = narrow(
-                    jnp.dot(spread_ref[s], res[s].reshape(-1, width), preferred_element_type=jnp.float32)
-                )
-                kept_refs[s][...] = both[:tokens]
-                given_refs[s][...] = both[tokens:]
+            choose = select_ref[:, s].reshape(local_experts * slots, 2 * tokens)
+            picked = jnp.dot(
+                choose[:, :tokens], mine_refs[s][...], preferred_element_type=jnp.float32
+            ) + jnp.dot(choose[:, tokens:], other_refs[s][...], preferred_element_type=jnp.float32)
+            scale = lax.rsqrt(jnp.sum(picked * picked, axis=1, keepdims=True) * (1.0 / width) + 1e-06)
+            rows = narrow(picked * scale * gain_ref[...])
+            for e in range(local_experts):
+                xg[e, s * slots : (s + 1) * slots, :] = rows[e * slots : (e + 1) * slots]
+        for e in range(local_experts):
+            for at in range(0, subs, batch):
+                span = slice(at * slots, (at + batch) * slots)
+                rows = xg[e, span, :]
+                if at == 0:
+                    arrive(e, 0)
+                gate = jnp.dot(rows, first[e % held, 0], preferred_element_type=jnp.float32)
+                if at == 0:
+                    arrive(e, 1)
+                up = jnp.dot(rows, first[e % held, 1], preferred_element_type=jnp.float32)
+                act = narrow(gate / (1.0 + jnp.exp(-gate)) * up)
+                if at == 0:
+                    arrive(e, 2)
+                part = jnp.dot(act, second[e % held], preferred_element_type=jnp.float32)
+                scaled = narrow(part * gate_ref[e, span, :])
+                for s in range(batch):
+                    res[at + s, e * slots : (e + 1) * slots, :] = scaled[s * slots : (s + 1) * slots]
+        for s in range(subs):
+            both = narrow(jnp.dot(spread_ref[s], res[s], preferred_element_type=jnp.float32))
+            kept_refs[s][...] = both[:tokens]
+            given_refs[s][...] = both[tokens:]
 
     flops = local_experts * subs * slots * width * hidden * 6
     moved = (expert_in.size + expert_out.size + 8 * subs * tokens * width) * 2
-
-    def whole(shape):
-        return pl.BlockSpec(shape, lambda e: (0,) * len(shape), pipeline_mode=pl.Buffered(1))
-
     outs = pl.pallas_call(
         kernel,
-        grid=(local_experts,),
         out_shape=[jax.ShapeDtypeStruct((tokens, width), jnp.bfloat16)] * (2 * subs),
-        in_specs=[
-            whole(select.shape),
-            whole(spread.shape),
-            whole(row_gate.shape),
-            whole((1, width)),
-            pl.BlockSpec((1, width, hidden), lambda e: (e, 0, 0)),
-            pl.BlockSpec((1, width, hidden), lambda e: (e, 0, 1)),
-            pl.BlockSpec((1, hidden, width), lambda e: (e, 0, 0)),
-        ]
-        + [whole((tokens, width))] * (2 * subs),
-        out_specs=[whole((tokens, width))] * (2 * subs),
+        in_specs=[vmem] * 4 + [unread] * 2 + [vmem] * (2 * subs),
+        out_specs=[vmem] * (2 * subs),
         scratch_shapes=[
+            pltpu.VMEM((held, 2, width, hidden), jnp.bfloat16),
+            pltpu.VMEM((held, hidden, width), jnp.bfloat16),
             pltpu.VMEM((local_experts, subs * slots, width), jnp.bfloat16),
-            pltpu.VMEM((subs, local_experts, slots, width), jnp.bfloat16),
+            pltpu.VMEM((subs, local_experts * slots, width), jnp.bfloat16),
+            pltpu.SemaphoreType.DMA((held, 3)),
         ],
-        compiler_params=limit(34),
+        compiler_params=limit(room * 9 // 8 // 2**20),
         cost_estimate=pl.CostEstimate(flops=flops, bytes_accessed=moved, transcendentals=0),
         name="experts",
-    )(
-        select,
-        spread,
-        row_gate,
-        norm_gain.reshape(1, -1),
-        expert_in,
-        expert_in,
-        expert_out,
-        *mine,
-        *other,
-    )
+    )(select, spread, row_gate, norm_gain.reshape(1, -1), expert_in, expert_out, *mine, *other)
     return outs[:subs], outs[subs:]
 
 

time: 190 us -> 182 us (0.958)
  starting transfers between devices: 40.4 us -> 35.1 us
  local copies, waits for them, and re-layouts: 6.06 us -> 2.73 us
    ppermute x3, starting transfers between devices: 8.36 us -> 4.43 us  [attention_block(): parts.append(lax.ppermute(narrow(chip[d]), 'seq', ring(size, -d)))]
    unnamed x20 -> x14, local copies, waits for them, and re-layouts: 5.57 us -> 2.25 us
    pallas_call x1, Pallas kernels: 0.17 us -> 2.18 us  [pack_heads(): pl.pallas_call(kernel, out_shape=[jax.ShapeDtypeStruct((rows + lines, col...]
  transfers between devices with their start and end apart: 41 -> 41, of which waited for: 21 -> 21; matrix products, arithmetic and copies ran while one was open for 1% -> 1% of each run, Pallas kernels for 4% -> 5%
where the time goes in v5:
time: 182 us
  waiting for transfers between devices  112 us (62%)
  starting transfers between devices  35.1 us (19%)
  Pallas kernels  28.9 us (16%)
  local copies, waits for them, and re-layouts  2.73 us (2%)
  other arithmetic  2.2 us (1%)
    ppermute x3, waiting for transfers between devices, expert_block(): along.append(lax.ppermute(along[d], 'seq', ring(size, 1)))  25.5 us
    ppermute x3, waiting for transfers between devices, attention_block(): parts.append(lax.ppermute(narrow(chip[d]), 'seq', ring(size, -d)))  22.6 us
    ppermute x4, waiting for transfers between devices, expert_block(): there = lax.ppermute(narrow(pair[rows:]), 'seq', swap(size))  18.9 us
    pallas_call x1, Pallas kernels, run_experts(): pl.pallas_call(kernel, out_shape=[jax.ShapeDtypeStruct((tokens, width), j...  16.3 us
    ppermute x3, waiting for transfers between devices, attention_block(): message[d] = lax.ppermute(message[d], 'seq', ring(size, d))  12.4 us
    ppermute x3, waiting for transfers between devices, attention_block(): weight[d] = lax.ppermute(weight[d], 'seq', ring(size, d))  7.58 us
    ppermute x3, waiting for transfers between devices, expert_block(): chip = wide(lax.ppermute(narrow(chip), 'seq', ring(size, -d)))  7.08 us
    ppermute x3, starting transfers between devices, attention_block(): weight[d] = lax.ppermute(weight[d], 'seq', ring(size, d))  6.87 us
  transfers between devices with their start and end apart: 41, of which 21 were waited for; matrix products, arithmetic and copies ran while one was open for 1% of the time, Pallas kernels for 5%

profile of v5, /device:TPU:0, one launch (start us, length us, event | category | flops | bytes accessed | tf_op | source)
XLA Modules:
  0.0 181.5 jit_solution(8862123077697300855)
XLA Ops:
  0.0 2.2 %pack_heads.1 = (bf16[144,768]{1,0:T(8,128)(2,1)}, bf16[144,768]{1,0:T(8,128)(2,1)}, bf16[144,768]{1,0:T(8,128)(2,1)}, bf16[144,768]{1,0:T(8,128)(2,1)}, bf16[144,256]{1,0:T(8,128)(2,1)}) custom-call(s32[1]{0:T(128)} %bitcast.5.z_ref, bf16[128,2048]{1,0:T(8,128)(2,1)} %query_ref.1, bf16[128,256]{1,0:T(8,128)(2,1)} %key_ref.1, bf16[128,256]{1,0:T(8,128)(2,1)} %value_ref.1, ...), custom_call_target="tpu_custom_call" | custom-call | tf_op jit(solution)/shard_map/pack_heads/pallas_call | solution.py:64
  2.2 3.0 %collective-permute-start.3 = (bf16[144,256]{1,0:T(8,128)(2,1)}, bf16[144,256]{1,0:T(8,128)(2,1)S(1)}, u32[]{:S(2)}, u32[]{:S(2)}) collective-permute-start(bf16[144,256]{1,0:T(8,128)(2,1)} %get-tuple-element.37), channel_id=1, source_target_pairs={{0,2},{2,0},{4,6},{6,4},{8,10},{10,8},{12,14},{14,12},{1,3},{3,1},... | collective-permute-start | bytes 221192 | tf_op jit(solution)/shard_map/ppermute | solution.py:241
  5.2 1.6 collective-permute-start
  6.7 2.6 %collective-permute-start.1 = (bf16[144,768]{1,0:T(8,128)(2,1)}, bf16[144,768]{1,0:T(8,128)(2,1)S(1)}, u32[]{:S(2)}, u32[]{:S(2)}) collective-permute-start(bf16[144,768]{1,0:T(8,128)(2,1)} %get-tuple-element.35), channel_id=1, source_target_pairs={{0,8},{2,10},{4,12},{6,14},{8,0},{10,2},{12,4},{14,6},{1,9},{3,11}... | collective-permute-start | bytes 663560 | tf_op jit(solution)/shard_map/ppermute | solution.py:238
  11.0 4.6 %collective-permute-done.refs_1_.refs_2_ = bf16[144,768]{1,0:T(8,128)(2,1)S(1)} collective-permute-done((bf16[144,768]{1,0:T(8,128)(2,1)}, bf16[144,768]{1,0:T(8,128)(2,1)S(1)}, u32[]{:S(2)}, u32[]{:S(2)}) %collective-permute-start) | collective-permute-done | bytes 221216 | tf_op jit(solution)/shard_map/ppermute | solution.py:238
  15.9 7.8 %collective-permute-done.1.refs_2_.refs_0_.refs_4_ = bf16[144,768]{1,0:T(8,128)(2,1)S(1)} collective-permute-done((bf16[144,768]{1,0:T(8,128)(2,1)}, bf16[144,768]{1,0:T(8,128)(2,1)S(1)}, u32[]{:S(2)}, u32[]{:S(2)}) %collective-permute-start.1) | collective-permute-done | bytes 221216 | tf_op jit(solution)/shard_map/ppermute | solution.py:238
  25.0 3.6 %collective-permute-start.8 = (bf16[256,512]{1,0:T(8,128)(2,1)S(1)}, bf16[256,512]{1,0:T(8,128)(2,1)S(1)}, u32[]{:S(2)}, u32[]{:S(2)}) collective-permute-start(bf16[256,512]{1,0:T(8,128)(2,1)S(1)} %get-tuple-element.43), channel_id=1, source_target_pairs={{0,4},{2,6},{4,8},{6,10},{8,12},{10,14},{12,0},{14,2},{1,5},{3,7},... | collective-permute-start | bytes 786440 | tf_op jit(solution)/shard_map/ppermute | solution.py:246
  28.6 3.3 %collective-permute-start.10 = (bf16[256,512]{1,0:T(8,128)(2,1)S(1)}, bf16[256,512]{1,0:T(8,128)(2,1)S(1)}, u32[]{:S(2)}, u32[]{:S(2)}) collective-permute-start(bf16[256,512]{1,0:T(8,128)(2,1)S(1)} %get-tuple-element.44), channel_id=1, source_target_pairs={{0,8},{2,10},{4,12},{6,14},{8,0},{10,2},{12,4},{14,6},{1,9},{3,11}... | collective-permute-start | bytes 786440 | tf_op jit(solution)/shard_map/ppermute | solution.py:246
  34.1 2.5 %collective-permute-done.5.refs_6_.refs_5_ = bf16[144,256]{1,0:T(8,128)(2,1)S(1)} collective-permute-done((bf16[144,256]{1,0:T(8,128)(2,1)S(1)}, bf16[144,256]{1,0:T(8,128)(2,1)S(1)}, u32[]{:S(2)}, u32[]{:S(2)}) %collective-permute-start.5) | collective-permute-done | bytes 73760 | tf_op jit(solution)/shard_map/ppermute | solution.py:241
  40.2 7.6 %collective-permute-done.10.refs_8_ = bf16[256,512]{1,0:T(8,128)(2,1)S(1)} collective-permute-done((bf16[256,512]{1,0:T(8,128)(2,1)S(1)}, bf16[256,512]{1,0:T(8,128)(2,1)S(1)}, u32[]{:S(2)}, u32[]{:S(2)}) %collective-permute-start.10) | collective-permute-done | bytes 262176 | tf_op jit(solution)/shard_map/ppermute | solution.py:246
  49.8 4.4 %attend.1 = (bf16[128,512]{1,0:T(8,128)(2,1)S(1)}, bf16[128,512]{1,0:T(8,128)(2,1)S(1)}, bf16[128,512]{1,0:T(8,128)(2,1)S(1)}, bf16[128,512]{1,0:T(8,128)(2,1)S(1)}) custom-call(s32[1]{0:T(128)} %bitcast.2.core_ref, s32[4]{0:T(128)S(1)} %multiply_bitcast_fusion.starts_ref, s32[1,1024]{1,0:T(1,128)S(1)} %bitcast.20, bf16[144,768]{1,0:T(8,128)(2,1)S(1)} %copy-done.3, ...), custom_call_target="tpu_custom_call" | custom-call | flops 42949672960 | bytes 2097152 | tf_op jit(solution)/shard_map/attend/pallas_call | solution.py:146
  54.3 3.9 %routing.1 = (bf16[4,4,48,256]{3,2,1,0:T(8,128)(2,1)S(1)}, bf16[4,256,192]{2,1,0:T(8,128)(2,1)S(1)}, f32[4,192,1]{2,1,0:T(8,128)S(1)}) custom-call(s32[1]{0:T(128)} %bitcast.8.first_ref, bf16[128,256]{1,0:T(8,128)(2,1)S(1)} %collect_meta.1.mine_ref, bf16[128,256]{1,0:T(8,128)(2,1)S(1)} %collective-permute-done.14.other_ref, ...), custom_call_target="tpu_custom_call" | custom-call | tf_op jit(solution)/shard_map/routing/pallas_call | solution.py:310
  58.2 3.4 %collective-permute-done.13.refs_11_ = bf16[256,512]{1,0:T(8,128)(2,1)S(1)} collective-permute-done((bf16[256,512]{1,0:T(8,128)(2,1)S(1)}, bf16[256,512]{1,0:T(8,128)(2,1)S(1)}, u32[]{:S(2)}, u32[]{:S(2)}) %collective-permute-start.13) | collective-permute-done | bytes 262176 | tf_op jit(solution)/shard_map/ppermute | solution.py:247
  61.6 1.9 %project.1 = (bf16[4,64,2048]{2,1,0:T(8,128)(2,1)S(1)}, bf16[4,64,2048]{2,1,0:T(8,128)(2,1)S(1)}) custom-call(s32[8]{0:T(128)S(1)} %add.107.place_ref, bf16[128,512]{1,0:T(8,128)(2,1)S(1)} %get-tuple-element.38.refs_0_, bf16[128,512]{1,0:T(8,128)(2,1)S(1)} %get-tuple-element.39.refs_1_, bf16[128,512]{1,0:T(8,128)(2,1)S(1)} %get-tuple-element.40.refs_2_, ...), custom_call_target="tpu_custom_call" | custom-call | flops 1073741824 | bytes 6815744 | tf_op jit(solution)/shard_map/project/pallas_call | solution.py:189
  63.5 2.6 %collective-permute-done.15 = bf16[4,64,2048]{2,1,0:T(8,128)(2,1)S(1)} collective-permute-done((bf16[4,64,2048]{2,1,0:T(8,128)(2,1)S(1)}, bf16[4,64,2048]{2,1,0:T(8,128)(2,1)S(1)}, u32[]{:S(2)}, u32[]{:S(2)}) %collective-permute-start.15) | collective-permute-done | bytes 1048608 | tf_op jit(solution)/shard_map/ppermute | solution.py:260
  66.7 2.7 %collective-permute-start.18 = (bf16[64,2048]{1,0:T(8,128)(2,1)S(1)}, bf16[64,2048]{1,0:T(8,128)(2,1)S(1)}, u32[]{:S(2)}, u32[]{:S(2)}) collective-permute-start(bf16[64,2048]{1,0:T(8,128)(2,1)S(1)} %get-tuple-element.63), channel_id=1, source_target_pairs={{0,4},{2,6},{4,8},{6,10},{8,12},{10,14},{12,0},{14,2},{1,5},{3,7},... | collective-permute-start | bytes 786440 | tf_op jit(solution)/shard_map/ppermute | solution.py:263
  71.2 6.6 %collective-permute-done.18.refs_4_ = bf16[64,2048]{1,0:T(8,128)(2,1)S(1)} collective-permute-done((bf16[64,2048]{1,0:T(8,128)(2,1)S(1)}, bf16[64,2048]{1,0:T(8,128)(2,1)S(1)}, u32[]{:S(2)}, u32[]{:S(2)}) %collective-permute-start.18) | collective-permute-done | bytes 262176 | tf_op jit(solution)/shard_map/ppermute | solution.py:263
  77.7 4.8 %collective-permute-done.17.refs_3_ = bf16[64,2048]{1,0:T(8,128)(2,1)S(1)} collective-permute-done((bf16[64,2048]{1,0:T(8,128)(2,1)S(1)}, bf16[64,2048]{1,0:T(8,128)(2,1)S(1)}, u32[]{:S(2)}, u32[]{:S(2)}) %collective-permute-start.17) | collective-permute-done | bytes 262176 | tf_op jit(solution)/shard_map/ppermute | solution.py:263
  82.5 11.2 %collective-permute-done.16.refs_2_ = bf16[64,2048]{1,0:T(8,128)(2,1)S(1)} collective-permute-done((bf16[64,2048]{1,0:T(8,128)(2,1)S(1)}, bf16[64,2048]{1,0:T(8,128)(2,1)S(1)}, u32[]{:S(2)}, u32[]{:S(2)}) %collective-permute-start.16) | collective-permute-done | bytes 262176 | tf_op jit(solution)/shard_map/ppermute | solution.py:263
  94.6 9.4 %collective-permute-done.20 = bf16[64,2048]{1,0:T(8,128)(2,1)S(1)} collective-permute-done((bf16[64,2048]{1,0:T(8,128)(2,1)S(1)}, bf16[64,2048]{1,0:T(8,128)(2,1)S(1)}, u32[]{:S(2)}, u32[]{:S(2)}) %collective-permute-start.20) | collective-permute-done | bytes 262176 | tf_op jit(solution)/shard_map/ppermute | solution.py:412
  104.7 8.5 %collective-permute-done.22 = bf16[64,2048]{1,0:T(8,128)(2,1)S(1)} collective-permute-done((bf16[64,2048]{1,0:T(8,128)(2,1)S(1)}, bf16[64,2048]{1,0:T(8,128)(2,1)S(1)}, u32[]{:S(2)}, u32[]{:S(2)}) %collective-permute-start.22) | collective-permute-done | bytes 262176 | tf_op jit(solution)/shard_map/ppermute | solution.py:412
  113.9 7.6 %collective-permute-done.24 = bf16[64,2048]{1,0:T(8,128)(2,1)S(1)} collective-permute-done((bf16[64,2048]{1,0:T(8,128)(2,1)S(1)}, bf16[64,2048]{1,0:T(8,128)(2,1)S(1)}, u32[]{:S(2)}, u32[]{:S(2)}) %collective-permute-start.24) | collective-permute-done | bytes 262176 | tf_op jit(solution)/shard_map/ppermute | solution.py:412
  122.1 5.7 %collective-permute-done.25 = bf16[64,2048]{1,0:T(8,128)(2,1)S(1)} collective-permute-done((bf16[64,2048]{1,0:T(8,128)(2,1)S(1)}, bf16[64,2048]{1,0:T(8,128)(2,1)S(1)}, u32[]{:S(2)}, u32[]{:S(2)}) %collective-permute-start.25) | collective-permute-done | bytes 262176 | tf_op jit(solution)/shard_map/ppermute | solution.py:413
  128.0 1.9 %collective-permute-done.29.refs_7_ = bf16[128,2048]{1,0:T(8,128)(2,1)S(1)} collective-permute-done((bf16[128,2048]{1,0:T(8,128)(2,1)S(1)}, bf16[128,2048]{1,0:T(8,128)(2,1)S(1)}, u32[]{:S(2)}, u32[]{:S(2)}) %collective-permute-start.29) | collective-permute-done | bytes 524320 | tf_op jit(solution)/shard_map/ppermute | solution.py:414
  129.8 16.3 %experts.1 = (bf16[128,2048]{1,0:T(8,128)(2,1)S(1)}, bf16[128,2048]{1,0:T(8,128)(2,1)S(1)}, bf16[128,2048]{1,0:T(8,128)(2,1)S(1)}, bf16[128,2048]{1,0:T(8,128)(2...) custom-call(bf16[4,4,48,256]{3,2,1,0:T(8,128)(2,1)S(1)} %get-tuple-e, ...), custom_call_target="tpu_custom_call" | custom-call | flops 7247757312 | bytes 54525952 | tf_op jit(solution)/shard_map/experts/pallas_call | solution.py:385
  149.0 1.5 collective-permute-start.34
  151.5 1.5 collective-permute-start.40
  153.1 4.4 %collective-permute-done.31 = bf16[64,2048]{1,0:T(8,128)(2,1)S(1)} collective-permute-done((bf16[64,2048]{1,0:T(8,128)(2,1)S(1)}, bf16[64,2048]{1,0:T(8,128)(2,1)S(1)}, u32[]{:S(2)}, u32[]{:S(2)}) %collective-permute-start.31) | collective-permute-done | bytes 262176 | tf_op jit(solution)/shard_map/ppermute | solution.py:420
  157.6 5.5 %collective-permute-done.34 = bf16[64,2048]{1,0:T(8,128)(2,1)S(1)} collective-permute-done((bf16[64,2048]{1,0:T(8,128)(2,1)S(1)}, bf16[64,2048]{1,0:T(8,128)(2,1)S(1)}, u32[]{:S(2)}, u32[]{:S(2)}) %collective-permute-start.34) | collective-permute-done | bytes 262176 | tf_op jit(solution)/shard_map/ppermute | solution.py:420
  164.4 4.3 %collective-permute-done.37 = bf16[64,2048]{1,0:T(8,128)(2,1)S(1)} collective-permute-done((bf16[64,2048]{1,0:T(8,128)(2,1)S(1)}, bf16[64,2048]{1,0:T(8,128)(2,1)S(1)}, u32[]{:S(2)}, u32[]{:S(2)}) %collective-permute-start.37) | collective-permute-done | bytes 262176 | tf_op jit(solution)/shard_map/ppermute | solution.py:420
  168.8 4.7 %collective-permute-done.40 = bf16[64,2048]{1,0:T(8,128)(2,1)S(1)} collective-permute-done((bf16[64,2048]{1,0:T(8,128)(2,1)S(1)}, bf16[64,2048]{1,0:T(8,128)(2,1)S(1)}, u32[]{:S(2)}, u32[]{:S(2)}) %collective-permute-start.40) | collective-permute-done | bytes 262176 | tf_op jit(solution)/shard_map/ppermute | solution.py:420
  173.5 7.1 %collective-permute-done.35 = bf16[64,2048]{1,0:T(8,128)(2,1)S(1)} collective-permute-done((bf16[64,2048]{1,0:T(8,128)(2,1)S(1)}, bf16[64,2048]{1,0:T(8,128)(2,1)S(1)}, u32[]{:S(2)}, u32[]{:S(2)}) %collective-permute-start.35) | collective-permute-done | bytes 262176 | tf_op jit(solution)/shard_map/ppermute | solution.py:423
  (102 shorter events, 22.5 us)
Async XLA Ops:
  2.2 29.8 %collective-permute-start.3 = (bf16[144,256]{1,0:T(8,128)(2,1)}, bf16[144,256]{1,0:T(8,128)(2,1)S(1)}, u32[]{:S(2)}, u32[]{:S(2)}) collective-permute-start(bf16[144,256]{1,0:T(8,128)(2,1)} %get-tuple-element.37), channel_id=1, source_target_pairs={{0,2},{2,0},{4,6},{6,4},{8,10},{10,8},{12,14},{14,12},{1,3},{3,1},... | collective-permute-start | bytes 221192 | tf_op jit(solution)/shard_map/ppermute | solution.py:241
  5.2 10.5 %collective-permute-start = (bf16[144,768]{1,0:T(8,128)(2,1)}, bf16[144,768]{1,0:T(8,128)(2,1)S(1)}, u32[]{:S(2)}, u32[]{:S(2)}) collective-permute-start(bf16[144,768]{1,0:T(8,128)(2,1)} %get-tuple-element.34), channel_id=1, source_target_pairs={{0,4},{2,6},{4,8},{6,10},{8,12},{10,14},{12,0},{14,2},{1,5},{3,7},... | collective-permute-start | bytes 663560 | tf_op jit(solution)/shard_map/ppermute | solution.py:238
  6.7 17.0 %collective-permute-start.1 = (bf16[144,768]{1,0:T(8,128)(2,1)}, bf16[144,768]{1,0:T(8,128)(2,1)S(1)}, u32[]{:S(2)}, u32[]{:S(2)}) collective-permute-start(bf16[144,768]{1,0:T(8,128)(2,1)} %get-tuple-element.35), channel_id=1, source_target_pairs={{0,8},{2,10},{4,12},{6,14},{8,0},{10,2},{12,4},{14,6},{1,9},{3,11}... | collective-permute-start | bytes 663560 | tf_op jit(solution)/shard_map/ppermute | solution.py:238
  9.3 22.6 %collective-permute-start.2 = (bf16[144,768]{1,0:T(8,128)(2,1)}, bf16[144,768]{1,0:T(8,128)(2,1)S(1)}, u32[]{:S(2)}, u32[]{:S(2)}) collective-permute-start(bf16[144,768]{1,0:T(8,128)(2,1)} %get-tuple-element.36), channel_id=1, source_target_pairs={{0,12},{2,14},{4,0},{6,2},{8,4},{10,6},{12,8},{14,10},{1,13},{3,15... | collective-permute-start | bytes 663560 | tf_op jit(solution)/shard_map/ppermute | solution.py:238
  15.6 16.9 %collective-permute-start.4 = (bf16[144,256]{1,0:T(8,128)(2,1)S(1)}, bf16[144,256]{1,0:T(8,128)(2,1)S(1)}, u32[]{:S(2)}, u32[]{:S(2)}) collective-permute-start(bf16[144,256]{1,0:T(8,128)(2,1)S(1)} %slice.71), channel_id=1, source_target_pairs={{0,2},{2,0},{4,6},{6,4},{8,10},{10,8},{12,14},{14,12},{1,3},{3,1},... | collective-permute-start | bytes 221192 | tf_op jit(solution)/shard_map/ppermute | solution.py:241
  25.0 14.2 %collective-permute-start.8 = (bf16[256,512]{1,0:T(8,128)(2,1)S(1)}, bf16[256,512]{1,0:T(8,128)(2,1)S(1)}, u32[]{:S(2)}, u32[]{:S(2)}) collective-permute-start(bf16[256,512]{1,0:T(8,128)(2,1)S(1)} %get-tuple-element.43), channel_id=1, source_target_pairs={{0,4},{2,6},{4,8},{6,10},{8,12},{10,14},{12,0},{14,2},{1,5},{3,7},... | collective-permute-start | bytes 786440 | tf_op jit(solution)/shard_map/ppermute | solution.py:246
  28.6 19.2 %collective-permute-start.10 = (bf16[256,512]{1,0:T(8,128)(2,1)S(1)}, bf16[256,512]{1,0:T(8,128)(2,1)S(1)}, u32[]{:S(2)}, u32[]{:S(2)}) collective-permute-start(bf16[256,512]{1,0:T(8,128)(2,1)S(1)} %get-tuple-element.44), channel_id=1, source_target_pairs={{0,8},{2,10},{4,12},{6,14},{8,0},{10,2},{12,4},{14,6},{1,9},{3,11}... | collective-permute-start | bytes 786440 | tf_op jit(solution)/shard_map/ppermute | solution.py:246
  31.9 16.4 %collective-permute-start.12 = (bf16[256,512]{1,0:T(8,128)(2,1)S(1)}, bf16[256,512]{1,0:T(8,128)(2,1)S(1)}, u32[]{:S(2)}, u32[]{:S(2)}) collective-permute-start(bf16[256,512]{1,0:T(8,128)(2,1)S(1)} %get-tuple-element.45), channel_id=1, source_target_pairs={{0,12},{2,14},{4,0},{6,2},{8,4},{10,6},{12,8},{14,10},{1,13},{3,15... | collective-permute-start | bytes 786440 | tf_op jit(solution)/shard_map/ppermute | solution.py:246
  36.6 17.7 %collective-permute-start.7 = (bf16[256,512]{1,0:T(8,128)(2,1)S(1)}, bf16[256,512]{1,0:T(8,128)(2,1)S(1)}, u32[]{:S(2)}, u32[]{:S(2)}) collective-permute-start(bf16[256,512]{1,0:T(8,128)(2,1)S(1)} %get-tuple-element.42.refs_4_), channel_id=1, source_target_pairs={{0,2},{2,0},{4,6},{6,4},{8,10},{10,8},{12,14},{14,12},{1,3},{3,1},... | collective-permute-start | bytes 786440 | tf_op jit(solution)/shard_map/ppermute | solution.py:244
  39.2 15.1 %collective-permute-start.14 = (bf16[128,256]{1,0:T(8,128)(2,1)S(1)}, bf16[128,256]{1,0:T(8,128)(2,1)S(1)}, u32[]{:S(2)}, u32[]{:S(2)}) collective-permute-start(bf16[128,256]{1,0:T(8,128)(2,1)S(1)} %collect_meta.1.mine_ref), channel_id=1, source_target_pairs={{0,1},{1,0},{2,3},{3,2},{4,5},{5,4},{6,7},{7,6},{8,9},{9,8},{10,11... | collective-permute-start | bytes 196616 | tf_op jit(solution)/shard_map/ppermute | solution.py:250
  39.2 19.0 %collective-permute-start.9 = (bf16[256,512]{1,0:T(8,128)(2,1)S(1)}, bf16[256,512]{1,0:T(8,128)(2,1)S(1)}, u32[]{:S(2)}, u32[]{:S(2)}) collective-permute-start(bf16[256,512]{1,0:T(8,128)(2,1)S(1)} %collective-permute-done.8.refs_6_), channel_id=1, source_target_pairs={{0,2},{2,0},{4,6},{6,4},{8,10},{10,8},{12,14},{14,12},{1,3},{3,1},... | collective-permute-start | bytes 786440 | tf_op jit(solution)/shard_map/ppermute | solution.py:247
  47.8 10.4 %collective-permute-start.11 = (bf16[256,512]{1,0:T(8,128)(2,1)S(1)}, bf16[256,512]{1,0:T(8,128)(2,1)S(1)}, u32[]{:S(2)}, u32[]{:S(2)}) collective-permute-start(bf16[256,512]{1,0:T(8,128)(2,1)S(1)} %collective-permute-done.10.refs_8_), channel_id=1, source_target_pairs={{0,2},{2,0},{4,6},{6,4},{8,10},{10,8},{12,14},{14,12},{1,3},{3,1},... | collective-permute-start | bytes 786440 | tf_op jit(solution)/shard_map/ppermute | solution.py:247
  48.3 13.2 %collective-permute-start.13 = (bf16[256,512]{1,0:T(8,128)(2,1)S(1)}, bf16[256,512]{1,0:T(8,128)(2,1)S(1)}, u32[]{:S(2)}, u32[]{:S(2)}) collective-permute-start(bf16[256,512]{1,0:T(8,128)(2,1)S(1)} %collective-permute-done.12.refs_10_), channel_id=1, source_target_pairs={{0,2},{2,0},{4,6},{6,4},{8,10},{10,8},{12,14},{14,12},{1,3},{3,1},... | collective-permute-start | bytes 786440 | tf_op jit(solution)/shard_map/ppermute | solution.py:247
  66.7 11.0 %collective-permute-start.18 = (bf16[64,2048]{1,0:T(8,128)(2,1)S(1)}, bf16[64,2048]{1,0:T(8,128)(2,1)S(1)}, u32[]{:S(2)}, u32[]{:S(2)}) collective-permute-start(bf16[64,2048]{1,0:T(8,128)(2,1)S(1)} %get-tuple-element.63), channel_id=1, source_target_pairs={{0,4},{2,6},{4,8},{6,10},{8,12},{10,14},{12,0},{14,2},{1,5},{3,7},... | collective-permute-start | bytes 786440 | tf_op jit(solution)/shard_map/ppermute | solution.py:263
  69.4 13.1 %collective-permute-start.17 = (bf16[64,2048]{1,0:T(8,128)(2,1)S(1)}, bf16[64,2048]{1,0:T(8,128)(2,1)S(1)}, u32[]{:S(2)}, u32[]{:S(2)}) collective-permute-start(bf16[64,2048]{1,0:T(8,128)(2,1)S(1)} %get-tuple-element.64), channel_id=1, source_target_pairs={{0,12},{2,14},{4,0},{6,2},{8,4},{10,6},{12,8},{14,10},{1,13},{3,15... | collective-permute-start | bytes 786440 | tf_op jit(solution)/shard_map/ppermute | solution.py:263
  70.6 23.2 %collective-permute-start.16 = (bf16[64,2048]{1,0:T(8,128)(2,1)S(1)}, bf16[64,2048]{1,0:T(8,128)(2,1)S(1)}, u32[]{:S(2)}, u32[]{:S(2)}) collective-permute-start(bf16[64,2048]{1,0:T(8,128)(2,1)S(1)} %get-tuple-element.65), channel_id=1, source_target_pairs={{0,8},{2,10},{4,12},{6,14},{8,0},{10,2},{12,4},{14,6},{1,9},{3,11}... | collective-permute-start | bytes 786440 | tf_op jit(solution)/shard_map/ppermute | solution.py:263
  93.9 10.1 %collective-permute-start.20 = (bf16[64,2048]{1,0:T(8,128)(2,1)S(1)}, bf16[64,2048]{1,0:T(8,128)(2,1)S(1)}, u32[]{:S(2)}, u32[]{:S(2)}) collective-permute-start(bf16[64,2048]{1,0:T(8,128)(2,1)S(1)} %get-tuple-element.52), channel_id=1, source_target_pairs={{0,4},{2,6},{4,8},{6,10},{8,12},{10,14},{12,0},{14,2},{1,5},{3,7},... | collective-permute-start | bytes 786440 | tf_op jit(solution)/shard_map/ppermute | solution.py:412
  94.0 10.5 %collective-permute-start.19 = (bf16[64,2048]{1,0:T(8,128)(2,1)S(1)}, bf16[64,2048]{1,0:T(8,128)(2,1)S(1)}, u32[]{:S(2)}, u32[]{:S(2)}) collective-permute-start(bf16[64,2048]{1,0:T(8,128)(2,1)S(1)} %get-tuple-element.52), channel_id=1, source_target_pairs={{0,2},{2,0},{4,6},{6,4},{8,10},{10,8},{12,14},{14,12},{1,3},{3,1},... | collective-permute-start | bytes 786440 | tf_op jit(solution)/shard_map/ppermute | solution.py:413
  104.0 9.2 %collective-permute-start.22 = (bf16[64,2048]{1,0:T(8,128)(2,1)S(1)}, bf16[64,2048]{1,0:T(8,128)(2,1)S(1)}, u32[]{:S(2)}, u32[]{:S(2)}) collective-permute-start(bf16[64,2048]{1,0:T(8,128)(2,1)S(1)} %collective-permute-done.20), channel_id=1, source_target_pairs={{0,4},{2,6},{4,8},{6,10},{8,12},{10,14},{12,0},{14,2},{1,5},{3,7},... | collective-permute-start | bytes 786440 | tf_op jit(solution)/shard_map/ppermute | solution.py:412
  104.0 9.7 %collective-permute-start.21 = (bf16[64,2048]{1,0:T(8,128)(2,1)S(1)}, bf16[64,2048]{1,0:T(8,128)(2,1)S(1)}, u32[]{:S(2)}, u32[]{:S(2)}) collective-permute-start(bf16[64,2048]{1,0:T(8,128)(2,1)S(1)} %collective-permute-done.20), channel_id=1, source_target_pairs={{0,2},{2,0},{4,6},{6,4},{8,10},{10,8},{12,14},{14,12},{1,3},{3,1},... | collective-permute-start | bytes 786440 | tf_op jit(solution)/shard_map/ppermute | solution.py:413
  104.6 23.4 %collective-permute-start.26 = (bf16[128,2048]{1,0:T(8,128)(2,1)S(1)}, bf16[128,2048]{1,0:T(8,128)(2,1)S(1)}, u32[]{:S(2)}, u32[]{:S(2)}) collective-permute-start(bf16[128,2048]{1,0:T(8,128)(2,1)S(1)} %constant_dynamic-update-slice_fusion.refs_0_), channel_id=1, source_target_pairs={{0,1},{1,0},{2,3},{3,2},{4,5},{5,4},{6,7},{7,6},{8,9},{9,8},{10,11... | collective-permute-start | bytes 1572872 | tf_op jit(solution)/shard_map/ppermute | solution.py:414
  113.2 8.3 %collective-permute-start.24 = (bf16[64,2048]{1,0:T(8,128)(2,1)S(1)}, bf16[64,2048]{1,0:T(8,128)(2,1)S(1)}, u32[]{:S(2)}, u32[]{:S(2)}) collective-permute-start(bf16[64,2048]{1,0:T(8,128)(2,1)S(1)} %collective-permute-done.22), channel_id=1, source_target_pairs={{0,4},{2,6},{4,8},{6,10},{8,12},{10,14},{12,0},{14,2},{1,5},{3,7},... | collective-permute-start | bytes 786440 | tf_op jit(solution)/shard_map/ppermute | solution.py:412
  113.2 8.8 %collective-permute-start.23 = (bf16[64,2048]{1,0:T(8,128)(2,1)S(1)}, bf16[64,2048]{1,0:T(8,128)(2,1)S(1)}, u32[]{:S(2)}, u32[]{:S(2)}) collective-permute-start(bf16[64,2048]{1,0:T(8,128)(2,1)S(1)} %collective-permute-done.22), channel_id=1, source_target_pairs={{0,2},{2,0},{4,6},{6,4},{8,10},{10,8},{12,14},{14,12},{1,3},{3,1},... | collective-permute-start | bytes 786440 | tf_op jit(solution)/shard_map/ppermute | solution.py:413
  113.8 14.2 %collective-permute-start.27 = (bf16[128,2048]{1,0:T(8,128)(2,1)S(1)}, bf16[128,2048]{1,0:T(8,128)(2,1)S(1)}, u32[]{:S(2)}, u32[]{:S(2)}) collective-permute-start(bf16[128,2048]{1,0:T(8,128)(2,1)S(1)} %constant_dynamic-update-slice_fusion.2.refs_1_), channel_id=1, source_target_pairs={{0,1},{1,0},{2,3},{3,2},{4,5},{5,4},{6,7},{7,6},{8,9},{9,8},{10,11... | collective-permute-start | bytes 1572872 | tf_op jit(solution)/shard_map/ppermute | solution.py:414
  121.5 6.4 %collective-permute-start.25 = (bf16[64,2048]{1,0:T(8,128)(2,1)S(1)}, bf16[64,2048]{1,0:T(8,128)(2,1)S(1)}, u32[]{:S(2)}, u32[]{:S(2)}) collective-permute-start(bf16[64,2048]{1,0:T(8,128)(2,1)S(1)} %collective-permute-done.24), channel_id=1, source_target_pairs={{0,2},{2,0},{4,6},{6,4},{8,10},{10,8},{12,14},{14,12},{1,3},{3,1},... | collective-permute-start | bytes 786440 | tf_op jit(solution)/shard_map/ppermute | solution.py:413
  148.2 9.2 %collective-permute-start.31 = (bf16[64,2048]{1,0:T(8,128)(2,1)S(1)}, bf16[64,2048]{1,0:T(8,128)(2,1)S(1)}, u32[]{:S(2)}, u32[]{:S(2)}) collective-permute-start(bf16[64,2048]{1,0:T(8,128)(2,1)S(1)} %slice.112), channel_id=1, source_target_pairs={{0,2},{2,0},{4,6},{6,4},{8,10},{10,8},{12,14},{14,12},{1,3},{3,1},... | collective-permute-start | bytes 786440 | tf_op jit(solution)/shard_map/ppermute | solution.py:420
  149.0 14.0 %collective-permute-start.34 = (bf16[64,2048]{1,0:T(8,128)(2,1)S(1)}, bf16[64,2048]{1,0:T(8,128)(2,1)S(1)}, u32[]{:S(2)}, u32[]{:S(2)}) collective-permute-start(bf16[64,2048]{1,0:T(8,128)(2,1)S(1)} %slice.111), channel_id=1, source_target_pairs={{0,2},{2,0},{4,6},{6,4},{8,10},{10,8},{12,14},{14,12},{1,3},{3,1},... | collective-permute-start | bytes 786440 | tf_op jit(solution)/shard_map/ppermute | solution.py:420
  150.7 18.0 %collective-permute-start.37 = (bf16[64,2048]{1,0:T(8,128)(2,1)S(1)}, bf16[64,2048]{1,0:T(8,128)(2,1)S(1)}, u32[]{:S(2)}, u32[]{:S(2)}) collective-permute-start(bf16[64,2048]{1,0:T(8,128)(2,1)S(1)} %slice.110), channel_id=1, source_target_pairs={{0,2},{2,0},{4,6},{6,4},{8,10},{10,8},{12,14},{14,12},{1,3},{3,1},... | collective-permute-start | bytes 786440 | tf_op jit(solution)/shard_map/ppermute | solution.py:420
  151.5 22.0 %collective-permute-start.40 = (bf16[64,2048]{1,0:T(8,128)(2,1)S(1)}, bf16[64,2048]{1,0:T(8,128)(2,1)S(1)}, u32[]{:S(2)}, u32[]{:S(2)}) collective-permute-start(bf16[64,2048]{1,0:T(8,128)(2,1)S(1)} %slice.109), channel_id=1, source_target_pairs={{0,2},{2,0},{4,6},{6,4},{8,10},{10,8},{12,14},{14,12},{1,3},{3,1},... | collective-permute-start | bytes 786440 | tf_op jit(solution)/shard_map/ppermute | solution.py:420
  157.5 16.0 %collective-permute-start.32 = (bf16[64,2048]{1,0:T(8,128)(2,1)S(1)}, bf16[64,2048]{1,0:T(8,128)(2,1)S(1)}, u32[]{:S(2)}, u32[]{:S(2)}) collective-permute-start(bf16[64,2048]{1,0:T(8,128)(2,1)S(1)} %fusion.4), channel_id=1, source_target_pairs={{0,8},{2,10},{4,12},{6,14},{8,0},{10,2},{12,4},{14,6},{1,9},{3,11}... | collective-permute-start | bytes 786440 | tf_op jit(solution)/shard_map/ppermute | solution.py:423
  163.1 17.5 %collective-permute-start.35 = (bf16[64,2048]{1,0:T(8,128)(2,1)S(1)}, bf16[64,2048]{1,0:T(8,128)(2,1)S(1)}, u32[]{:S(2)}, u32[]{:S(2)}) collective-permute-start(bf16[64,2048]{1,0:T(8,128)(2,1)S(1)} %fusion.3), channel_id=1, source_target_pairs={{0,12},{2,14},{4,0},{6,2},{8,4},{10,6},{12,8},{14,10},{1,13},{3,15... | collective-permute-start | bytes 786440 | tf_op jit(solution)/shard_map/ppermute | solution.py:423
  168.7 11.9 %collective-permute-start.38 = (bf16[64,2048]{1,0:T(8,128)(2,1)S(1)}, bf16[64,2048]{1,0:T(8,128)(2,1)S(1)}, u32[]{:S(2)}, u32[]{:S(2)}) collective-permute-start(bf16[64,2048]{1,0:T(8,128)(2,1)S(1)} %fusion.2), channel_id=1, source_target_pairs={{0,4},{2,6},{4,8},{6,10},{8,12},{10,14},{12,0},{14,2},{1,5},{3,7},... | collective-permute-start | bytes 786440 | tf_op jit(solution)/shard_map/ppermute | solution.py:423
  (14 other events, 124.0 us)

commit v6 on v5

--- a/solution.py
+++ b/solution.py
@@ -7,6 +7,7 @@
 
 HD = 128
 CAP = 12
+AHEAD = 3
 
 neg_large = -1e30
 smem = pl.BlockSpec(memory_space=pltpu.SMEM)
@@ -333,7 +334,7 @@
     def kernel(select_ref, spread_ref, gate_ref, gain_ref, wi_ref, wo_ref, *refs):
         mine_refs, other_refs = refs[:subs], refs[subs : 2 * subs]
         kept_refs, given_refs = refs[2 * subs : 3 * subs], refs[3 * subs : 4 * subs]
-        first, second, xg, res, sem = refs[4 * subs :]
+        first, second, x, xg, res, sem = refs[4 * subs :]
 
         def copy(e, part):
             if part < 2:
@@ -344,16 +345,17 @@
 
         def arrive(e, part):
             copy(e, part).wait()
-            if e + 1 < local_experts:
-                copy(e + 1, part).start()
-
-        for part in range(3):
+            coming = 3 * e + part + AHEAD
+            if coming < 3 * local_experts:
+                copy(coming // 3, coming % 3).start()
+
+        for part in range(AHEAD):
             copy(0, part).start()
         for s in range(subs):
             choose = select_ref[:, s].reshape(local_experts * slots, 2 * tokens)
-            picked = jnp.dot(
-                choose[:, :tokens], mine_refs[s][...], preferred_element_type=jnp.float32
-            ) + jnp.dot(choose[:, tokens:], other_refs[s][...], preferred_element_type=jnp.float32)
+            x[s % 2, :tokens, :] = mine_refs[s][...]
+            x[s % 2, tokens:, :] = other_refs[s][...]
+            picked = jnp.dot(choose, x[s % 2], preferred_element_type=jnp.float32)
             scale = lax.rsqrt(jnp.sum(picked * picked, axis=1, keepdims=True) * (1.0 / width) + 1e-06)
             rows = narrow(picked * scale * gain_ref[...])
             for e in range(local_experts):
@@ -390,11 +392,12 @@
         scratch_shapes=[
             pltpu.VMEM((held, 2, width, hidden), jnp.bfloat16),
             pltpu.VMEM((held, hidden, width), jnp.bfloat16),
+            pltpu.VMEM((2, 2 * tokens, width), jnp.bfloat16),
             pltpu.VMEM((local_experts, subs * slots, width), jnp.bfloat16),
             pltpu.VMEM((subs, local_experts * slots, width), jnp.bfloat16),
             pltpu.SemaphoreType.DMA((held, 3)),
         ],
-        compiler_params=limit(room * 9 // 8 // 2**20),
+        compiler_params=limit(room * 19 // 16 // 2**20),
         cost_estimate=pl.CostEstimate(flops=flops, bytes_accessed=moved, transcendentals=0),
         name="experts",
     )(select, spread, row_gate, norm_gain.reshape(1, -1), expert_in, expert_out, *mine, *other)
@@ -410,19 +413,26 @@
     for d in range(depth):
         if d + 1 < depth:
             along.append(lax.ppermute(along[d], "seq", ring(size, 1)))
-        mine.append(jnp.concatenate([along[d], lax.ppermute(along[d], "seq", swap(size))]))
+        if 0 < d == depth - 1:
+            across = lax.ppermute(first, "seq", ring(size, d))
+        else:
+            across = lax.ppermute(along[d], "seq", swap(size))
+        if d == 0:
+            first = across
+        mine.append(jnp.concatenate([along[d], across]))
         other.append(lax.ppermute(mine[d], "exp", swap(2)))
     kept, given = run_experts(mine, other, *route, norm_gain, expert_in, expert_out)
 
-    total = mixed
-    for d in far_first(depth) + [0]:
-        pair = wide(kept[d]) + wide(lax.ppermute(given[d], "exp", swap(2)))
-        there = lax.ppermute(narrow(pair[rows:]), "seq", swap(size))
-        chip = pair[:rows] + wide(there)
-        if d:
-            chip = wide(lax.ppermute(narrow(chip), "seq", ring(size, -d)))
-        total = total + chip
-    return narrow(total)
+    pair = [wide(kept[d]) + wide(lax.ppermute(given[d], "exp", swap(2))) for d in range(depth)]
+    last = depth - 1
+    there = wide(lax.ppermute(narrow(pair[last]), "seq", ring(size, -last)))
+    total = mixed + pair[0][:rows] + there[:rows]
+    for d in far_first(depth):
+        if d != last:
+            chip = pair[d][:rows] + wide(lax.ppermute(narrow(pair[d][rows:]), "seq", swap(size)))
+            total = total + wide(lax.ppermute(narrow(chip), "seq", ring(size, -d)))
+    across = narrow(pair[0][rows:] + there[rows:])
+    return narrow(total + wide(lax.ppermute(across, "seq", swap(size))))
 
 
 def on_device(

time: 182 us -> 177 us (0.973); the launches traced: 182 us -> 174 us
  waiting for transfers between devices: 112 us -> 101 us
  starting transfers between devices: 35.1 us -> 40.6 us
    ppermute x15 -> x14, waiting for transfers between devices: 32.6 us -> 25.9 us  [the longest x2 10.7 us: expert_block(): lax.ppermute(narrow(pair[d][rows:]), 'seq', swap(size))]
    ppermute x15 -> x14, starting transfers between devices: 8.97 us -> 14.2 us  [the longest x1 3.87 us: expert_block(): across = lax.ppermute(first, 'seq', ring(size, d))]
    ppermute x3, waiting for transfers between devices: 25.5 us -> 20.6 us  [expert_block(): along.append(lax.ppermute(along[d], 'seq', ring(size, 1)))]
  transfers between devices with their start and end apart: 41 -> 40, of which waited for: 21 -> 21; matrix products, arithmetic and copies ran while one was open for 1% -> 1% of each run, Pallas kernels for 5% -> 5%
where the time goes in v6:
time: 177 us; the launch traced here: 174 us
  waiting for transfers between devices  101 us (57%)
  starting transfers between devices  40.6 us (23%)
  Pallas kernels  27.7 us (16%)
  local copies, waits for them, and re-layouts  2.67 us (2%)
  other arithmetic  2.3 us (1%)
    ppermute x3, waiting for transfers between devices, attention_block(): parts.append(lax.ppermute(narrow(chip[d]), 'seq', ring(size, -d)))  22.6 us
    ppermute x3, waiting for transfers between devices, expert_block(): along.append(lax.ppermute(along[d], 'seq', ring(size, 1)))  20.6 us
    pallas_call x1, Pallas kernels, run_experts(): pl.pallas_call(kernel, out_shape=[jax.ShapeDtypeStruct((tokens, width), j...  15.1 us
    ppermute x3, waiting for transfers between devices, attention_block(): message[d] = lax.ppermute(message[d], 'seq', ring(size, d))  12.4 us
    ppermute x2, waiting for transfers between devices, expert_block(): lax.ppermute(narrow(pair[d][rows:]), 'seq', swap(size))  10.7 us
    ppermute x2, waiting for transfers between devices, expert_block(): total = total + wide(lax.ppermute(narrow(chip), 'seq', ring(size, -d)))  8.31 us
    ppermute x3, waiting for transfers between devices, attention_block(): weight[d] = lax.ppermute(weight[d], 'seq', ring(size, d))  7.58 us
    ppermute x3, starting transfers between devices, attention_block(): weight[d] = lax.ppermute(weight[d], 'seq', ring(size, d))  6.87 us
  transfers between devices with their start and end apart: 40, of which 21 were waited for; matrix products, arithmetic and copies ran while one was open for 1% of the time, Pallas kernels for 5%

profile of v6, /device:TPU:0, one launch (start us, length us, event | category | flops | bytes accessed | tf_op | source)
XLA Modules:
  0.0 174.3 jit_solution(6576784156732217661)
XLA Ops:
  0.0 2.2 %pack_heads.1 = (bf16[144,768]{1,0:T(8,128)(2,1)}, bf16[144,768]{1,0:T(8,128)(2,1)}, bf16[144,768]{1,0:T(8,128)(2,1)}, bf16[144,768]{1,0:T(8,128)(2,1)}, bf16[144,256]{1,0:T(8,128)(2,1)}) custom-call(s32[1]{0:T(128)} %bitcast.5.z_ref, bf16[128,2048]{1,0:T(8,128)(2,1)} %query_ref.1, bf16[128,256]{1,0:T(8,128)(2,1)} %key_ref.1, bf16[128,256]{1,0:T(8,128)(2,1)} %value_ref.1, ...), custom_call_target="tpu_custom_call" | custom-call | tf_op jit(solution)/shard_map/pack_heads/pallas_call | solution.py:65
  2.2 3.0 %collective-permute-start.3 = (bf16[144,256]{1,0:T(8,128)(2,1)}, bf16[144,256]{1,0:T(8,128)(2,1)S(1)}, u32[]{:S(2)}, u32[]{:S(2)}) collective-permute-start(bf16[144,256]{1,0:T(8,128)(2,1)} %get-tuple-element.37), channel_id=1, source_target_pairs={{0,2},{2,0},{4,6},{6,4},{8,10},{10,8},{12,14},{14,12},{1,3},{3,1},... | collective-permute-start | bytes 221192 | tf_op jit(solution)/shard_map/ppermute | solution.py:242
  5.1 1.6 collective-permute-start
  6.7 2.6 %collective-permute-start.1 = (bf16[144,768]{1,0:T(8,128)(2,1)}, bf16[144,768]{1,0:T(8,128)(2,1)S(1)}, u32[]{:S(2)}, u32[]{:S(2)}) collective-permute-start(bf16[144,768]{1,0:T(8,128)(2,1)} %get-tuple-element.35), channel_id=1, source_target_pairs={{0,8},{2,10},{4,12},{6,14},{8,0},{10,2},{12,4},{14,6},{1,9},{3,11}... | collective-permute-start | bytes 663560 | tf_op jit(solution)/shard_map/ppermute | solution.py:239
  11.0 4.6 %collective-permute-done.refs_1_.refs_2_ = bf16[144,768]{1,0:T(8,128)(2,1)S(1)} collective-permute-done((bf16[144,768]{1,0:T(8,128)(2,1)}, bf16[144,768]{1,0:T(8,128)(2,1)S(1)}, u32[]{:S(2)}, u32[]{:S(2)}) %collective-permute-start) | collective-permute-done | bytes 221216 | tf_op jit(solution)/shard_map/ppermute | solution.py:239
  15.9 7.8 %collective-permute-done.1.refs_2_.refs_0_.refs_4_ = bf16[144,768]{1,0:T(8,128)(2,1)S(1)} collective-permute-done((bf16[144,768]{1,0:T(8,128)(2,1)}, bf16[144,768]{1,0:T(8,128)(2,1)S(1)}, u32[]{:S(2)}, u32[]{:S(2)}) %collective-permute-start.1) | collective-permute-done | bytes 221216 | tf_op jit(solution)/shard_map/ppermute | solution.py:239
  25.0 3.6 %collective-permute-start.8 = (bf16[256,512]{1,0:T(8,128)(2,1)S(1)}, bf16[256,512]{1,0:T(8,128)(2,1)S(1)}, u32[]{:S(2)}, u32[]{:S(2)}) collective-permute-start(bf16[256,512]{1,0:T(8,128)(2,1)S(1)} %get-tuple-element.43), channel_id=1, source_target_pairs={{0,4},{2,6},{4,8},{6,10},{8,12},{10,14},{12,0},{14,2},{1,5},{3,7},... | collective-permute-start | bytes 786440 | tf_op jit(solution)/shard_map/ppermute | solution.py:247
  28.6 3.3 %collective-permute-start.10 = (bf16[256,512]{1,0:T(8,128)(2,1)S(1)}, bf16[256,512]{1,0:T(8,128)(2,1)S(1)}, u32[]{:S(2)}, u32[]{:S(2)}) collective-permute-start(bf16[256,512]{1,0:T(8,128)(2,1)S(1)} %get-tuple-element.44), channel_id=1, source_target_pairs={{0,8},{2,10},{4,12},{6,14},{8,0},{10,2},{12,4},{14,6},{1,9},{3,11}... | collective-permute-start | bytes 786440 | tf_op jit(solution)/shard_map/ppermute | solution.py:247
  34.1 2.5 %collective-permute-done.5.refs_6_.refs_5_ = bf16[144,256]{1,0:T(8,128)(2,1)S(1)} collective-permute-done((bf16[144,256]{1,0:T(8,128)(2,1)S(1)}, bf16[144,256]{1,0:T(8,128)(2,1)S(1)}, u32[]{:S(2)}, u32[]{:S(2)}) %collective-permute-start.5) | collective-permute-done | bytes 73760 | tf_op jit(solution)/shard_map/ppermute | solution.py:242
  40.2 7.6 %collective-permute-done.10.refs_8_ = bf16[256,512]{1,0:T(8,128)(2,1)S(1)} collective-permute-done((bf16[256,512]{1,0:T(8,128)(2,1)S(1)}, bf16[256,512]{1,0:T(8,128)(2,1)S(1)}, u32[]{:S(2)}, u32[]{:S(2)}) %collective-permute-start.10) | collective-permute-done | bytes 262176 | tf_op jit(solution)/shard_map/ppermute | solution.py:247
  49.8 4.4 %attend.1 = (bf16[128,512]{1,0:T(8,128)(2,1)S(1)}, bf16[128,512]{1,0:T(8,128)(2,1)S(1)}, bf16[128,512]{1,0:T(8,128)(2,1)S(1)}, bf16[128,512]{1,0:T(8,128)(2,1)S(1)}) custom-call(s32[1]{0:T(128)} %bitcast.2.core_ref, s32[4]{0:T(128)S(1)} %multiply_bitcast_fusion.starts_ref, s32[1,1024]{1,0:T(1,128)S(1)} %bitcast.20, bf16[144,768]{1,0:T(8,128)(2,1)S(1)} %copy-done.3, ...), custom_call_target="tpu_custom_call" | custom-call | flops 42949672960 | bytes 2097152 | tf_op jit(solution)/shard_map/attend/pallas_call | solution.py:147
  54.3 3.9 %routing.1 = (bf16[4,4,48,256]{3,2,1,0:T(8,128)(2,1)S(1)}, bf16[4,256,192]{2,1,0:T(8,128)(2,1)S(1)}, f32[4,192,1]{2,1,0:T(8,128)S(1)}) custom-call(s32[1]{0:T(128)} %bitcast.8.first_ref, bf16[128,256]{1,0:T(8,128)(2,1)S(1)} %collect_meta.1.mine_ref, bf16[128,256]{1,0:T(8,128)(2,1)S(1)} %collective-permute-done.14.other_ref, ...), custom_call_target="tpu_custom_call" | custom-call | tf_op jit(solution)/shard_map/routing/pallas_call | solution.py:311
  58.2 3.4 %collective-permute-done.13.refs_11_ = bf16[256,512]{1,0:T(8,128)(2,1)S(1)} collective-permute-done((bf16[256,512]{1,0:T(8,128)(2,1)S(1)}, bf16[256,512]{1,0:T(8,128)(2,1)S(1)}, u32[]{:S(2)}, u32[]{:S(2)}) %collective-permute-start.13) | collective-permute-done | bytes 262176 | tf_op jit(solution)/shard_map/ppermute | solution.py:248
  61.6 1.9 %project.1 = (bf16[4,64,2048]{2,1,0:T(8,128)(2,1)S(1)}, bf16[4,64,2048]{2,1,0:T(8,128)(2,1)S(1)}) custom-call(s32[8]{0:T(128)S(1)} %add.107.place_ref, bf16[128,512]{1,0:T(8,128)(2,1)S(1)} %get-tuple-element.38.refs_0_, bf16[128,512]{1,0:T(8,128)(2,1)S(1)} %get-tuple-element.39.refs_1_, bf16[128,512]{1,0:T(8,128)(2,1)S(1)} %get-tuple-element.40.refs_2_, ...), custom_call_target="tpu_custom_call" | custom-call | flops 1073741824 | bytes 6815744 | tf_op jit(solution)/shard_map/project/pallas_call | solution.py:190
  63.5 2.6 %collective-permute-done.15 = bf16[4,64,2048]{2,1,0:T(8,128)(2,1)S(1)} collective-permute-done((bf16[4,64,2048]{2,1,0:T(8,128)(2,1)S(1)}, bf16[4,64,2048]{2,1,0:T(8,128)(2,1)S(1)}, u32[]{:S(2)}, u32[]{:S(2)}) %collective-permute-start.15) | collective-permute-done | bytes 1048608 | tf_op jit(solution)/shard_map/ppermute | solution.py:261
  66.7 2.7 %collective-permute-start.18 = (bf16[64,2048]{1,0:T(8,128)(2,1)S(1)}, bf16[64,2048]{1,0:T(8,128)(2,1)S(1)}, u32[]{:S(2)}, u32[]{:S(2)}) collective-permute-start(bf16[64,2048]{1,0:T(8,128)(2,1)S(1)} %get-tuple-element.63), channel_id=1, source_target_pairs={{0,4},{2,6},{4,8},{6,10},{8,12},{10,14},{12,0},{14,2},{1,5},{3,7},... | collective-permute-start | bytes 786440 | tf_op jit(solution)/shard_map/ppermute | solution.py:264
  71.2 6.6 %collective-permute-done.18.refs_4_ = bf16[64,2048]{1,0:T(8,128)(2,1)S(1)} collective-permute-done((bf16[64,2048]{1,0:T(8,128)(2,1)S(1)}, bf16[64,2048]{1,0:T(8,128)(2,1)S(1)}, u32[]{:S(2)}, u32[]{:S(2)}) %collective-permute-start.18) | collective-permute-done | bytes 262176 | tf_op jit(solution)/shard_map/ppermute | solution.py:264
  77.7 4.8 %collective-permute-done.17.refs_3_ = bf16[64,2048]{1,0:T(8,128)(2,1)S(1)} collective-permute-done((bf16[64,2048]{1,0:T(8,128)(2,1)S(1)}, bf16[64,2048]{1,0:T(8,128)(2,1)S(1)}, u32[]{:S(2)}, u32[]{:S(2)}) %collective-permute-start.17) | collective-permute-done | bytes 262176 | tf_op jit(solution)/shard_map/ppermute | solution.py:264
  82.5 11.2 %collective-permute-done.16.refs_2_ = bf16[64,2048]{1,0:T(8,128)(2,1)S(1)} collective-permute-done((bf16[64,2048]{1,0:T(8,128)(2,1)S(1)}, bf16[64,2048]{1,0:T(8,128)(2,1)S(1)}, u32[]{:S(2)}, u32[]{:S(2)}) %collective-permute-start.16) | collective-permute-done | bytes 262176 | tf_op jit(solution)/shard_map/ppermute | solution.py:264
  94.6 9.4 %collective-permute-done.20 = bf16[64,2048]{1,0:T(8,128)(2,1)S(1)} collective-permute-done((bf16[64,2048]{1,0:T(8,128)(2,1)S(1)}, bf16[64,2048]{1,0:T(8,128)(2,1)S(1)}, u32[]{:S(2)}, u32[]{:S(2)}) %collective-permute-start.20) | collective-permute-done | bytes 262176 | tf_op jit(solution)/shard_map/ppermute | solution.py:415
  104.6 3.9 %collective-permute-start.25 = (bf16[64,2048]{1,0:T(8,128)(2,1)S(1)}, bf16[64,2048]{1,0:T(8,128)(2,1)S(1)}, u32[]{:S(2)}, u32[]{:S(2)}) collective-permute-start(bf16[64,2048]{1,0:T(8,128)(2,1)S(1)} %collective-permute-done.19), channel_id=1, source_target_pairs={{0,12},{2,14},{4,0},{6,2},{8,4},{10,6},{12,8},{14,10},{1,13},{3,15... | collective-permute-start | bytes 786440 | tf_op jit(solution)/shard_map/ppermute | solution.py:417
  108.5 6.6 %collective-permute-done.22 = bf16[64,2048]{1,0:T(8,128)(2,1)S(1)} collective-permute-done((bf16[64,2048]{1,0:T(8,128)(2,1)S(1)}, bf16[64,2048]{1,0:T(8,128)(2,1)S(1)}, u32[]{:S(2)}, u32[]{:S(2)}) %collective-permute-start.22) | collective-permute-done | bytes 262176 | tf_op jit(solution)/shard_map/ppermute | solution.py:415
  116.0 5.5 %collective-permute-done.23 = bf16[64,2048]{1,0:T(8,128)(2,1)S(1)} collective-permute-done((bf16[64,2048]{1,0:T(8,128)(2,1)S(1)}, bf16[64,2048]{1,0:T(8,128)(2,1)S(1)}, u32[]{:S(2)}, u32[]{:S(2)}) %collective-permute-start.23) | collective-permute-done | bytes 262176 | tf_op jit(solution)/shard_map/ppermute | solution.py:419
  121.6 4.7 %collective-permute-done.24 = bf16[64,2048]{1,0:T(8,128)(2,1)S(1)} collective-permute-done((bf16[64,2048]{1,0:T(8,128)(2,1)S(1)}, bf16[64,2048]{1,0:T(8,128)(2,1)S(1)}, u32[]{:S(2)}, u32[]{:S(2)}) %collective-permute-start.24) | collective-permute-done | bytes 262176 | tf_op jit(solution)/shard_map/ppermute | solution.py:415
  126.4 1.9 %collective-permute-done.29.refs_7_ = bf16[128,2048]{1,0:T(8,128)(2,1)S(1)} collective-permute-done((bf16[128,2048]{1,0:T(8,128)(2,1)S(1)}, bf16[128,2048]{1,0:T(8,128)(2,1)S(1)}, u32[]{:S(2)}, u32[]{:S(2)}) %collective-permute-start.29) | collective-permute-done | bytes 524320 | tf_op jit(solution)/shard_map/ppermute | solution.py:423
  128.2 15.1 %experts.1 = (bf16[128,2048]{1,0:T(8,128)(2,1)S(1)}, bf16[128,2048]{1,0:T(8,128)(2,1)S(1)}, bf16[128,2048]{1,0:T(8,128)(2,1)S(1)}, bf16[128,2048]{1,0:T(8,128)(2...) custom-call(bf16[4,4,48,256]{3,2,1,0:T(8,128)(2,1)S(1)} %get-tuple-e, ...), custom_call_target="tpu_custom_call" | custom-call | flops 7247757312 | bytes 54525952 | tf_op jit(solution)/shard_map/experts/pallas_call | solution.py:387
  146.2 1.6 collective-permute-start.34
  149.4 6.0 %collective-permute-done.34 = bf16[64,2048]{1,0:T(8,128)(2,1)S(1)} collective-permute-done((bf16[64,2048]{1,0:T(8,128)(2,1)S(1)}, bf16[64,2048]{1,0:T(8,128)(2,1)S(1)}, u32[]{:S(2)}, u32[]{:S(2)}) %collective-permute-start.34) | collective-permute-done | bytes 262176 | tf_op jit(solution)/shard_map/ppermute | solution.py:432
  155.6 4.7 %collective-permute-done.37 = bf16[64,2048]{1,0:T(8,128)(2,1)S(1)} collective-permute-done((bf16[64,2048]{1,0:T(8,128)(2,1)S(1)}, bf16[64,2048]{1,0:T(8,128)(2,1)S(1)}, u32[]{:S(2)}, u32[]{:S(2)}) %collective-permute-start.37) | collective-permute-done | bytes 262176 | tf_op jit(solution)/shard_map/ppermute | solution.py:432
  160.3 3.0 %collective-permute-start.38 = (bf16[64,2048]{1,0:T(8,128)(2,1)S(1)}, bf16[64,2048]{1,0:T(8,128)(2,1)S(1)}, u32[]{:S(2)}, u32[]{:S(2)}) collective-permute-start(bf16[64,2048]{1,0:T(8,128)(2,1)S(1)} %fusion.1), channel_id=1, source_target_pairs={{0,12},{2,14},{4,0},{6,2},{8,4},{10,6},{12,8},{14,10},{1,13},{3,15... | collective-permute-start | bytes 786440 | tf_op jit(solution)/shard_map/ppermute | solution.py:433
  163.5 1.6 collective-permute-start.39
  165.1 7.5 %collective-permute-done.35 = bf16[64,2048]{1,0:T(8,128)(2,1)S(1)} collective-permute-done((bf16[64,2048]{1,0:T(8,128)(2,1)S(1)}, bf16[64,2048]{1,0:T(8,128)(2,1)S(1)}, u32[]{:S(2)}, u32[]{:S(2)}) %collective-permute-start.35) | collective-permute-done | bytes 262176 | tf_op jit(solution)/shard_map/ppermute | solution.py:433
  (99 shorter events, 22.4 us)
Async XLA Ops:
  2.2 29.8 %collective-permute-start.3 = (bf16[144,256]{1,0:T(8,128)(2,1)}, bf16[144,256]{1,0:T(8,128)(2,1)S(1)}, u32[]{:S(2)}, u32[]{:S(2)}) collective-permute-start(bf16[144,256]{1,0:T(8,128)(2,1)} %get-tuple-element.37), channel_id=1, source_target_pairs={{0,2},{2,0},{4,6},{6,4},{8,10},{10,8},{12,14},{14,12},{1,3},{3,1},... | collective-permute-start | bytes 221192 | tf_op jit(solution)/shard_map/ppermute | solution.py:242
  5.1 10.5 %collective-permute-start = (bf16[144,768]{1,0:T(8,128)(2,1)}, bf16[144,768]{1,0:T(8,128)(2,1)S(1)}, u32[]{:S(2)}, u32[]{:S(2)}) collective-permute-start(bf16[144,768]{1,0:T(8,128)(2,1)} %get-tuple-element.34), channel_id=1, source_target_pairs={{0,4},{2,6},{4,8},{6,10},{8,12},{10,14},{12,0},{14,2},{1,5},{3,7},... | collective-permute-start | bytes 663560 | tf_op jit(solution)/shard_map/ppermute | solution.py:239
  6.7 17.0 %collective-permute-start.1 = (bf16[144,768]{1,0:T(8,128)(2,1)}, bf16[144,768]{1,0:T(8,128)(2,1)S(1)}, u32[]{:S(2)}, u32[]{:S(2)}) collective-permute-start(bf16[144,768]{1,0:T(8,128)(2,1)} %get-tuple-element.35), channel_id=1, source_target_pairs={{0,8},{2,10},{4,12},{6,14},{8,0},{10,2},{12,4},{14,6},{1,9},{3,11}... | collective-permute-start | bytes 663560 | tf_op jit(solution)/shard_map/ppermute | solution.py:239
  9.3 22.6 %collective-permute-start.2 = (bf16[144,768]{1,0:T(8,128)(2,1)}, bf16[144,768]{1,0:T(8,128)(2,1)S(1)}, u32[]{:S(2)}, u32[]{:S(2)}) collective-permute-start(bf16[144,768]{1,0:T(8,128)(2,1)} %get-tuple-element.36), channel_id=1, source_target_pairs={{0,12},{2,14},{4,0},{6,2},{8,4},{10,6},{12,8},{14,10},{1,13},{3,15... | collective-permute-start | bytes 663560 | tf_op jit(solution)/shard_map/ppermute | solution.py:239
  15.6 16.9 %collective-permute-start.4 = (bf16[144,256]{1,0:T(8,128)(2,1)S(1)}, bf16[144,256]{1,0:T(8,128)(2,1)S(1)}, u32[]{:S(2)}, u32[]{:S(2)}) collective-permute-start(bf16[144,256]{1,0:T(8,128)(2,1)S(1)} %slice.69), channel_id=1, source_target_pairs={{0,2},{2,0},{4,6},{6,4},{8,10},{10,8},{12,14},{14,12},{1,3},{3,1},... | collective-permute-start | bytes 221192 | tf_op jit(solution)/shard_map/ppermute | solution.py:242
  25.0 14.2 %collective-permute-start.8 = (bf16[256,512]{1,0:T(8,128)(2,1)S(1)}, bf16[256,512]{1,0:T(8,128)(2,1)S(1)}, u32[]{:S(2)}, u32[]{:S(2)}) collective-permute-start(bf16[256,512]{1,0:T(8,128)(2,1)S(1)} %get-tuple-element.43), channel_id=1, source_target_pairs={{0,4},{2,6},{4,8},{6,10},{8,12},{10,14},{12,0},{14,2},{1,5},{3,7},... | collective-permute-start | bytes 786440 | tf_op jit(solution)/shard_map/ppermute | solution.py:247
  28.6 19.2 %collective-permute-start.10 = (bf16[256,512]{1,0:T(8,128)(2,1)S(1)}, bf16[256,512]{1,0:T(8,128)(2,1)S(1)}, u32[]{:S(2)}, u32[]{:S(2)}) collective-permute-start(bf16[256,512]{1,0:T(8,128)(2,1)S(1)} %get-tuple-element.44), channel_id=1, source_target_pairs={{0,8},{2,10},{4,12},{6,14},{8,0},{10,2},{12,4},{14,6},{1,9},{3,11}... | collective-permute-start | bytes 786440 | tf_op jit(solution)/shard_map/ppermute | solution.py:247
  31.9 16.4 %collective-permute-start.12 = (bf16[256,512]{1,0:T(8,128)(2,1)S(1)}, bf16[256,512]{1,0:T(8,128)(2,1)S(1)}, u32[]{:S(2)}, u32[]{:S(2)}) collective-permute-start(bf16[256,512]{1,0:T(8,128)(2,1)S(1)} %get-tuple-element.45), channel_id=1, source_target_pairs={{0,12},{2,14},{4,0},{6,2},{8,4},{10,6},{12,8},{14,10},{1,13},{3,15... | collective-permute-start | bytes 786440 | tf_op jit(solution)/shard_map/ppermute | solution.py:247
  32.6 5.7 %collective-permute-start.6 = (bf16[144,256]{1,0:T(8,128)(2,1)S(1)}, bf16[144,256]{1,0:T(8,128)(2,1)S(1)}, u32[]{:S(2)}, u32[]{:S(2)}) collective-permute-start(bf16[144,256]{1,0:T(8,128)(2,1)S(1)} %slice.71), channel_id=1, source_target_pairs={{0,2},{2,0},{4,6},{6,4},{8,10},{10,8},{12,14},{14,12},{1,3},{3,1},... | collective-permute-start | bytes 221192 | tf_op jit(solution)/shard_map/ppermute | solution.py:242
  36.6 17.7 %collective-permute-start.7 = (bf16[256,512]{1,0:T(8,128)(2,1)S(1)}, bf16[256,512]{1,0:T(8,128)(2,1)S(1)}, u32[]{:S(2)}, u32[]{:S(2)}) collective-permute-start(bf16[256,512]{1,0:T(8,128)(2,1)S(1)} %get-tuple-element.42.refs_4_), channel_id=1, source_target_pairs={{0,2},{2,0},{4,6},{6,4},{8,10},{10,8},{12,14},{14,12},{1,3},{3,1},... | collective-permute-start | bytes 786440 | tf_op jit(solution)/shard_map/ppermute | solution.py:245
  39.2 15.1 %collective-permute-start.14 = (bf16[128,256]{1,0:T(8,128)(2,1)S(1)}, bf16[128,256]{1,0:T(8,128)(2,1)S(1)}, u32[]{:S(2)}, u32[]{:S(2)}) collective-permute-start(bf16[128,256]{1,0:T(8,128)(2,1)S(1)} %collect_meta.1.mine_ref), channel_id=1, source_target_pairs={{0,1},{1,0},{2,3},{3,2},{4,5},{5,4},{6,7},{7,6},{8,9},{9,8},{10,11... | collective-permute-start | bytes 196616 | tf_op jit(solution)/shard_map/ppermute | solution.py:251
  39.2 19.0 %collective-permute-start.9 = (bf16[256,512]{1,0:T(8,128)(2,1)S(1)}, bf16[256,512]{1,0:T(8,128)(2,1)S(1)}, u32[]{:S(2)}, u32[]{:S(2)}) collective-permute-start(bf16[256,512]{1,0:T(8,128)(2,1)S(1)} %collective-permute-done.8.refs_6_), channel_id=1, source_target_pairs={{0,2},{2,0},{4,6},{6,4},{8,10},{10,8},{12,14},{14,12},{1,3},{3,1},... | collective-permute-start | bytes 786440 | tf_op jit(solution)/shard_map/ppermute | solution.py:248
  47.8 10.4 %collective-permute-start.11 = (bf16[256,512]{1,0:T(8,128)(2,1)S(1)}, bf16[256,512]{1,0:T(8,128)(2,1)S(1)}, u32[]{:S(2)}, u32[]{:S(2)}) collective-permute-start(bf16[256,512]{1,0:T(8,128)(2,1)S(1)} %collective-permute-done.10.refs_8_), channel_id=1, source_target_pairs={{0,2},{2,0},{4,6},{6,4},{8,10},{10,8},{12,14},{14,12},{1,3},{3,1},... | collective-permute-start | bytes 786440 | tf_op jit(solution)/shard_map/ppermute | solution.py:248
  48.3 13.2 %collective-permute-start.13 = (bf16[256,512]{1,0:T(8,128)(2,1)S(1)}, bf16[256,512]{1,0:T(8,128)(2,1)S(1)}, u32[]{:S(2)}, u32[]{:S(2)}) collective-permute-start(bf16[256,512]{1,0:T(8,128)(2,1)S(1)} %collective-permute-done.12.refs_10_), channel_id=1, source_target_pairs={{0,2},{2,0},{4,6},{6,4},{8,10},{10,8},{12,14},{14,12},{1,3},{3,1},... | collective-permute-start | bytes 786440 | tf_op jit(solution)/shard_map/ppermute | solution.py:248
  66.7 11.0 %collective-permute-start.18 = (bf16[64,2048]{1,0:T(8,128)(2,1)S(1)}, bf16[64,2048]{1,0:T(8,128)(2,1)S(1)}, u32[]{:S(2)}, u32[]{:S(2)}) collective-permute-start(bf16[64,2048]{1,0:T(8,128)(2,1)S(1)} %get-tuple-element.63), channel_id=1, source_target_pairs={{0,4},{2,6},{4,8},{6,10},{8,12},{10,14},{12,0},{14,2},{1,5},{3,7},... | collective-permute-start | bytes 786440 | tf_op jit(solution)/shard_map/ppermute | solution.py:264
  69.4 13.1 %collective-permute-start.17 = (bf16[64,2048]{1,0:T(8,128)(2,1)S(1)}, bf16[64,2048]{1,0:T(8,128)(2,1)S(1)}, u32[]{:S(2)}, u32[]{:S(2)}) collective-permute-start(bf16[64,2048]{1,0:T(8,128)(2,1)S(1)} %get-tuple-element.64), channel_id=1, source_target_pairs={{0,12},{2,14},{4,0},{6,2},{8,4},{10,6},{12,8},{14,10},{1,13},{3,15... | collective-permute-start | bytes 786440 | tf_op jit(solution)/shard_map/ppermute | solution.py:264
  70.6 23.2 %collective-permute-start.16 = (bf16[64,2048]{1,0:T(8,128)(2,1)S(1)}, bf16[64,2048]{1,0:T(8,128)(2,1)S(1)}, u32[]{:S(2)}, u32[]{:S(2)}) collective-permute-start(bf16[64,2048]{1,0:T(8,128)(2,1)S(1)} %get-tuple-element.65), channel_id=1, source_target_pairs={{0,8},{2,10},{4,12},{6,14},{8,0},{10,2},{12,4},{14,6},{1,9},{3,11}... | collective-permute-start | bytes 786440 | tf_op jit(solution)/shard_map/ppermute | solution.py:264
  93.9 10.1 %collective-permute-start.20 = (bf16[64,2048]{1,0:T(8,128)(2,1)S(1)}, bf16[64,2048]{1,0:T(8,128)(2,1)S(1)}, u32[]{:S(2)}, u32[]{:S(2)}) collective-permute-start(bf16[64,2048]{1,0:T(8,128)(2,1)S(1)} %get-tuple-element.52), channel_id=1, source_target_pairs={{0,4},{2,6},{4,8},{6,10},{8,12},{10,14},{12,0},{14,2},{1,5},{3,7},... | collective-permute-start | bytes 786440 | tf_op jit(solution)/shard_map/ppermute | solution.py:415
  94.0 10.5 %collective-permute-start.19 = (bf16[64,2048]{1,0:T(8,128)(2,1)S(1)}, bf16[64,2048]{1,0:T(8,128)(2,1)S(1)}, u32[]{:S(2)}, u32[]{:S(2)}) collective-permute-start(bf16[64,2048]{1,0:T(8,128)(2,1)S(1)} %get-tuple-element.52), channel_id=1, source_target_pairs={{0,2},{2,0},{4,6},{6,4},{8,10},{10,8},{12,14},{14,12},{1,3},{3,1},... | collective-permute-start | bytes 786440 | tf_op jit(solution)/shard_map/ppermute | solution.py:419
  104.0 11.1 %collective-permute-start.22 = (bf16[64,2048]{1,0:T(8,128)(2,1)S(1)}, bf16[64,2048]{1,0:T(8,128)(2,1)S(1)}, u32[]{:S(2)}, u32[]{:S(2)}) collective-permute-start(bf16[64,2048]{1,0:T(8,128)(2,1)S(1)} %collective-permute-done.20), channel_id=1, source_target_pairs={{0,4},{2,6},{4,8},{6,10},{8,12},{10,14},{12,0},{14,2},{1,5},{3,7},... | collective-permute-start | bytes 786440 | tf_op jit(solution)/shard_map/ppermute | solution.py:415
  104.0 11.6 %collective-permute-start.21 = (bf16[64,2048]{1,0:T(8,128)(2,1)S(1)}, bf16[64,2048]{1,0:T(8,128)(2,1)S(1)}, u32[]{:S(2)}, u32[]{:S(2)}) collective-permute-start(bf16[64,2048]{1,0:T(8,128)(2,1)S(1)} %collective-permute-done.20), channel_id=1, source_target_pairs={{0,2},{2,0},{4,6},{6,4},{8,10},{10,8},{12,14},{14,12},{1,3},{3,1},... | collective-permute-start | bytes 786440 | tf_op jit(solution)/shard_map/ppermute | solution.py:419
  104.5 21.8 %collective-permute-start.26 = (bf16[128,2048]{1,0:T(8,128)(2,1)S(1)}, bf16[128,2048]{1,0:T(8,128)(2,1)S(1)}, u32[]{:S(2)}, u32[]{:S(2)}) collective-permute-start(bf16[128,2048]{1,0:T(8,128)(2,1)S(1)} %constant_dynamic-update-slice_fusion.refs_0_), channel_id=1, source_target_pairs={{0,1},{1,0},{2,3},{3,2},{4,5},{5,4},{6,7},{7,6},{8,9},{9,8},{10,11... | collective-permute-start | bytes 1572872 | tf_op jit(solution)/shard_map/ppermute | solution.py:423
  104.6 21.6 %collective-permute-start.25 = (bf16[64,2048]{1,0:T(8,128)(2,1)S(1)}, bf16[64,2048]{1,0:T(8,128)(2,1)S(1)}, u32[]{:S(2)}, u32[]{:S(2)}) collective-permute-start(bf16[64,2048]{1,0:T(8,128)(2,1)S(1)} %collective-permute-done.19), channel_id=1, source_target_pairs={{0,12},{2,14},{4,0},{6,2},{8,4},{10,6},{12,8},{14,10},{1,13},{3,15... | collective-permute-start | bytes 786440 | tf_op jit(solution)/shard_map/ppermute | solution.py:417
  115.1 6.4 %collective-permute-start.23 = (bf16[64,2048]{1,0:T(8,128)(2,1)S(1)}, bf16[64,2048]{1,0:T(8,128)(2,1)S(1)}, u32[]{:S(2)}, u32[]{:S(2)}) collective-permute-start(bf16[64,2048]{1,0:T(8,128)(2,1)S(1)} %collective-permute-done.22), channel_id=1, source_target_pairs={{0,2},{2,0},{4,6},{6,4},{8,10},{10,8},{12,14},{14,12},{1,3},{3,1},... | collective-permute-start | bytes 786440 | tf_op jit(solution)/shard_map/ppermute | solution.py:419
  115.6 10.7 %collective-permute-start.27 = (bf16[128,2048]{1,0:T(8,128)(2,1)S(1)}, bf16[128,2048]{1,0:T(8,128)(2,1)S(1)}, u32[]{:S(2)}, u32[]{:S(2)}) collective-permute-start(bf16[128,2048]{1,0:T(8,128)(2,1)S(1)} %constant_dynamic-update-slice_fusion.2.refs_1_), channel_id=1, source_target_pairs={{0,1},{1,0},{2,3},{3,2},{4,5},{5,4},{6,7},{7,6},{8,9},{9,8},{10,11... | collective-permute-start | bytes 1572872 | tf_op jit(solution)/shard_map/ppermute | solution.py:423
  115.7 10.5 %collective-permute-start.24 = (bf16[64,2048]{1,0:T(8,128)(2,1)S(1)}, bf16[64,2048]{1,0:T(8,128)(2,1)S(1)}, u32[]{:S(2)}, u32[]{:S(2)}) collective-permute-start(bf16[64,2048]{1,0:T(8,128)(2,1)S(1)} %collective-permute-done.22), channel_id=1, source_target_pairs={{0,4},{2,6},{4,8},{6,10},{8,12},{10,14},{12,0},{14,2},{1,5},{3,7},... | collective-permute-start | bytes 786440 | tf_op jit(solution)/shard_map/ppermute | solution.py:415
  145.5 17.9 %collective-permute-start.32 = (bf16[128,2048]{1,0:T(8,128)(2,1)S(1)}, bf16[128,2048]{1,0:T(8,128)(2,1)S(1)}, u32[]{:S(2)}, u32[]{:S(2)}) collective-permute-start(bf16[128,2048]{1,0:T(8,128)(2,1)S(1)} %add_convert_fusion), channel_id=1, source_target_pairs={{0,4},{2,6},{4,8},{6,10},{8,12},{10,14},{12,0},{14,2},{1,5},{3,7},... | collective-permute-start | bytes 1572872 | tf_op jit(solution)/shard_map/ppermute | solution.py:428
  146.2 9.2 %collective-permute-start.34 = (bf16[64,2048]{1,0:T(8,128)(2,1)S(1)}, bf16[64,2048]{1,0:T(8,128)(2,1)S(1)}, u32[]{:S(2)}, u32[]{:S(2)}) collective-permute-start(bf16[64,2048]{1,0:T(8,128)(2,1)S(1)} %slice.114), channel_id=1, source_target_pairs={{0,2},{2,0},{4,6},{6,4},{8,10},{10,8},{12,14},{14,12},{1,3},{3,1},... | collective-permute-start | bytes 786440 | tf_op jit(solution)/shard_map/ppermute | solution.py:432
  148.0 12.3 %collective-permute-start.37 = (bf16[64,2048]{1,0:T(8,128)(2,1)S(1)}, bf16[64,2048]{1,0:T(8,128)(2,1)S(1)}, u32[]{:S(2)}, u32[]{:S(2)}) collective-permute-start(bf16[64,2048]{1,0:T(8,128)(2,1)S(1)} %slice.113), channel_id=1, source_target_pairs={{0,2},{2,0},{4,6},{6,4},{8,10},{10,8},{12,14},{14,12},{1,3},{3,1},... | collective-permute-start | bytes 786440 | tf_op jit(solution)/shard_map/ppermute | solution.py:432
  155.5 17.1 %collective-permute-start.35 = (bf16[64,2048]{1,0:T(8,128)(2,1)S(1)}, bf16[64,2048]{1,0:T(8,128)(2,1)S(1)}, u32[]{:S(2)}, u32[]{:S(2)}) collective-permute-start(bf16[64,2048]{1,0:T(8,128)(2,1)S(1)} %fusion.2), channel_id=1, source_target_pairs={{0,8},{2,10},{4,12},{6,14},{8,0},{10,2},{12,4},{14,6},{1,9},{3,11}... | collective-permute-start | bytes 786440 | tf_op jit(solution)/shard_map/ppermute | solution.py:433
  160.3 13.1 %collective-permute-start.38 = (bf16[64,2048]{1,0:T(8,128)(2,1)S(1)}, bf16[64,2048]{1,0:T(8,128)(2,1)S(1)}, u32[]{:S(2)}, u32[]{:S(2)}) collective-permute-start(bf16[64,2048]{1,0:T(8,128)(2,1)S(1)} %fusion.1), channel_id=1, source_target_pairs={{0,12},{2,14},{4,0},{6,2},{8,4},{10,6},{12,8},{14,10},{1,13},{3,15... | collective-permute-start | bytes 786440 | tf_op jit(solution)/shard_map/ppermute | solution.py:433
  163.5 9.9 %collective-permute-start.39 = (bf16[64,2048]{1,0:T(8,128)(2,1)S(1)}, bf16[64,2048]{1,0:T(8,128)(2,1)S(1)}, u32[]{:S(2)}, u32[]{:S(2)}) collective-permute-start(bf16[64,2048]{1,0:T(8,128)(2,1)S(1)} %fusion), channel_id=1, source_target_pairs={{0,2},{2,0},{4,6},{6,4},{8,10},{10,8},{12,14},{14,12},{1,3},{3,1},... | collective-permute-start | bytes 786440 | tf_op jit(solution)/shard_map/ppermute | solution.py:435
  (13 other events, 116.4 us)

commit v7 on v6

--- a/solution.py
+++ b/solution.py
@@ -154,7 +154,7 @@
             pltpu.VMEM((length, 2 * HD), jnp.bfloat16),
         ],
         compiler_params=limit(24),
-        cost_estimate=pl.CostEstimate(flops=160 * work, bytes_accessed=depth * rows * columns * 8, transcendentals=work // HD),
+        cost_estimate=pl.CostEstimate(flops=4 * work, bytes_accessed=depth * rows * columns * 8, transcendentals=work // HD),
         name="attend",
     )(core, starts, key_pos, *messages, *across)
 
@@ -163,16 +163,16 @@
     depth, blocks = len(context), len(weights)
     rows, columns = context[0].shape[0] // 2, context[0].shape[1]
     features = weights[0].shape[0]
-    shape = (depth, rows, blocks * features)
+    shape = (rows, blocks * features)
     if features % HD:
         weight = jnp.stack(weights)[jnp.argsort(place)]
         left = jnp.stack(context).reshape(depth, 2, rows, columns)
         result = jnp.einsum("dcrk,bfk->cdrbf", left, weight, preferred_element_type=jnp.float32)
-        result = narrow(result.reshape((2,) + shape))
-        return result[0], result[1]
+        result = narrow(result.reshape((2, depth) + shape))
+        return [[result[core, d] for d in range(depth)] for core in range(2)]
 
     def kernel(place_ref, *refs):
-        context_refs, weight_refs, out_refs = refs[:depth], refs[depth : depth + blocks], refs[-3:-1]
+        context_refs, weight_refs, out_refs = refs[:depth], refs[depth : depth + blocks], refs[-1 - 2 * depth : -1]
         left_ref = refs[-1]
         for d in range(depth):
             left_ref[2 * d * rows : 2 * (d + 1) * rows, :] = context_refs[d][...]
@@ -184,14 +184,15 @@
                 )
             ).reshape(depth, 2, rows, features)
             there = pl.ds(pl.multiple_of(place_ref[i] * features, HD), features)
-            for core in range(2):
-                out_refs[core][:, :, there] = part[:, core]
-
-    return pl.pallas_call(
-        kernel,
-        out_shape=[jax.ShapeDtypeStruct(shape, jnp.bfloat16)] * 2,
+            for d in range(depth):
+                for core in range(2):
+                    out_refs[core * depth + d][:, there] = part[d, core]
+
+    outs = pl.pallas_call(
+        kernel,
+        out_shape=[jax.ShapeDtypeStruct(shape, jnp.bfloat16)] * (2 * depth),
         in_specs=[smem] + [vmem] * (depth + blocks) + [unread] * len(before),
-        out_specs=[vmem, vmem],
+        out_specs=[vmem] * (2 * depth),
         scratch_shapes=[pltpu.VMEM((2 * depth * rows, columns), jnp.bfloat16)],
         compiler_params=limit(20),
         cost_estimate=pl.CostEstimate(
@@ -201,6 +202,7 @@
         ),
         name="project",
     )(place, *context, *weights, *before)
+    return outs[:depth], outs[depth:]
 
 
 def add_up(parts):
@@ -258,8 +260,8 @@
     kept, given = project(
         block.reshape(-1), context, [part for d in range(depth) for part in (weight[d], weight_across[d])], route[1:]
     )
-    chip = wide(kept) + wide(lax.ppermute(given, "exp", swap(2)))
-    parts = [stream, chip[0]]
+    chip = {d: wide(kept[d]) + wide(lax.ppermute(given[d], "exp", swap(2))) for d in steps + [0]}
+    parts = [wide(stream) + chip[0]]
     for d in steps:
         parts.append(lax.ppermute(narrow(chip[d]), "seq", ring(size, -d)))
     return *add_up(parts), route

time: 177 us -> 175 us (0.989)
  waiting for transfers between devices: 101 us -> 83.2 us
  starting transfers between devices: 40.6 us -> 53.6 us
    ppermute x3, starting transfers between devices: 0.3 us -> 9.12 us  [expert_block(): along.append(lax.ppermute(along[d], 'seq', ring(size, 1)))]
    ppermute x3, waiting for transfers between devices: 22.6 us -> 16.6 us  [attention_block(): parts.append(lax.ppermute(narrow(chip[d]), 'seq', ring(size, -d)))]
    ppermute x3, waiting for transfers between devices: 5.48 us -> 1.19 us  [expert_block(): across = lax.ppermute(along[d], 'seq', swap(size))]
    ppermute x3, waiting for transfers between devices: 20.6 us -> 17.9 us  [expert_block(): along.append(lax.ppermute(along[d], 'seq', ring(size, 1)))]
    ppermute x1 -> x4, waiting for transfers between devices: 2.65 us -> 0.52 us  [attention_block(): lax.ppermute(given[d], 'exp', swap(2))]
    ppermute x3, starting transfers between devices: 1.62 us -> 3.56 us  [expert_block(): across = lax.ppermute(along[d], 'seq', swap(size))]
    ppermute x3, waiting for transfers between devices: 3.36 us -> 1.47 us  [attention_block(): weight_across[d] = lax.ppermute(weight[d], 'seq', swap(size))]
    unnamed x14 -> x12, local copies, waits for them, and re-layouts: 2.25 us -> 3.86 us
  transfers between devices with their start and end apart: 40 -> 43, of which waited for: 21 -> 20; matrix products, arithmetic and copies ran while one was open for 1% -> 2% of each run, Pallas kernels for 5% -> 5%
where the time goes in v7:
time: 175 us; the launch traced here: 172 us
  waiting for transfers between devices  83.2 us (48%)
  starting transfers between devices  53.6 us (31%)
  Pallas kernels  27.6 us (16%)
  local copies, waits for them, and re-layouts  4.19 us (2%)
  other arithmetic  3.12 us (2%)
    ppermute x3, waiting for transfers between devices, expert_block(): along.append(lax.ppermute(along[d], 'seq', ring(size, 1)))  17.9 us
    ppermute x3, waiting for transfers between devices, attention_block(): parts.append(lax.ppermute(narrow(chip[d]), 'seq', ring(size, -d)))  16.6 us
    pallas_call x1, Pallas kernels, run_experts(): pl.pallas_call(kernel, out_shape=[jax.ShapeDtypeStruct((tokens, width), j...  15.1 us
    ppermute x3, waiting for transfers between devices, attention_block(): message[d] = lax.ppermute(message[d], 'seq', ring(size, d))  12.7 us
    ppermute x2, waiting for transfers between devices, expert_block(): lax.ppermute(narrow(pair[d][rows:]), 'seq', swap(size))  9.38 us
    ppermute x3, starting transfers between devices, expert_block(): along.append(lax.ppermute(along[d], 'seq', ring(size, 1)))  9.12 us
    ppermute x2, waiting for transfers between devices, expert_block(): total = total + wide(lax.ppermute(narrow(chip), 'seq', ring(size, -d)))  8.73 us
    ppermute x3, waiting for transfers between devices, attention_block(): weight[d] = lax.ppermute(weight[d], 'seq', ring(size, d))  7.62 us
  transfers between devices with their start and end apart: 43, of which 20 were waited for; matrix products, arithmetic and copies ran while one was open for 2% of the time, Pallas kernels for 5%

profile of v7, /device:TPU:0, one launch (start us, length us, event | category | flops | bytes accessed | tf_op | source)
XLA Modules:
  0.0 172.1 jit_solution(7213344106417991320)
XLA Ops:
  0.0 2.2 %pack_heads.1 = (bf16[144,768]{1,0:T(8,128)(2,1)}, bf16[144,768]{1,0:T(8,128)(2,1)}, bf16[144,768]{1,0:T(8,128)(2,1)}, bf16[144,768]{1,0:T(8,128)(2,1)}, bf16[144,256]{1,0:T(8,128)(2,1)}) custom-call(s32[1]{0:T(128)} %bitcast.5.z_ref, bf16[128,2048]{1,0:T(8,128)(2,1)} %query_ref.1, bf16[128,256]{1,0:T(8,128)(2,1)} %key_ref.1, bf16[128,256]{1,0:T(8,128)(2,1)} %value_ref.1, ...), custom_call_target="tpu_custom_call" | custom-call | tf_op jit(solution)/shard_map/pack_heads/pallas_call | solution.py:65
  2.2 3.0 %collective-permute-start.3 = (bf16[144,256]{1,0:T(8,128)(2,1)}, bf16[144,256]{1,0:T(8,128)(2,1)S(1)}, u32[]{:S(2)}, u32[]{:S(2)}) collective-permute-start(bf16[144,256]{1,0:T(8,128)(2,1)} %get-tuple-element.43), channel_id=1, source_target_pairs={{0,2},{2,0},{4,6},{6,4},{8,10},{10,8},{12,14},{14,12},{1,3},{3,1},... | collective-permute-start | bytes 221192 | tf_op jit(solution)/shard_map/ppermute | solution.py:244
  5.1 1.6 collective-permute-start
  6.7 2.6 %collective-permute-start.1 = (bf16[144,768]{1,0:T(8,128)(2,1)}, bf16[144,768]{1,0:T(8,128)(2,1)S(1)}, u32[]{:S(2)}, u32[]{:S(2)}) collective-permute-start(bf16[144,768]{1,0:T(8,128)(2,1)} %get-tuple-element.41), channel_id=1, source_target_pairs={{0,8},{2,10},{4,12},{6,14},{8,0},{10,2},{12,4},{14,6},{1,9},{3,11}... | collective-permute-start | bytes 663560 | tf_op jit(solution)/shard_map/ppermute | solution.py:241
  11.0 12.7 %collective-permute-done.1.refs_2_.refs_0_.refs_4_ = bf16[144,768]{1,0:T(8,128)(2,1)S(1)} collective-permute-done((bf16[144,768]{1,0:T(8,128)(2,1)}, bf16[144,768]{1,0:T(8,128)(2,1)S(1)}, u32[]{:S(2)}, u32[]{:S(2)}) %collective-permute-start.1) | collective-permute-done | bytes 221216 | tf_op jit(solution)/shard_map/ppermute | solution.py:241
  25.0 3.6 %collective-permute-start.8 = (bf16[256,512]{1,0:T(8,128)(2,1)S(1)}, bf16[256,512]{1,0:T(8,128)(2,1)S(1)}, u32[]{:S(2)}, u32[]{:S(2)}) collective-permute-start(bf16[256,512]{1,0:T(8,128)(2,1)S(1)} %get-tuple-element.49), channel_id=1, source_target_pairs={{0,4},{2,6},{4,8},{6,10},{8,12},{10,14},{12,0},{14,2},{1,5},{3,7},... | collective-permute-start | bytes 786440 | tf_op jit(solution)/shard_map/ppermute | solution.py:249
  28.6 3.3 %collective-permute-start.10 = (bf16[256,512]{1,0:T(8,128)(2,1)S(1)}, bf16[256,512]{1,0:T(8,128)(2,1)S(1)}, u32[]{:S(2)}, u32[]{:S(2)}) collective-permute-start(bf16[256,512]{1,0:T(8,128)(2,1)S(1)} %get-tuple-element.50), channel_id=1, source_target_pairs={{0,8},{2,10},{4,12},{6,14},{8,0},{10,2},{12,4},{14,6},{1,9},{3,11}... | collective-permute-start | bytes 786440 | tf_op jit(solution)/shard_map/ppermute | solution.py:249
  32.5 1.5 collective-permute-start.5
  34.1 2.5 %collective-permute-done.4.refs_5_.refs_3_ = bf16[144,256]{1,0:T(8,128)(2,1)S(1)} collective-permute-done((bf16[144,256]{1,0:T(8,128)(2,1)S(1)}, bf16[144,256]{1,0:T(8,128)(2,1)S(1)}, u32[]{:S(2)}, u32[]{:S(2)}) %collective-permute-start.4) | collective-permute-done | bytes 73760 | tf_op jit(solution)/shard_map/ppermute | solution.py:244
  40.2 7.6 %collective-permute-done.10.refs_8_ = bf16[256,512]{1,0:T(8,128)(2,1)S(1)} collective-permute-done((bf16[256,512]{1,0:T(8,128)(2,1)S(1)}, bf16[256,512]{1,0:T(8,128)(2,1)S(1)}, u32[]{:S(2)}, u32[]{:S(2)}) %collective-permute-start.10) | collective-permute-done | bytes 262176 | tf_op jit(solution)/shard_map/ppermute | solution.py:249
  48.3 1.5 collective-permute-start.13
  51.7 4.4 %attend.1 = (bf16[128,512]{1,0:T(8,128)(2,1)S(1)}, bf16[128,512]{1,0:T(8,128)(2,1)S(1)}, bf16[128,512]{1,0:T(8,128)(2,1)S(1)}, bf16[128,512]{1,0:T(8,128)(2,1)S(1)}) custom-call(s32[1]{0:T(128)} %bitcast.2.core_ref, s32[4]{0:T(128)S(1)} %multiply_bitcast_fusion.starts_ref, s32[1,1024]{1,0:T(1,128)S(1)} %bitcast.12, bf16[144,768]{1,0:T(8,128)(2,1)S(1)} %copy-done.2, ...), custom_call_target="tpu_custom_call" | custom-call | flops 1073741824 | bytes 2097152 | tf_op jit(solution)/shard_map/attend/pallas_call | solution.py:147
  56.2 3.9 %routing.1 = (bf16[4,4,48,256]{3,2,1,0:T(8,128)(2,1)S(1)}, bf16[4,256,192]{2,1,0:T(8,128)(2,1)S(1)}, f32[4,192,1]{2,1,0:T(8,128)S(1)}) custom-call(s32[1]{0:T(128)} %bitcast.8.first_ref, bf16[128,256]{1,0:T(8,128)(2,1)S(1)} %collect_meta.1.mine_ref, bf16[128,256]{1,0:T(8,128)(2,1)S(1)} %collective-permute-done.14.other_ref, ...), custom_call_target="tpu_custom_call" | custom-call | tf_op jit(solution)/shard_map/routing/pallas_call | solution.py:313
  61.5 1.8 %project.1 = (bf16[64,2048]{1,0:T(8,128)(2,1)S(1)}, bf16[64,2048]{1,0:T(8,128)(2,1)S(1)}, bf16[64,2048]{1,0:T(8,128)(2,1)S(1)}, bf16[64,2048]{1,0:T(8,128)(2,1)S...) custom-call(s32[8]{0:T(128)S(1)} %add.119.place_ref, ...), custom_call_target="tpu_custom_call" | custom-call | flops 1073741824 | bytes 6815744 | tf_op jit(solution)/shard_map/project/pallas_call | solution.py:191
  65.1 2.4 %collective-permute-start.17 = (bf16[64,2048]{1,0:T(8,128)(2,1)S(1)}, bf16[64,2048]{1,0:T(8,128)(2,1)S(1)}, u32[]{:S(2)}, u32[]{:S(2)}) collective-permute-start(bf16[64,2048]{1,0:T(8,128)(2,1)S(1)} %add_convert_fusion.3), channel_id=1, source_target_pairs={{0,8},{2,10},{4,12},{6,14},{8,0},{10,2},{12,4},{14,6},{1,9},{3,11}... | collective-permute-start | bytes 786440 | tf_op jit(solution)/shard_map/ppermute | solution.py:266
  67.5 3.3 %collective-permute-start.19 = (bf16[64,2048]{1,0:T(8,128)(2,1)S(1)}, bf16[64,2048]{1,0:T(8,128)(2,1)S(1)}, u32[]{:S(2)}, u32[]{:S(2)}) collective-permute-start(bf16[64,2048]{1,0:T(8,128)(2,1)S(1)} %add_convert_fusion.2), channel_id=1, source_target_pairs={{0,12},{2,14},{4,0},{6,2},{8,4},{10,6},{12,8},{14,10},{1,13},{3,15... | collective-permute-start | bytes 786440 | tf_op jit(solution)/shard_map/ppermute | solution.py:266
  72.1 8.7 %collective-permute-done.17.refs_1_ = bf16[64,2048]{1,0:T(8,128)(2,1)S(1)} collective-permute-done((bf16[64,2048]{1,0:T(8,128)(2,1)S(1)}, bf16[64,2048]{1,0:T(8,128)(2,1)S(1)}, u32[]{:S(2)}, u32[]{:S(2)}) %collective-permute-start.17) | collective-permute-done | bytes 262176 | tf_op jit(solution)/shard_map/ppermute | solution.py:266
  80.8 7.9 %collective-permute-done.21.refs_3_ = bf16[64,2048]{1,0:T(8,128)(2,1)S(1)} collective-permute-done((bf16[64,2048]{1,0:T(8,128)(2,1)S(1)}, bf16[64,2048]{1,0:T(8,128)(2,1)S(1)}, u32[]{:S(2)}, u32[]{:S(2)}) %collective-permute-start.21) | collective-permute-done | bytes 262176 | tf_op jit(solution)/shard_map/ppermute | solution.py:266
  88.8 3.2 %collective-permute-start.23 = (bf16[64,2048]{1,0:T(8,128)(2,1)S(1)}, bf16[64,2048]{1,0:T(8,128)(2,1)S(1)}, u32[]{:S(2)}, u32[]{:S(2)}) collective-permute-start(bf16[64,2048]{1,0:T(8,128)(2,1)S(1)} %get-tuple-element.64), channel_id=1, source_target_pairs={{0,4},{2,6},{4,8},{6,10},{8,12},{10,14},{12,0},{14,2},{1,5},{3,7},... | collective-permute-start | bytes 786440 | tf_op jit(solution)/shard_map/ppermute | solution.py:417
  93.4 5.0 %collective-permute-done.23 = bf16[64,2048]{1,0:T(8,128)(2,1)S(1)} collective-permute-done((bf16[64,2048]{1,0:T(8,128)(2,1)S(1)}, bf16[64,2048]{1,0:T(8,128)(2,1)S(1)}, u32[]{:S(2)}, u32[]{:S(2)}) %collective-permute-start.23) | collective-permute-done | bytes 262176 | tf_op jit(solution)/shard_map/ppermute | solution.py:417
  98.4 1.9 %collective-permute-start.25 = (bf16[64,2048]{1,0:T(8,128)(2,1)S(1)}, bf16[64,2048]{1,0:T(8,128)(2,1)S(1)}, u32[]{:S(2)}, u32[]{:S(2)}) collective-permute-start(bf16[64,2048]{1,0:T(8,128)(2,1)S(1)} %collective-permute-done.23), channel_id=1, source_target_pairs={{0,4},{2,6},{4,8},{6,10},{8,12},{10,14},{12,0},{14,2},{1,5},{3,7},... | collective-permute-start | bytes 786440 | tf_op jit(solution)/shard_map/ppermute | solution.py:417
  101.5 2.3 %collective-permute-start.28 = (bf16[64,2048]{1,0:T(8,128)(2,1)S(1)}, bf16[64,2048]{1,0:T(8,128)(2,1)S(1)}, u32[]{:S(2)}, u32[]{:S(2)}) collective-permute-start(bf16[64,2048]{1,0:T(8,128)(2,1)S(1)} %collective-permute-done.22), channel_id=1, source_target_pairs={{0,12},{2,14},{4,0},{6,2},{8,4},{10,6},{12,8},{14,10},{1,13},{3,15... | collective-permute-start | bytes 786440 | tf_op jit(solution)/shard_map/ppermute | solution.py:419
  103.9 5.5 %collective-permute-done.25 = bf16[64,2048]{1,0:T(8,128)(2,1)S(1)} collective-permute-done((bf16[64,2048]{1,0:T(8,128)(2,1)S(1)}, bf16[64,2048]{1,0:T(8,128)(2,1)S(1)}, u32[]{:S(2)}, u32[]{:S(2)}) %collective-permute-start.25) | collective-permute-done | bytes 262176 | tf_op jit(solution)/shard_map/ppermute | solution.py:417
  110.6 4.0 %collective-permute-start.27 = (bf16[64,2048]{1,0:T(8,128)(2,1)S(1)}, bf16[64,2048]{1,0:T(8,128)(2,1)S(1)}, u32[]{:S(2)}, u32[]{:S(2)}) collective-permute-start(bf16[64,2048]{1,0:T(8,128)(2,1)S(1)} %collective-permute-done.25), channel_id=1, source_target_pairs={{0,4},{2,6},{4,8},{6,10},{8,12},{10,14},{12,0},{14,2},{1,5},{3,7},... | collective-permute-start | bytes 786440 | tf_op jit(solution)/shard_map/ppermute | solution.py:417
  115.9 7.4 %collective-permute-done.27 = bf16[64,2048]{1,0:T(8,128)(2,1)S(1)} collective-permute-done((bf16[64,2048]{1,0:T(8,128)(2,1)S(1)}, bf16[64,2048]{1,0:T(8,128)(2,1)S(1)}, u32[]{:S(2)}, u32[]{:S(2)}) %collective-permute-start.27) | collective-permute-done | bytes 262176 | tf_op jit(solution)/shard_map/ppermute | solution.py:417
  123.4 1.9 %collective-permute-done.32.refs_7_ = bf16[128,2048]{1,0:T(8,128)(2,1)S(1)} collective-permute-done((bf16[128,2048]{1,0:T(8,128)(2,1)S(1)}, bf16[128,2048]{1,0:T(8,128)(2,1)S(1)}, u32[]{:S(2)}, u32[]{:S(2)}) %collective-permute-start.32) | collective-permute-done | bytes 524320 | tf_op jit(solution)/shard_map/ppermute | solution.py:425
  126.0 15.1 %experts.1 = (bf16[128,2048]{1,0:T(8,128)(2,1)S(1)}, bf16[128,2048]{1,0:T(8,128)(2,1)S(1)}, bf16[128,2048]{1,0:T(8,128)(2,1)S(1)}, bf16[128,2048]{1,0:T(8,128)(2...) custom-call(bf16[4,4,48,256]{3,2,1,0:T(8,128)(2,1)S(1)} %get-tuple-e, ...), custom_call_target="tpu_custom_call" | custom-call | flops 7247757312 | bytes 54525952 | tf_op jit(solution)/shard_map/experts/pallas_call | solution.py:389
  146.8 6.4 %collective-permute-done.37 = bf16[64,2048]{1,0:T(8,128)(2,1)S(1)} collective-permute-done((bf16[64,2048]{1,0:T(8,128)(2,1)S(1)}, bf16[64,2048]{1,0:T(8,128)(2,1)S(1)}, u32[]{:S(2)}, u32[]{:S(2)}) %collective-permute-start.37) | collective-permute-done | bytes 262176 | tf_op jit(solution)/shard_map/ppermute | solution.py:434
  153.3 1.8 %collective-permute-start.38 = (bf16[64,2048]{1,0:T(8,128)(2,1)S(1)}, bf16[64,2048]{1,0:T(8,128)(2,1)S(1)}, u32[]{:S(2)}, u32[]{:S(2)}) collective-permute-start(bf16[64,2048]{1,0:T(8,128)(2,1)S(1)} %fusion.2), channel_id=1, source_target_pairs={{0,8},{2,10},{4,12},{6,14},{8,0},{10,2},{12,4},{14,6},{1,9},{3,11}... | collective-permute-start | bytes 786440 | tf_op jit(solution)/shard_map/ppermute | solution.py:435
  155.1 2.9 %collective-permute-done.40 = bf16[64,2048]{1,0:T(8,128)(2,1)S(1)} collective-permute-done((bf16[64,2048]{1,0:T(8,128)(2,1)S(1)}, bf16[64,2048]{1,0:T(8,128)(2,1)S(1)}, u32[]{:S(2)}, u32[]{:S(2)}) %collective-permute-start.40) | collective-permute-done | bytes 262176 | tf_op jit(solution)/shard_map/ppermute | solution.py:434
  158.1 3.0 %collective-permute-start.41 = (bf16[64,2048]{1,0:T(8,128)(2,1)S(1)}, bf16[64,2048]{1,0:T(8,128)(2,1)S(1)}, u32[]{:S(2)}, u32[]{:S(2)}) collective-permute-start(bf16[64,2048]{1,0:T(8,128)(2,1)S(1)} %fusion.1), channel_id=1, source_target_pairs={{0,12},{2,14},{4,0},{6,2},{8,4},{10,6},{12,8},{14,10},{1,13},{3,15... | collective-permute-start | bytes 786440 | tf_op jit(solution)/shard_map/ppermute | solution.py:435
  162.4 8.0 %collective-permute-done.38 = bf16[64,2048]{1,0:T(8,128)(2,1)S(1)} collective-permute-done((bf16[64,2048]{1,0:T(8,128)(2,1)S(1)}, bf16[64,2048]{1,0:T(8,128)(2,1)S(1)}, u32[]{:S(2)}, u32[]{:S(2)}) %collective-permute-start.38) | collective-permute-done | bytes 262176 | tf_op jit(solution)/shard_map/ppermute | solution.py:435
  (104 shorter events, 28.8 us)
Async XLA Ops:
  2.2 29.7 %collective-permute-start.3 = (bf16[144,256]{1,0:T(8,128)(2,1)}, bf16[144,256]{1,0:T(8,128)(2,1)S(1)}, u32[]{:S(2)}, u32[]{:S(2)}) collective-permute-start(bf16[144,256]{1,0:T(8,128)(2,1)} %get-tuple-element.43), channel_id=1, source_target_pairs={{0,2},{2,0},{4,6},{6,4},{8,10},{10,8},{12,14},{14,12},{1,3},{3,1},... | collective-permute-start | bytes 221192 | tf_op jit(solution)/shard_map/ppermute | solution.py:244
  5.1 26.7 %collective-permute-start = (bf16[144,768]{1,0:T(8,128)(2,1)}, bf16[144,768]{1,0:T(8,128)(2,1)S(1)}, u32[]{:S(2)}, u32[]{:S(2)}) collective-permute-start(bf16[144,768]{1,0:T(8,128)(2,1)} %get-tuple-element.40), channel_id=1, source_target_pairs={{0,4},{2,6},{4,8},{6,10},{8,12},{10,14},{12,0},{14,2},{1,5},{3,7},... | collective-permute-start | bytes 663560 | tf_op jit(solution)/shard_map/ppermute | solution.py:241
  6.7 17.0 %collective-permute-start.1 = (bf16[144,768]{1,0:T(8,128)(2,1)}, bf16[144,768]{1,0:T(8,128)(2,1)S(1)}, u32[]{:S(2)}, u32[]{:S(2)}) collective-permute-start(bf16[144,768]{1,0:T(8,128)(2,1)} %get-tuple-element.41), channel_id=1, source_target_pairs={{0,8},{2,10},{4,12},{6,14},{8,0},{10,2},{12,4},{14,6},{1,9},{3,11}... | collective-permute-start | bytes 663560 | tf_op jit(solution)/shard_map/ppermute | solution.py:241
  9.3 23.2 %collective-permute-start.2 = (bf16[144,768]{1,0:T(8,128)(2,1)}, bf16[144,768]{1,0:T(8,128)(2,1)S(1)}, u32[]{:S(2)}, u32[]{:S(2)}) collective-permute-start(bf16[144,768]{1,0:T(8,128)(2,1)} %get-tuple-element.42), channel_id=1, source_target_pairs={{0,12},{2,14},{4,0},{6,2},{8,4},{10,6},{12,8},{14,10},{1,13},{3,15... | collective-permute-start | bytes 663560 | tf_op jit(solution)/shard_map/ppermute | solution.py:241
  25.0 13.9 %collective-permute-start.8 = (bf16[256,512]{1,0:T(8,128)(2,1)S(1)}, bf16[256,512]{1,0:T(8,128)(2,1)S(1)}, u32[]{:S(2)}, u32[]{:S(2)}) collective-permute-start(bf16[256,512]{1,0:T(8,128)(2,1)S(1)} %get-tuple-element.49), channel_id=1, source_target_pairs={{0,4},{2,6},{4,8},{6,10},{8,12},{10,14},{12,0},{14,2},{1,5},{3,7},... | collective-permute-start | bytes 786440 | tf_op jit(solution)/shard_map/ppermute | solution.py:249
  28.6 19.2 %collective-permute-start.10 = (bf16[256,512]{1,0:T(8,128)(2,1)S(1)}, bf16[256,512]{1,0:T(8,128)(2,1)S(1)}, u32[]{:S(2)}, u32[]{:S(2)}) collective-permute-start(bf16[256,512]{1,0:T(8,128)(2,1)S(1)} %get-tuple-element.50), channel_id=1, source_target_pairs={{0,8},{2,10},{4,12},{6,14},{8,0},{10,2},{12,4},{14,6},{1,9},{3,11}... | collective-permute-start | bytes 786440 | tf_op jit(solution)/shard_map/ppermute | solution.py:249
  31.9 16.4 %collective-permute-start.12 = (bf16[256,512]{1,0:T(8,128)(2,1)S(1)}, bf16[256,512]{1,0:T(8,128)(2,1)S(1)}, u32[]{:S(2)}, u32[]{:S(2)}) collective-permute-start(bf16[256,512]{1,0:T(8,128)(2,1)S(1)} %get-tuple-element.51), channel_id=1, source_target_pairs={{0,12},{2,14},{4,0},{6,2},{8,4},{10,6},{12,8},{14,10},{1,13},{3,15... | collective-permute-start | bytes 786440 | tf_op jit(solution)/shard_map/ppermute | solution.py:249
  36.6 13.3 %collective-permute-start.6 = (bf16[144,256]{1,0:T(8,128)(2,1)S(1)}, bf16[144,256]{1,0:T(8,128)(2,1)S(1)}, u32[]{:S(2)}, u32[]{:S(2)}) collective-permute-start(bf16[144,256]{1,0:T(8,128)(2,1)S(1)} %slice.52), channel_id=1, source_target_pairs={{0,2},{2,0},{4,6},{6,4},{8,10},{10,8},{12,14},{14,12},{1,3},{3,1},... | collective-permute-start | bytes 221192 | tf_op jit(solution)/shard_map/ppermute | solution.py:244
  38.2 18.0 %collective-permute-start.7 = (bf16[256,512]{1,0:T(8,128)(2,1)S(1)}, bf16[256,512]{1,0:T(8,128)(2,1)S(1)}, u32[]{:S(2)}, u32[]{:S(2)}) collective-permute-start(bf16[256,512]{1,0:T(8,128)(2,1)S(1)} %get-tuple-element.48.refs_4_), channel_id=1, source_target_pairs={{0,2},{2,0},{4,6},{6,4},{8,10},{10,8},{12,14},{14,12},{1,3},{3,1},... | collective-permute-start | bytes 786440 | tf_op jit(solution)/shard_map/ppermute | solution.py:247
  38.9 21.1 %collective-permute-start.9 = (bf16[256,512]{1,0:T(8,128)(2,1)S(1)}, bf16[256,512]{1,0:T(8,128)(2,1)S(1)}, u32[]{:S(2)}, u32[]{:S(2)}) collective-permute-start(bf16[256,512]{1,0:T(8,128)(2,1)S(1)} %collective-permute-done.8.refs_6_), channel_id=1, source_target_pairs={{0,2},{2,0},{4,6},{6,4},{8,10},{10,8},{12,14},{14,12},{1,3},{3,1},... | collective-permute-start | bytes 786440 | tf_op jit(solution)/shard_map/ppermute | solution.py:250
  47.8 12.3 %collective-permute-start.11 = (bf16[256,512]{1,0:T(8,128)(2,1)S(1)}, bf16[256,512]{1,0:T(8,128)(2,1)S(1)}, u32[]{:S(2)}, u32[]{:S(2)}) collective-permute-start(bf16[256,512]{1,0:T(8,128)(2,1)S(1)} %collective-permute-done.10.refs_8_), channel_id=1, source_target_pairs={{0,2},{2,0},{4,6},{6,4},{8,10},{10,8},{12,14},{14,12},{1,3},{3,1},... | collective-permute-start | bytes 786440 | tf_op jit(solution)/shard_map/ppermute | solution.py:250
  48.3 13.2 %collective-permute-start.13 = (bf16[256,512]{1,0:T(8,128)(2,1)S(1)}, bf16[256,512]{1,0:T(8,128)(2,1)S(1)}, u32[]{:S(2)}, u32[]{:S(2)}) collective-permute-start(bf16[256,512]{1,0:T(8,128)(2,1)S(1)} %collective-permute-done.12.refs_10_), channel_id=1, source_target_pairs={{0,2},{2,0},{4,6},{6,4},{8,10},{10,8},{12,14},{14,12},{1,3},{3,1},... | collective-permute-start | bytes 786440 | tf_op jit(solution)/shard_map/ppermute | solution.py:250
  63.5 7.6 %collective-permute-start.15 = (bf16[64,2048]{1,0:T(8,128)(2,1)S(1)}, bf16[64,2048]{1,0:T(8,128)(2,1)S(1)}, u32[]{:S(2)}, u32[]{:S(2)}) collective-permute-start(bf16[64,2048]{1,0:T(8,128)(2,1)S(1)} %get-tuple-element.55), channel_id=1, source_target_pairs={{0,1},{1,0},{2,3},{3,2},{4,5},{5,4},{6,7},{7,6},{8,9},{9,8},{10,11... | collective-permute-start | bytes 786440 | tf_op jit(solution)/shard_map/ppermute | solution.py:263
  64.0 6.8 %collective-permute-start.20 = (bf16[64,2048]{1,0:T(8,128)(2,1)S(1)}, bf16[64,2048]{1,0:T(8,128)(2,1)S(1)}, u32[]{:S(2)}, u32[]{:S(2)}) collective-permute-start(bf16[64,2048]{1,0:T(8,128)(2,1)S(1)} %get-tuple-element.61), channel_id=1, source_target_pairs={{0,1},{1,0},{2,3},{3,2},{4,5},{5,4},{6,7},{7,6},{8,9},{9,8},{10,11... | collective-permute-start | bytes 786440 | tf_op jit(solution)/shard_map/ppermute | solution.py:263
  65.1 15.7 %collective-permute-start.17 = (bf16[64,2048]{1,0:T(8,128)(2,1)S(1)}, bf16[64,2048]{1,0:T(8,128)(2,1)S(1)}, u32[]{:S(2)}, u32[]{:S(2)}) collective-permute-start(bf16[64,2048]{1,0:T(8,128)(2,1)S(1)} %add_convert_fusion.3), channel_id=1, source_target_pairs={{0,8},{2,10},{4,12},{6,14},{8,0},{10,2},{12,4},{14,6},{1,9},{3,11}... | collective-permute-start | bytes 786440 | tf_op jit(solution)/shard_map/ppermute | solution.py:266
  67.5 13.2 %collective-permute-start.19 = (bf16[64,2048]{1,0:T(8,128)(2,1)S(1)}, bf16[64,2048]{1,0:T(8,128)(2,1)S(1)}, u32[]{:S(2)}, u32[]{:S(2)}) collective-permute-start(bf16[64,2048]{1,0:T(8,128)(2,1)S(1)} %add_convert_fusion.2), channel_id=1, source_target_pairs={{0,12},{2,14},{4,0},{6,2},{8,4},{10,6},{12,8},{14,10},{1,13},{3,15... | collective-permute-start | bytes 786440 | tf_op jit(solution)/shard_map/ppermute | solution.py:266
  71.0 17.7 %collective-permute-start.21 = (bf16[64,2048]{1,0:T(8,128)(2,1)S(1)}, bf16[64,2048]{1,0:T(8,128)(2,1)S(1)}, u32[]{:S(2)}, u32[]{:S(2)}) collective-permute-start(bf16[64,2048]{1,0:T(8,128)(2,1)S(1)} %add_convert_fusion.1), channel_id=1, source_target_pairs={{0,4},{2,6},{4,8},{6,10},{8,12},{10,14},{12,0},{14,2},{1,5},{3,7},... | collective-permute-start | bytes 786440 | tf_op jit(solution)/shard_map/ppermute | solution.py:266
  88.8 9.6 %collective-permute-start.23 = (bf16[64,2048]{1,0:T(8,128)(2,1)S(1)}, bf16[64,2048]{1,0:T(8,128)(2,1)S(1)}, u32[]{:S(2)}, u32[]{:S(2)}) collective-permute-start(bf16[64,2048]{1,0:T(8,128)(2,1)S(1)} %get-tuple-element.64), channel_id=1, source_target_pairs={{0,4},{2,6},{4,8},{6,10},{8,12},{10,14},{12,0},{14,2},{1,5},{3,7},... | collective-permute-start | bytes 786440 | tf_op jit(solution)/shard_map/ppermute | solution.py:417
  92.0 9.4 %collective-permute-start.22 = (bf16[64,2048]{1,0:T(8,128)(2,1)S(1)}, bf16[64,2048]{1,0:T(8,128)(2,1)S(1)}, u32[]{:S(2)}, u32[]{:S(2)}) collective-permute-start(bf16[64,2048]{1,0:T(8,128)(2,1)S(1)} %get-tuple-element.64), channel_id=1, source_target_pairs={{0,2},{2,0},{4,6},{6,4},{8,10},{10,8},{12,14},{14,12},{1,3},{3,1},... | collective-permute-start | bytes 786440 | tf_op jit(solution)/shard_map/ppermute | solution.py:421
  98.4 11.0 %collective-permute-start.25 = (bf16[64,2048]{1,0:T(8,128)(2,1)S(1)}, bf16[64,2048]{1,0:T(8,128)(2,1)S(1)}, u32[]{:S(2)}, u32[]{:S(2)}) collective-permute-start(bf16[64,2048]{1,0:T(8,128)(2,1)S(1)} %collective-permute-done.23), channel_id=1, source_target_pairs={{0,4},{2,6},{4,8},{6,10},{8,12},{10,14},{12,0},{14,2},{1,5},{3,7},... | collective-permute-start | bytes 786440 | tf_op jit(solution)/shard_map/ppermute | solution.py:417
  100.3 10.2 %collective-permute-start.24 = (bf16[64,2048]{1,0:T(8,128)(2,1)S(1)}, bf16[64,2048]{1,0:T(8,128)(2,1)S(1)}, u32[]{:S(2)}, u32[]{:S(2)}) collective-permute-start(bf16[64,2048]{1,0:T(8,128)(2,1)S(1)} %collective-permute-done.23), channel_id=1, source_target_pairs={{0,2},{2,0},{4,6},{6,4},{8,10},{10,8},{12,14},{14,12},{1,3},{3,1},... | collective-permute-start | bytes 786440 | tf_op jit(solution)/shard_map/ppermute | solution.py:421
  101.5 22.0 %collective-permute-start.29 = (bf16[128,2048]{1,0:T(8,128)(2,1)S(1)}, bf16[128,2048]{1,0:T(8,128)(2,1)S(1)}, u32[]{:S(2)}, u32[]{:S(2)}) collective-permute-start(bf16[128,2048]{1,0:T(8,128)(2,1)S(1)} %constant_dynamic-update-slice_fusion.refs_0_), channel_id=1, source_target_pairs={{0,1},{1,0},{2,3},{3,2},{4,5},{5,4},{6,7},{7,6},{8,9},{9,8},{10,11... | collective-permute-start | bytes 1572872 | tf_op jit(solution)/shard_map/ppermute | solution.py:425
  101.5 21.8 %collective-permute-start.28 = (bf16[64,2048]{1,0:T(8,128)(2,1)S(1)}, bf16[64,2048]{1,0:T(8,128)(2,1)S(1)}, u32[]{:S(2)}, u32[]{:S(2)}) collective-permute-start(bf16[64,2048]{1,0:T(8,128)(2,1)S(1)} %collective-permute-done.22), channel_id=1, source_target_pairs={{0,12},{2,14},{4,0},{6,2},{8,4},{10,6},{12,8},{14,10},{1,13},{3,15... | collective-permute-start | bytes 786440 | tf_op jit(solution)/shard_map/ppermute | solution.py:419
  110.5 12.9 %collective-permute-start.30 = (bf16[128,2048]{1,0:T(8,128)(2,1)S(1)}, bf16[128,2048]{1,0:T(8,128)(2,1)S(1)}, u32[]{:S(2)}, u32[]{:S(2)}) collective-permute-start(bf16[128,2048]{1,0:T(8,128)(2,1)S(1)} %constant_dynamic-update-slice_fusion.2.refs_1_), channel_id=1, source_target_pairs={{0,1},{1,0},{2,3},{3,2},{4,5},{5,4},{6,7},{7,6},{8,9},{9,8},{10,11... | collective-permute-start | bytes 1572872 | tf_op jit(solution)/shard_map/ppermute | solution.py:425
  110.6 12.7 %collective-permute-start.27 = (bf16[64,2048]{1,0:T(8,128)(2,1)S(1)}, bf16[64,2048]{1,0:T(8,128)(2,1)S(1)}, u32[]{:S(2)}, u32[]{:S(2)}) collective-permute-start(bf16[64,2048]{1,0:T(8,128)(2,1)S(1)} %collective-permute-done.25), channel_id=1, source_target_pairs={{0,4},{2,6},{4,8},{6,10},{8,12},{10,14},{12,0},{14,2},{1,5},{3,7},... | collective-permute-start | bytes 786440 | tf_op jit(solution)/shard_map/ppermute | solution.py:417
  115.8 7.6 %collective-permute-start.31 = (bf16[128,2048]{1,0:T(8,128)(2,1)S(1)}, bf16[128,2048]{1,0:T(8,128)(2,1)S(1)}, u32[]{:S(2)}, u32[]{:S(2)}) collective-permute-start(bf16[128,2048]{1,0:T(8,128)(2,1)S(1)} %constant_dynamic-update-slice_fusion.4.refs_2_), channel_id=1, source_target_pairs={{0,1},{1,0},{2,3},{3,2},{4,5},{5,4},{6,7},{7,6},{8,9},{9,8},{10,11... | collective-permute-start | bytes 1572872 | tf_op jit(solution)/shard_map/ppermute | solution.py:425
  143.2 17.9 %collective-permute-start.35 = (bf16[128,2048]{1,0:T(8,128)(2,1)S(1)}, bf16[128,2048]{1,0:T(8,128)(2,1)S(1)}, u32[]{:S(2)}, u32[]{:S(2)}) collective-permute-start(bf16[128,2048]{1,0:T(8,128)(2,1)S(1)} %add_convert_fusion), channel_id=1, source_target_pairs={{0,4},{2,6},{4,8},{6,10},{8,12},{10,14},{12,0},{14,2},{1,5},{3,7},... | collective-permute-start | bytes 1572872 | tf_op jit(solution)/shard_map/ppermute | solution.py:430
  144.0 9.2 %collective-permute-start.37 = (bf16[64,2048]{1,0:T(8,128)(2,1)S(1)}, bf16[64,2048]{1,0:T(8,128)(2,1)S(1)}, u32[]{:S(2)}, u32[]{:S(2)}) collective-permute-start(bf16[64,2048]{1,0:T(8,128)(2,1)S(1)} %slice.87), channel_id=1, source_target_pairs={{0,2},{2,0},{4,6},{6,4},{8,10},{10,8},{12,14},{14,12},{1,3},{3,1},... | collective-permute-start | bytes 786440 | tf_op jit(solution)/shard_map/ppermute | solution.py:434
  145.5 12.5 %collective-permute-start.40 = (bf16[64,2048]{1,0:T(8,128)(2,1)S(1)}, bf16[64,2048]{1,0:T(8,128)(2,1)S(1)}, u32[]{:S(2)}, u32[]{:S(2)}) collective-permute-start(bf16[64,2048]{1,0:T(8,128)(2,1)S(1)} %slice.86), channel_id=1, source_target_pairs={{0,2},{2,0},{4,6},{6,4},{8,10},{10,8},{12,14},{14,12},{1,3},{3,1},... | collective-permute-start | bytes 786440 | tf_op jit(solution)/shard_map/ppermute | solution.py:434
  153.3 17.1 %collective-permute-start.38 = (bf16[64,2048]{1,0:T(8,128)(2,1)S(1)}, bf16[64,2048]{1,0:T(8,128)(2,1)S(1)}, u32[]{:S(2)}, u32[]{:S(2)}) collective-permute-start(bf16[64,2048]{1,0:T(8,128)(2,1)S(1)} %fusion.2), channel_id=1, source_target_pairs={{0,8},{2,10},{4,12},{6,14},{8,0},{10,2},{12,4},{14,6},{1,9},{3,11}... | collective-permute-start | bytes 786440 | tf_op jit(solution)/shard_map/ppermute | solution.py:435
  158.1 13.1 %collective-permute-start.41 = (bf16[64,2048]{1,0:T(8,128)(2,1)S(1)}, bf16[64,2048]{1,0:T(8,128)(2,1)S(1)}, u32[]{:S(2)}, u32[]{:S(2)}) collective-permute-start(bf16[64,2048]{1,0:T(8,128)(2,1)S(1)} %fusion.1), channel_id=1, source_target_pairs={{0,12},{2,14},{4,0},{6,2},{8,4},{10,6},{12,8},{14,10},{1,13},{3,15... | collective-permute-start | bytes 786440 | tf_op jit(solution)/shard_map/ppermute | solution.py:435
  161.3 9.9 %collective-permute-start.42 = (bf16[64,2048]{1,0:T(8,128)(2,1)S(1)}, bf16[64,2048]{1,0:T(8,128)(2,1)S(1)}, u32[]{:S(2)}, u32[]{:S(2)}) collective-permute-start(bf16[64,2048]{1,0:T(8,128)(2,1)S(1)} %fusion), channel_id=1, source_target_pairs={{0,2},{2,0},{4,6},{6,4},{8,10},{10,8},{12,14},{14,12},{1,3},{3,1},... | collective-permute-start | bytes 786440 | tf_op jit(solution)/shard_map/ppermute | solution.py:437
  (15 other events, 45.9 us)

commit v8 on v7

--- a/solution.py
+++ b/solution.py
@@ -324,9 +324,11 @@
     )(first.astype(jnp.int32).reshape(1), *meta, *before)
 
 
-def run_experts(mine, other, select, spread, row_gate, norm_gain, expert_in, expert_out):
-    subs = len(mine)
-    tokens, width = mine[0].shape
+def run_experts(pieces, select, spread, row_gate, norm_gain, expert_in, expert_out):
+    subs = len(pieces)
+    counts = [len(arrays) for arrays in pieces]
+    flat = [array for arrays in pieces for array in arrays]
+    tokens, width = sum(array.shape[0] for array in pieces[0]) // 2, flat[0].shape[1]
     local_experts, hidden, _ = expert_out.shape
     slots = select.shape[2]
     held = min(local_experts, 2)
@@ -334,9 +336,9 @@
     room = 8 * subs * tokens * width + 6 * held * hidden * width + 4 * local_experts * subs * slots * width
 
     def kernel(select_ref, spread_ref, gate_ref, gain_ref, wi_ref, wo_ref, *refs):
-        mine_refs, other_refs = refs[:subs], refs[subs : 2 * subs]
-        kept_refs, given_refs = refs[2 * subs : 3 * subs], refs[3 * subs : 4 * subs]
-        first, second, x, xg, res, sem = refs[4 * subs :]
+        piece_refs, refs = refs[: len(flat)], refs[len(flat) :]
+        kept_refs, given_refs = refs[:subs], refs[subs : 2 * subs]
+        first, second, x, xg, res, sem = refs[2 * subs :]
 
         def copy(e, part):
             if part < 2:
@@ -355,8 +357,10 @@
             copy(0, part).start()
         for s in range(subs):
             choose = select_ref[:, s].reshape(local_experts * slots, 2 * tokens)
-            x[s % 2, :tokens, :] = mine_refs[s][...]
-            x[s % 2, tokens:, :] = other_refs[s][...]
+            at = 0
+            for ref in piece_refs[sum(counts[:s]) : sum(counts[: s + 1])]:
+                x[s % 2, at : at + ref.shape[0], :] = ref[...]
+                at += ref.shape[0]
             picked = jnp.dot(choose, x[s % 2], preferred_element_type=jnp.float32)
             scale = lax.rsqrt(jnp.sum(picked * picked, axis=1, keepdims=True) * (1.0 / width) + 1e-06)
             rows = narrow(picked * scale * gain_ref[...])
@@ -389,7 +393,7 @@
     outs = pl.pallas_call(
         kernel,
         out_shape=[jax.ShapeDtypeStruct((tokens, width), jnp.bfloat16)] * (2 * subs),
-        in_specs=[vmem] * 4 + [unread] * 2 + [vmem] * (2 * subs),
+        in_specs=[vmem] * 4 + [unread] * 2 + [vmem] * len(flat),
         out_specs=[vmem] * (2 * subs),
         scratch_shapes=[
             pltpu.VMEM((held, 2, width, hidden), jnp.bfloat16),
@@ -402,7 +406,7 @@
         compiler_params=limit(room * 19 // 16 // 2**20),
         cost_estimate=pl.CostEstimate(flops=flops, bytes_accessed=moved, transcendentals=0),
         name="experts",
-    )(select, spread, row_gate, norm_gain.reshape(1, -1), expert_in, expert_out, *mine, *other)
+    )(select, spread, row_gate, norm_gain.reshape(1, -1), expert_in, expert_out, *flat)
     return outs[:subs], outs[subs:]
 
 
@@ -411,7 +415,7 @@
     depth = size // 2
     rows = mixed.shape[0]
 
-    along, mine, other = [rounded], [], []
+    along, pieces = [rounded], []
     for d in range(depth):
         if d + 1 < depth:
             along.append(lax.ppermute(along[d], "seq", ring(size, 1)))
@@ -421,9 +425,11 @@
             across = lax.ppermute(along[d], "seq", swap(size))
         if d == 0:
             first = across
-        mine.append(jnp.concatenate([along[d], across]))
-        other.append(lax.ppermute(mine[d], "exp", swap(2)))
-    kept, given = run_experts(mine, other, *route, norm_gain, expert_in, expert_out)
+        mine = [along[d], across]
+        if d + 1 < depth:
+            mine = [jnp.concatenate(mine)]
+        pieces.append(mine + [lax.ppermute(part, "exp", swap(2)) for part in mine])
+    kept, given = run_experts(pieces, *route, norm_gain, expert_in, expert_out)
 
     pair = [wide(kept[d]) + wide(lax.ppermute(given[d], "exp", swap(2))) for d in range(depth)]
     last = depth - 1

time: 175 us -> 174 us (level)
    unnamed x12 -> x11, local copies, waits for them, and re-layouts: 3.86 us -> 3.84 us
  transfers between devices with their start and end apart: 43 -> 44, of which waited for: 20 -> 20; matrix products, arithmetic and copies ran while one was open for 2% -> 2% of each run, Pallas kernels for 5% -> 5%
where the time goes in v8:
time: 174 us; the launch traced here: 171 us
  waiting for transfers between devices  82.3 us (47%)
  starting transfers between devices  54 us (31%)
  Pallas kernels  27.1 us (16%)
  local copies, waits for them, and re-layouts  4.16 us (2%)
  other arithmetic  3.14 us (2%)
    ppermute x3, waiting for transfers between devices, expert_block(): along.append(lax.ppermute(along[d], 'seq', ring(size, 1)))  17.4 us
    ppermute x3, waiting for transfers between devices, attention_block(): parts.append(lax.ppermute(narrow(chip[d]), 'seq', ring(size, -d)))  16.6 us
    pallas_call x1, Pallas kernels, run_experts(): pl.pallas_call(kernel, out_shape=[jax.ShapeDtypeStruct((tokens, width), j...  14.6 us
    ppermute x3, waiting for transfers between devices, attention_block(): message[d] = lax.ppermute(message[d], 'seq', ring(size, d))  12.7 us
    ppermute x2, waiting for transfers between devices, expert_block(): lax.ppermute(narrow(pair[d][rows:]), 'seq', swap(size))  9.4 us
    ppermute x3, starting transfers between devices, expert_block(): along.append(lax.ppermute(along[d], 'seq', ring(size, 1)))  9.07 us
    ppermute x2, waiting for transfers between devices, expert_block(): total = total + wide(lax.ppermute(narrow(chip), 'seq', ring(size, -d)))  8.73 us
    ppermute x3, waiting for transfers between devices, attention_block(): weight[d] = lax.ppermute(weight[d], 'seq', ring(size, d))  7.62 us
  transfers between devices with their start and end apart: 44, of which 20 were waited for; matrix products, arithmetic and copies ran while one was open for 2% of the time, Pallas kernels for 5%

profile of v8, /device:TPU:0, one launch (start us, length us, event | category | flops | bytes accessed | tf_op | source)
XLA Modules:
  0.0 171.1 jit_solution(13711831580942622605)
XLA Ops:
  0.0 2.2 %pack_heads.1 = (bf16[144,768]{1,0:T(8,128)(2,1)}, bf16[144,768]{1,0:T(8,128)(2,1)}, bf16[144,768]{1,0:T(8,128)(2,1)}, bf16[144,768]{1,0:T(8,128)(2,1)}, bf16[144,256]{1,0:T(8,128)(2,1)}) custom-call(s32[1]{0:T(128)} %bitcast.5.z_ref, bf16[128,2048]{1,0:T(8,128)(2,1)} %query_ref.1, bf16[128,256]{1,0:T(8,128)(2,1)} %key_ref.1, bf16[128,256]{1,0:T(8,128)(2,1)} %value_ref.1, ...), custom_call_target="tpu_custom_call" | custom-call | tf_op jit(solution)/shard_map/pack_heads/pallas_call | solution.py:65
  2.2 3.0 %collective-permute-start.3 = (bf16[144,256]{1,0:T(8,128)(2,1)}, bf16[144,256]{1,0:T(8,128)(2,1)S(1)}, u32[]{:S(2)}, u32[]{:S(2)}) collective-permute-start(bf16[144,256]{1,0:T(8,128)(2,1)} %get-tuple-element.43), channel_id=1, source_target_pairs={{0,2},{2,0},{4,6},{6,4},{8,10},{10,8},{12,14},{14,12},{1,3},{3,1},... | collective-permute-start | bytes 221192 | tf_op jit(solution)/shard_map/ppermute | solution.py:244
  5.2 1.6 collective-permute-start
  6.7 2.6 %collective-permute-start.1 = (bf16[144,768]{1,0:T(8,128)(2,1)}, bf16[144,768]{1,0:T(8,128)(2,1)S(1)}, u32[]{:S(2)}, u32[]{:S(2)}) collective-permute-start(bf16[144,768]{1,0:T(8,128)(2,1)} %get-tuple-element.41), channel_id=1, source_target_pairs={{0,8},{2,10},{4,12},{6,14},{8,0},{10,2},{12,4},{14,6},{1,9},{3,11}... | collective-permute-start | bytes 663560 | tf_op jit(solution)/shard_map/ppermute | solution.py:241
  11.0 12.7 %collective-permute-done.1.refs_2_.refs_0_.refs_4_ = bf16[144,768]{1,0:T(8,128)(2,1)S(1)} collective-permute-done((bf16[144,768]{1,0:T(8,128)(2,1)}, bf16[144,768]{1,0:T(8,128)(2,1)S(1)}, u32[]{:S(2)}, u32[]{:S(2)}) %collective-permute-start.1) | collective-permute-done | bytes 221216 | tf_op jit(solution)/shard_map/ppermute | solution.py:241
  25.0 3.6 %collective-permute-start.8 = (bf16[256,512]{1,0:T(8,128)(2,1)S(1)}, bf16[256,512]{1,0:T(8,128)(2,1)S(1)}, u32[]{:S(2)}, u32[]{:S(2)}) collective-permute-start(bf16[256,512]{1,0:T(8,128)(2,1)S(1)} %get-tuple-element.49), channel_id=1, source_target_pairs={{0,4},{2,6},{4,8},{6,10},{8,12},{10,14},{12,0},{14,2},{1,5},{3,7},... | collective-permute-start | bytes 786440 | tf_op jit(solution)/shard_map/ppermute | solution.py:249
  28.6 3.3 %collective-permute-start.10 = (bf16[256,512]{1,0:T(8,128)(2,1)S(1)}, bf16[256,512]{1,0:T(8,128)(2,1)S(1)}, u32[]{:S(2)}, u32[]{:S(2)}) collective-permute-start(bf16[256,512]{1,0:T(8,128)(2,1)S(1)} %get-tuple-element.50), channel_id=1, source_target_pairs={{0,8},{2,10},{4,12},{6,14},{8,0},{10,2},{12,4},{14,6},{1,9},{3,11}... | collective-permute-start | bytes 786440 | tf_op jit(solution)/shard_map/ppermute | solution.py:249
  32.5 1.5 collective-permute-start.5
  34.1 2.5 %collective-permute-done.4.refs_5_.refs_3_ = bf16[144,256]{1,0:T(8,128)(2,1)S(1)} collective-permute-done((bf16[144,256]{1,0:T(8,128)(2,1)S(1)}, bf16[144,256]{1,0:T(8,128)(2,1)S(1)}, u32[]{:S(2)}, u32[]{:S(2)}) %collective-permute-start.4) | collective-permute-done | bytes 73760 | tf_op jit(solution)/shard_map/ppermute | solution.py:244
  40.2 7.6 %collective-permute-done.10.refs_8_ = bf16[256,512]{1,0:T(8,128)(2,1)S(1)} collective-permute-done((bf16[256,512]{1,0:T(8,128)(2,1)S(1)}, bf16[256,512]{1,0:T(8,128)(2,1)S(1)}, u32[]{:S(2)}, u32[]{:S(2)}) %collective-permute-start.10) | collective-permute-done | bytes 262176 | tf_op jit(solution)/shard_map/ppermute | solution.py:249
  48.3 1.5 collective-permute-start.13
  51.7 4.4 %attend.1 = (bf16[128,512]{1,0:T(8,128)(2,1)S(1)}, bf16[128,512]{1,0:T(8,128)(2,1)S(1)}, bf16[128,512]{1,0:T(8,128)(2,1)S(1)}, bf16[128,512]{1,0:T(8,128)(2,1)S(1)}) custom-call(s32[1]{0:T(128)} %bitcast.2.core_ref, s32[4]{0:T(128)S(1)} %multiply_bitcast_fusion.starts_ref, s32[1,1024]{1,0:T(1,128)S(1)} %bitcast.12, bf16[144,768]{1,0:T(8,128)(2,1)S(1)} %copy-done.2, ...), custom_call_target="tpu_custom_call" | custom-call | flops 1073741824 | bytes 2097152 | tf_op jit(solution)/shard_map/attend/pallas_call | solution.py:147
  56.2 3.9 %routing.1 = (bf16[4,4,48,256]{3,2,1,0:T(8,128)(2,1)S(1)}, bf16[4,256,192]{2,1,0:T(8,128)(2,1)S(1)}, f32[4,192,1]{2,1,0:T(8,128)S(1)}) custom-call(s32[1]{0:T(128)} %bitcast.8.first_ref, bf16[128,256]{1,0:T(8,128)(2,1)S(1)} %collect_meta.1.mine_ref, bf16[128,256]{1,0:T(8,128)(2,1)S(1)} %collective-permute-done.14.other_ref, ...), custom_call_target="tpu_custom_call" | custom-call | tf_op jit(solution)/shard_map/routing/pallas_call | solution.py:313
  61.6 1.8 %project.1 = (bf16[64,2048]{1,0:T(8,128)(2,1)S(1)}, bf16[64,2048]{1,0:T(8,128)(2,1)S(1)}, bf16[64,2048]{1,0:T(8,128)(2,1)S(1)}, bf16[64,2048]{1,0:T(8,128)(2,1)S...) custom-call(s32[8]{0:T(128)S(1)} %add.119.place_ref, ...), custom_call_target="tpu_custom_call" | custom-call | flops 1073741824 | bytes 6815744 | tf_op jit(solution)/shard_map/project/pallas_call | solution.py:191
  65.1 2.4 %collective-permute-start.17 = (bf16[64,2048]{1,0:T(8,128)(2,1)S(1)}, bf16[64,2048]{1,0:T(8,128)(2,1)S(1)}, u32[]{:S(2)}, u32[]{:S(2)}) collective-permute-start(bf16[64,2048]{1,0:T(8,128)(2,1)S(1)} %add_convert_fusion.3), channel_id=1, source_target_pairs={{0,8},{2,10},{4,12},{6,14},{8,0},{10,2},{12,4},{14,6},{1,9},{3,11}... | collective-permute-start | bytes 786440 | tf_op jit(solution)/shard_map/ppermute | solution.py:266
  67.6 3.3 %collective-permute-start.19 = (bf16[64,2048]{1,0:T(8,128)(2,1)S(1)}, bf16[64,2048]{1,0:T(8,128)(2,1)S(1)}, u32[]{:S(2)}, u32[]{:S(2)}) collective-permute-start(bf16[64,2048]{1,0:T(8,128)(2,1)S(1)} %add_convert_fusion.2), channel_id=1, source_target_pairs={{0,12},{2,14},{4,0},{6,2},{8,4},{10,6},{12,8},{14,10},{1,13},{3,15... | collective-permute-start | bytes 786440 | tf_op jit(solution)/shard_map/ppermute | solution.py:266
  72.1 8.7 %collective-permute-done.17.refs_1_ = bf16[64,2048]{1,0:T(8,128)(2,1)S(1)} collective-permute-done((bf16[64,2048]{1,0:T(8,128)(2,1)S(1)}, bf16[64,2048]{1,0:T(8,128)(2,1)S(1)}, u32[]{:S(2)}, u32[]{:S(2)}) %collective-permute-start.17) | collective-permute-done | bytes 262176 | tf_op jit(solution)/shard_map/ppermute | solution.py:266
  80.8 7.9 %collective-permute-done.21.refs_3_ = bf16[64,2048]{1,0:T(8,128)(2,1)S(1)} collective-permute-done((bf16[64,2048]{1,0:T(8,128)(2,1)S(1)}, bf16[64,2048]{1,0:T(8,128)(2,1)S(1)}, u32[]{:S(2)}, u32[]{:S(2)}) %collective-permute-start.21) | collective-permute-done | bytes 262176 | tf_op jit(solution)/shard_map/ppermute | solution.py:266
  88.8 3.2 %collective-permute-start.24 = (bf16[64,2048]{1,0:T(8,128)(2,1)S(1)}, bf16[64,2048]{1,0:T(8,128)(2,1)S(1)}, u32[]{:S(2)}, u32[]{:S(2)}) collective-permute-start(bf16[64,2048]{1,0:T(8,128)(2,1)S(1)} %get-tuple-element.64), channel_id=1, source_target_pairs={{0,4},{2,6},{4,8},{6,10},{8,12},{10,14},{12,0},{14,2},{1,5},{3,7},... | collective-permute-start | bytes 786440 | tf_op jit(solution)/shard_map/ppermute | solution.py:421
  93.4 5.0 %collective-permute-done.24 = bf16[64,2048]{1,0:T(8,128)(2,1)S(1)} collective-permute-done((bf16[64,2048]{1,0:T(8,128)(2,1)S(1)}, bf16[64,2048]{1,0:T(8,128)(2,1)S(1)}, u32[]{:S(2)}, u32[]{:S(2)}) %collective-permute-start.24) | collective-permute-done | bytes 262176 | tf_op jit(solution)/shard_map/ppermute | solution.py:421
  98.4 1.9 %collective-permute-start.27 = (bf16[64,2048]{1,0:T(8,128)(2,1)S(1)}, bf16[64,2048]{1,0:T(8,128)(2,1)S(1)}, u32[]{:S(2)}, u32[]{:S(2)}) collective-permute-start(bf16[64,2048]{1,0:T(8,128)(2,1)S(1)} %collective-permute-done.24), channel_id=1, source_target_pairs={{0,4},{2,6},{4,8},{6,10},{8,12},{10,14},{12,0},{14,2},{1,5},{3,7},... | collective-permute-start | bytes 786440 | tf_op jit(solution)/shard_map/ppermute | solution.py:421
  101.6 2.3 %collective-permute-start.31 = (bf16[64,2048]{1,0:T(8,128)(2,1)S(1)}, bf16[64,2048]{1,0:T(8,128)(2,1)S(1)}, u32[]{:S(2)}, u32[]{:S(2)}) collective-permute-start(bf16[64,2048]{1,0:T(8,128)(2,1)S(1)} %collective-permute-done.22), channel_id=1, source_target_pairs={{0,12},{2,14},{4,0},{6,2},{8,4},{10,6},{12,8},{14,10},{1,13},{3,15... | collective-permute-start | bytes 786440 | tf_op jit(solution)/shard_map/ppermute | solution.py:423
  103.9 5.5 %collective-permute-done.27 = bf16[64,2048]{1,0:T(8,128)(2,1)S(1)} collective-permute-done((bf16[64,2048]{1,0:T(8,128)(2,1)S(1)}, bf16[64,2048]{1,0:T(8,128)(2,1)S(1)}, u32[]{:S(2)}, u32[]{:S(2)}) %collective-permute-start.27) | collective-permute-done | bytes 262176 | tf_op jit(solution)/shard_map/ppermute | solution.py:421
  110.6 4.0 %collective-permute-start.30 = (bf16[64,2048]{1,0:T(8,128)(2,1)S(1)}, bf16[64,2048]{1,0:T(8,128)(2,1)S(1)}, u32[]{:S(2)}, u32[]{:S(2)}) collective-permute-start(bf16[64,2048]{1,0:T(8,128)(2,1)S(1)} %collective-permute-done.27), channel_id=1, source_target_pairs={{0,4},{2,6},{4,8},{6,10},{8,12},{10,14},{12,0},{14,2},{1,5},{3,7},... | collective-permute-start | bytes 786440 | tf_op jit(solution)/shard_map/ppermute | solution.py:421
  116.4 6.9 %collective-permute-done.30.refs_6_ = bf16[64,2048]{1,0:T(8,128)(2,1)S(1)} collective-permute-done((bf16[64,2048]{1,0:T(8,128)(2,1)S(1)}, bf16[64,2048]{1,0:T(8,128)(2,1)S(1)}, u32[]{:S(2)}, u32[]{:S(2)}) %collective-permute-start.30) | collective-permute-done | bytes 262176 | tf_op jit(solution)/shard_map/ppermute | solution.py:421
  123.3 1.5 collective-permute-done.32.refs_8_
  125.5 14.6 %experts.1 = (bf16[128,2048]{1,0:T(8,128)(2,1)S(1)}, bf16[128,2048]{1,0:T(8,128)(2,1)S(1)}, bf16[128,2048]{1,0:T(8,128)(2,1)S(1)}, bf16[128,2048]{1,0:T(8,128)(2...) custom-call(bf16[4,4,48,256]{3,2,1,0:T(8,128)(2,1)S(1)} %get-tuple-e, ...), custom_call_target="tpu_custom_call" | custom-call | flops 7247757312 | bytes 54525952 | tf_op jit(solution)/shard_map/experts/pallas_call | solution.py:393
  145.7 6.5 %collective-permute-done.38 = bf16[64,2048]{1,0:T(8,128)(2,1)S(1)} collective-permute-done((bf16[64,2048]{1,0:T(8,128)(2,1)S(1)}, bf16[64,2048]{1,0:T(8,128)(2,1)S(1)}, u32[]{:S(2)}, u32[]{:S(2)}) %collective-permute-start.38) | collective-permute-done | bytes 262176 | tf_op jit(solution)/shard_map/ppermute | solution.py:440
  152.3 1.8 %collective-permute-start.39 = (bf16[64,2048]{1,0:T(8,128)(2,1)S(1)}, bf16[64,2048]{1,0:T(8,128)(2,1)S(1)}, u32[]{:S(2)}, u32[]{:S(2)}) collective-permute-start(bf16[64,2048]{1,0:T(8,128)(2,1)S(1)} %fusion.2), channel_id=1, source_target_pairs={{0,8},{2,10},{4,12},{6,14},{8,0},{10,2},{12,4},{14,6},{1,9},{3,11}... | collective-permute-start | bytes 786440 | tf_op jit(solution)/shard_map/ppermute | solution.py:441
  154.1 2.9 %collective-permute-done.41 = bf16[64,2048]{1,0:T(8,128)(2,1)S(1)} collective-permute-done((bf16[64,2048]{1,0:T(8,128)(2,1)S(1)}, bf16[64,2048]{1,0:T(8,128)(2,1)S(1)}, u32[]{:S(2)}, u32[]{:S(2)}) %collective-permute-start.41) | collective-permute-done | bytes 262176 | tf_op jit(solution)/shard_map/ppermute | solution.py:440
  157.1 3.0 %collective-permute-start.42 = (bf16[64,2048]{1,0:T(8,128)(2,1)S(1)}, bf16[64,2048]{1,0:T(8,128)(2,1)S(1)}, u32[]{:S(2)}, u32[]{:S(2)}) collective-permute-start(bf16[64,2048]{1,0:T(8,128)(2,1)S(1)} %fusion.1), channel_id=1, source_target_pairs={{0,12},{2,14},{4,0},{6,2},{8,4},{10,6},{12,8},{14,10},{1,13},{3,15... | collective-permute-start | bytes 786440 | tf_op jit(solution)/shard_map/ppermute | solution.py:441
  161.4 8.0 %collective-permute-done.39 = bf16[64,2048]{1,0:T(8,128)(2,1)S(1)} collective-permute-done((bf16[64,2048]{1,0:T(8,128)(2,1)S(1)}, bf16[64,2048]{1,0:T(8,128)(2,1)S(1)}, u32[]{:S(2)}, u32[]{:S(2)}) %collective-permute-start.39) | collective-permute-done | bytes 262176 | tf_op jit(solution)/shard_map/ppermute | solution.py:441
  (104 shorter events, 29.2 us)
Async XLA Ops:
  2.2 29.7 %collective-permute-start.3 = (bf16[144,256]{1,0:T(8,128)(2,1)}, bf16[144,256]{1,0:T(8,128)(2,1)S(1)}, u32[]{:S(2)}, u32[]{:S(2)}) collective-permute-start(bf16[144,256]{1,0:T(8,128)(2,1)} %get-tuple-element.43), channel_id=1, source_target_pairs={{0,2},{2,0},{4,6},{6,4},{8,10},{10,8},{12,14},{14,12},{1,3},{3,1},... | collective-permute-start | bytes 221192 | tf_op jit(solution)/shard_map/ppermute | solution.py:244
  5.2 26.7 %collective-permute-start = (bf16[144,768]{1,0:T(8,128)(2,1)}, bf16[144,768]{1,0:T(8,128)(2,1)S(1)}, u32[]{:S(2)}, u32[]{:S(2)}) collective-permute-start(bf16[144,768]{1,0:T(8,128)(2,1)} %get-tuple-element.40), channel_id=1, source_target_pairs={{0,4},{2,6},{4,8},{6,10},{8,12},{10,14},{12,0},{14,2},{1,5},{3,7},... | collective-permute-start | bytes 663560 | tf_op jit(solution)/shard_map/ppermute | solution.py:241
  6.7 17.0 %collective-permute-start.1 = (bf16[144,768]{1,0:T(8,128)(2,1)}, bf16[144,768]{1,0:T(8,128)(2,1)S(1)}, u32[]{:S(2)}, u32[]{:S(2)}) collective-permute-start(bf16[144,768]{1,0:T(8,128)(2,1)} %get-tuple-element.41), channel_id=1, source_target_pairs={{0,8},{2,10},{4,12},{6,14},{8,0},{10,2},{12,4},{14,6},{1,9},{3,11}... | collective-permute-start | bytes 663560 | tf_op jit(solution)/shard_map/ppermute | solution.py:241
  9.3 23.2 %collective-permute-start.2 = (bf16[144,768]{1,0:T(8,128)(2,1)}, bf16[144,768]{1,0:T(8,128)(2,1)S(1)}, u32[]{:S(2)}, u32[]{:S(2)}) collective-permute-start(bf16[144,768]{1,0:T(8,128)(2,1)} %get-tuple-element.42), channel_id=1, source_target_pairs={{0,12},{2,14},{4,0},{6,2},{8,4},{10,6},{12,8},{14,10},{1,13},{3,15... | collective-permute-start | bytes 663560 | tf_op jit(solution)/shard_map/ppermute | solution.py:241
  25.0 13.9 %collective-permute-start.8 = (bf16[256,512]{1,0:T(8,128)(2,1)S(1)}, bf16[256,512]{1,0:T(8,128)(2,1)S(1)}, u32[]{:S(2)}, u32[]{:S(2)}) collective-permute-start(bf16[256,512]{1,0:T(8,128)(2,1)S(1)} %get-tuple-element.49), channel_id=1, source_target_pairs={{0,4},{2,6},{4,8},{6,10},{8,12},{10,14},{12,0},{14,2},{1,5},{3,7},... | collective-permute-start | bytes 786440 | tf_op jit(solution)/shard_map/ppermute | solution.py:249
  28.6 19.2 %collective-permute-start.10 = (bf16[256,512]{1,0:T(8,128)(2,1)S(1)}, bf16[256,512]{1,0:T(8,128)(2,1)S(1)}, u32[]{:S(2)}, u32[]{:S(2)}) collective-permute-start(bf16[256,512]{1,0:T(8,128)(2,1)S(1)} %get-tuple-element.50), channel_id=1, source_target_pairs={{0,8},{2,10},{4,12},{6,14},{8,0},{10,2},{12,4},{14,6},{1,9},{3,11}... | collective-permute-start | bytes 786440 | tf_op jit(solution)/shard_map/ppermute | solution.py:249
  31.9 16.4 %collective-permute-start.12 = (bf16[256,512]{1,0:T(8,128)(2,1)S(1)}, bf16[256,512]{1,0:T(8,128)(2,1)S(1)}, u32[]{:S(2)}, u32[]{:S(2)}) collective-permute-start(bf16[256,512]{1,0:T(8,128)(2,1)S(1)} %get-tuple-element.51), channel_id=1, source_target_pairs={{0,12},{2,14},{4,0},{6,2},{8,4},{10,6},{12,8},{14,10},{1,13},{3,15... | collective-permute-start | bytes 786440 | tf_op jit(solution)/shard_map/ppermute | solution.py:249
  36.6 13.3 %collective-permute-start.6 = (bf16[144,256]{1,0:T(8,128)(2,1)S(1)}, bf16[144,256]{1,0:T(8,128)(2,1)S(1)}, u32[]{:S(2)}, u32[]{:S(2)}) collective-permute-start(bf16[144,256]{1,0:T(8,128)(2,1)S(1)} %slice.52), channel_id=1, source_target_pairs={{0,2},{2,0},{4,6},{6,4},{8,10},{10,8},{12,14},{14,12},{1,3},{3,1},... | collective-permute-start | bytes 221192 | tf_op jit(solution)/shard_map/ppermute | solution.py:244
  38.2 18.0 %collective-permute-start.7 = (bf16[256,512]{1,0:T(8,128)(2,1)S(1)}, bf16[256,512]{1,0:T(8,128)(2,1)S(1)}, u32[]{:S(2)}, u32[]{:S(2)}) collective-permute-start(bf16[256,512]{1,0:T(8,128)(2,1)S(1)} %get-tuple-element.48.refs_4_), channel_id=1, source_target_pairs={{0,2},{2,0},{4,6},{6,4},{8,10},{10,8},{12,14},{14,12},{1,3},{3,1},... | collective-permute-start | bytes 786440 | tf_op jit(solution)/shard_map/ppermute | solution.py:247
  38.9 21.1 %collective-permute-start.9 = (bf16[256,512]{1,0:T(8,128)(2,1)S(1)}, bf16[256,512]{1,0:T(8,128)(2,1)S(1)}, u32[]{:S(2)}, u32[]{:S(2)}) collective-permute-start(bf16[256,512]{1,0:T(8,128)(2,1)S(1)} %collective-permute-done.8.refs_6_), channel_id=1, source_target_pairs={{0,2},{2,0},{4,6},{6,4},{8,10},{10,8},{12,14},{14,12},{1,3},{3,1},... | collective-permute-start | bytes 786440 | tf_op jit(solution)/shard_map/ppermute | solution.py:250
  47.8 12.3 %collective-permute-start.11 = (bf16[256,512]{1,0:T(8,128)(2,1)S(1)}, bf16[256,512]{1,0:T(8,128)(2,1)S(1)}, u32[]{:S(2)}, u32[]{:S(2)}) collective-permute-start(bf16[256,512]{1,0:T(8,128)(2,1)S(1)} %collective-permute-done.10.refs_8_), channel_id=1, source_target_pairs={{0,2},{2,0},{4,6},{6,4},{8,10},{10,8},{12,14},{14,12},{1,3},{3,1},... | collective-permute-start | bytes 786440 | tf_op jit(solution)/shard_map/ppermute | solution.py:250
  48.3 13.2 %collective-permute-start.13 = (bf16[256,512]{1,0:T(8,128)(2,1)S(1)}, bf16[256,512]{1,0:T(8,128)(2,1)S(1)}, u32[]{:S(2)}, u32[]{:S(2)}) collective-permute-start(bf16[256,512]{1,0:T(8,128)(2,1)S(1)} %collective-permute-done.12.refs_10_), channel_id=1, source_target_pairs={{0,2},{2,0},{4,6},{6,4},{8,10},{10,8},{12,14},{14,12},{1,3},{3,1},... | collective-permute-start | bytes 786440 | tf_op jit(solution)/shard_map/ppermute | solution.py:250
  63.5 7.6 %collective-permute-start.15 = (bf16[64,2048]{1,0:T(8,128)(2,1)S(1)}, bf16[64,2048]{1,0:T(8,128)(2,1)S(1)}, u32[]{:S(2)}, u32[]{:S(2)}) collective-permute-start(bf16[64,2048]{1,0:T(8,128)(2,1)S(1)} %get-tuple-element.55), channel_id=1, source_target_pairs={{0,1},{1,0},{2,3},{3,2},{4,5},{5,4},{6,7},{7,6},{8,9},{9,8},{10,11... | collective-permute-start | bytes 786440 | tf_op jit(solution)/shard_map/ppermute | solution.py:263
  65.1 15.7 %collective-permute-start.17 = (bf16[64,2048]{1,0:T(8,128)(2,1)S(1)}, bf16[64,2048]{1,0:T(8,128)(2,1)S(1)}, u32[]{:S(2)}, u32[]{:S(2)}) collective-permute-start(bf16[64,2048]{1,0:T(8,128)(2,1)S(1)} %add_convert_fusion.3), channel_id=1, source_target_pairs={{0,8},{2,10},{4,12},{6,14},{8,0},{10,2},{12,4},{14,6},{1,9},{3,11}... | collective-permute-start | bytes 786440 | tf_op jit(solution)/shard_map/ppermute | solution.py:266
  67.6 13.2 %collective-permute-start.19 = (bf16[64,2048]{1,0:T(8,128)(2,1)S(1)}, bf16[64,2048]{1,0:T(8,128)(2,1)S(1)}, u32[]{:S(2)}, u32[]{:S(2)}) collective-permute-start(bf16[64,2048]{1,0:T(8,128)(2,1)S(1)} %add_convert_fusion.2), channel_id=1, source_target_pairs={{0,12},{2,14},{4,0},{6,2},{8,4},{10,6},{12,8},{14,10},{1,13},{3,15... | collective-permute-start | bytes 786440 | tf_op jit(solution)/shard_map/ppermute | solution.py:266
  71.0 17.7 %collective-permute-start.21 = (bf16[64,2048]{1,0:T(8,128)(2,1)S(1)}, bf16[64,2048]{1,0:T(8,128)(2,1)S(1)}, u32[]{:S(2)}, u32[]{:S(2)}) collective-permute-start(bf16[64,2048]{1,0:T(8,128)(2,1)S(1)} %add_convert_fusion.1), channel_id=1, source_target_pairs={{0,4},{2,6},{4,8},{6,10},{8,12},{10,14},{12,0},{14,2},{1,5},{3,7},... | collective-permute-start | bytes 786440 | tf_op jit(solution)/shard_map/ppermute | solution.py:266
  88.8 9.6 %collective-permute-start.24 = (bf16[64,2048]{1,0:T(8,128)(2,1)S(1)}, bf16[64,2048]{1,0:T(8,128)(2,1)S(1)}, u32[]{:S(2)}, u32[]{:S(2)}) collective-permute-start(bf16[64,2048]{1,0:T(8,128)(2,1)S(1)} %get-tuple-element.64), channel_id=1, source_target_pairs={{0,4},{2,6},{4,8},{6,10},{8,12},{10,14},{12,0},{14,2},{1,5},{3,7},... | collective-permute-start | bytes 786440 | tf_op jit(solution)/shard_map/ppermute | solution.py:421
  92.0 9.4 %collective-permute-start.22 = (bf16[64,2048]{1,0:T(8,128)(2,1)S(1)}, bf16[64,2048]{1,0:T(8,128)(2,1)S(1)}, u32[]{:S(2)}, u32[]{:S(2)}) collective-permute-start(bf16[64,2048]{1,0:T(8,128)(2,1)S(1)} %get-tuple-element.64), channel_id=1, source_target_pairs={{0,2},{2,0},{4,6},{6,4},{8,10},{10,8},{12,14},{14,12},{1,3},{3,1},... | collective-permute-start | bytes 786440 | tf_op jit(solution)/shard_map/ppermute | solution.py:425
  98.4 11.0 %collective-permute-start.27 = (bf16[64,2048]{1,0:T(8,128)(2,1)S(1)}, bf16[64,2048]{1,0:T(8,128)(2,1)S(1)}, u32[]{:S(2)}, u32[]{:S(2)}) collective-permute-start(bf16[64,2048]{1,0:T(8,128)(2,1)S(1)} %collective-permute-done.24), channel_id=1, source_target_pairs={{0,4},{2,6},{4,8},{6,10},{8,12},{10,14},{12,0},{14,2},{1,5},{3,7},... | collective-permute-start | bytes 786440 | tf_op jit(solution)/shard_map/ppermute | solution.py:421
  100.3 10.3 %collective-permute-start.25 = (bf16[64,2048]{1,0:T(8,128)(2,1)S(1)}, bf16[64,2048]{1,0:T(8,128)(2,1)S(1)}, u32[]{:S(2)}, u32[]{:S(2)}) collective-permute-start(bf16[64,2048]{1,0:T(8,128)(2,1)S(1)} %collective-permute-done.24), channel_id=1, source_target_pairs={{0,2},{2,0},{4,6},{6,4},{8,10},{10,8},{12,14},{14,12},{1,3},{3,1},... | collective-permute-start | bytes 786440 | tf_op jit(solution)/shard_map/ppermute | solution.py:425
  101.5 21.8 %collective-permute-start.23 = (bf16[128,2048]{1,0:T(8,128)(2,1)S(1)}, bf16[128,2048]{1,0:T(8,128)(2,1)S(1)}, u32[]{:S(2)}, u32[]{:S(2)}) collective-permute-start(bf16[128,2048]{1,0:T(8,128)(2,1)S(1)} %constant_dynamic-update-slice_fusion.refs_0_), channel_id=1, source_target_pairs={{0,1},{1,0},{2,3},{3,2},{4,5},{5,4},{6,7},{7,6},{8,9},{9,8},{10,11... | collective-permute-start | bytes 1572872 | tf_op jit(solution)/shard_map/ppermute | solution.py:431
  101.6 14.3 %collective-permute-start.31 = (bf16[64,2048]{1,0:T(8,128)(2,1)S(1)}, bf16[64,2048]{1,0:T(8,128)(2,1)S(1)}, u32[]{:S(2)}, u32[]{:S(2)}) collective-permute-start(bf16[64,2048]{1,0:T(8,128)(2,1)S(1)} %collective-permute-done.22), channel_id=1, source_target_pairs={{0,12},{2,14},{4,0},{6,2},{8,4},{10,6},{12,8},{14,10},{1,13},{3,15... | collective-permute-start | bytes 786440 | tf_op jit(solution)/shard_map/ppermute | solution.py:423
  110.6 14.3 %collective-permute-start.26 = (bf16[128,2048]{1,0:T(8,128)(2,1)S(1)}, bf16[128,2048]{1,0:T(8,128)(2,1)S(1)}, u32[]{:S(2)}, u32[]{:S(2)}) collective-permute-start(bf16[128,2048]{1,0:T(8,128)(2,1)S(1)} %constant_dynamic-update-slice_fusion.2.refs_2_), channel_id=1, source_target_pairs={{0,1},{1,0},{2,3},{3,2},{4,5},{5,4},{6,7},{7,6},{8,9},{9,8},{10,11... | collective-permute-start | bytes 1572872 | tf_op jit(solution)/shard_map/ppermute | solution.py:431
  110.6 12.6 %collective-permute-start.30 = (bf16[64,2048]{1,0:T(8,128)(2,1)S(1)}, bf16[64,2048]{1,0:T(8,128)(2,1)S(1)}, u32[]{:S(2)}, u32[]{:S(2)}) collective-permute-start(bf16[64,2048]{1,0:T(8,128)(2,1)S(1)} %collective-permute-done.27), channel_id=1, source_target_pairs={{0,4},{2,6},{4,8},{6,10},{8,12},{10,14},{12,0},{14,2},{1,5},{3,7},... | collective-permute-start | bytes 786440 | tf_op jit(solution)/shard_map/ppermute | solution.py:421
  115.8 9.0 %collective-permute-start.29 = (bf16[128,2048]{1,0:T(8,128)(2,1)S(1)}, bf16[128,2048]{1,0:T(8,128)(2,1)S(1)}, u32[]{:S(2)}, u32[]{:S(2)}) collective-permute-start(bf16[128,2048]{1,0:T(8,128)(2,1)S(1)} %constant_dynamic-update-slice_fusion.4.refs_4_), channel_id=1, source_target_pairs={{0,1},{1,0},{2,3},{3,2},{4,5},{5,4},{6,7},{7,6},{8,9},{9,8},{10,11... | collective-permute-start | bytes 1572872 | tf_op jit(solution)/shard_map/ppermute | solution.py:431
  115.9 7.4 %collective-permute-start.33 = (bf16[64,2048]{1,0:T(8,128)(2,1)S(1)}, bf16[64,2048]{1,0:T(8,128)(2,1)S(1)}, u32[]{:S(2)}, u32[]{:S(2)}) collective-permute-start(bf16[64,2048]{1,0:T(8,128)(2,1)S(1)} %collective-permute-done.31.refs_7_), channel_id=1, source_target_pairs={{0,1},{1,0},{2,3},{3,2},{4,5},{5,4},{6,7},{7,6},{8,9},{9,8},{10,11... | collective-permute-start | bytes 786440 | tf_op jit(solution)/shard_map/ppermute | solution.py:431
  142.2 17.9 %collective-permute-start.36 = (bf16[128,2048]{1,0:T(8,128)(2,1)S(1)}, bf16[128,2048]{1,0:T(8,128)(2,1)S(1)}, u32[]{:S(2)}, u32[]{:S(2)}) collective-permute-start(bf16[128,2048]{1,0:T(8,128)(2,1)S(1)} %add_convert_fusion), channel_id=1, source_target_pairs={{0,4},{2,6},{4,8},{6,10},{8,12},{10,14},{12,0},{14,2},{1,5},{3,7},... | collective-permute-start | bytes 1572872 | tf_op jit(solution)/shard_map/ppermute | solution.py:436
  143.0 9.2 %collective-permute-start.38 = (bf16[64,2048]{1,0:T(8,128)(2,1)S(1)}, bf16[64,2048]{1,0:T(8,128)(2,1)S(1)}, u32[]{:S(2)}, u32[]{:S(2)}) collective-permute-start(bf16[64,2048]{1,0:T(8,128)(2,1)S(1)} %slice.87), channel_id=1, source_target_pairs={{0,2},{2,0},{4,6},{6,4},{8,10},{10,8},{12,14},{14,12},{1,3},{3,1},... | collective-permute-start | bytes 786440 | tf_op jit(solution)/shard_map/ppermute | solution.py:440
  144.5 12.5 %collective-permute-start.41 = (bf16[64,2048]{1,0:T(8,128)(2,1)S(1)}, bf16[64,2048]{1,0:T(8,128)(2,1)S(1)}, u32[]{:S(2)}, u32[]{:S(2)}) collective-permute-start(bf16[64,2048]{1,0:T(8,128)(2,1)S(1)} %slice.86), channel_id=1, source_target_pairs={{0,2},{2,0},{4,6},{6,4},{8,10},{10,8},{12,14},{14,12},{1,3},{3,1},... | collective-permute-start | bytes 786440 | tf_op jit(solution)/shard_map/ppermute | solution.py:440
  152.3 17.1 %collective-permute-start.39 = (bf16[64,2048]{1,0:T(8,128)(2,1)S(1)}, bf16[64,2048]{1,0:T(8,128)(2,1)S(1)}, u32[]{:S(2)}, u32[]{:S(2)}) collective-permute-start(bf16[64,2048]{1,0:T(8,128)(2,1)S(1)} %fusion.2), channel_id=1, source_target_pairs={{0,8},{2,10},{4,12},{6,14},{8,0},{10,2},{12,4},{14,6},{1,9},{3,11}... | collective-permute-start | bytes 786440 | tf_op jit(solution)/shard_map/ppermute | solution.py:441
  157.1 13.1 %collective-permute-start.42 = (bf16[64,2048]{1,0:T(8,128)(2,1)S(1)}, bf16[64,2048]{1,0:T(8,128)(2,1)S(1)}, u32[]{:S(2)}, u32[]{:S(2)}) collective-permute-start(bf16[64,2048]{1,0:T(8,128)(2,1)S(1)} %fusion.1), channel_id=1, source_target_pairs={{0,12},{2,14},{4,0},{6,2},{8,4},{10,6},{12,8},{14,10},{1,13},{3,15... | collective-permute-start | bytes 786440 | tf_op jit(solution)/shard_map/ppermute | solution.py:441
  160.3 9.9 %collective-permute-start.43 = (bf16[64,2048]{1,0:T(8,128)(2,1)S(1)}, bf16[64,2048]{1,0:T(8,128)(2,1)S(1)}, u32[]{:S(2)}, u32[]{:S(2)}) collective-permute-start(bf16[64,2048]{1,0:T(8,128)(2,1)S(1)} %fusion), channel_id=1, source_target_pairs={{0,2},{2,0},{4,6},{6,4},{8,10},{10,8},{12,14},{14,12},{1,3},{3,1},... | collective-permute-start | bytes 786440 | tf_op jit(solution)/shard_map/ppermute | solution.py:443
  (16 other events, 52.4 us)
